TPU v7x, 32 devices: a whole 2x2x4 slice. The times are simulated.
32 devices in a mesh: dp: 8 (over y, x, core), tensor: 4 (over z).
Axes of the slice: x: 2, y: 2, z: 4, core: 2. Of those that a mesh axis runs over, the one named last changes fastest.
Arguments:
- inputs: float32 [8192, 2048], P(('dp', 'tensor')), may hold values from -6 to 6
- lengths: int32 [8], P('dp'), may hold values from 128 to 1024, as said below
- gain_mix: bfloat16 [2048], P(('dp', 'tensor')), may hold values from 0.5 to 1.5
- gain_glu: bfloat16 [2048], P(('dp', 'tensor')), may hold values from 0.5 to 1.5
- lower_bound: bfloat16 [2048], P(('dp', 'tensor')), may hold values from 0 to 0.997
- w_input: bfloat16 [2048, 2048], P(('dp', 'tensor')), may hold values from -0.125 to 0.125
- w_forget: bfloat16 [2048, 2048], P(('dp', 'tensor')), may hold values from -0.125 to 0.125
- w_gate_mix: bfloat16 [2048, 2048], P(('dp', 'tensor')), may hold values from -0.125 to 0.125
- w_out: bfloat16 [2048, 2048], P(('dp', 'tensor')), may hold values from -0.5 to 0.5
- w_gate: bfloat16 [2048, 5632], P('dp', 'tensor'), may hold values from -0.125 to 0.125
- w_up: bfloat16 [2048, 5632], P('dp', 'tensor'), may hold values from -0.125 to 0.125
- w_down: bfloat16 [5632, 2048], P('tensor', 'dp'), may hold values from -0.15625 to 0.15625
- cotangent: float32 [8192, 2048], P(('dp', 'tensor')), may hold values from -6 to 6
Outputs:
- output: float32 [8192, 2048], P(('dp', 'tensor'))
- grad_inputs: float32 [8192, 2048], P(('dp', 'tensor'))
- grad_gain_mix: float32 [2048], P(('dp', 'tensor'))
- grad_gain_glu: float32 [2048], P(('dp', 'tensor'))
- grad_lower_bound: float32 [2048], P(('dp', 'tensor'))
- grad_w_input: float32 [2048, 2048], P(('dp', 'tensor'))
- grad_w_forget: float32 [2048, 2048], P(('dp', 'tensor'))
- grad_w_gate_mix: float32 [2048, 2048], P(('dp', 'tensor'))
- grad_w_out: float32 [2048, 2048], P(('dp', 'tensor'))
- grad_w_gate: float32 [2048, 5632], P('dp', 'tensor')
- grad_w_up: float32 [2048, 5632], P('dp', 'tensor')
- grad_w_down: float32 [5632, 2048], P('tensor', 'dp')
Inputs may be any that keep to these rules, and one draw needn't show every extreme that they name: `lengths`: each entry is the live length of one sequence, its live rows first; in every draw one entry equals 1024.
All inputs are finite; a program needn't handle non-finite values.
Results may differ from a plain program's by a relative error of at most 0.0087.
Values may be sent and summed in bfloat16 or wider, within the bound.
A program may use at most 320 MiB of HBM per device.

v0:
```python
import jax
import jax.numpy as jnp
from jax import lax
from jax.sharding import PartitionSpec as P

epsilon = 1e-06


def matmul(left, right):
    return jnp.dot(left, right, preferred_element_type=jnp.float32)


def matmul_rt(left, right):
    return lax.dot_general(
        left, right, (((1,), (1,)), ((), ())), preferred_element_type=jnp.float32
    )


def matmul_lt(left, right):
    return lax.dot_general(
        left, right, (((0,), (0,)), ((), ())), preferred_element_type=jnp.float32
    )


def silu_of(value):
    return value * jax.nn.sigmoid(value)


def silu_slope(value):
    squash = jax.nn.sigmoid(value)
    return squash * (1.0 + value * (1.0 - squash))


def doubling_scan(coef, drive, reverse):
    total_rows, width = coef.shape
    decay = coef
    state = drive
    stride = 1
    while stride < total_rows:
        ones_rows = jnp.ones((stride, width), jnp.float32)
        zero_rows = jnp.zeros((stride, width), jnp.float32)
        if reverse:
            other_decay = jnp.concatenate([decay[stride:], ones_rows], axis=0)
            other_state = jnp.concatenate([state[stride:], zero_rows], axis=0)
        else:
            other_decay = jnp.concatenate([ones_rows, decay[:-stride]], axis=0)
            other_state = jnp.concatenate([zero_rows, state[:-stride]], axis=0)
        state = decay * other_state + state
        decay = decay * other_decay
        stride = stride * 2
    return (decay, state)


def norm_rows(value):
    scale = lax.rsqrt(jnp.mean(value * value, axis=-1, keepdims=True) + epsilon)
    return (scale, value * scale)


def mixer_front(normed, input_w, forget_w, gate_w, bound):
    input_pre = matmul(normed, input_w)
    forget_pre = matmul(normed, forget_w)
    gate_pre = matmul(normed, gate_w)
    forget_sig = jax.nn.sigmoid(forget_pre)
    forget = bound + (1.0 - bound) * forget_sig
    return (input_pre, gate_pre, forget_sig, forget, silu_of(input_pre), silu_of(gate_pre))


def recurrence_back(carried, prior_state, live, forget, forget_sig, input_act, input_pre, bound):
    grad_forget = carried * prior_state - carried * live * input_act
    grad_input_pre = (carried * live * (1.0 - forget) * silu_slope(input_pre)).astype(jnp.bfloat16)
    grad_bound = jnp.sum(grad_forget * (1.0 - forget_sig), axis=0)
    grad_forget_pre = (grad_forget * (1.0 - bound) * forget_sig * (1.0 - forget_sig)).astype(
        jnp.bfloat16
    )
    return (grad_input_pre, grad_forget_pre, grad_bound)


def norm_back(grad_norm, unit, scale, gain):
    scaled = grad_norm * gain
    return scale * (scaled - unit * jnp.mean(scaled * unit, axis=-1, keepdims=True))


def on_device(
    inputs,
    lengths,
    gain_mix,
    gain_glu,
    lower_bound,
    w_input,
    w_forget,
    w_gate_mix,
    w_out,
    w_gate,
    w_up,
    w_down,
    cotangent,
):
    tensor_parts = lax.axis_size("tensor")
    data_parts = lax.axis_size("dp")
    tensor_index = lax.axis_index("tensor")
    rows_here = inputs.shape[0]
    width = inputs.shape[1]
    seq_len = rows_here * tensor_parts
    block = width // (data_parts * tensor_parts)
    full_input_w, full_forget_w, full_gate_w, full_out_w, gain_one, gain_two, bound_low = (
        lax.all_gather(w_input, ("dp", "tensor"), axis=0, tiled=True),
        lax.all_gather(w_forget, ("dp", "tensor"), axis=0, tiled=True),
        lax.all_gather(w_gate_mix, ("dp", "tensor"), axis=0, tiled=True),
        lax.all_gather(w_out, ("dp", "tensor"), axis=0, tiled=True),
        lax.all_gather(gain_mix, ("dp", "tensor"), axis=0, tiled=True),
        lax.all_gather(gain_glu, ("dp", "tensor"), axis=0, tiled=True),
        lax.all_gather(lower_bound, ("dp", "tensor"), axis=0, tiled=True),
    )
    gain_one = gain_one.astype(jnp.float32)
    gain_two = gain_two.astype(jnp.float32)
    bound = bound_low.astype(jnp.float32)
    glu_gate_w, glu_up_w, glu_down_w = (
        lax.all_gather(w_gate, "dp", axis=0, tiled=True),
        lax.all_gather(w_up, "dp", axis=0, tiled=True),
        lax.all_gather(w_down, "dp", axis=1, tiled=True),
    )
    position = jnp.arange(seq_len, dtype=jnp.int32)
    live_mask = (position < lengths[0]).astype(jnp.float32)[:, None]

    def mine(value):
        return lax.dynamic_slice_in_dim(value, tensor_index * rows_here, rows_here, 0)

    def pick_cols(value):
        shaped = value.reshape(value.shape[0], data_parts, tensor_parts, block)
        taken = lax.dynamic_index_in_dim(shaped, tensor_index, axis=2, keepdims=False)
        return taken.reshape(value.shape[0], data_parts * block)

    def pick_vec(value):
        return pick_cols(value[None, :])[0]

    live_own = mine(live_mask)
    full_input = lax.all_gather(inputs, "tensor", axis=0, tiled=True)
    scale_one, unit_one = norm_rows(full_input)
    normed_one = (unit_one * gain_one).astype(jnp.bfloat16)
    input_pre, gate_pre, forget_sig, forget, input_act, gate_act = mixer_front(
        normed_one, full_input_w, full_forget_w, full_gate_w, bound
    )
    inflow = live_mask * (1.0 - forget) * input_act
    _, state = doubling_scan(forget, inflow, False)
    mixed_low = (state * gate_act).astype(jnp.bfloat16)
    stream = full_input + matmul(mixed_low, full_out_w)
    scale_two, unit_two = norm_rows(stream)
    normed_two = (unit_two * gain_two).astype(jnp.bfloat16)
    stream_own = mine(stream)
    glu_gate = matmul(normed_two, glu_gate_w)
    glu_up = matmul(normed_two, glu_up_w)
    hidden = (silu_of(glu_gate) * glu_up).astype(jnp.bfloat16)
    glu_rows = lax.psum_scatter(
        matmul(hidden, glu_down_w), "tensor", scatter_dimension=0, tiled=True
    )
    output = live_own * (stream_own + glu_rows)
    upstream = lax.all_gather(cotangent, "tensor", axis=0, tiled=True)
    masked_grad = live_mask * upstream
    masked_low = masked_grad.astype(jnp.bfloat16)
    grad_down = matmul_lt(hidden, masked_low)
    grad_hidden = matmul_rt(masked_low, glu_down_w)
    grad_gate_low = (grad_hidden * glu_up * silu_slope(glu_gate)).astype(jnp.bfloat16)
    grad_up_low = (grad_hidden * silu_of(glu_gate)).astype(jnp.bfloat16)
    grad_gate_w = matmul_lt(normed_two, grad_gate_low)
    grad_up_w = matmul_lt(normed_two, grad_up_low)
    grad_norm_two = matmul_rt(grad_gate_low, glu_gate_w) + matmul_rt(grad_up_low, glu_up_w)
    grad_gate_mine, grad_up_mine, grad_down_mine = (
        lax.psum_scatter(grad_gate_w, "dp", scatter_dimension=0, tiled=True),
        lax.psum_scatter(grad_up_w, "dp", scatter_dimension=0, tiled=True),
        lax.psum_scatter(grad_down, "dp", scatter_dimension=1, tiled=True),
    )
    gain_two_part = jnp.sum(grad_norm_two * unit_two, axis=0)
    stream_part = norm_back(grad_norm_two, unit_two, scale_two, gain_two)
    gain_two_blocks = (
        gain_two_part.reshape(data_parts, tensor_parts, block)
        .transpose(1, 0, 2)
        .reshape(tensor_parts, data_parts * block)
    )
    stream_rows, gain_two_sum = (
        lax.psum_scatter(stream_part, "tensor", scatter_dimension=0, tiled=True),
        lax.psum_scatter(gain_two_blocks, "tensor", scatter_dimension=0, tiled=True),
    )
    stream_rows = stream_rows + mine(masked_grad)
    grad_stream = lax.all_gather(stream_rows, "tensor", axis=0, tiled=True)
    stream_low = grad_stream.astype(jnp.bfloat16)
    grad_out_w = matmul_lt(pick_cols(mixed_low), stream_low)
    grad_mixed = matmul_rt(stream_low, full_out_w)
    grad_gate_pre = (grad_mixed * state * silu_slope(gate_pre)).astype(jnp.bfloat16)
    grad_state = grad_mixed * gate_act
    zero_row = jnp.zeros((1, width), jnp.float32)
    next_forget = jnp.concatenate([forget[1:], zero_row], axis=0)
    _, carried = doubling_scan(next_forget, grad_state, True)
    prior_state = jnp.concatenate([zero_row, state[:-1]], axis=0)
    grad_input_pre, grad_forget_pre, grad_bound = recurrence_back(
        carried, prior_state, live_mask, forget, forget_sig, input_act, input_pre, bound
    )
    normed_pick = pick_cols(normed_one)
    grad_input_w = matmul_lt(normed_pick, grad_input_pre)
    grad_forget_w = matmul_lt(normed_pick, grad_forget_pre)
    grad_gmix_w = matmul_lt(normed_pick, grad_gate_pre)
    grad_norm_one = (
        matmul_rt(grad_input_pre, full_input_w)
        + matmul_rt(grad_forget_pre, full_forget_w)
        + matmul_rt(grad_gate_pre, full_gate_w)
    )
    gain_one_grad = jnp.sum(grad_norm_one * unit_one, axis=0)
    grad_full = grad_stream + norm_back(grad_norm_one, unit_one, scale_one, gain_one)
    grad_inputs = mine(grad_full)
    gin_w, gfo_w, ggm_w, gout_w, gone, gtwo, gbound = (
        lax.psum_scatter(grad_input_w, "dp", scatter_dimension=0, tiled=True),
        lax.psum_scatter(grad_forget_w, "dp", scatter_dimension=0, tiled=True),
        lax.psum_scatter(grad_gmix_w, "dp", scatter_dimension=0, tiled=True),
        lax.psum_scatter(grad_out_w, "dp", scatter_dimension=0, tiled=True),
        lax.psum_scatter(pick_vec(gain_one_grad), "dp", scatter_dimension=0, tiled=True),
        lax.psum_scatter(gain_two_sum[0], "dp", scatter_dimension=0, tiled=True),
        lax.psum_scatter(pick_vec(grad_bound), "dp", scatter_dimension=0, tiled=True),
    )
    return (
        output,
        grad_inputs,
        gone,
        gtwo,
        gbound,
        gin_w,
        gfo_w,
        ggm_w,
        gout_w,
        grad_gate_mine,
        grad_up_mine,
        grad_down_mine,
    )


def solution(mesh):
    placed = (
        P(("dp", "tensor"), None),
        P("dp"),
        P(("dp", "tensor")),
        P(("dp", "tensor")),
        P(("dp", "tensor")),
        P(("dp", "tensor"), None),
        P(("dp", "tensor"), None),
        P(("dp", "tensor"), None),
        P(("dp", "tensor"), None),
        P("dp", "tensor"),
        P("dp", "tensor"),
        P("tensor", "dp"),
        P(("dp", "tensor"), None),
    )
    return jax.shard_map(
        on_device,
        mesh=mesh,
        in_specs=placed,
        out_specs=(
            P(("dp", "tensor"), None),
            P(("dp", "tensor"), None),
            P(("dp", "tensor")),
            P(("dp", "tensor")),
            P(("dp", "tensor")),
            P(("dp", "tensor"), None),
            P(("dp", "tensor"), None),
            P(("dp", "tensor"), None),
            P(("dp", "tensor"), None),
            P("dp", "tensor"),
            P("dp", "tensor"),
            P("tensor", "dp"),
        ),
        check_vma=False,
    )
```

profile of v0, /device:TPU:0, one launch (start us, length us, event | category | flops | bytes accessed | tf_op | source)
XLA Modules:
  0.0 1812.3 jit_solution(9793494873875599918)
XLA Ops:
  16.0 51.0 %all-reduce.48 = (bf16[2048]{0:T(1024)(128)(2,1)S(1)}, bf16[2048]{0:T(1024)(128)(2,1)S(1)}, bf16[2048]{0:T(1024)(128)(2,1)S(1)}) all-reduce(bf16[2048]{0:T(1024)(128)(2,1)S(1)} %dynamic-update-slice.1, bf16[2048]{0:T(1024)(128)(2,1)S(1)} %dynamic-update-slice, ...), channel_id=1, replica_groups=mesh['dp'=8,'tensor'=4] {'dp','tensor'}, use_global_device_ids=true, to_apply=%add.41 | all-reduce | flops 6144 | bytes 24576
  68.3 94.7 %all-gather.11.cloned.1.call-done = f32[1024,2048]{1,0:T(8,128)} async-done(((f32[256,2048]{1,0:T(8,128)}), f32[1024,2048]{1,0:T(8,128)}) %all-gather.11.cloned.1.call-update) | async-done | bytes 8388624 | tf_op jit(solution)/shard_map/all_gather | solution.py:137
  174.4 67.2 %all-gather.13.cloned.1.call-done = bf16[2048,2048]{1,0:T(8,128)(2,1)} async-done(((bf16[64,2048]{1,0:T(8,128)(2,1)}), bf16[2048,2048]{1,0:T(8,128)(2,1)}) %all-gather.13.cloned.1.call-update) | async-done | bytes 8388624 | tf_op jit(solution)/shard_map/all_gather | solution.py:107
  241.6 15.3 add_divide_fusion.2
  256.9 134.5 %all-gather.27.cloned.1.call-done = f32[1024,2048]{1,0:T(8,128)} async-done(((f32[256,2048]{1,0:T(8,128)}), f32[1024,2048]{1,0:T(8,128)}) %all-gather.27.cloned.1.call-update) | async-done | bytes 8388624 | tf_op jit(solution)/shard_map/all_gather | solution.py:157
  391.4 78.4 %all-gather.15.cloned.1.call-done = bf16[2048,2048]{1,0:T(8,128)(2,1)} async-done(((bf16[64,2048]{1,0:T(8,128)(2,1)}), bf16[2048,2048]{1,0:T(8,128)(2,1)}) %all-gather.15.cloned.1.call-update) | async-done | bytes 8388624 | tf_op jit(solution)/shard_map/all_gather | solution.py:106
  469.9 25.0 %multiply_multiply_fusion = (f32[1024,2048]{1,0:T(8,128)}, f32[1024,2048]{1,0:T(8,128)}, f32[1024,2048]{1,0:T(8,128)}, f32[1024,2048]{1,0:T(8,128)}) fusion(f32[1024]{0:T(1024)S(1)} %fusion.13, f32[1024,2048]{1,0:T(8,128)} %add_divide_fusion.2, f32[2048]{0:T(1024)S(1)} %broadcast_subtract_fusion, f32[2048]{0:T(1024)S(1)} %convert_element_type.50, ...), kind=kOutput, calls=%fused_computation.46 | convolution fusion | flops 8610906112 | bytes 62935040 | tf_op jit(solution)/shard_map/dot_general | solution.py:10
  494.8 13.9 fusion.14
  516.6 20.7 %multiply_add_fusion.18 = (f32[1024,2048]{1,0:T(8,128)}, f32[1024,2048]{1,0:T(8,128)}) fusion(f32[1024,2048]{1,0:T(8,128)} %multiply_add_fusion.19, f32[1022,2048]{1,0:T(8,128)} %bitcast.63, f32[1024,2048]{1,0:T(8,128)} %get-tuple-element.59, f32[1023,2048]{1,0:T(8,128)} %get-tuple-element.68), kind=kLoop, calls=%fused_computation.42 | loop fusion | flops 6291456 | bytes 50307072 | tf_op jit(solution)/shard_map/add | solution.py:48
  537.3 19.6 %multiply_add_fusion.17 = (f32[1024,2048]{1,0:T(8,128)}, f32[1024,2048]{1,0:T(8,128)}) fusion(f32[1024,2048]{1,0:T(8,128)} %get-tuple-element.56, f32[1020,2048]{1,0:T(8,128)} %bitcast.61, f32[1024,2048]{1,0:T(8,128)} %get-tuple-element.57, f32[1022,2048]{1,0:T(8,128)} %bitcast.62), kind=kLoop, calls=%fused_computation.41 | loop fusion | flops 6291456 | bytes 50282496 | tf_op jit(solution)/shard_map/add | solution.py:48
  556.9 8.0 slice.172
  564.8 18.4 %multiply_add_fusion.16 = (f32[1024,2048]{1,0:T(8,128)}, f32[1024,2048]{1,0:T(8,128)}) fusion(f32[1024,2048]{1,0:T(8,128)} %get-tuple-element.54, f32[1016,2048]{1,0:T(8,128)} %slice.172, f32[1024,2048]{1,0:T(8,128)} %get-tuple-element.55, f32[1020,2048]{1,0:T(8,128)} %bitcast.60), kind=kLoop, calls=%fused_computation.40 | loop fusion | flops 6291456 | bytes 50233344 | tf_op jit(solution)/shard_map/add | solution.py:48
  583.2 7.9 slice.173
  595.4 20.5 %multiply_add_fusion.15 = (f32[1024,2048]{1,0:T(8,128)}, f32[1024,2048]{1,0:T(8,128)}) fusion(f32[1024,2048]{1,0:T(8,128)} %get-tuple-element.52, f32[1008,2048]{1,0:T(8,128)} %slice.173, f32[1024,2048]{1,0:T(8,128)} %get-tuple-element.53, f32[1016,2048]{1,0:T(8,128)} %slice.163), kind=kLoop, calls=%fused_computation.39 | loop fusion | flops 6291456 | bytes 50135040 | tf_op jit(solution)/shard_map/add | solution.py:48
  615.9 7.8 slice.174
  628.0 20.4 %multiply_add_fusion.14 = (f32[1024,2048]{1,0:T(8,128)}, f32[1024,2048]{1,0:T(8,128)}) fusion(f32[1024,2048]{1,0:T(8,128)} %get-tuple-element.50, f32[992,2048]{1,0:T(8,128)} %slice.174, f32[1024,2048]{1,0:T(8,128)} %get-tuple-element.51, f32[1008,2048]{1,0:T(8,128)} %slice.164), kind=kLoop, calls=%fused_computation.38 | loop fusion | flops 6291456 | bytes 49938432 | tf_op jit(solution)/shard_map/add | solution.py:48
  648.4 8.4 slice.175
  661.9 19.5 %multiply_add_fusion.13 = (f32[1024,2048]{1,0:T(8,128)}, f32[1024,2048]{1,0:T(8,128)}) fusion(f32[1024,2048]{1,0:T(8,128)} %get-tuple-element.48, f32[960,2048]{1,0:T(8,128)} %slice.175, f32[1024,2048]{1,0:T(8,128)} %get-tuple-element.49, f32[992,2048]{1,0:T(8,128)} %slice.165), kind=kLoop, calls=%fused_computation.37 | loop fusion | flops 6291456 | bytes 49545216 | tf_op jit(solution)/shard_map/add | solution.py:48
  692.4 20.3 %multiply_add_fusion.12 = (f32[1024,2048]{1,0:T(8,128)}, f32[1024,2048]{1,0:T(8,128)}) fusion(f32[1024,2048]{1,0:T(8,128)} %get-tuple-element.46, f32[896,2048]{1,0:T(8,128)} %slice.176, f32[1024,2048]{1,0:T(8,128)} %get-tuple-element.47, f32[960,2048]{1,0:T(8,128)} %slice.166), kind=kLoop, calls=%fused_computation.36 | loop fusion | flops 6291456 | bytes 48758784 | tf_op jit(solution)/shard_map/add | solution.py:48
  722.0 15.3 multiply_add_fusion.11
  746.8 25.4 %multiply_convert_fusion.4 = (bf16[1024,2048]{1,0:T(8,128)(2,1)}, f32[1024,2048]{1,0:T(8,128)}, f32[1024,2048]{1,0:T(8,128)}) fusion(f32[1024,2048]{1,0:T(8,128)} %get-tuple-element.42, f32[512,2048]{1,0:T(8,128)} %slice.178, f32[1024,2048]{1,0:T(8,128)} %get-tuple-element.43, f32[768,2048]{1,0:T(8,128)} %slice.168, ...), kind=kOutput, calls=%fused_computation.31 | convolution fusion | flops 8608808960 | bytes 60817408 | tf_op jit(solution)/shard_map/dot_general | solution.py:10
  772.2 13.9 multiply_reduce_fusion.5
  792.1 11.7 fusion.15
  803.8 12.1 fusion.16
  815.9 16.6 multiply_convert_fusion.6
  832.5 11.9 fusion.18
  844.4 16.8 multiply_reduce_fusion.1
  867.8 143.6 %reduce-scatter.12.cloned.1.call-done = f32[256,2048]{1,0:T(8,128)} async-done(((f32[1024,2048]{1,0:T(8,128)}), f32[256,2048]{1,0:T(8,128)}) %reduce-scatter.12.cloned.1.call-update) | async-done | bytes 2097168 | tf_op jit(solution)/shard_map/reduce_scatter | solution.py:180
  1015.4 11.0 fusion.17
  1026.5 12.3 fusion.24
  1038.8 11.9 fusion.25
  1064.0 9.7 slice_multiply_fusion
  1073.7 9.1 fusion.8
  1082.9 83.0 %all-gather.29.cloned.1.call-done = f32[1024,2048]{1,0:T(8,128)} async-done(((f32[256,2048]{1,0:T(8,128)}), f32[1024,2048]{1,0:T(8,128)}) %all-gather.29.cloned.1.call-update) | async-done | bytes 8388624 | tf_op jit(solution)/shard_map/all_gather | solution.py:184
  1165.9 23.9 %multiply_convert_fusion = (bf16[1024,2048]{1,0:T(8,128)(2,1)}, f32[1024,2048]{1,0:T(8,128)}) fusion(f32[1024,2048]{1,0:T(8,128)} %get-tuple-element.71, f32[1024,2048]{1,0:T(8,128)} %get-tuple-element.41, bf16[2048,2048]{1,0:T(8,128)(2,1)} %all-gather.19.cloned.1.call-done, f32[1024,2048]{1,0:T(8,128)} %all-gather.29.cloned.1.call-done), kind=kOutput, calls=%fused_computation.5 | convolution fusion | flops 8617197568 | bytes 46137344 | tf_op jit(solution)/shard_map/dot_general | solution.py:14
  1189.8 8.6 slice.189
  1198.4 13.8 multiply_add_fusion.9
  1212.2 8.5 slice.190
  1220.7 14.1 multiply_add_fusion.8
  1234.8 8.7 slice.191
  1243.5 23.1 %multiply_add_fusion.7 = (f32[1024,2048]{1,0:T(8,128)}, f32[1024,2048]{1,0:T(8,128)}) fusion(f32[1024,2048]{1,0:T(8,128)} %multiply_add_fusion.8, f32[1020,2048]{1,0:T(8,128)} %slice.191, f32[1022,2048]{1,0:T(8,128)} %slice_multiply_fusion, f32[1023,2048]{1,0:T(8,128)} %copy-done.1, f32[1023,2048]{1,0:T(8,128)} %get-tuple-element.67), kind=kLoop, calls=%fused_computation.17 | loop fusion | flops 8388608 | bytes 58654720 | tf_op jit(solution)/shard_map/add | solution.py:48
  1266.6 8.0 slice.192
  1278.8 19.3 %multiply_add_fusion.6 = (f32[1024,2048]{1,0:T(8,128)}, f32[1024,2048]{1,0:T(8,128)}) fusion(f32[1024,2048]{1,0:T(8,128)} %get-tuple-element.38, f32[1016,2048]{1,0:T(8,128)} %slice.192, f32[1024,2048]{1,0:T(8,128)} %get-tuple-element.39, f32[1020,2048]{1,0:T(8,128)} %slice.182), kind=kLoop, calls=%fused_computation.16 | loop fusion | flops 6291456 | bytes 50233344 | tf_op jit(solution)/shard_map/add | solution.py:48
  1298.1 7.9 slice.193
  1310.2 20.2 %multiply_add_fusion.5 = (f32[1024,2048]{1,0:T(8,128)}, f32[1024,2048]{1,0:T(8,128)}) fusion(f32[1024,2048]{1,0:T(8,128)} %get-tuple-element.36, f32[1008,2048]{1,0:T(8,128)} %slice.193, f32[1024,2048]{1,0:T(8,128)} %get-tuple-element.37, f32[1016,2048]{1,0:T(8,128)} %slice.183), kind=kLoop, calls=%fused_computation.15 | loop fusion | flops 6291456 | bytes 50135040 | tf_op jit(solution)/shard_map/add | solution.py:48
  1330.4 8.9 slice.194
  1344.0 20.5 %multiply_add_fusion.4 = (f32[1024,2048]{1,0:T(8,128)}, f32[1024,2048]{1,0:T(8,128)}) fusion(f32[1024,2048]{1,0:T(8,128)} %get-tuple-element.34, f32[992,2048]{1,0:T(8,128)} %slice.194, f32[1024,2048]{1,0:T(8,128)} %get-tuple-element.35, f32[1008,2048]{1,0:T(8,128)} %slice.184), kind=kLoop, calls=%fused_computation.14 | loop fusion | flops 6291456 | bytes 49938432 | tf_op jit(solution)/shard_map/add | solution.py:48
  1364.5 7.6 slice.195
  1376.2 20.8 %multiply_add_fusion.3 = (f32[1024,2048]{1,0:T(8,128)}, f32[1024,2048]{1,0:T(8,128)}) fusion(f32[1024,2048]{1,0:T(8,128)} %get-tuple-element.32, f32[960,2048]{1,0:T(8,128)} %slice.195, f32[1024,2048]{1,0:T(8,128)} %get-tuple-element.33, f32[992,2048]{1,0:T(8,128)} %slice.185), kind=kLoop, calls=%fused_computation.13 | loop fusion | flops 6291456 | bytes 49545216 | tf_op jit(solution)/shard_map/add | solution.py:48
  1404.8 17.0 multiply_add_fusion.2
  1433.8 13.7 multiply_add_fusion.1
  1456.2 21.6 %multiply_reduce_fusion = (f32[2048]{0:T(1024)S(1)}, f32[1024,2048]{1,0:T(8,128)}, f32[1024,2048]{1,0:T(8,128)}) fusion(f32[1024,2048]{1,0:T(8,128)} %add_divide_fusion.2, f32[1024,2048]{1,0:T(8,128)} %get-tuple-element.70, f32[1024]{0:T(1024)S(1)} %copy-done.17, f32[1023,2048]{1,0:T(8,128)} %bitcast.79, f32[1024,2048]{1,0:T(8,128)} %get-tuple-element.26, ...), kind=kLoop, calls=%fused_computation.1 | loop fusion | flops 29358080 | bytes 69210112 | tf_op jit(solution)/shard_map/reduce_sum | solution.py:71
  1477.8 8.1 multiply_convert_fusion.2
  1506.3 7.8 fusion.23
  1523.4 9.3 all-reduce.44
  1538.8 8.1 fusion.4
  1547.0 15.1 fusion.19
  1562.1 13.4 fusion.20
  1575.4 20.4 %multiply_reduce_fusion.2 = (f32[2048]{0:T(1024)S(1)}, f32[1024]{0:T(1024)S(1)}, f32[1024,2048]{1,0:T(8,128)}) fusion(f32[1024,2048]{1,0:T(8,128)} %get-tuple-element.61, f32[2048]{0:T(1024)S(1)} %copy-done.19, bf16[1024,2048]{1,0:T(8,128)(2,1)} %get-tuple-element.62, bf16[2048,2048]{1,0:T(8,128)(2,1)} %all-gather.17.cloned.1.call-done, ...), kind=kOutput, calls=%fused_computation.3 | convolution fusion | flops 8604611584 | bytes 46157824 | tf_op jit(solution)/shard_map/dot_general | solution.py:14
  1596.3 13.1 all-reduce.47
  1615.8 23.3 %reduce-scatter.14.cloned.1.call-done = f32[64,2048]{1,0:T(8,128)} async-done(((f32[512,2048]{1,0:T(8,128)}), f32[64,2048]{1,0:T(8,128)}) %reduce-scatter.14.cloned.1.call-update) | async-done | bytes 524304 | tf_op jit(solution)/shard_map/reduce_scatter | solution.py:210
  1639.1 55.5 %reduce-scatter.16.cloned.1.call-done = f32[64,2048]{1,0:T(8,128)} async-done(((f32[512,2048]{1,0:T(8,128)}), f32[64,2048]{1,0:T(8,128)}) %reduce-scatter.16.cloned.1.call-update) | async-done | bytes 524304 | tf_op jit(solution)/shard_map/reduce_scatter | solution.py:211
  1694.6 55.1 %reduce-scatter.18.cloned.1.call-done = f32[64,2048]{1,0:T(8,128)} async-done(((f32[512,2048]{1,0:T(8,128)}), f32[64,2048]{1,0:T(8,128)}) %reduce-scatter.18.cloned.1.call-update) | async-done | bytes 524304 | tf_op jit(solution)/shard_map/reduce_scatter | solution.py:212
  1749.7 55.6 %reduce-scatter.20.cloned.1.call-done = f32[64,2048]{1,0:T(8,128)} async-done(((f32[512,2048]{1,0:T(8,128)}), f32[64,2048]{1,0:T(8,128)}) %reduce-scatter.20.cloned.1.call-update) | async-done | bytes 524304 | tf_op jit(solution)/shard_map/reduce_scatter | solution.py:213
  (221 shorter events, 189.4 us)
Async XLA Ops:
  7.2 155.8 %all-gather.11.cloned.1.call-start = ((), (), s32[]{:S(2)}) async-start(), calls=%async_computation.9 | async-start | bytes 10485760 | tf_op jit(solution)/shard_map/all_gather | solution.py:137
  7.9 233.7 %all-gather.13.cloned.1.call-start = ((), (), s32[]{:S(2)}) async-start(), calls=%async_computation.10 | async-start | bytes 8650752 | tf_op jit(solution)/shard_map/all_gather | solution.py:107
  8.7 382.8 %all-gather.27.cloned.1.call-start = ((), (), s32[]{:S(2)}) async-start(), calls=%async_computation.18 | async-start | bytes 10485760 | tf_op jit(solution)/shard_map/all_gather | solution.py:157
  9.4 460.5 %all-gather.15.cloned.1.call-start = ((), (), s32[]{:S(2)}) async-start(), calls=%async_computation.11 | async-start | bytes 8650752 | tf_op jit(solution)/shard_map/all_gather | solution.py:106
  10.0 736.8 %all-gather.17.cloned.1.call-start = ((), (), s32[]{:S(2)}) async-start(), calls=%async_computation.12 | async-start | bytes 8650752 | tf_op jit(solution)/shard_map/all_gather | solution.py:108
  10.6 761.6 %all-gather.19.cloned.1.call-start = ((), (), s32[]{:S(2)}) async-start(), calls=%async_computation.13 | async-start | bytes 8650752 | tf_op jit(solution)/shard_map/all_gather | solution.py:109
  11.1 781.0 %all-gather.21.cloned.1.call-start = ((), (), s32[]{:S(2)}) async-start(), calls=%async_computation.14 | async-start | bytes 6488064 | tf_op jit(solution)/shard_map/all_gather | solution.py:118
  11.9 791.9 %all-gather.23.cloned.1.call-start = ((), (), s32[]{:S(2)}) async-start(), calls=%async_computation.15 | async-start | bytes 6488064 | tf_op jit(solution)/shard_map/all_gather | solution.py:119
  12.6 803.2 %all-gather.25.cloned.1.call-start = ((), (), s32[]{:S(2)}) async-start(), calls=%async_computation.16 | async-start | bytes 6488064 | tf_op jit(solution)/shard_map/all_gather | solution.py:120
  13.4 998.1 %reduce-scatter.12.cloned.1.call-start = ((), (), s32[]{:S(2)}) async-start(), calls=%async_computation.19 | async-start | bytes 10485760 | tf_op jit(solution)/shard_map/reduce_scatter | solution.py:180
  66.9 402.9 %copy-start.20 = (f32[2048]{0:T(1024)}, f32[2048]{0:T(1024)S(1)}, u32[]{:S(2)}) copy-start(f32[2048]{0:T(1024)S(1)} %broadcast_subtract_fusion) | copy-start | bytes 24580
  67.6 402.2 %copy-start.16 = (f32[1024]{0:T(1024)}, f32[1024]{0:T(1024)S(1)}, u32[]{:S(2)}) copy-start(f32[1024]{0:T(1024)S(1)} %fusion.13) | copy-start | bytes 12292
  67.6 106.8 %copy-start.18 = (f32[2048]{0:T(1024)}, f32[2048]{0:T(1024)S(1)}, u32[]{:S(2)}) copy-start(f32[2048]{0:T(1024)S(1)} %convert_element_type.51) | copy-start | bytes 24580
  163.0 5.8 copy-start.8
  494.8 13.9 copy-start
  494.8 16.6 copy-start.9
  583.2 7.9 slice-start.8
  583.2 7.9 slice-start.9
  615.9 7.8 slice-start.10
  615.9 7.8 slice-start.11
  648.4 8.4 slice-start.14
  648.4 9.4 slice-start.15
  681.5 7.2 copy-start.2
  712.8 5.3 copy-start.4
  737.3 6.4 copy-start.10
  772.2 17.2 copy-start.15
  786.0 3.3 copy-start.7
  832.5 28.7 %slice-start.18 = ((s8[8388608]{0:T(1024)(128)(4,1)}), s8[4194304]{0:T(1024)(128)(4,1)S(1)}, s32[]{:S(2)}) async-start(s8[8388608]{0:T(1024)(128)(4,1)} %bitcast.76), calls=%async_computation.46 | async-start | bytes 8388608
  844.4 16.8 slice-start.19
  867.8 298.1 %all-gather.29.cloned.1.call-start = ((), (), s32[]{:S(2)}) async-start(), calls=%async_computation.20 | async-start | bytes 10485760 | tf_op jit(solution)/shard_map/all_gather | solution.py:184
  1015.3 519.4 %reduce-scatter.10.cloned.1.call-start = ((), (), s32[]{:S(2)}) async-start(), calls=%async_computation.17 | async-start | bytes 10485760 | tf_op jit(solution)/shard_map/reduce_scatter | solution.py:153
  1026.4 589.4 %reduce-scatter.22.cloned.1.call-start = ((), (), s32[]{:S(2)}) async-start(), calls=%async_computation.25 | async-start | bytes 12976128 | tf_op jit(solution)/shard_map/reduce_scatter | solution.py:168
  1038.8 577.0 %reduce-scatter.24.cloned.1.call-start = ((), (), s32[]{:S(2)}) async-start(), calls=%async_computation.26 | async-start | bytes 12976128 | tf_op jit(solution)/shard_map/reduce_scatter | solution.py:169
  1050.7 565.0 %reduce-scatter.26.cloned.1.call-start = ((), (), s32[]{:S(2)}) async-start(), calls=%async_computation.27 | async-start | bytes 12976128 | tf_op jit(solution)/shard_map/reduce_scatter | solution.py:170
  1059.5 14.2 slice-start.20
  1064.0 9.7 copy-start.1
  1064.0 9.7 slice-start.21
  1082.8 556.3 %reduce-scatter.14.cloned.1.call-start = ((), (), s32[]{:S(2)}) async-start(), calls=%async_computation.21 | async-start | bytes 4718592 | tf_op jit(solution)/shard_map/reduce_scatter | solution.py:210
  1189.7 31.0 %slice-start = ((s8[8388608]{0:T(1024)(128)(4,1)}), s8[4194304]{0:T(1024)(128)(4,1)S(1)}, s32[]{:S(2)}) async-start(s8[8388608]{0:T(1024)(128)(4,1)} %bitcast.54), calls=%async_computation.28 | async-start | bytes 8388608
  1198.4 22.3 %slice-start.1 = ((s8[8388608]{0:T(1024)(128)(4,1)}), s8[4194304]{0:T(1024)(128)(4,1)S(1)}, s32[]{:S(2)}) async-start(s8[8388608]{0:T(1024)(128)(4,1)} %bitcast.54), calls=%async_computation.29 | async-start | bytes 8388608
  1266.6 8.0 slice-start.4
  1266.6 8.0 slice-start.5
  1298.1 7.9 slice-start.6
  1298.1 7.9 slice-start.7
  1330.4 8.9 slice-start.12
  1330.4 8.9 slice-start.13
  1364.5 7.7 slice-start.16
  1364.5 7.7 slice-start.17
  1397.1 7.2 copy-start.3
  1421.8 8.2 copy-start.5
  1447.5 5.0 copy-start.6
  1450.3 5.8 copy-start.17
  1452.5 25.3 %slice-start.2 = ((s8[8388608]{0:T(1024)(128)(4,1)}), s8[4194304]{0:T(1024)(128)(4,1)S(1)}, s32[]{:S(2)}) async-start(s8[8388608]{0:T(1024)(128)(4,1)} %bitcast.56), calls=%async_computation.30 | async-start | bytes 8388608
  1456.2 21.6 %slice-start.3 = ((s8[8388608]{0:T(1024)(128)(4,1)}), s8[4194304]{0:T(1024)(128)(4,1)S(1)}, s32[]{:S(2)}) async-start(s8[8388608]{0:T(1024)(128)(4,1)} %bitcast.56), calls=%async_computation.31 | async-start | bytes 8388608
  1477.8 10.1 copy-start.14
  1487.9 4.5 copy-start.21
  1492.4 202.2 %reduce-scatter.16.cloned.1.call-start = ((), (), s32[]{:S(2)}) async-start(), calls=%async_computation.22 | async-start | bytes 4718592 | tf_op jit(solution)/shard_map/reduce_scatter | solution.py:211
  1506.2 243.5 %reduce-scatter.18.cloned.1.call-start = ((), (), s32[]{:S(2)}) async-start(), calls=%async_computation.23 | async-start | bytes 4718592 | tf_op jit(solution)/shard_map/reduce_scatter | solution.py:212
  1506.3 8.0 copy-start.25
  1506.3 8.6 copy-start.24
  1514.1 9.1 copy-start.23
  1514.1 291.2 %reduce-scatter.20.cloned.1.call-start = ((), (), s32[]{:S(2)}) async-start(), calls=%async_computation.24 | async-start | bytes 4718592 | tf_op jit(solution)/shard_map/reduce_scatter | solution.py:213
  1547.0 15.1 copy-start.12
  1562.1 13.4 copy-start.19
  (3 other events, 4.5 us)
Sparse Core Ops, SparseCore 0:
  9.6 153.3 all-gather.10
  165.9 75.6 all-gather.12
  243.2 148.2 all-gather.26
  394.2 75.6 all-gather.14
  472.6 75.9 all-gather.16
  551.4 75.9 all-gather.18
  629.3 41.8 all-gather.20
  673.2 43.3 all-gather.22
  718.4 44.3 all-gather.24
  867.9 143.5 reduce-scatter.11
  1015.5 150.3 all-gather.28
  1168.1 142.6 reduce-scatter.9
  1314.9 87.5 reduce-scatter.21
  1406.4 86.7 reduce-scatter.23
  1497.1 86.8 reduce-scatter.25
  1587.7 51.3 reduce-scatter.13
  1643.2 51.2 reduce-scatter.15
  1698.4 51.3 reduce-scatter.17
  1754.0 51.2 reduce-scatter.19
where the time goes:
time: 1820 us; the launch traced here: 1810 us
  waiting for transfers between devices  797 us (44%)
  other arithmetic  401 us (22%)
  matrix products  291 us (16%)
  local copies, waits for them, and re-layouts  233 us (13%)
  blocking collectives  73.3 us (4%)
    add x18, other arithmetic, doubling_scan(): state = decay * other_state + state  322 us
    reduce_scatter x1, waiting for transfers between devices, on_device(): lax.psum_scatter(stream_part, 'tensor', scatter_dimension=0, tiled=True)  144 us
    all_gather x1, waiting for transfers between devices, on_device(): upstream = lax.all_gather(cotangent, 'tensor', axis=0, tiled=True)  135 us
    dot_general x7, matrix products, matmul_rt(): lax.dot_general(left, right, (((1,), (1,)), ((), ())), preferred_element_...  118 us
    dot_general x7, matrix products, matmul(): return jnp.dot(left, right, preferred_element_type=jnp.float32)  114 us
    all_gather x1, waiting for transfers between devices, on_device(): full_input = lax.all_gather(inputs, 'tensor', axis=0, tiled=True)  94.7 us
    all_gather x1, waiting for transfers between devices, on_device(): grad_stream = lax.all_gather(stream_rows, 'tensor', axis=0, tiled=True)  83 us
    all_gather x1, waiting for transfers between devices, on_device(): lax.all_gather(w_input, ('dp', 'tensor'), axis=0, tiled=True)  78.4 us
  transfers between devices with their start and end apart: 19, of which 10 were waited for; matrix products, arithmetic and copies ran while one was open for 47% of the time, Pallas kernels for 0%

commit v1 on v0

v1 whole, which is shorter than its diff:
```python
import functools

import jax
import jax.numpy as jnp
from jax import lax
from jax.experimental import pallas as pl
from jax.experimental.pallas import tpu as pltpu
from jax.sharding import PartitionSpec as P

epsilon = 1e-06
bf16 = jnp.bfloat16
f32 = jnp.float32


def matmul(left, right):
    return jnp.dot(left, right, preferred_element_type=f32)


def matmul_rt(left, right):
    return lax.dot_general(left, right, (((1,), (1,)), ((), ())), preferred_element_type=f32)


def matmul_lt(left, right):
    return lax.dot_general(left, right, (((0,), (0,)), ((), ())), preferred_element_type=f32)


def silu_of(value):
    return value * jax.nn.sigmoid(value)


def silu_slope(value):
    squash = jax.nn.sigmoid(value)
    return squash * (1.0 + value * (1.0 - squash))


def norm_rows(value):
    scale = lax.rsqrt(jnp.mean(value * value, axis=-1, keepdims=True) + epsilon)
    return (scale, value * scale)


def norm_back(grad_norm, unit, scale, gain):
    scaled = grad_norm * gain
    return scale * (scaled - unit * jnp.mean(scaled * unit, axis=-1, keepdims=True))


def swap(value, mask):
    return lax.ppermute(value, "dp", [(i, i ^ mask) for i in range(lax.axis_size("dp"))])


def own_bit(mask):
    return lax.rem(lax.div(lax.axis_index("dp"), mask), 2)


def gather_bits(value, order):
    base = value.shape
    done = []
    for mask in order:
        other = swap(value, mask)
        at = sum(1 for seen in done if seen > mask)
        low = jnp.stack([value, other], axis=at)
        high = jnp.stack([other, value], axis=at)
        value = jnp.where(own_bit(mask) == 0, low, high)
        done.append(mask)
    return value.reshape((1 << len(order),) + base)


def scatter_bits(value, order):
    count = len(order)
    value = value.reshape((2,) * count + value.shape[1:])
    left = sorted(order, reverse=True)
    for mask in order:
        at = left.index(mask)
        left.remove(mask)
        bit = own_bit(mask)
        send = lax.dynamic_index_in_dim(value, 1 - bit, at, keepdims=False)
        keep = lax.dynamic_index_in_dim(value, bit, at, keepdims=False)
        total = keep.astype(f32) + swap(send.astype(bf16), mask).astype(f32)
        value = total.astype(bf16) if left else total
    return value


def orders(masks):
    down = sorted(masks, reverse=True)
    if len(down) < 3:
        return down, down
    return down, [down[1], down[0]] + down[2:]


def gather_rows(value, masks):
    first, second = orders(masks)
    half = value.shape[0] // 2
    return jnp.concatenate(
        [gather_bits(value[:half], first), gather_bits(value[half:], second)], axis=1
    )


def scatter_rows(value, masks):
    first, second = orders(masks)
    half = value.shape[1] // 2
    return jnp.concatenate(
        [
            scatter_bits(value[:, :half], first[::-1]),
            scatter_bits(value[:, half:], second[::-1]),
        ],
        axis=0,
    )


def ring(value):
    parts = lax.axis_size("tensor")
    return lax.ppermute(value, "tensor", [(i, (i + 1) % parts) for i in range(parts)])


def ring_blocks(value):
    blocks = [value]
    for _ in range(lax.axis_size("tensor") - 1):
        blocks.append(ring(blocks[-1]))
    return blocks


def ring_scatter(blocks):
    total = blocks[1 % len(blocks)]
    for k in range(2, len(blocks) + 1):
        moved = ring(total.astype(bf16)).astype(f32)
        total = moved + blocks[k % len(blocks)].astype(f32)
    return total


def forward_kernel(steps, seqs, forget_ref, drive_ref, state_ref, decay_ref):
    width = forget_ref.shape[1]

    def step(at, carry):
        state, decay = carry
        rows = pl.ds(at, seqs, stride=steps)
        forget = forget_ref[rows, :]
        state = forget * state + drive_ref[rows, :]
        decay = decay * forget
        state_ref[rows, :] = state
        decay_ref[rows, :] = decay
        return state, decay

    lax.fori_loop(
        0, steps, step, (jnp.zeros((seqs, width), f32), jnp.ones((seqs, width), f32)), unroll=8
    )


def backward_kernel(steps, seqs, forget_ref, drive_ref, carried_ref, decay_ref):
    width = forget_ref.shape[1]

    def step(k, carry):
        coming, decay = carry
        rows = pl.ds(steps - 1 - k, seqs, stride=steps)
        forget = forget_ref[rows, :]
        carried = drive_ref[rows, :] + coming
        carried_ref[rows, :] = carried
        decay_ref[rows, :] = decay
        return forget * carried, decay * forget

    lax.fori_loop(
        0, steps, step, (jnp.zeros((seqs, width), f32), jnp.ones((seqs, width), f32)), unroll=8
    )


def local_scan(body, seqs, forget, drive):
    rows, width = forget.shape
    lanes = 128 if width % 128 == 0 else width
    spec = pl.BlockSpec((rows, lanes), lambda c: (0, c))
    return pl.pallas_call(
        functools.partial(body, rows // seqs, seqs),
        grid=(width // lanes,),
        in_specs=[spec, spec],
        out_specs=[spec, spec],
        out_shape=[jax.ShapeDtypeStruct((rows, width), f32)] * 2,
        compiler_params=pltpu.CompilerParams(vmem_limit_bytes=32 * 1024 * 1024),
        cost_estimate=pl.CostEstimate(
            flops=4 * rows * width, bytes_accessed=16 * rows * width, transcendentals=0
        ),
    )(forget, drive)


def on_device(
    inputs,
    lengths,
    gain_mix,
    gain_glu,
    lower_bound,
    w_input,
    w_forget,
    w_gate_mix,
    w_out,
    w_gate,
    w_up,
    w_down,
    cotangent,
):
    tensor_parts = lax.axis_size("tensor")
    data_parts = lax.axis_size("dp")
    tensor_index = lax.axis_index("tensor")
    data_index = lax.axis_index("dp")
    rows_here, width = inputs.shape
    group = min(8, data_parts)
    copies = data_parts // group
    group_index = lax.div(data_index, copies)
    copy_index = lax.rem(data_index, copies)
    group_masks = [copies << k for k in range(group.bit_length() - 1)]
    copy_masks = [1 << k for k in range(copies.bit_length() - 1)]
    all_masks = [1 << k for k in range(data_parts.bit_length() - 1)]
    group_lists = [[g * copies + o for g in range(group)] for o in range(copies)]
    channels = width // group
    own_rows = w_input.shape[0]

    high = lax.div(lengths, 32).astype(bf16)
    low = lax.rem(lengths, 32).astype(bf16)
    length_row = jnp.concatenate([high, low, jnp.zeros((own_rows - 2,), bf16)])
    small = jnp.stack([gain_mix, gain_glu, lower_bound, length_row])
    small = lax.all_gather(small, ("dp", "tensor"), axis=0, tiled=False).astype(f32)
    gain_one = small[:, 0].reshape(width)
    gain_two = small[:, 1].reshape(width)
    bound = lax.dynamic_slice_in_dim(small[:, 2].reshape(width), group_index * channels, channels)
    every_length = small[:, 3].reshape(data_parts, tensor_parts, own_rows)[:, 0, :2]
    every_length = (every_length[:, 0] * 32.0 + every_length[:, 1]).astype(jnp.int32)
    group_lengths = lax.dynamic_index_in_dim(
        every_length.reshape(group, copies), copy_index, axis=1, keepdims=False
    )
    position = tensor_index * rows_here + jnp.arange(rows_here, dtype=jnp.int32)
    live_own = (position < lengths[0]).astype(f32)[:, None]
    live = (position[None, :] < group_lengths[:, None]).astype(f32)
    live = live.reshape(group * rows_here, 1)

    def spread(weight):
        return weight.reshape(own_rows, group, channels).transpose(1, 0, 2)

    pieces = jnp.concatenate([spread(w_input), spread(w_forget), spread(w_gate_mix)], axis=2)
    pieces = lax.all_to_all(
        pieces, "dp", 0, 0, axis_index_groups=group_lists if copies > 1 else None, tiled=True
    )
    out_piece = w_out
    if copies > 1:
        pieces = gather_bits(pieces, copy_masks[::-1]).transpose(1, 0, 2, 3)
        out_piece = gather_bits(out_piece, copy_masks[::-1])
    pieces = pieces.reshape(group * copies, own_rows, 3 * channels)
    out_piece = out_piece.reshape(copies, own_rows, width)
    mixer_w = lax.all_gather(pieces, "tensor", axis=1, tiled=False)
    mixer_w = mixer_w.reshape(width, 3 * channels)
    out_w = lax.all_gather(out_piece, "tensor", axis=1, tiled=False).reshape(channels, width)

    first, second = orders(all_masks)
    half = w_gate.shape[0] // 2
    down_t = w_down.T
    hidden_here = w_gate.shape[1]
    gate_w = gather_bits(w_gate, first).reshape(width, hidden_here)
    up_w = gather_bits(w_up, second).reshape(width, hidden_here)
    down_w = jnp.concatenate(
        [gather_bits(down_t[:half], first), gather_bits(down_t[half:], second)], axis=1
    ).reshape(width, hidden_here)

    masked_grad = live_own * cotangent
    masked_blocks = ring_blocks(masked_grad.astype(bf16))

    scale_one, unit_one = norm_rows(inputs)
    normed_one = gather_rows((unit_one * gain_one).astype(bf16), group_masks)
    normed_one = normed_one.reshape(group * rows_here, width)
    pre = matmul(normed_one, mixer_w)
    input_pre = pre[:, :channels]
    forget_sig = jax.nn.sigmoid(pre[:, channels : 2 * channels])
    gate_pre = pre[:, 2 * channels :]
    forget = bound + (1.0 - bound) * forget_sig
    input_act = silu_of(input_pre)
    gate_act = silu_of(gate_pre)
    inflow = live * (1.0 - forget) * input_act
    part_state, part_decay = local_scan(forward_kernel, group, forget, inflow)
    shaped = (group, rows_here, channels)
    part_state = part_state.reshape(shaped)
    part_decay = part_decay.reshape(shaped)
    ends = jnp.stack([part_state[:, -1], part_decay[:, -1]])
    all_ends = lax.all_gather(ends, "tensor", axis=0, tiled=False)
    coming = jnp.zeros((group, channels), f32)
    entering = coming
    for k in range(tensor_parts - 1):
        coming = all_ends[k, 1] * coming + all_ends[k, 0]
        entering = jnp.where(tensor_index == k + 1, coming, entering)
    state = part_state + part_decay * entering[:, None, :]
    prior_state = jnp.concatenate([entering[:, None, :], state[:, :-1]], axis=1)
    state = state.reshape(group * rows_here, channels)
    prior_state = prior_state.reshape(group * rows_here, channels)
    mixed_low = (state * gate_act).astype(bf16)
    mixed = matmul(mixed_low, out_w).astype(bf16).reshape(group, rows_here, width)
    stream = inputs + scatter_rows(mixed, group_masks)

    scale_two, unit_two = norm_rows(stream)
    normed_blocks = ring_blocks((unit_two * gain_two).astype(bf16))
    hidden_blocks, gate_low, up_low, back_parts, out_parts = [], [], [], [], []
    for normed, masked in zip(normed_blocks, masked_blocks):
        glu_gate = matmul(normed, gate_w)
        glu_up = matmul(normed, up_w)
        hidden = (silu_of(glu_gate) * glu_up).astype(bf16)
        grad_hidden = matmul(masked, down_w)
        grad_gate = (grad_hidden * glu_up * silu_slope(glu_gate)).astype(bf16)
        grad_up = (grad_hidden * silu_of(glu_gate)).astype(bf16)
        back_parts.append((matmul_rt(grad_gate, gate_w) + matmul_rt(grad_up, up_w)).astype(bf16))
        out_parts.append(matmul_rt(hidden, down_w).astype(bf16))
        hidden_blocks.append(hidden)
        gate_low.append(grad_gate)
        up_low.append(grad_up)
    grad_norm_two = ring_scatter(back_parts)
    output = live_own * (stream + ring_scatter(out_parts))

    all_normed = jnp.concatenate(normed_blocks)
    all_masked = jnp.concatenate(masked_blocks)
    by_owner = (data_parts, width // data_parts, hidden_here)
    grad_gate_w = matmul_lt(all_normed, jnp.concatenate(gate_low)).astype(bf16).reshape(by_owner)
    grad_up_w = matmul_lt(all_normed, jnp.concatenate(up_low)).astype(bf16).reshape(by_owner)
    grad_down_t = (
        matmul_lt(all_masked, jnp.concatenate(hidden_blocks)).astype(bf16).reshape(by_owner)
    )
    grad_gate_mine = scatter_bits(grad_gate_w, first[::-1])
    grad_up_mine = scatter_bits(grad_up_w, second[::-1])
    grad_down_mine = scatter_rows(grad_down_t, all_masks).T

    gain_two_part = jnp.sum(grad_norm_two * unit_two, axis=0)
    grad_stream = masked_grad + norm_back(grad_norm_two, unit_two, scale_two, gain_two)
    stream_low = gather_rows(grad_stream.astype(bf16), group_masks)
    stream_low = stream_low.reshape(group * rows_here, width)

    grad_out_w = matmul_lt(mixed_low, stream_low).astype(bf16)
    grad_mixed = matmul_rt(stream_low, out_w)
    grad_gate_pre = (grad_mixed * state * silu_slope(gate_pre)).astype(bf16)
    grad_state = grad_mixed * gate_act
    part_carried, part_after = local_scan(backward_kernel, group, forget, grad_state)
    part_carried = part_carried.reshape(shaped)
    part_after = part_after.reshape(shaped)
    first_forget = forget.reshape(shaped)[:, 0]
    begins = jnp.stack([first_forget * part_carried[:, 0], first_forget * part_after[:, 0]])
    all_begins = lax.all_gather(begins, "tensor", axis=0, tiled=False)
    coming = jnp.zeros((group, channels), f32)
    entering = coming
    for k in range(tensor_parts - 1, 0, -1):
        coming = all_begins[k, 1] * coming + all_begins[k, 0]
        entering = jnp.where(tensor_index == k - 1, coming, entering)
    carried = (part_carried + part_after * entering[:, None, :]).reshape(
        group * rows_here, channels
    )
    grad_forget = carried * prior_state - carried * live * input_act
    grad_input_pre = (carried * live * (1.0 - forget) * silu_slope(input_pre)).astype(bf16)
    grad_bound = jnp.sum(grad_forget * (1.0 - forget_sig), axis=0)
    grad_forget_pre = (grad_forget * (1.0 - bound) * forget_sig * (1.0 - forget_sig)).astype(bf16)
    grad_pre = jnp.concatenate([grad_input_pre, grad_forget_pre, grad_gate_pre], axis=1)
    grad_normed = matmul_rt(grad_pre, mixer_w).astype(bf16).reshape(group, rows_here, width)
    grad_norm_one = scatter_rows(grad_normed, group_masks)
    gain_one_part = jnp.sum(grad_norm_one * unit_one, axis=0)
    grad_inputs = grad_stream + norm_back(grad_norm_one, unit_one, scale_one, gain_one)

    grad_mixer = matmul_lt(normed_one, grad_pre).astype(bf16)
    grad_mixer = grad_mixer.reshape(data_parts, tensor_parts, own_rows, 3 * channels)
    grad_mixer = grad_mixer.transpose(1, 0, 2, 3)
    grad_mixer = lax.psum_scatter(grad_mixer, "tensor", scatter_dimension=0, tiled=False)
    grad_out = grad_out_w.reshape(copies, tensor_parts, own_rows, width).transpose(1, 0, 2, 3)
    grad_out = lax.psum_scatter(grad_out, "tensor", scatter_dimension=0, tiled=False)
    if copies > 1:
        grad_mixer = grad_mixer.reshape(group, copies, own_rows, 3 * channels)
        grad_mixer = scatter_bits(grad_mixer.transpose(1, 0, 2, 3), copy_masks).astype(bf16)
        grad_out = scatter_bits(grad_out, copy_masks)
    grad_mixer = grad_mixer.reshape(group, own_rows, 3 * channels)
    grad_mixer = lax.all_to_all(
        grad_mixer, "dp", 0, 0, axis_index_groups=group_lists if copies > 1 else None, tiled=True
    )
    grad_mixer = grad_mixer.reshape(group, own_rows, 3, channels).transpose(2, 1, 0, 3)
    grad_mixer = grad_mixer.reshape(3, own_rows, width).astype(f32)
    grad_out = grad_out.reshape(own_rows, width).astype(f32)

    bound_part = lax.dynamic_update_slice_in_dim(
        jnp.zeros((width,), f32), grad_bound, group_index * channels, 0
    )
    sums = jnp.stack([gain_one_part, gain_two_part, bound_part])
    sums = sums.reshape(3, data_parts * tensor_parts, own_rows).transpose(1, 0, 2)
    sums = lax.psum_scatter(sums, ("dp", "tensor"), scatter_dimension=0, tiled=False)
    return (
        output,
        grad_inputs,
        sums[0],
        sums[1],
        sums[2],
        grad_mixer[0],
        grad_mixer[1],
        grad_mixer[2],
        grad_out,
        grad_gate_mine,
        grad_up_mine,
        grad_down_mine,
    )


def solution(mesh):
    both = ("dp", "tensor")
    placed = (
        P(both, None),
        P("dp"),
        P(both),
        P(both),
        P(both),
        P(both, None),
        P(both, None),
        P(both, None),
        P(both, None),
        P("dp", "tensor"),
        P("dp", "tensor"),
        P("tensor", "dp"),
        P(both, None),
    )
    return jax.shard_map(
        on_device,
        mesh=mesh,
        in_specs=placed,
        out_specs=(
            P(both, None),
            P(both, None),
            P(both),
            P(both),
            P(both),
            P(both, None),
            P(both, None),
            P(both, None),
            P(both, None),
            P("dp", "tensor"),
            P("dp", "tensor"),
            P("tensor", "dp"),
        ),
        check_vma=False,
    )
```

time: 1820 us -> 927 us (0.51)
  waiting for transfers between devices: 797 us -> 334 us
  other arithmetic: 401 us -> 121 us
  local copies, waits for them, and re-layouts: 233 us -> 84 us
  matrix products: 291 us -> 148 us
  blocking collectives: 73.3 us -> 155 us
  starting transfers between devices: 0.76 us -> 46.7 us
    all_gather x10 -> x2, waiting for transfers between devices: 458 us -> 0.02 us  [the longest x1 0.02 us: on_device(): lax.all_gather(out_piece, 'tensor', axis=1, tiled=False)]
    reduce_scatter x9 -> x2, waiting for transfers between devices: 333 us -> 0.01 us  [the longest x1 0.01 us: on_device(): lax.psum_scatter(grad_out, 'tensor', scatter_dimension=0, tiled=False)]
    ppermute x0 -> x60, waiting for transfers between devices: none -> 325 us  [the longest x48 204 us: swap(): lax.ppermute(value, 'dp', [(i, i ^ mask) for i in range(lax.axis_size('dp...]
    add x19 -> x10, other arithmetic: 326 us -> 8.08 us  [the longest x8 7.74 us: scatter_bits(): total = keep.astype(f32) + swap(send.astype(bf16), mask).astype(f32)]
    slice x32 -> x17, local copies, waits for them, and re-layouts: 191 us -> 10.9 us  [the longest x3 7.07 us: scatter_rows(): value[:, :half]]
    all_gather x0 -> x3, blocking collectives: none -> 96.8 us  [the longest x1 67.5 us: on_device(): lax.all_gather(small, ('dp', 'tensor'), axis=0, tiled=False).astype(f32)]
    dot_general x7 -> x14, matrix products: 118 us -> 44.8 us  [matmul_rt(): lax.dot_general(left, right, (((1,), (1,)), ((), ())), preferred_element_...]
    dot_general x7 -> x14, matrix products: 114 us -> 50 us  [matmul(): return jnp.dot(left, right, preferred_element_type=f32)]
  transfers between devices with their start and end apart: 19 -> 65, of which waited for: 10 -> 27; matrix products, arithmetic and copies ran while one was open for 47% -> 35% of each run, Pallas kernels for 0% -> 1%
where the time goes in v1:
time: 927 us; the launch traced here: 918 us
  waiting for transfers between devices  334 us (36%)
  blocking collectives  155 us (17%)
  matrix products  148 us (16%)
  other arithmetic  121 us (13%)
  local copies, waits for them, and re-layouts  84 us (9%)
  starting transfers between devices  46.7 us (5%)
  between operations  16.9 us (2%)
  Pallas kernels  12.6 us (1%)
    ppermute x48, waiting for transfers between devices, swap(): lax.ppermute(value, 'dp', [(i, i ^ mask) for i in range(lax.axis_size('dp...  204 us
    ppermute x12, waiting for transfers between devices, ring(): lax.ppermute(value, 'tensor', [(i, (i + 1) % parts) for i in range(parts)])  121 us
    all_gather x1, blocking collectives, on_device(): lax.all_gather(small, ('dp', 'tensor'), axis=0, tiled=False).astype(f32)  67.5 us
    dot_general x5, matrix products, matmul_lt(): lax.dot_general(left, right, (((0,), (0,)), ((), ())), preferred_element_...  53.2 us
    dot_general x14, matrix products, matmul(): return jnp.dot(left, right, preferred_element_type=f32)  50 us
    select_n x40, other arithmetic, gather_bits(): value = jnp.where(own_bit(mask) == 0, low, high)  47.6 us
    dot_general x14, matrix products, matmul_rt(): lax.dot_general(left, right, (((1,), (1,)), ((), ())), preferred_element_...  44.8 us
    unnamed x1, blocking collectives  40 us
  transfers between devices with their start and end apart: 65, of which 27 were waited for; matrix products, arithmetic and copies ran while one was open for 35% of the time, Pallas kernels for 1%

profile of v1, /device:TPU:0, one launch (start us, length us, event | category | flops | bytes accessed | tf_op | source)
XLA Modules:
  0.0 917.7 jit_solution(3766409690565716627)
XLA Ops:
  10.5 17.7 %all_to_all.10 = bf16[8,64,768]{2,1,0:T(8,128)(2,1)S(1)} all-to-all(bf16[8,64,768]{2,1,0:T(8,128)(2,1)S(1)} %copy.152), channel_id=1, replica_groups=mesh['dp'=8,'tensor'=4] {'dp'}, dimensions={0} | all-to-all | bytes 1572864 | tf_op jit(solution)/shard_map/all_to_all | solution.py:234
  30.3 67.5 %all-gather.5 = bf16[32,4,64]{2,1,0:T(4,128)(2,1)S(1)} all-gather(bf16[1,4,64]{2,1,0:T(4,128)(2,1)S(1)} %maximum_bitcast_fusion.6), channel_id=2, replica_groups=mesh['dp'=8,'tensor'=4] {'dp','tensor'}, dimensions={0}, use_global_device_ids=true | all-gather | bytes 16896 | tf_op jit(solution)/shard_map/all_gather | solution.py:216
  109.8 11.2 %collective-permute-done.22 = bf16[128,1408]{1,0:T(8,128)(2,1)S(1)} collective-permute-done((bf16[128,1408]{1,0:T(8,128)(2,1)}, bf16[128,1408]{1,0:T(8,128)(2,1)S(1)}, u32[]{:S(2)}, u32[]{:S(2)}) %collective-permute-start.22) | collective-permute-done | bytes 360480 | tf_op jit(solution)/shard_map/ppermute | solution.py:47
  133.6 6.5 collective-permute-done.16
  145.9 12.3 %collective-permute-done.23 = bf16[2,128,1408]{2,1,0:T(8,128)(2,1)S(1)} collective-permute-done((bf16[2,128,1408]{2,1,0:T(8,128)(2,1)S(1)}, bf16[2,128,1408]{2,1,0:T(8,128)(2,1)S(1)}, u32[]{:S(2)}, u32[]{:S(2)}) %collective-permute-start.23) | collective-permute-done | bytes 720928 | tf_op jit(solution)/shard_map/ppermute | solution.py:47
  162.7 17.9 %collective-permute-done.4 = bf16[2,128,2048]{2,1,0:T(8,128)(2,1)S(1)} collective-permute-done((bf16[2,128,2048]{2,1,0:T(8,128)(2,1)S(1)}, bf16[2,128,2048]{2,1,0:T(8,128)(2,1)S(1)}, u32[]{:S(2)}, u32[]{:S(2)}) %collective-permute-start.4) | collective-permute-done | bytes 1048608 | tf_op jit(solution)/shard_map/ppermute | solution.py:47
  185.2 20.4 %collective-permute-done.17 = bf16[2,256,1408]{2,1,0:T(8,128)(2,1)S(1)} collective-permute-done((bf16[2,256,1408]{2,1,0:T(8,128)(2,1)S(1)}, bf16[2,256,1408]{2,1,0:T(8,128)(2,1)S(1)}, u32[]{:S(2)}, u32[]{:S(2)}) %collective-permute-start.17) | collective-permute-done | bytes 1441824 | tf_op jit(solution)/shard_map/ppermute | solution.py:47
  216.9 5.0 fusion.95
  221.9 4.1 fusion.89
  226.0 4.2 fusion.91
  230.2 2.8 maximum_select_fusion.3
  235.3 2.8 maximum_select_fusion.2
  240.3 8.4 pad_maximum_fusion
  251.3 10.2 %fusion.84 = f32[2048,768]{1,0:T(8,128)S(1)} fusion(bf16[2048,2048]{1,0:T(8,128)(2,1)} %bitcast.464, bf16[2048,768]{1,0:T(8,128)(2,1)S(1)} %bitcast.528), kind=kOutput, calls=%fused_computation.319 | convolution fusion | flops 6442450944 | bytes 17825792 | tf_op jit(solution)/shard_map/dot_general | solution.py:16
  262.7 5.9 shard_map.220
  268.7 16.2 %all-gather.2 = f32[8,8,256]{2,1,0:T(8,128)S(1)} all-gather(f32[2,8,256]{2,1,0:T(8,128)S(1)} %pad_maximum_fusion.16), channel_id=4, replica_groups=mesh['dp'=8,'tensor'=4] {'tensor'}, dimensions={0}, use_global_device_ids=true | all-gather | bytes 81920 | tf_op jit(solution)/shard_map/all_gather | solution.py:276
  285.7 4.0 convolution_convert_fusion.4
  292.4 4.1 fusion.93
  299.0 4.2 maximum_select_fusion.1
  303.2 4.1 maximum_select_fusion
  311.7 22.2 %collective-permute-done.10 = bf16[2,128,2048]{2,1,0:T(8,128)(2,1)S(1)} collective-permute-done((bf16[2,128,2048]{2,1,0:T(8,128)(2,1)S(1)}, bf16[2,128,2048]{2,1,0:T(8,128)(2,1)S(1)}, u32[]{:S(2)}, u32[]{:S(2)}) %collective-permute-start.10) | collective-permute-done | bytes 1048608 | tf_op jit(solution)/shard_map/ppermute | solution.py:47
  339.3 8.7 collective-permute-done.11
  352.9 3.3 multiply_convert_fusion.8
  356.1 3.2 fusion.96
  359.3 3.2 fusion.46
  362.5 13.9 %collective-permute-done.12 = bf16[256,2048]{1,0:T(8,128)(2,1)S(1)} collective-permute-done((bf16[256,2048]{1,0:T(8,128)(2,1)S(1)}, bf16[256,2048]{1,0:T(8,128)(2,1)S(1)}, u32[]{:S(2)}, u32[]{:S(2)}) %collective-permute-start.12) | collective-permute-done | bytes 1048608 | tf_op jit(solution)/shard_map/ppermute | solution.py:111
  388.8 22.4 %collective-permute-done.26 = bf16[256,2048]{1,0:T(8,128)(2,1)S(1)} collective-permute-done((bf16[256,2048]{1,0:T(8,128)(2,1)S(1)}, bf16[256,2048]{1,0:T(8,128)(2,1)S(1)}, u32[]{:S(2)}, u32[]{:S(2)}) %collective-permute-start.26) | collective-permute-done | bytes 1048608 | tf_op jit(solution)/shard_map/ppermute | solution.py:111
  413.1 3.2 multiply_convert_fusion.12
  416.4 3.2 fusion.92
  419.6 14.2 %collective-permute-done.31 = bf16[256,2048]{1,0:T(8,128)(2,1)S(1)} collective-permute-done((bf16[256,2048]{1,0:T(8,128)(2,1)S(1)}, bf16[256,2048]{1,0:T(8,128)(2,1)S(1)}, u32[]{:S(2)}, u32[]{:S(2)}) %collective-permute-start.31) | collective-permute-done | bytes 1048608 | tf_op jit(solution)/shard_map/ppermute | solution.py:111
  433.7 3.6 add_convert_fusion.1
  437.4 18.8 %collective-permute-done.25 = bf16[256,2048]{1,0:T(8,128)(2,1)S(1)} collective-permute-done((bf16[256,2048]{1,0:T(8,128)(2,1)S(1)}, bf16[256,2048]{1,0:T(8,128)(2,1)S(1)}, u32[]{:S(2)}, u32[]{:S(2)}) %collective-permute-start.25) | collective-permute-done | bytes 1048608 | tf_op jit(solution)/shard_map/ppermute | solution.py:111
  458.2 20.5 %collective-permute-done.28 = bf16[256,2048]{1,0:T(8,128)(2,1)S(1)} collective-permute-done((bf16[256,2048]{1,0:T(8,128)(2,1)S(1)}, bf16[256,2048]{1,0:T(8,128)(2,1)S(1)}, u32[]{:S(2)}, u32[]{:S(2)}) %collective-permute-start.28) | collective-permute-done | bytes 1048608 | tf_op jit(solution)/shard_map/ppermute | solution.py:111
  482.9 3.1 fusion.94
  486.0 15.1 %collective-permute-done.33 = bf16[256,2048]{1,0:T(8,128)(2,1)S(1)} collective-permute-done((bf16[256,2048]{1,0:T(8,128)(2,1)S(1)}, bf16[256,2048]{1,0:T(8,128)(2,1)S(1)}, u32[]{:S(2)}, u32[]{:S(2)}) %collective-permute-start.33) | collective-permute-done | bytes 1048608 | tf_op jit(solution)/shard_map/ppermute | solution.py:111
  501.1 4.5 add_convert_fusion
  507.5 16.1 %collective-permute-done.27 = bf16[256,2048]{1,0:T(8,128)(2,1)S(1)} collective-permute-done((bf16[256,2048]{1,0:T(8,128)(2,1)S(1)}, bf16[256,2048]{1,0:T(8,128)(2,1)S(1)}, u32[]{:S(2)}, u32[]{:S(2)}) %collective-permute-start.27) | collective-permute-done | bytes 1048608 | tf_op jit(solution)/shard_map/ppermute | solution.py:111
  525.1 11.9 %convolution_convert_fusion.2 = bf16[2048,1408]{1,0:T(8,128)(2,1)} fusion(bf16[256,1408]{1,0:T(8,128)(2,1)} %copy-done.78, bf16[256,1408]{1,0:T(8,128)(2,1)} %copy-done.77, bf16[256,1408]{1,0:T(8,128)(2,1)} %copy-done.79, bf16[256,1408]{1,0:T(8,128)(2,1)} %get-tuple-element.97, bf16[256,2048]{1,0:T(8,128)(2,1)} %copy-done.76, ...), kind=kOutput, calls=%fused_computation.4 | convolution fusion | flops 5936775168 | bytes 12845056 | tf_op jit(solution)/shard_map/dot_general | solution.py:24
  537.0 4.7 constant_dynamic-slice_fusion.1
  543.6 12.4 %convolution_convert_fusion.1 = bf16[2048,1408]{1,0:T(8,128)(2,1)} fusion(bf16[256,1408]{1,0:T(8,128)(2,1)} %copy-done.87, bf16[256,1408]{1,0:T(8,128)(2,1)} %copy-done.84, bf16[256,1408]{1,0:T(8,128)(2,1)} %copy-done.83, bf16[256,1408]{1,0:T(8,128)(2,1)} %copy-done.82, bf16[256,2048]{1,0:T(8,128)(2,1)} %copy-done.76, bf16[256,2048]{1,0:T(8,128)(2,1)} %copy-done.75, ...), kind=kOutput, calls=%fused_computation.3 | convolution fusion | flops 5936775168 | bytes 12845056 | tf_op jit(solution)/shard_map/dot_general | solution.py:24
  556.0 3.7 dynamic-slice_bitcast_fusion
  560.3 11.3 %convolution_convert_fusion = bf16[2048,1408]{1,0:T(8,128)(2,1)} fusion(bf16[256,2048]{1,0:T(8,128)(2,1)} %collective-permute-done.34, bf16[256,2048]{1,0:T(8,128)(2,1)} %collective-permute-done.32, bf16[256,2048]{1,0:T(8,128)(2,1)} %collective-permute-done.30, bf16[256,2048]{1,0:T(8,128)(2,1)} %multiply_convert_fusion.6, ...), kind=kOutput, calls=%fused_computation.2 | convolution fusion | flops 5936775168 | bytes 12845056 | tf_op jit(solution)/shard_map/dot_general | solution.py:24
  571.6 3.3 fusion.80
  581.9 4.8 fusion.77
  595.4 7.1 collective-permute-done.39
  611.5 8.1 collective-permute-done.58
  622.1 28.0 %collective-permute-done.59 = bf16[128,1408]{1,0:T(8,128)(2,1)S(1)} collective-permute-done((bf16[128,1408]{1,0:T(8,128)(2,1)S(1)}, bf16[128,1408]{1,0:T(8,128)(2,1)S(1)}, u32[]{:S(2)}, u32[]{:S(2)}) %collective-permute-start.59) | collective-permute-done | bytes 360480 | tf_op jit(solution)/shard_map/ppermute | solution.py:47
  651.9 5.7 collective-permute-done.56
  676.6 22.3 %collective-permute-done.49 = bf16[2,256,1408]{2,1,0:T(8,128)(2,1)S(1)} collective-permute-done((bf16[2,256,1408]{2,1,0:T(8,128)(2,1)S(1)}, bf16[2,256,1408]{2,1,0:T(8,128)(2,1)S(1)}, u32[]{:S(2)}, u32[]{:S(2)}) %collective-permute-start.49) | collective-permute-done | bytes 1441824 | tf_op jit(solution)/shard_map/ppermute | solution.py:47
  711.1 8.4 pad_maximum_fusion.1
  719.5 6.8 convolution_convert_fusion.6
  726.8 5.4 fusion.68
  732.2 6.7 shard_map.221
  738.9 13.1 %all-gather.4 = f32[8,8,256]{2,1,0:T(8,128)S(1)} all-gather(f32[2,8,256]{2,1,0:T(8,128)S(1)} %pad_maximum_fusion.17), channel_id=6, replica_groups=mesh['dp'=8,'tensor'=4] {'tensor'}, dimensions={0}, use_global_device_ids=true | all-gather | bytes 81920 | tf_op jit(solution)/shard_map/all_gather | solution.py:334
  756.9 7.2 convolution_convert_fusion.3
  774.5 10.6 %convolution_convert_fusion.5 = bf16[2048,768]{1,0:T(8,128)(2,1)} fusion(bf16[2048,2048]{1,0:T(8,128)(2,1)} %bitcast.465, bf16[2048,256]{1,0:T(8,128)(2,1)S(1)} %get-tuple-element.77, bf16[2048,256]{1,0:T(8,128)(2,1)S(1)} %copy-done.54, bf16[2048,256]{1,0:T(8,128)(2,1)S(1)} %copy-done.51), kind=kOutput, calls=%fused_computation.34 | convolution fusion | flops 6453460992 | bytes 14680064 | tf_op jit(solution)/shard_map/dot_general | solution.py:24
  787.0 3.9 copy.311
  794.6 3.0 fusion.9
  805.8 17.7 %collective-permute-done.46 = bf16[2,128,2048]{2,1,0:T(8,128)(2,1)S(1)} collective-permute-done((bf16[2,128,2048]{2,1,0:T(8,128)(2,1)S(1)}, bf16[2,128,2048]{2,1,0:T(8,128)(2,1)S(1)}, u32[]{:S(2)}, u32[]{:S(2)}) %collective-permute-start.46) | collective-permute-done | bytes 1048608 | tf_op jit(solution)/shard_map/ppermute | solution.py:47
  831.8 7.1 collective-permute-done.47
  845.2 40.0 %all-reduce = f32[32,3,64]{2,1,0:T(4,128)S(1)} all-reduce(f32[32,3,64]{2,1,0:T(4,128)S(1)} %maximum_bitcast_fusion.5), channel_id=7, replica_groups=mesh['dp'=8,'tensor'=4] {'dp','tensor'}, use_global_device_ids=true, to_apply=%region_7.8.clone | all-reduce | flops 6144 | bytes 49152
  885.8 4.5 all-to-all-start.1
  890.3 3.7 multiply_add_fusion
  894.0 8.9 all-to-all-done.1
  (513 shorter events, 221.7 us)
Async XLA Ops:
  7.2 241.6 %all-gather.9.cloned.1.call-start = ((), (), s32[]{:S(2)}) async-start(), calls=%async_computation.6 | async-start | bytes 3932160 | tf_op jit(solution)/shard_map/all_gather | solution.py:243
  29.5 256.2 %all-gather.11.cloned.1.call-start = ((), (), s32[]{:S(2)}) async-start(), calls=%async_computation.7 | async-start | bytes 1310720 | tf_op jit(solution)/shard_map/all_gather | solution.py:245
  101.1 27.7 %collective-permute-start.3 = (bf16[128,2048]{1,0:T(8,128)(2,1)}, bf16[128,2048]{1,0:T(8,128)(2,1)S(1)}, u32[]{:S(2)}, u32[]{:S(2)}) collective-permute-start(bf16[128,2048]{1,0:T(8,128)(2,1)} %get-tuple-element.118), channel_id=1, source_target_pairs={{0,8},{4,12},{8,0},{12,4},{16,24},{20,28},{24,16},{28,20},{1,9},{5... | collective-permute-start | bytes 1572872 | tf_op jit(solution)/shard_map/ppermute | solution.py:47
  101.1 29.0 %collective-permute-start = (bf16[128,2048]{1,0:T(8,128)(2,1)}, bf16[128,2048]{1,0:T(8,128)(2,1)S(1)}, u32[]{:S(2)}, u32[]{:S(2)}) collective-permute-start(bf16[128,2048]{1,0:T(8,128)(2,1)} %get-tuple-element.119), channel_id=1, source_target_pairs={{0,16},{4,20},{8,24},{12,28},{16,0},{20,4},{24,8},{28,12},{1,17},{... | collective-permute-start | bytes 1572872 | tf_op jit(solution)/shard_map/ppermute | solution.py:47
  103.9 55.7 %collective-permute-start.30 = (bf16[256,2048]{1,0:T(8,128)(2,1)}, bf16[256,2048]{1,0:T(8,128)(2,1)}, u32[]{:S(2)}, u32[]{:S(2)}) collective-permute-start(bf16[256,2048]{1,0:T(8,128)(2,1)} %multiply_convert_fusion.6), channel_id=1, source_target_pairs={{0,1},{1,2},{2,3},{3,0},{4,5},{5,6},{6,7},{7,4},{8,9},{9,10},{10,1... | collective-permute-start | bytes 3145736 | tf_op jit(solution)/shard_map/ppermute | solution.py:111
  106.7 14.3 %collective-permute-start.22 = (bf16[128,1408]{1,0:T(8,128)(2,1)}, bf16[128,1408]{1,0:T(8,128)(2,1)S(1)}, u32[]{:S(2)}, u32[]{:S(2)}) collective-permute-start(bf16[128,1408]{1,0:T(8,128)(2,1)} %get-tuple-element.124), channel_id=1, source_target_pairs={{0,8},{4,12},{8,0},{12,4},{16,24},{20,28},{24,16},{28,20},{1,9},{5... | collective-permute-start | bytes 1081352 | tf_op jit(solution)/shard_map/ppermute | solution.py:47
  108.7 14.8 %collective-permute-start.19 = (bf16[128,1408]{1,0:T(8,128)(2,1)}, bf16[128,1408]{1,0:T(8,128)(2,1)}, u32[]{:S(2)}, u32[]{:S(2)}) collective-permute-start(bf16[128,1408]{1,0:T(8,128)(2,1)} %get-tuple-element.125), channel_id=1, source_target_pairs={{0,16},{4,20},{8,24},{12,28},{16,0},{20,4},{24,8},{28,12},{1,17},{... | collective-permute-start | bytes 1081352 | tf_op jit(solution)/shard_map/ppermute | solution.py:47
  109.3 720.6 %reduce-scatter.5.cloned.1.call-start = ((), (), s32[]{:S(2)}) async-start(), calls=%async_computation.5 | async-start | bytes 1310720 | tf_op jit(solution)/shard_map/reduce_scatter | solution.py:358
  121.1 19.1 %collective-permute-start.16 = (bf16[256,1408]{1,0:T(8,128)(2,1)S(1)}, bf16[256,1408]{1,0:T(8,128)(2,1)S(1)}, u32[]{:S(2)}, u32[]{:S(2)}) collective-permute-start(bf16[256,1408]{1,0:T(8,128)(2,1)S(1)} %copy-done.24), channel_id=1, source_target_pairs={{0,8},{4,12},{8,0},{12,4},{16,24},{20,28},{24,16},{28,20},{1,9},{5... | collective-permute-start | bytes 2162696 | tf_op jit(solution)/shard_map/ppermute | solution.py:47
  123.6 19.1 %collective-permute-start.13 = (bf16[256,1408]{1,0:T(8,128)(2,1)S(1)}, bf16[256,1408]{1,0:T(8,128)(2,1)S(1)}, u32[]{:S(2)}, u32[]{:S(2)}) collective-permute-start(bf16[256,1408]{1,0:T(8,128)(2,1)S(1)} %copy-done.25), channel_id=1, source_target_pairs={{0,16},{4,20},{8,24},{12,28},{16,0},{20,4},{24,8},{28,12},{1,17},{... | collective-permute-start | bytes 2162696 | tf_op jit(solution)/shard_map/ppermute | solution.py:47
  128.8 29.3 %collective-permute-start.23 = (bf16[2,128,1408]{2,1,0:T(8,128)(2,1)S(1)}, bf16[2,128,1408]{2,1,0:T(8,128)(2,1)S(1)}, u32[]{:S(2)}, u32[]{:S(2)}) collective-permute-start(bf16[2,128,1408]{2,1,0:T(8,128)(2,1)S(1)} %maximum_select_fusion.35), channel_id=1, source_target_pairs={{0,16},{4,20},{8,24},{12,28},{16,0},{20,4},{24,8},{28,12},{1,17},{... | collective-permute-start | bytes 2162696 | tf_op jit(solution)/shard_map/ppermute | solution.py:47
  130.1 31.6 %collective-permute-start.20 = (bf16[2,128,1408]{2,1,0:T(8,128)(2,1)S(1)}, bf16[2,128,1408]{2,1,0:T(8,128)(2,1)S(1)}, u32[]{:S(2)}, u32[]{:S(2)}) collective-permute-start(bf16[2,128,1408]{2,1,0:T(8,128)(2,1)S(1)} %maximum_select_fusion.33), channel_id=1, source_target_pairs={{0,8},{4,12},{8,0},{12,4},{16,24},{20,28},{24,16},{28,20},{1,9},{5... | collective-permute-start | bytes 2162696 | tf_op jit(solution)/shard_map/ppermute | solution.py:47
  140.1 40.5 %collective-permute-start.4 = (bf16[2,128,2048]{2,1,0:T(8,128)(2,1)S(1)}, bf16[2,128,2048]{2,1,0:T(8,128)(2,1)S(1)}, u32[]{:S(2)}, u32[]{:S(2)}) collective-permute-start(bf16[2,128,2048]{2,1,0:T(8,128)(2,1)S(1)} %maximum_select_fusion.27), channel_id=1, source_target_pairs={{0,16},{4,20},{8,24},{12,28},{16,0},{20,4},{24,8},{28,12},{1,17},{... | collective-permute-start | bytes 3145736 | tf_op jit(solution)/shard_map/ppermute | solution.py:47
  142.7 39.9 %collective-permute-start.1 = (bf16[2,128,2048]{2,1,0:T(8,128)(2,1)S(1)}, bf16[2,128,2048]{2,1,0:T(8,128)(2,1)S(1)}, u32[]{:S(2)}, u32[]{:S(2)}) collective-permute-start(bf16[2,128,2048]{2,1,0:T(8,128)(2,1)S(1)} %maximum_select_fusion.25), channel_id=1, source_target_pairs={{0,8},{4,12},{8,0},{12,4},{16,24},{20,28},{24,16},{28,20},{1,9},{5... | collective-permute-start | bytes 3145736 | tf_op jit(solution)/shard_map/ppermute | solution.py:47
  158.2 47.4 %collective-permute-start.17 = (bf16[2,256,1408]{2,1,0:T(8,128)(2,1)S(1)}, bf16[2,256,1408]{2,1,0:T(8,128)(2,1)S(1)}, u32[]{:S(2)}, u32[]{:S(2)}) collective-permute-start(bf16[2,256,1408]{2,1,0:T(8,128)(2,1)S(1)} %maximum_select_fusion.21), channel_id=1, source_target_pairs={{0,16},{4,20},{8,24},{12,28},{16,0},{20,4},{24,8},{28,12},{1,17},{... | collective-permute-start | bytes 4325384 | tf_op jit(solution)/shard_map/ppermute | solution.py:47
  159.7 48.2 %collective-permute-start.14 = (bf16[2,256,1408]{2,1,0:T(8,128)(2,1)S(1)}, bf16[2,256,1408]{2,1,0:T(8,128)(2,1)S(1)}, u32[]{:S(2)}, u32[]{:S(2)}) collective-permute-start(bf16[2,256,1408]{2,1,0:T(8,128)(2,1)S(1)} %maximum_select_fusion.19), channel_id=1, source_target_pairs={{0,8},{4,12},{8,0},{12,4},{16,24},{20,28},{24,16},{28,20},{1,9},{5... | collective-permute-start | bytes 4325384 | tf_op jit(solution)/shard_map/ppermute | solution.py:47
  161.7 45.6 %collective-permute-start.32 = (bf16[256,2048]{1,0:T(8,128)(2,1)}, bf16[256,2048]{1,0:T(8,128)(2,1)}, u32[]{:S(2)}, u32[]{:S(2)}) collective-permute-start(bf16[256,2048]{1,0:T(8,128)(2,1)} %collective-permute-done.30), channel_id=1, source_target_pairs={{0,1},{1,2},{2,3},{3,0},{4,5},{5,6},{6,7},{7,4},{8,9},{9,10},{10,1... | collective-permute-start | bytes 3145736 | tf_op jit(solution)/shard_map/ppermute | solution.py:111
  180.6 33.8 %collective-permute-start.24 = (bf16[2,2,128,1408]{3,2,1,0:T(8,128)(2,1)S(1)}, bf16[2,2,128,1408]{3,2,1,0:T(8,128)(2,1)S(1)}, u32[]{:S(2)}, u32[]{:S(2)}) collective-permute-start(bf16[2,2,128,1408]{3,2,1,0:T(8,128)(2,1)S(1)} %maximum_select_fusion.24), channel_id=1, source_target_pairs={{0,4},{4,0},{8,12},{12,8},{16,20},{20,16},{24,28},{28,24},{1,5},{5... | collective-permute-start | bytes 4325384 | tf_op jit(solution)/shard_map/ppermute | solution.py:47
  182.6 32.4 %collective-permute-start.21 = (bf16[2,2,128,1408]{3,2,1,0:T(8,128)(2,1)S(1)}, bf16[2,2,128,1408]{3,2,1,0:T(8,128)(2,1)S(1)}, u32[]{:S(2)}, u32[]{:S(2)}) collective-permute-start(bf16[2,2,128,1408]{3,2,1,0:T(8,128)(2,1)S(1)} %maximum_select_fusion.22), channel_id=1, source_target_pairs={{0,4},{4,0},{8,12},{12,8},{16,20},{20,16},{24,28},{28,24},{1,5},{5... | collective-permute-start | bytes 4325384 | tf_op jit(solution)/shard_map/ppermute | solution.py:47
  205.6 24.6 %collective-permute-start.5 = (bf16[2,2,128,2048]{3,2,1,0:T(8,128)(2,1)}, bf16[2,2,128,2048]{3,2,1,0:T(8,128)(2,1)}, u32[]{:S(2)}, u32[]{:S(2)}) collective-permute-start(bf16[2,2,128,2048]{3,2,1,0:T(8,128)(2,1)} %maximum_select_fusion.13), channel_id=1, source_target_pairs={{0,4},{4,0},{8,12},{12,8},{16,20},{20,16},{24,28},{28,24},{1,5},{5... | collective-permute-start | bytes 6291464 | tf_op jit(solution)/shard_map/ppermute | solution.py:47
  207.4 27.9 %collective-permute-start.2 = (bf16[2,2,128,2048]{3,2,0,1:T(8,128)(2,1)}, bf16[2,2,128,2048]{3,2,0,1:T(8,128)(2,1)}, u32[]{:S(2)}, u32[]{:S(2)}) collective-permute-start(bf16[2,2,128,2048]{3,2,0,1:T(8,128)(2,1)} %maximum_select_fusion.11), channel_id=1, source_target_pairs={{0,4},{4,0},{8,12},{12,8},{16,20},{20,16},{24,28},{28,24},{1,5},{5... | collective-permute-start | bytes 6291464 | tf_op jit(solution)/shard_map/ppermute | solution.py:47
  207.9 84.5 %collective-permute-start.34 = (bf16[256,2048]{1,0:T(8,128)(2,1)}, bf16[256,2048]{1,0:T(8,128)(2,1)}, u32[]{:S(2)}, u32[]{:S(2)}) collective-permute-start(bf16[256,2048]{1,0:T(8,128)(2,1)} %collective-permute-done.32), channel_id=1, source_target_pairs={{0,1},{1,2},{2,3},{3,0},{4,5},{5,6},{6,7},{7,4},{8,9},{9,10},{10,1... | collective-permute-start | bytes 3145736 | tf_op jit(solution)/shard_map/ppermute | solution.py:111
  214.4 83.5 %collective-permute-start.18 = (bf16[2,2,256,1408]{3,2,1,0:T(8,128)(2,1)}, bf16[2,2,256,1408]{3,2,1,0:T(8,128)(2,1)}, u32[]{:S(2)}, u32[]{:S(2)}) collective-permute-start(bf16[2,2,256,1408]{3,2,1,0:T(8,128)(2,1)} %maximum_select_fusion.7), channel_id=1, source_target_pairs={{0,4},{4,0},{8,12},{12,8},{16,20},{20,16},{24,28},{28,24},{1,5},{5... | collective-permute-start | bytes 8650760 | tf_op jit(solution)/shard_map/ppermute | solution.py:47
  215.0 88.2 %collective-permute-start.15 = (bf16[2,2,256,1408]{3,2,1,0:T(8,128)(2,1)}, bf16[2,2,256,1408]{3,2,1,0:T(8,128)(2,1)}, u32[]{:S(2)}, u32[]{:S(2)}) collective-permute-start(bf16[2,2,256,1408]{3,2,1,0:T(8,128)(2,1)} %maximum_select_fusion.6), channel_id=1, source_target_pairs={{0,4},{4,0},{8,12},{12,8},{16,20},{20,16},{24,28},{28,24},{1,5},{5... | collective-permute-start | bytes 8650760 | tf_op jit(solution)/shard_map/ppermute | solution.py:47
  292.4 14.9 %collective-permute-start.9 = (bf16[2,2,128,2048]{3,2,1,0:T(8,128)(2,1)}, bf16[2,2,128,2048]{3,2,1,0:T(8,128)(2,1)S(1)}, u32[]{:S(2)}, u32[]{:S(2)}) collective-permute-start(bf16[2,2,128,2048]{3,2,1,0:T(8,128)(2,1)} %dynamic-slice_bitcast_fusion.2), channel_id=1, source_target_pairs={{0,4},{4,0},{8,12},{12,8},{16,20},{20,16},{24,28},{28,24},{1,5},{5... | collective-permute-start | bytes 6291464 | tf_op jit(solution)/shard_map/ppermute | solution.py:47
  297.3 11.3 %collective-permute-start.6 = (bf16[2,2,128,2048]{3,2,0,1:T(8,128)(2,1)S(1)}, bf16[2,2,128,2048]{3,2,0,1:T(8,128)(2,1)S(1)}, u32[]{:S(2)}, u32[]{:S(2)}) collective-permute-start(bf16[2,2,128,2048]{3,2,0,1:T(8,128)(2,1)S(1)} %bitcast.536), channel_id=1, source_target_pairs={{0,4},{4,0},{8,12},{12,8},{16,20},{20,16},{24,28},{28,24},{1,5},{5... | collective-permute-start | bytes 6291464 | tf_op jit(solution)/shard_map/ppermute | solution.py:47
  308.2 25.6 %collective-permute-start.10 = (bf16[2,128,2048]{2,1,0:T(8,128)(2,1)S(1)}, bf16[2,128,2048]{2,1,0:T(8,128)(2,1)S(1)}, u32[]{:S(2)}, u32[]{:S(2)}) collective-permute-start(bf16[2,128,2048]{2,1,0:T(8,128)(2,1)S(1)} %dynamic-slice_bitcast_fusion.9), channel_id=1, source_target_pairs={{0,16},{4,20},{8,24},{12,28},{16,0},{20,4},{24,8},{28,12},{1,17},{... | collective-permute-start | bytes 3145736 | tf_op jit(solution)/shard_map/ppermute | solution.py:47
  309.5 26.7 %collective-permute-start.7 = (bf16[2,128,2048]{2,1,0:T(8,128)(2,1)S(1)}, bf16[2,128,2048]{2,1,0:T(8,128)(2,1)S(1)}, u32[]{:S(2)}, u32[]{:S(2)}) collective-permute-start(bf16[2,128,2048]{2,1,0:T(8,128)(2,1)S(1)} %dynamic-slice_bitcast_fusion.10), channel_id=1, source_target_pairs={{0,8},{4,12},{8,0},{12,4},{16,24},{20,28},{24,16},{28,20},{1,9},{5... | collective-permute-start | bytes 3145736 | tf_op jit(solution)/shard_map/ppermute | solution.py:47
  334.3 13.7 %collective-permute-start.11 = (bf16[128,2048]{1,0:T(8,128)(2,1)S(1)}, bf16[128,2048]{1,0:T(8,128)(2,1)S(1)}, u32[]{:S(2)}, u32[]{:S(2)}) collective-permute-start(bf16[128,2048]{1,0:T(8,128)(2,1)S(1)} %dynamic-slice_bitcast_fusion.17), channel_id=1, source_target_pairs={{0,8},{4,12},{8,0},{12,4},{16,24},{20,28},{24,16},{28,20},{1,9},{5... | collective-permute-start | bytes 1572872 | tf_op jit(solution)/shard_map/ppermute | solution.py:47
  336.7 13.3 %collective-permute-start.8 = (bf16[128,2048]{1,0:T(8,128)(2,1)S(1)}, bf16[128,2048]{1,0:T(8,128)(2,1)S(1)}, u32[]{:S(2)}, u32[]{:S(2)}) collective-permute-start(bf16[128,2048]{1,0:T(8,128)(2,1)S(1)} %dynamic-slice_bitcast_fusion.18), channel_id=1, source_target_pairs={{0,16},{4,20},{8,24},{12,28},{16,0},{20,4},{24,8},{28,12},{1,17},{... | collective-permute-start | bytes 1572872 | tf_op jit(solution)/shard_map/ppermute | solution.py:47
  350.8 25.6 %collective-permute-start.12 = (bf16[256,2048]{1,0:T(8,128)(2,1)S(1)}, bf16[256,2048]{1,0:T(8,128)(2,1)S(1)}, u32[]{:S(2)}, u32[]{:S(2)}) collective-permute-start(bf16[256,2048]{1,0:T(8,128)(2,1)S(1)} %multiply_convert_fusion.3), channel_id=1, source_target_pairs={{0,1},{1,2},{2,3},{3,0},{4,5},{5,6},{6,7},{7,4},{8,9},{9,10},{10,1... | collective-permute-start | bytes 3145736 | tf_op jit(solution)/shard_map/ppermute | solution.py:111
  383.3 27.9 %collective-permute-start.26 = (bf16[256,2048]{1,0:T(8,128)(2,1)S(1)}, bf16[256,2048]{1,0:T(8,128)(2,1)S(1)}, u32[]{:S(2)}, u32[]{:S(2)}) collective-permute-start(bf16[256,2048]{1,0:T(8,128)(2,1)S(1)} %collective-permute-done.12), channel_id=1, source_target_pairs={{0,1},{1,2},{2,3},{3,0},{4,5},{5,6},{6,7},{7,4},{8,9},{9,10},{10,1... | collective-permute-start | bytes 3145736 | tf_op jit(solution)/shard_map/ppermute | solution.py:111
  385.3 48.4 %collective-permute-start.31 = (bf16[256,2048]{1,0:T(8,128)(2,1)S(1)}, bf16[256,2048]{1,0:T(8,128)(2,1)S(1)}, u32[]{:S(2)}, u32[]{:S(2)}) collective-permute-start(bf16[256,2048]{1,0:T(8,128)(2,1)S(1)} %fusion.39), channel_id=1, source_target_pairs={{0,1},{1,2},{2,3},{3,0},{4,5},{5,6},{6,7},{7,4},{8,9},{9,10},{10,1... | collective-permute-start | bytes 3145736 | tf_op jit(solution)/shard_map/ppermute | solution.py:111
  387.7 68.5 %collective-permute-start.25 = (bf16[256,2048]{1,0:T(8,128)(2,1)S(1)}, bf16[256,2048]{1,0:T(8,128)(2,1)S(1)}, u32[]{:S(2)}, u32[]{:S(2)}) collective-permute-start(bf16[256,2048]{1,0:T(8,128)(2,1)S(1)} %convolution_convert_fusion.10), channel_id=1, source_target_pairs={{0,1},{1,2},{2,3},{3,0},{4,5},{5,6},{6,7},{7,4},{8,9},{9,10},{10,1... | collective-permute-start | bytes 3145736 | tf_op jit(solution)/shard_map/ppermute | solution.py:111
  413.1 65.6 %collective-permute-start.28 = (bf16[256,2048]{1,0:T(8,128)(2,1)S(1)}, bf16[256,2048]{1,0:T(8,128)(2,1)S(1)}, u32[]{:S(2)}, u32[]{:S(2)}) collective-permute-start(bf16[256,2048]{1,0:T(8,128)(2,1)S(1)} %collective-permute-done.26), channel_id=1, source_target_pairs={{0,1},{1,2},{2,3},{3,0},{4,5},{5,6},{6,7},{7,4},{8,9},{9,10},{10,1... | collective-permute-start | bytes 3145736 | tf_op jit(solution)/shard_map/ppermute | solution.py:111
  437.3 63.8 %collective-permute-start.33 = (bf16[256,2048]{1,0:T(8,128)(2,1)S(1)}, bf16[256,2048]{1,0:T(8,128)(2,1)S(1)}, u32[]{:S(2)}, u32[]{:S(2)}) collective-permute-start(bf16[256,2048]{1,0:T(8,128)(2,1)S(1)} %add_convert_fusion.1), channel_id=1, source_target_pairs={{0,1},{1,2},{2,3},{3,0},{4,5},{5,6},{6,7},{7,4},{8,9},{9,10},{10,1... | collective-permute-start | bytes 3145736 | tf_op jit(solution)/shard_map/ppermute | solution.py:111
  458.1 65.5 %collective-permute-start.27 = (bf16[256,2048]{1,0:T(8,128)(2,1)S(1)}, bf16[256,2048]{1,0:T(8,128)(2,1)S(1)}, u32[]{:S(2)}, u32[]{:S(2)}) collective-permute-start(bf16[256,2048]{1,0:T(8,128)(2,1)S(1)} %add_convert_fusion.3), channel_id=1, source_target_pairs={{0,1},{1,2},{2,3},{3,0},{4,5},{5,6},{6,7},{7,4},{8,9},{9,10},{10,1... | collective-permute-start | bytes 3145736 | tf_op jit(solution)/shard_map/ppermute | solution.py:111
  505.6 72.9 %collective-permute-start.35 = (bf16[256,2048]{1,0:T(8,128)(2,1)}, bf16[256,2048]{1,0:T(8,128)(2,1)S(1)}, u32[]{:S(2)}, u32[]{:S(2)}) collective-permute-start(bf16[256,2048]{1,0:T(8,128)(2,1)} %add_convert_fusion), channel_id=1, source_target_pairs={{0,1},{1,2},{2,3},{3,0},{4,5},{5,6},{6,7},{7,4},{8,9},{9,10},{10,1... | collective-permute-start | bytes 3145736 | tf_op jit(solution)/shard_map/ppermute | solution.py:111
  524.9 56.9 %collective-permute-start.29 = (bf16[256,2048]{1,0:T(8,128)(2,1)}, bf16[256,2048]{1,0:T(8,128)(2,1)}, u32[]{:S(2)}, u32[]{:S(2)}) collective-permute-start(bf16[256,2048]{1,0:T(8,128)(2,1)} %add_convert_fusion.2), channel_id=1, source_target_pairs={{0,1},{1,2},{2,3},{3,0},{4,5},{5,6},{6,7},{7,4},{8,9},{9,10},{10,1... | collective-permute-start | bytes 3145736 | tf_op jit(solution)/shard_map/ppermute | solution.py:111
  543.6 118.5 %collective-permute-start.48 = (bf16[2,2,256,1408]{3,2,0,1:T(8,128)(2,1)}, bf16[2,2,256,1408]{3,2,0,1:T(8,128)(2,1)}, u32[]{:S(2)}, u32[]{:S(2)}) collective-permute-start(bf16[2,2,256,1408]{3,2,0,1:T(8,128)(2,1)} %bitcast.421), channel_id=1, source_target_pairs={{0,4},{4,0},{8,12},{12,8},{16,20},{20,16},{24,28},{28,24},{1,5},{5... | collective-permute-start | bytes 8650760 | tf_op jit(solution)/shard_map/ppermute | solution.py:47
  559.8 107.1 %collective-permute-start.51 = (bf16[2,2,256,1408]{3,2,1,0:T(8,128)(2,1)}, bf16[2,2,256,1408]{3,2,1,0:T(8,128)(2,1)}, u32[]{:S(2)}, u32[]{:S(2)}) collective-permute-start(bf16[2,2,256,1408]{3,2,1,0:T(8,128)(2,1)} %dynamic-slice_bitcast_fusion), channel_id=1, source_target_pairs={{0,4},{4,0},{8,12},{12,8},{16,20},{20,16},{24,28},{28,24},{1,5},{5... | collective-permute-start | bytes 8650760 | tf_op jit(solution)/shard_map/ppermute | solution.py:47
  576.2 12.8 %collective-permute-start.57 = (bf16[2,2,128,1408]{3,2,1,0:T(8,128)(2,1)}, bf16[2,2,128,1408]{3,2,1,0:T(8,128)(2,1)}, u32[]{:S(2)}, u32[]{:S(2)}) collective-permute-start(bf16[2,2,128,1408]{3,2,1,0:T(8,128)(2,1)} %dynamic-slice_bitcast_fusion.3), channel_id=1, source_target_pairs={{0,4},{4,0},{8,12},{12,8},{16,20},{20,16},{24,28},{28,24},{1,5},{5... | collective-permute-start | bytes 4325384 | tf_op jit(solution)/shard_map/ppermute | solution.py:47
  578.5 14.4 %collective-permute-start.54 = (bf16[2,2,128,1408]{3,2,1,0:T(8,128)(2,1)}, bf16[2,2,128,1408]{3,2,1,0:T(8,128)(2,1)}, u32[]{:S(2)}, u32[]{:S(2)}) collective-permute-start(bf16[2,2,128,1408]{3,2,1,0:T(8,128)(2,1)} %dynamic-slice_bitcast_fusion.4), channel_id=1, source_target_pairs={{0,4},{4,0},{8,12},{12,8},{16,20},{20,16},{24,28},{28,24},{1,5},{5... | collective-permute-start | bytes 4325384 | tf_op jit(solution)/shard_map/ppermute | solution.py:47
  588.4 14.1 %collective-permute-start.39 = (bf16[128,2048]{1,0:T(8,128)(2,1)}, bf16[128,2048]{1,0:T(8,128)(2,1)S(1)}, u32[]{:S(2)}, u32[]{:S(2)}) collective-permute-start(bf16[128,2048]{1,0:T(8,128)(2,1)} %get-tuple-element.112), channel_id=1, source_target_pairs={{0,8},{4,12},{8,0},{12,4},{16,24},{20,28},{24,16},{28,20},{1,9},{5... | collective-permute-start | bytes 1572872 | tf_op jit(solution)/shard_map/ppermute | solution.py:47
  589.0 17.4 %collective-permute-start.36 = (bf16[128,2048]{1,0:T(8,128)(2,1)}, bf16[128,2048]{1,0:T(8,128)(2,1)S(1)}, u32[]{:S(2)}, u32[]{:S(2)}) collective-permute-start(bf16[128,2048]{1,0:T(8,128)(2,1)} %get-tuple-element.113), channel_id=1, source_target_pairs={{0,16},{4,20},{8,24},{12,28},{16,0},{20,4},{24,8},{28,12},{1,17},{... | collective-permute-start | bytes 1572872 | tf_op jit(solution)/shard_map/ppermute | solution.py:47
  592.9 26.6 %collective-permute-start.58 = (bf16[2,128,1408]{2,1,0:T(8,128)(2,1)S(1)}, bf16[2,128,1408]{2,1,0:T(8,128)(2,1)S(1)}, u32[]{:S(2)}, u32[]{:S(2)}) collective-permute-start(bf16[2,128,1408]{2,1,0:T(8,128)(2,1)S(1)} %dynamic-slice_bitcast_fusion.11), channel_id=1, source_target_pairs={{0,16},{4,20},{8,24},{12,28},{16,0},{20,4},{24,8},{28,12},{1,17},{... | collective-permute-start | bytes 2162696 | tf_op jit(solution)/shard_map/ppermute | solution.py:47
  602.5 18.9 %collective-permute-start.55 = (bf16[2,128,1408]{2,1,0:T(8,128)(2,1)S(1)}, bf16[2,128,1408]{2,1,0:T(8,128)(2,1)S(1)}, u32[]{:S(2)}, u32[]{:S(2)}) collective-permute-start(bf16[2,128,1408]{2,1,0:T(8,128)(2,1)S(1)} %dynamic-slice_bitcast_fusion.12), channel_id=1, source_target_pairs={{0,8},{4,12},{8,0},{12,4},{16,24},{20,28},{24,16},{28,20},{1,9},{5... | collective-permute-start | bytes 2162696 | tf_op jit(solution)/shard_map/ppermute | solution.py:47
  606.4 52.9 %collective-permute-start.40 = (bf16[2,128,2048]{2,1,0:T(8,128)(2,1)}, bf16[2,128,2048]{2,1,0:T(8,128)(2,1)}, u32[]{:S(2)}, u32[]{:S(2)}) collective-permute-start(bf16[2,128,2048]{2,1,0:T(8,128)(2,1)} %maximum_select_fusion.31), channel_id=1, source_target_pairs={{0,16},{4,20},{8,24},{12,28},{16,0},{20,4},{24,8},{28,12},{1,17},{... | collective-permute-start | bytes 3145736 | tf_op jit(solution)/shard_map/ppermute | solution.py:47
  619.6 50.6 %collective-permute-start.37 = (bf16[2,128,2048]{2,1,0:T(8,128)(2,1)}, bf16[2,128,2048]{2,1,0:T(8,128)(2,1)}, u32[]{:S(2)}, u32[]{:S(2)}) collective-permute-start(bf16[2,128,2048]{2,1,0:T(8,128)(2,1)} %maximum_select_fusion.29), channel_id=1, source_target_pairs={{0,8},{4,12},{8,0},{12,4},{16,24},{20,28},{24,16},{28,20},{1,9},{5... | collective-permute-start | bytes 3145736 | tf_op jit(solution)/shard_map/ppermute | solution.py:47
  621.3 28.8 %collective-permute-start.59 = (bf16[128,1408]{1,0:T(8,128)(2,1)S(1)}, bf16[128,1408]{1,0:T(8,128)(2,1)S(1)}, u32[]{:S(2)}, u32[]{:S(2)}) collective-permute-start(bf16[128,1408]{1,0:T(8,128)(2,1)S(1)} %dynamic-slice_bitcast_fusion.19), channel_id=1, source_target_pairs={{0,8},{4,12},{8,0},{12,4},{16,24},{20,28},{24,16},{28,20},{1,9},{5... | collective-permute-start | bytes 1081352 | tf_op jit(solution)/shard_map/ppermute | solution.py:47
  662.0 42.8 %collective-permute-start.41 = (bf16[2,2,128,2048]{3,2,1,0:T(8,128)(2,1)S(1)}, bf16[2,2,128,2048]{3,2,1,0:T(8,128)(2,1)S(1)}, u32[]{:S(2)}, u32[]{:S(2)}) collective-permute-start(bf16[2,2,128,2048]{3,2,1,0:T(8,128)(2,1)S(1)} %maximum_select_fusion.17), channel_id=1, source_target_pairs={{0,4},{4,0},{8,12},{12,8},{16,20},{20,16},{24,28},{28,24},{1,5},{5... | collective-permute-start | bytes 6291464 | tf_op jit(solution)/shard_map/ppermute | solution.py:47
  665.2 33.6 %collective-permute-start.49 = (bf16[2,256,1408]{2,1,0:T(8,128)(2,1)S(1)}, bf16[2,256,1408]{2,1,0:T(8,128)(2,1)S(1)}, u32[]{:S(2)}, u32[]{:S(2)}) collective-permute-start(bf16[2,256,1408]{2,1,0:T(8,128)(2,1)S(1)} %dynamic-slice_bitcast_fusion.6), channel_id=1, source_target_pairs={{0,8},{4,12},{8,0},{12,4},{16,24},{20,28},{24,16},{28,20},{1,9},{5... | collective-permute-start | bytes 4325384 | tf_op jit(solution)/shard_map/ppermute | solution.py:47
  669.5 33.8 %collective-permute-start.52 = (bf16[2,256,1408]{2,1,0:T(8,128)(2,1)S(1)}, bf16[2,256,1408]{2,1,0:T(8,128)(2,1)S(1)}, u32[]{:S(2)}, u32[]{:S(2)}) collective-permute-start(bf16[2,256,1408]{2,1,0:T(8,128)(2,1)S(1)} %dynamic-slice_bitcast_fusion.5), channel_id=1, source_target_pairs={{0,16},{4,20},{8,24},{12,28},{16,0},{20,4},{24,8},{28,12},{1,17},{... | collective-permute-start | bytes 4325384 | tf_op jit(solution)/shard_map/ppermute | solution.py:47
  672.6 35.6 %collective-permute-start.38 = (bf16[2,2,128,2048]{3,2,0,1:T(8,128)(2,1)S(1)}, bf16[2,2,128,2048]{3,2,0,1:T(8,128)(2,1)S(1)}, u32[]{:S(2)}, u32[]{:S(2)}) collective-permute-start(bf16[2,2,128,2048]{3,2,0,1:T(8,128)(2,1)S(1)} %maximum_select_fusion.15), channel_id=1, source_target_pairs={{0,4},{4,0},{8,12},{12,8},{16,20},{20,16},{24,28},{28,24},{1,5},{5... | collective-permute-start | bytes 6291464 | tf_op jit(solution)/shard_map/ppermute | solution.py:47
  700.3 90.7 %collective-permute-start.50 = (bf16[256,1408]{1,0:T(8,128)(2,1)}, bf16[256,1408]{1,0:T(8,128)(2,1)}, u32[]{:S(2)}, u32[]{:S(2)}) collective-permute-start(bf16[256,1408]{1,0:T(8,128)(2,1)} %dynamic-slice_bitcast_fusion.14), channel_id=1, source_target_pairs={{0,16},{4,20},{8,24},{12,28},{16,0},{20,4},{24,8},{28,12},{1,17},{... | collective-permute-start | bytes 2162696 | tf_op jit(solution)/shard_map/ppermute | solution.py:47
  704.7 97.7 %collective-permute-start.53 = (bf16[256,1408]{1,0:T(8,128)(2,1)}, bf16[256,1408]{1,0:T(8,128)(2,1)}, u32[]{:S(2)}, u32[]{:S(2)}) collective-permute-start(bf16[256,1408]{1,0:T(8,128)(2,1)} %dynamic-slice_bitcast_fusion.13), channel_id=1, source_target_pairs={{0,8},{4,12},{8,0},{12,4},{16,24},{20,28},{24,16},{28,20},{1,9},{5... | collective-permute-start | bytes 2162696 | tf_op jit(solution)/shard_map/ppermute | solution.py:47
  769.2 25.4 %collective-permute-start.45 = (bf16[2,2,128,2048]{3,2,1,0:T(8,128)(2,1)}, bf16[2,2,128,2048]{3,2,1,0:T(8,128)(2,1)}, u32[]{:S(2)}, u32[]{:S(2)}) collective-permute-start(bf16[2,2,128,2048]{3,2,1,0:T(8,128)(2,1)} %dynamic-slice_bitcast_fusion.1), channel_id=1, source_target_pairs={{0,4},{4,0},{8,12},{12,8},{16,20},{20,16},{24,28},{28,24},{1,5},{5... | collective-permute-start | bytes 6291464 | tf_op jit(solution)/shard_map/ppermute | solution.py:47
  769.3 116.6 %reduce-scatter.3.cloned.1.call-start = ((), (), s32[]{:S(2)}) async-start(), calls=%async_computation.4 | async-start | bytes 3932160 | tf_op jit(solution)/shard_map/reduce_scatter | solution.py:356
  773.8 25.9 %collective-permute-start.42 = (bf16[2,2,128,2048]{3,2,0,1:T(8,128)(2,1)}, bf16[2,2,128,2048]{3,2,0,1:T(8,128)(2,1)}, u32[]{:S(2)}, u32[]{:S(2)}) collective-permute-start(bf16[2,2,128,2048]{3,2,0,1:T(8,128)(2,1)} %bitcast.422), channel_id=1, source_target_pairs={{0,4},{4,0},{8,12},{12,8},{16,20},{20,16},{24,28},{28,24},{1,5},{5... | collective-permute-start | bytes 6291464 | tf_op jit(solution)/shard_map/ppermute | solution.py:47
  797.8 25.7 %collective-permute-start.46 = (bf16[2,128,2048]{2,1,0:T(8,128)(2,1)S(1)}, bf16[2,128,2048]{2,1,0:T(8,128)(2,1)S(1)}, u32[]{:S(2)}, u32[]{:S(2)}) collective-permute-start(bf16[2,128,2048]{2,1,0:T(8,128)(2,1)S(1)} %dynamic-slice_bitcast_fusion.7), channel_id=1, source_target_pairs={{0,16},{4,20},{8,24},{12,28},{16,0},{20,4},{24,8},{28,12},{1,17},{... | collective-permute-start | bytes 3145736 | tf_op jit(solution)/shard_map/ppermute | solution.py:47
  802.2 26.1 %collective-permute-start.43 = (bf16[2,128,2048]{2,1,0:T(8,128)(2,1)S(1)}, bf16[2,128,2048]{2,1,0:T(8,128)(2,1)S(1)}, u32[]{:S(2)}, u32[]{:S(2)}) collective-permute-start(bf16[2,128,2048]{2,1,0:T(8,128)(2,1)S(1)} %dynamic-slice_bitcast_fusion.8), channel_id=1, source_target_pairs={{0,8},{4,12},{8,0},{12,4},{16,24},{20,28},{24,16},{28,20},{1,9},{5... | collective-permute-start | bytes 3145736 | tf_op jit(solution)/shard_map/ppermute | solution.py:47
  824.0 14.9 %collective-permute-start.47 = (bf16[128,2048]{1,0:T(8,128)(2,1)S(1)}, bf16[128,2048]{1,0:T(8,128)(2,1)}, u32[]{:S(2)}, u32[]{:S(2)}) collective-permute-start(bf16[128,2048]{1,0:T(8,128)(2,1)S(1)} %dynamic-slice_bitcast_fusion.15), channel_id=1, source_target_pairs={{0,8},{4,12},{8,0},{12,4},{16,24},{20,28},{24,16},{28,20},{1,9},{5... | collective-permute-start | bytes 1572872 | tf_op jit(solution)/shard_map/ppermute | solution.py:47
  829.9 13.0 %collective-permute-start.44 = (bf16[128,2048]{1,0:T(8,128)(2,1)}, bf16[128,2048]{1,0:T(8,128)(2,1)}, u32[]{:S(2)}, u32[]{:S(2)}) collective-permute-start(bf16[128,2048]{1,0:T(8,128)(2,1)} %dynamic-slice_bitcast_fusion.16), channel_id=1, source_target_pairs={{0,16},{4,20},{8,24},{12,28},{16,0},{20,4},{24,8},{28,12},{1,17},{... | collective-permute-start | bytes 1572872 | tf_op jit(solution)/shard_map/ppermute | solution.py:47
  885.8 17.1 %all-to-all-start.1 = ((bf16[8,64,768]{2,1,0:T(8,128)(2,1)}), bf16[8,64,768]{2,1,0:T(8,128)(2,1)}, u32[]{:S(2)}, u32[]{:S(2)}) async-start(bf16[8,64,768]{2,1,0:T(8,128)(2,1)} %bitcast.547), calls=%async_computation.2 | async-start | bytes 1572864 | tf_op jit(solution)/shard_map/all_to_all | solution.py:364
  (103 other events, 1330.5 us)
Sparse Core Ops, SparseCore 0:
  29.6 63.0 all-gather.8
  109.4 34.9 all-gather.10
  769.4 28.1 reduce-scatter.4
  799.8 58.8 reduce-scatter.2

commit v2 on v1

--- a/solution.py
+++ b/solution.py
@@ -41,6 +41,22 @@
 def norm_back(grad_norm, unit, scale, gain):
     scaled = grad_norm * gain
     return scale * (scaled - unit * jnp.mean(scaled * unit, axis=-1, keepdims=True))
+
+
+def untouched_kernel(*refs):
+    pass
+
+
+def after(value, *others):
+    somewhere = pl.BlockSpec(memory_space=pl.ANY)
+    return pl.pallas_call(
+        untouched_kernel,
+        out_shape=jax.ShapeDtypeStruct(value.shape, value.dtype),
+        in_specs=[somewhere] * (1 + len(others)),
+        out_specs=somewhere,
+        input_output_aliases={0: 0},
+        cost_estimate=pl.CostEstimate(flops=0, bytes_accessed=0, transcendentals=0),
+    )(value, *others)
 
 
 def swap(value, mask):
@@ -64,7 +80,7 @@
     return value.reshape((1 << len(order),) + base)
 
 
-def scatter_bits(value, order):
+def scatter_bits(value, order, sent=bf16, hold=(None, None)):
     count = len(order)
     value = value.reshape((2,) * count + value.shape[1:])
     left = sorted(order, reverse=True)
@@ -72,10 +88,12 @@
         at = left.index(mask)
         left.remove(mask)
         bit = own_bit(mask)
-        send = lax.dynamic_index_in_dim(value, 1 - bit, at, keepdims=False)
+        send = lax.dynamic_index_in_dim(value, 1 - bit, at, keepdims=False).astype(sent)
         keep = lax.dynamic_index_in_dim(value, bit, at, keepdims=False)
-        total = keep.astype(f32) + swap(send.astype(bf16), mask).astype(f32)
-        value = total.astype(bf16) if left else total
+        if hold[0] == count - len(left) - 1:
+            send = after(send, hold[1])
+        total = keep.astype(f32) + swap(send, mask).astype(f32)
+        value = total.astype(sent) if left else total
     return value
 
 
@@ -86,23 +104,16 @@
     return down, [down[1], down[0]] + down[2:]
 
 
-def gather_rows(value, masks):
+def gather_halves(value, masks):
     first, second = orders(masks)
-    half = value.shape[0] // 2
+    half = value.shape[-1] // 2
+    return gather_bits(value[..., :half], first), gather_bits(value[..., half:], second)
+
+
+def scatter_halves(left, right, masks):
+    first, second = orders(masks)
     return jnp.concatenate(
-        [gather_bits(value[:half], first), gather_bits(value[half:], second)], axis=1
-    )
-
-
-def scatter_rows(value, masks):
-    first, second = orders(masks)
-    half = value.shape[1] // 2
-    return jnp.concatenate(
-        [
-            scatter_bits(value[:, :half], first[::-1]),
-            scatter_bits(value[:, half:], second[::-1]),
-        ],
-        axis=0,
+        [scatter_bits(left, first[::-1]), scatter_bits(right, second[::-1])], axis=-1
     )
 
 
@@ -120,10 +131,721 @@
 
 def ring_scatter(blocks):
     total = blocks[1 % len(blocks)]
+    totals = [total]
     for k in range(2, len(blocks) + 1):
-        moved = ring(total.astype(bf16)).astype(f32)
+        moved = ring(total).astype(f32)
         total = moved + blocks[k % len(blocks)].astype(f32)
+        if k < len(blocks):
+            total = total.astype(bf16)
+            totals.append(total)
+    return total, totals
+
+
+def shifted_blocks(value):
+    parts = lax.axis_size("tensor")
+    blocks = [value]
+    for k in range(1, parts):
+        blocks.append(lax.ppermute(value, "tensor", [(i, (i + k) % parts) for i in range(parts)]))
+    return blocks
+
+
+def scatter_straight(value):
+    here = lax.axis_index("tensor")
+    parts = lax.axis_size("tensor")
+    total = lax.dynamic_index_in_dim(value, here, 0, keepdims=False)
+    for k in range(1, parts):
+        send = lax.dynamic_index_in_dim(value, lax.rem(here + k, parts), 0, keepdims=False)
+        total += lax.ppermute(send, "tensor", [(i, (i + k) % parts) for i in range(parts)])
     return total
+
+
+def in_order(blocks):
+    here = lax.axis_index("tensor")
+    parts = len(blocks)
+    stacked = jnp.stack(blocks[::-1] + blocks[::-1])
+    return lax.dynamic_slice_in_dim(stacked, parts - 1 - here, parts, 0)
+
+
+def partner(mask):
+    me = lax.axis_index("dp")
+    return me + mask * (1 - 2 * lax.rem(lax.div(me, mask), 2))
+
+
+def greet(masks, ring_too=False):
+    barrier = pltpu.get_barrier_semaphore()
+    others = [{"dp": partner(mask)} for mask in masks]
+    if ring_too:
+        others += [{"tensor": beside(1)}, {"tensor": beside(-1)}]
+    for other in others:
+        pl.semaphore_signal(
+            barrier, inc=1, device_id=other, device_id_type=pl.DeviceIdType.MESH
+        )
+    pl.semaphore_wait(barrier, len(others))
+
+
+def beside(step):
+    parts = lax.axis_size("tensor")
+    return lax.rem(lax.axis_index("tensor") + step + parts, parts)
+
+
+def slot_of(copies, masks):
+    me = lax.axis_index("dp")
+    for mask in masks:
+        me = me + mask * (1 - 2 * lax.rem(lax.div(me, mask), 2))
+    return lax.div(me, copies)
+
+
+def to_right(source, target, send_sem, recv_sem):
+    return pltpu.make_async_remote_copy(
+        src_ref=source,
+        dst_ref=target,
+        send_sem=send_sem,
+        recv_sem=recv_sem,
+        device_id={"tensor": beside(1)},
+        device_id_type=pl.DeviceIdType.MESH,
+    )
+
+
+def plane_gather_kernel(
+    copies, value_ref, all_ref, own_sem, send_sem, recv_sem, weight_ref=None, weights_ref=None,
+    ring_send=None, ring_recv=None,
+):
+    near, one, two = copies, 2 * copies, 4 * copies
+    half = value_ref.shape[0] // 2
+    top, low = pl.ds(0, half), pl.ds(half, half)
+    mine = slot_of(copies, ())
+    at_one, at_two = slot_of(copies, (one,)), slot_of(copies, (two,))
+    at_both = slot_of(copies, (one, two))
+    greet((near, one, two), weight_ref is not None)
+    local = pltpu.make_async_copy(value_ref, all_ref.at[mine], own_sem.at[0])
+    local.start()
+    copies_out = []
+    ring_steps = []
+    if weight_ref is not None:
+        own = beside(0)
+        keep = pltpu.make_async_copy(weight_ref, weights_ref.at[own], own_sem.at[1])
+        keep.start()
+        for k in range(lax.axis_size("tensor") - 1):
+            source = weight_ref if k == 0 else weights_ref.at[beside(-k)]
+            ring_steps.append(
+                to_right(source, weights_ref.at[beside(-k)], ring_send.at[k], ring_recv.at[k])
+            )
+        ring_steps[0].start()
+
+    def send(source, slot, rows, mask):
+        index = len(copies_out)
+        copy = pltpu.make_async_remote_copy(
+            src_ref=source,
+            dst_ref=all_ref.at[slot, rows],
+            send_sem=send_sem.at[index],
+            recv_sem=recv_sem.at[index],
+            device_id={"dp": partner(mask)},
+            device_id_type=pl.DeviceIdType.MESH,
+        )
+        copy.start()
+        copies_out.append(copy)
+        return copy
+
+    def forward(slot, rows, mask):
+        return send(all_ref.at[slot, rows], slot, rows, mask)
+
+    two_top = send(value_ref.at[top], mine, top, two)
+    one_low = send(value_ref.at[low], mine, low, one)
+    two_low = send(value_ref.at[low], mine, low, two)
+    one_top = send(value_ref.at[top], mine, top, one)
+    last = [send(value_ref.at[top], mine, top, near), send(value_ref.at[low], mine, low, near)]
+    two_top.wait_recv()
+    over_one = forward(at_two, top, one)
+    last.append(forward(at_two, top, near))
+    one_low.wait_recv()
+    over_two = forward(at_one, low, two)
+    last.append(forward(at_one, low, near))
+    two_low.wait_recv()
+    last.append(forward(at_two, low, near))
+    one_top.wait_recv()
+    last.append(forward(at_one, top, near))
+    over_one.wait_recv()
+    last.append(forward(at_both, top, near))
+    over_two.wait_recv()
+    last.append(forward(at_both, low, near))
+    for k, step in enumerate(ring_steps):
+        step.wait_recv()
+        if k + 1 < len(ring_steps):
+            ring_steps[k + 1].start()
+    for copy in last:
+        copy.wait_recv()
+    for copy in copies_out + ring_steps:
+        copy.wait_send()
+    local.wait()
+    if weight_ref is not None:
+        keep.wait()
+
+
+def gather_late_kernel(copies, late, weighty, value_ref, *refs):
+    if weighty:
+        weight_ref, all_ref, weights_ref = refs[0], refs[1 + late], refs[2 + late]
+        own_sem, send_sem, recv_sem, ring_send, ring_recv = refs[3 + late :]
+        plane_gather_kernel(
+            copies, value_ref, all_ref, own_sem, send_sem, recv_sem, weight_ref, weights_ref,
+            ring_send, ring_recv,
+        )
+    else:
+        plane_gather_kernel(copies, value_ref, *refs[late:])
+
+
+def plane_gather(value, copies, collective, weight=None, before=()):
+    rows, width = value.shape
+    parts = lax.axis_size("tensor")
+    somewhere = pl.BlockSpec(memory_space=pl.ANY)
+    shapes = [jax.ShapeDtypeStruct((8, rows, width), value.dtype)]
+    operands = [value]
+    scratch = [
+        pltpu.SemaphoreType.DMA((2,)),
+        pltpu.SemaphoreType.DMA((14,)),
+        pltpu.SemaphoreType.DMA((14,)),
+    ]
+    if weight is not None:
+        shapes.append(jax.ShapeDtypeStruct((parts,) + weight.shape, weight.dtype))
+        operands.append(weight)
+        scratch += [pltpu.SemaphoreType.DMA((parts - 1,))] * 2
+    operands += before
+    return pl.pallas_call(
+        functools.partial(gather_late_kernel, copies, len(before), weight is not None),
+        out_shape=shapes,
+        in_specs=[somewhere] * len(operands),
+        out_specs=[somewhere] * len(shapes),
+        scratch_shapes=scratch,
+        compiler_params=pltpu.CompilerParams(collective_id=collective, has_side_effects=True),
+        cost_estimate=pl.CostEstimate(
+            flops=0, bytes_accessed=320 * rows * width, transcendentals=0
+        ),
+    )(*operands)
+
+
+def plane_scatter_kernel(
+    copies, transposed, left_ref, right_ref, sum_ref, near_ref, one_ref, two_ref, part_ref,
+    send_sem, recv_sem, block_ref=None, blocks_ref=None, ring_send=None, ring_recv=None,
+    total_ref=None, shares=None, ring_buf=None, load_sem=None,
+):
+    near, one, two = copies, 2 * copies, 4 * copies
+    rows, width = sum_ref.shape
+    half = rows // 2
+    top, low = pl.ds(0, half), pl.ds(half, half)
+    tile = min(512, width)
+    greet((near, one, two), ring_send is not None)
+    ring_steps = []
+    parts = lax.axis_size("tensor")
+    if shares is not None:
+        loads = [
+            pltpu.make_async_copy(block_ref.at[beside(-k)], shares.at[k], load_sem.at[k])
+            for k in range(parts)
+        ]
+        for load in loads:
+            load.start()
+        for load in loads:
+            load.wait()
+        sum_steps = [
+            to_right(shares.at[k + 1], ring_buf.at[k], ring_send.at[k], ring_recv.at[k])
+            for k in range(parts - 1)
+        ]
+        sum_steps[0].start()
+    elif block_ref is not None:
+        for k in range(blocks_ref.shape[0]):
+            source = block_ref if k == 0 else blocks_ref.at[k - 1]
+            ring_steps.append(
+                to_right(source, blocks_ref.at[k], ring_send.at[k], ring_recv.at[k])
+            )
+        ring_steps[0].start()
+    flips = [(), (one,), (two,), (one, two)]
+    copies_out = []
+
+    def send(source, target, mask):
+        index = len(copies_out)
+        copy = pltpu.make_async_remote_copy(
+            src_ref=source,
+            dst_ref=target,
+            send_sem=send_sem.at[index],
+            recv_sem=recv_sem.at[index],
+            device_id={"dp": partner(mask)},
+            device_id_type=pl.DeviceIdType.MESH,
+        )
+        copy.start()
+        copies_out.append(copy)
+        return copy
+
+    def each_tile(body):
+        @pl.loop(0, width // tile)
+        def _(k):
+            body(pl.ds(pl.multiple_of(k * tile, tile), tile))
+
+    def product(slot, columns):
+        left = left_ref[slot]
+        if transposed:
+            return matmul_rt(left, right_ref[columns, :])
+        return matmul(left, right_ref[:, columns])
+
+    arriving = {}
+    for k in (3, 1, 2, 0):
+        slot = slot_of(copies, flips[k] + (near,))
+
+        def theirs(columns, k=k, slot=slot):
+            part_ref[k, :, columns] = product(slot, columns).astype(bf16)
+
+        each_tile(theirs)
+        arriving[k] = send(part_ref.at[k], near_ref.at[k], near)
+
+    def added(k):
+        slot = slot_of(copies, flips[k])
+        arriving[k].wait_recv()
+
+        def mine(columns):
+            total = product(slot, columns) + near_ref[k, :, columns].astype(f32)
+            if k == 0:
+                sum_ref[:, columns] = total
+            else:
+                near_ref[k, :, columns] = total.astype(bf16)
+
+        each_tile(mine)
+
+    added(3)
+    one_first = send(near_ref.at[3, top], one_ref.at[0], one)
+    two_first = send(near_ref.at[3, low], two_ref.at[0], two)
+    added(1)
+    one_second = send(near_ref.at[1, top], one_ref.at[1], one)
+    added(2)
+    two_second = send(near_ref.at[2, low], two_ref.at[1], two)
+    added(0)
+
+    one_first.wait_recv()
+
+    def pass_top(columns):
+        total = near_ref[2, top, columns].astype(f32) + one_ref[0, :, columns].astype(f32)
+        near_ref[2, top, columns] = total.astype(bf16)
+
+    each_tile(pass_top)
+    two_last = send(near_ref.at[2, top], two_ref.at[2], two)
+    two_first.wait_recv()
+
+    def pass_low(columns):
+        total = near_ref[1, low, columns].astype(f32) + two_ref[0, :, columns].astype(f32)
+        near_ref[1, low, columns] = total.astype(bf16)
+
+    each_tile(pass_low)
+    one_last = send(near_ref.at[1, low], one_ref.at[2], one)
+
+    def finish(rows_at, first, at_first, second, at_second):
+        def body(columns):
+            sum_ref[rows_at, columns] += (
+                first[at_first, :, columns].astype(f32) + second[at_second, :, columns].astype(f32)
+            )
+
+        each_tile(body)
+
+    def sum_step(k):
+        sum_steps[k].wait_recv()
+        many = shares.shape[1] // 4
+
+        @pl.loop(0, 4)
+        def _(n):
+            some = pl.ds(pl.multiple_of(n * many, many), many)
+            at = (k + 2) % parts
+            total = shares[at, some, :].astype(f32) + ring_buf[k, some, :].astype(f32)
+            if at:
+                shares[at, some, :] = total.astype(bf16)
+            else:
+                total_ref[some, :] = total
+
+        if k + 1 < parts - 1:
+            sum_steps[k + 1].start()
+
+    if shares is not None:
+        sum_step(0)
+    for k, step in enumerate(ring_steps):
+        step.wait_recv()
+        if k + 1 < len(ring_steps):
+            ring_steps[k + 1].start()
+    one_second.wait_recv()
+    two_last.wait_recv()
+    finish(top, one_ref, 1, two_ref, 2)
+    two_second.wait_recv()
+    one_last.wait_recv()
+    finish(low, two_ref, 1, one_ref, 2)
+    if shares is not None:
+        for k in range(1, parts - 1):
+            sum_step(k)
+        ring_steps = sum_steps
+    for copy in copies_out + ring_steps:
+        copy.wait_send()
+
+
+def scatter_late_kernel(copies, transposed, late, left_ref, right_ref, block_ref, *refs):
+    sum_ref, blocks_ref = refs[late : late + 2]
+    refs = refs[late + 2 :]
+    if len(refs) == 8:
+        plane_scatter_kernel(
+            copies, transposed, left_ref, right_ref, sum_ref, *refs[:6], block_ref, blocks_ref,
+            *refs[6:],
+        )
+    else:
+        plane_scatter_kernel(
+            copies, transposed, left_ref, right_ref, sum_ref, *refs[:6], block_ref, None,
+            *refs[6:8], blocks_ref, *refs[8:],
+        )
+
+
+def plane_scatter(left, right, copies, transposed, collective, block=None, sums=None, before=()):
+    group, rows, depth = left.shape
+    width = right.shape[0] if transposed else right.shape[1]
+    half = rows // 2
+    vmem = pl.BlockSpec(memory_space=pltpu.VMEM)
+    somewhere = pl.BlockSpec(memory_space=pl.ANY)
+    scratch = [
+        pltpu.VMEM((4, rows, width), bf16),
+        pltpu.VMEM((3, half, width), bf16),
+        pltpu.VMEM((3, half, width), bf16),
+        pltpu.VMEM((4, rows, width), bf16),
+        pltpu.SemaphoreType.DMA((10,)),
+        pltpu.SemaphoreType.DMA((10,)),
+    ]
+    shapes = [jax.ShapeDtypeStruct((rows, width), f32)]
+    out_specs = [vmem]
+    parts = lax.axis_size("tensor")
+    if block is not None:
+        operands = [left, right, block]
+        steps = parts - 2
+        shapes.append(jax.ShapeDtypeStruct((steps,) + block.shape, block.dtype))
+        out_specs.append(somewhere)
+        scratch += [pltpu.SemaphoreType.DMA((steps,))] * 2
+    else:
+        operands = [left, right, sums]
+        shapes.append(jax.ShapeDtypeStruct(sums.shape[1:], f32))
+        out_specs.append(vmem)
+        scratch += [pltpu.SemaphoreType.DMA((parts - 1,))] * 2
+        scratch += [
+            pltpu.VMEM(sums.shape, bf16),
+            pltpu.VMEM((parts - 1,) + sums.shape[1:], bf16),
+            pltpu.SemaphoreType.DMA((parts,)),
+        ]
+    operands += before
+    return pl.pallas_call(
+        functools.partial(
+            scatter_late_kernel, copies, transposed, len(before)
+        ),
+        out_shape=shapes,
+        in_specs=[vmem, vmem] + [somewhere] * (len(operands) - 2),
+        out_specs=out_specs,
+        scratch_shapes=scratch,
+        compiler_params=pltpu.CompilerParams(
+            collective_id=collective, has_side_effects=True, vmem_limit_bytes=48 * 1024 * 1024
+        ),
+        cost_estimate=pl.CostEstimate(
+            flops=2 * group * rows * depth * width,
+            bytes_accessed=400 * rows * width,
+            transcendentals=0,
+        ),
+    )(*operands)
+
+
+def column_tiles(width, most=512):
+    return [(at, min(most, width - at)) for at in range(0, width, most)]
+
+
+def swiglu_kernel(
+    copies,
+    normed_ref, own_ref, first_ref, others_ref, gate_hbm, up_hbm, down_hbm,
+    rows_out, norm_sum, gate_sum, up_sum, down_sum,
+    normed, masked, gate_w, up_w, down_w, hidden, gate_low, up_low, back, rows, ring_buf,
+    one_buf, two_buf, in_sem, out_sem, send_sem, recv_sem, sum_send, sum_recv, near_send,
+    near_recv, one_send, one_recv, two_send, two_recv, ready_sem,
+):
+    parts = lax.axis_size("tensor")
+    near, one, two = copies, 2 * copies, 4 * copies
+    greet((near, one, two), True)
+    own = pltpu.make_async_copy(normed_ref, normed.at[0], in_sem.at[0])
+    own.start()
+    loads = [
+        pltpu.make_async_copy(gate_hbm, gate_w, in_sem.at[1]),
+        pltpu.make_async_copy(up_hbm, up_w, in_sem.at[2]),
+        pltpu.make_async_copy(own_ref, masked.at[0], in_sem.at[3]),
+        pltpu.make_async_copy(down_hbm, down_w, in_sem.at[4]),
+        pltpu.make_async_copy(first_ref, masked.at[1], in_sem.at[5]),
+        pltpu.make_async_copy(others_ref, masked.at[pl.ds(2, parts - 2)], in_sem.at[6]),
+    ]
+    own.wait()
+    for load in loads:
+        load.start()
+    width = normed.shape[2]
+    tile = min(512, width)
+
+    def hop(k):
+        return to_right(normed.at[k], normed.at[k + 1], send_sem.at[k], recv_sem.at[k])
+
+    def sum_hop(k):
+        return to_right(back.at[k + 1], ring_buf.at[k], sum_send.at[k], sum_recv.at[k])
+
+    hop(0).start()
+    for load in loads:
+        load.wait()
+
+    def store(k):
+        home = lax.rem(lax.axis_index("tensor") + parts - k, parts)
+        slot = lax.rem(k, 2)
+        return pltpu.make_async_copy(rows.at[slot], rows_out.at[home], out_sem.at[slot])
+
+    def block(k, nothing):
+        @pl.when(k > 0)
+        def _():
+            hop(k - 1).wait_recv()
+
+        @pl.when(jnp.logical_and(k > 0, k < parts - 1))
+        def _():
+            hop(k).start()
+
+        @pl.when(k == parts - 1)
+        def _():
+            sum_hop(0).start()
+
+        for at, size in column_tiles(hidden.shape[2]):
+            columns = pl.ds(at, size)
+            glu_gate = matmul(normed[k], gate_w[:, columns])
+            glu_up = matmul(normed[k], up_w[:, columns])
+            grad_hidden = matmul(masked[k], down_w[:, columns])
+            squash = jax.nn.sigmoid(glu_gate)
+            act = glu_gate * squash
+            slope = squash * (1.0 + glu_gate * (1.0 - squash))
+            hidden[k, :, columns] = (act * glu_up).astype(bf16)
+            gate_low[k, :, columns] = (grad_hidden * glu_up * slope).astype(bf16)
+            up_low[k, :, columns] = (grad_hidden * act).astype(bf16)
+
+        @pl.when(k > 1)
+        def _():
+            store(k - 2).wait()
+
+        slot = lax.rem(k, 2)
+
+        @pl.loop(0, width // tile)
+        def _(n):
+            some = pl.ds(pl.multiple_of(n * tile, tile), tile)
+            back[k, :, some] = (
+                matmul_rt(gate_low[k], gate_w[some, :]) + matmul_rt(up_low[k], up_w[some, :])
+            ).astype(bf16)
+            rows[slot, :, some] = matmul_rt(hidden[k], down_w[some, :]).astype(bf16)
+
+        store(k).start()
+        return nothing
+
+    lax.fori_loop(0, parts, block, 0)
+
+    pl.semaphore_signal(
+        ready_sem,
+        inc=1,
+        device_id={"dp": partner(near)},
+        device_id_type=pl.DeviceIdType.MESH,
+    )
+    share = width // 8
+    half = share // 2
+    hidden_width = hidden.shape[2]
+    tall = parts * normed.shape[1]
+    kinds = (
+        (normed, gate_low, gate_w, gate_sum),
+        (normed, up_low, up_w, up_sum),
+        (masked, hidden, down_w, down_sum),
+    )
+
+    def product(kind, slot):
+        left, right, _, _ = kinds[kind]
+        some = pl.ds(pl.multiple_of(slot * share, share), share)
+        return matmul_lt(
+            left[:, :, some].reshape(tall, share), right[...].reshape(tall, hidden_width)
+        )
+
+    def part_at(k):
+        return pl.ds(pl.multiple_of(k * share, share), share)
+
+    def near_at(k):
+        return pl.ds(pl.multiple_of((4 + k) * share, share), share)
+
+    def halves(k):
+        at = (4 + k) * share
+        return (
+            pl.ds(pl.multiple_of(at, half), half),
+            pl.ds(pl.multiple_of(at + half, half), half),
+        )
+
+    def across(source, target, send, recv, mask):
+        return pltpu.make_async_remote_copy(
+            src_ref=source,
+            dst_ref=target,
+            send_sem=send,
+            recv_sem=recv,
+            device_id={"dp": partner(mask)},
+            device_id_type=pl.DeviceIdType.MESH,
+        )
+
+    def near_copy(kind, k):
+        room = kinds[kind][2]
+        return across(
+            room.at[part_at(k)], room.at[near_at(k)], near_send.at[kind, k],
+            near_recv.at[kind, k], near,
+        )
+
+    def one_copy(kind, n):
+        room = kinds[kind][2]
+        rows_at = (halves(3)[0], halves(1)[0], halves(1)[1])[n]
+        return across(
+            room.at[rows_at], one_buf.at[kind, n], one_send.at[kind, n], one_recv.at[kind, n], one
+        )
+
+    def two_copy(kind, n):
+        room = kinds[kind][2]
+        rows_at = (halves(3)[1], halves(2)[1], halves(2)[0])[n]
+        return across(
+            room.at[rows_at], two_buf.at[kind, n], two_send.at[kind, n], two_recv.at[kind, n], two
+        )
+
+    def flipped(k, near_too):
+        me = lax.axis_index("dp")
+
+        def turn(mask, on):
+            return on * mask * (1 - 2 * lax.rem(lax.div(me, mask), 2))
+
+        there = me + turn(one, lax.rem(k, 2)) + turn(two, lax.div(k, 2)) + turn(near, near_too)
+        return lax.div(there, copies)
+
+    def in_turn(i):
+        return 3 - 2 * i + 3 * lax.div(i, 2)
+
+    def sum_step(k):
+        sum_hop(k).wait_recv()
+        if k + 1 < parts - 1:
+
+            @pl.loop(0, width // tile)
+            def _(n):
+                some = pl.ds(pl.multiple_of(n * tile, tile), tile)
+                total = back[k + 2, :, some].astype(f32) + ring_buf[k, :, some].astype(f32)
+                back[k + 2, :, some] = total.astype(bf16)
+
+            sum_hop(k + 1).start()
+        else:
+
+            @pl.loop(0, width // tile)
+            def _(n):
+                some = pl.ds(pl.multiple_of(n * tile, tile), tile)
+                norm_sum[:, some] = back[0, :, some].astype(f32) + ring_buf[k, :, some].astype(f32)
+
+    pl.semaphore_wait(ready_sem, 1)
+
+    def theirs(i, nothing):
+        k = in_turn(i)
+        slot = flipped(k, 1)
+        for kind in range(3):
+            kinds[kind][2][part_at(k), :] = product(kind, slot).astype(bf16)
+            near_copy(kind, k).start()
+        return nothing
+
+    lax.fori_loop(0, 4, theirs, 0)
+    sum_step(0)
+
+    def mine(i, nothing):
+        k = in_turn(i)
+        slot = flipped(k, 0)
+        for kind in range(3):
+            near_copy(kind, k).wait_recv()
+            room = kinds[kind][2]
+            total = product(kind, slot) + room[near_at(k), :].astype(f32)
+            room[near_at(k), :] = total.astype(bf16)
+
+            @pl.when(k == 3)
+            def _():
+                one_copy(kind, 0).start()
+                two_copy(kind, 0).start()
+
+            @pl.when(k == 1)
+            def _():
+                one_copy(kind, 1).start()
+
+            @pl.when(k == 2)
+            def _():
+                two_copy(kind, 1).start()
+
+        return nothing
+
+    lax.fori_loop(0, 3, mine, 0)
+    for k in range(1, parts - 2):
+        sum_step(k)
+    for kind in range(3):
+        near_copy(kind, 0).wait_recv()
+        room, total_ref = kinds[kind][2:]
+        total_ref[...] = product(kind, flipped(0, 0)) + room[near_at(0), :].astype(f32)
+    for kind in range(3):
+        room = kinds[kind][2]
+        one_copy(kind, 0).wait_recv()
+        at = halves(2)[0]
+        room[at, :] = (room[at, :].astype(f32) + one_buf[kind, 0].astype(f32)).astype(bf16)
+        two_copy(kind, 2).start()
+        two_copy(kind, 0).wait_recv()
+        at = halves(1)[1]
+        room[at, :] = (room[at, :].astype(f32) + two_buf[kind, 0].astype(f32)).astype(bf16)
+        one_copy(kind, 2).start()
+    sum_step(parts - 2)
+    for kind in range(3):
+        total_ref = kinds[kind][3]
+        one_copy(kind, 1).wait_recv()
+        two_copy(kind, 2).wait_recv()
+        total_ref[:half, :] += one_buf[kind, 1].astype(f32) + two_buf[kind, 2].astype(f32)
+        two_copy(kind, 1).wait_recv()
+        one_copy(kind, 2).wait_recv()
+        total_ref[half:, :] += two_buf[kind, 1].astype(f32) + one_buf[kind, 2].astype(f32)
+    for kind in range(3):
+        for k in range(4):
+            near_copy(kind, k).wait_send()
+        for n in range(3):
+            one_copy(kind, n).wait_send()
+            two_copy(kind, n).wait_send()
+    for k in range(parts - 1):
+        hop(k).wait_send()
+        sum_hop(k).wait_send()
+    for k in (parts - 2, parts - 1):
+        store(k).wait()
+
+
+def swiglu(normed, own, first, others, gate_w, up_w, down_w, copies, collective):
+    parts = lax.axis_size("tensor")
+    rows, width = normed.shape
+    hidden = gate_w.shape[1]
+    share = width // 8
+    somewhere = pl.BlockSpec(memory_space=pl.ANY)
+    vmem = pl.BlockSpec(memory_space=pltpu.VMEM)
+    wide, narrow = (parts, rows, width), (parts, rows, hidden)
+    return pl.pallas_call(
+        functools.partial(swiglu_kernel, copies),
+        out_shape=[jax.ShapeDtypeStruct(wide, bf16), jax.ShapeDtypeStruct((rows, width), f32)]
+        + [jax.ShapeDtypeStruct((share, hidden), f32)] * 3,
+        in_specs=[somewhere] * 7,
+        out_specs=[somewhere] + [vmem] * 4,
+        scratch_shapes=[pltpu.VMEM(wide, bf16)] * 2
+        + [pltpu.VMEM((width, hidden), bf16)] * 3
+        + [pltpu.VMEM(narrow, bf16)] * 3
+        + [
+            pltpu.VMEM(wide, bf16),
+            pltpu.VMEM((2, rows, width), bf16),
+            pltpu.VMEM((parts - 1, rows, width), bf16),
+        ]
+        + [pltpu.VMEM((3, 3, share // 2, hidden), bf16)] * 2
+        + [pltpu.SemaphoreType.DMA((7,)), pltpu.SemaphoreType.DMA((2,))]
+        + [pltpu.SemaphoreType.DMA((parts - 1,))] * 4
+        + [pltpu.SemaphoreType.DMA((3, 4))] * 2
+        + [pltpu.SemaphoreType.DMA((3, 3))] * 4
+        + [pltpu.SemaphoreType.REGULAR],
+        compiler_params=pltpu.CompilerParams(
+            collective_id=collective, has_side_effects=True, vmem_limit_bytes=60 * 1024 * 1024
+        ),
+        cost_estimate=pl.CostEstimate(
+            flops=18 * parts * rows * width * hidden,
+            bytes_accessed=1100 * rows * width,
+            transcendentals=parts * rows * hidden,
+        ),
+    )(normed, own, first, others, gate_w, up_w, down_w)
 
 
 def forward_kernel(steps, seqs, forget_ref, drive_ref, state_ref, decay_ref):
@@ -213,7 +935,9 @@
     low = lax.rem(lengths, 32).astype(bf16)
     length_row = jnp.concatenate([high, low, jnp.zeros((own_rows - 2,), bf16)])
     small = jnp.stack([gain_mix, gain_glu, lower_bound, length_row])
-    small = lax.all_gather(small, ("dp", "tensor"), axis=0, tiled=False).astype(f32)
+    small = in_order(shifted_blocks(small))
+    small = gather_bits(small, sorted(all_masks, reverse=True)).astype(f32)
+    small = small.reshape((data_parts * tensor_parts,) + small.shape[2:])
     gain_one = small[:, 0].reshape(width)
     gain_two = small[:, 1].reshape(width)
     bound = lax.dynamic_slice_in_dim(small[:, 2].reshape(width), group_index * channels, channels)
@@ -234,32 +958,34 @@
     pieces = lax.all_to_all(
         pieces, "dp", 0, 0, axis_index_groups=group_lists if copies > 1 else None, tiled=True
     )
-    out_piece = w_out
+    pieces = jnp.concatenate([pieces, spread(w_out)], axis=2)
     if copies > 1:
-        pieces = gather_bits(pieces, copy_masks[::-1]).transpose(1, 0, 2, 3)
-        out_piece = gather_bits(out_piece, copy_masks[::-1])
-    pieces = pieces.reshape(group * copies, own_rows, 3 * channels)
-    out_piece = out_piece.reshape(copies, own_rows, width)
-    mixer_w = lax.all_gather(pieces, "tensor", axis=1, tiled=False)
-    mixer_w = mixer_w.reshape(width, 3 * channels)
-    out_w = lax.all_gather(out_piece, "tensor", axis=1, tiled=False).reshape(channels, width)
+        pieces = gather_bits(pieces, copy_masks[::-1])
+    pieces = pieces.reshape(copies, group, own_rows, 4 * channels)
+    masked_grad = live_own * cotangent
+    masked_own = masked_grad.astype(bf16)
+    masked_first = ring(masked_own)
+
+    scale_one, unit_one = norm_rows(inputs)
+    normed_one, pieces = plane_gather(
+        (unit_one * gain_one).astype(bf16),
+        copies,
+        1,
+        pieces.reshape(copies * group * own_rows, 4 * channels),
+        [masked_first],
+    )
+    rows_all = group * rows_here
+    normed_one = normed_one.reshape(rows_all, width)
+    pieces = pieces.reshape(tensor_parts, copies, group, own_rows, 4 * channels)
+    mixer_w = pieces[..., : 3 * channels].transpose(2, 1, 0, 3, 4).reshape(width, 3 * channels)
+    out_w = pieces[..., 3 * channels :].transpose(1, 0, 3, 2, 4).reshape(channels, width)
 
     first, second = orders(all_masks)
-    half = w_gate.shape[0] // 2
-    down_t = w_down.T
     hidden_here = w_gate.shape[1]
-    gate_w = gather_bits(w_gate, first).reshape(width, hidden_here)
-    up_w = gather_bits(w_up, second).reshape(width, hidden_here)
-    down_w = jnp.concatenate(
-        [gather_bits(down_t[:half], first), gather_bits(down_t[half:], second)], axis=1
-    ).reshape(width, hidden_here)
-
-    masked_grad = live_own * cotangent
-    masked_blocks = ring_blocks(masked_grad.astype(bf16))
-
-    scale_one, unit_one = norm_rows(inputs)
-    normed_one = gather_rows((unit_one * gain_one).astype(bf16), group_masks)
-    normed_one = normed_one.reshape(group * rows_here, width)
+    gate_w, up_w, down_w = (
+        lax.all_gather(weight, "dp", axis=0, tiled=True) for weight in (w_gate, w_up, w_down.T)
+    )
+
     pre = matmul(normed_one, mixer_w)
     input_pre = pre[:, :channels]
     forget_sig = jax.nn.sigmoid(pre[:, channels : 2 * channels])
@@ -273,7 +999,7 @@
     part_state = part_state.reshape(shaped)
     part_decay = part_decay.reshape(shaped)
     ends = jnp.stack([part_state[:, -1], part_decay[:, -1]])
-    all_ends = lax.all_gather(ends, "tensor", axis=0, tiled=False)
+    all_ends = in_order(shifted_blocks(ends))
     coming = jnp.zeros((group, channels), f32)
     entering = coming
     for k in range(tensor_parts - 1):
@@ -284,43 +1010,30 @@
     state = state.reshape(group * rows_here, channels)
     prior_state = prior_state.reshape(group * rows_here, channels)
     mixed_low = (state * gate_act).astype(bf16)
-    mixed = matmul(mixed_low, out_w).astype(bf16).reshape(group, rows_here, width)
-    stream = inputs + scatter_rows(mixed, group_masks)
+    mixed = mixed_low.reshape(shaped)
+    mixed_sum, masked_others = plane_scatter(mixed, out_w, copies, False, 2, masked_first)
+    stream = inputs + mixed_sum
 
     scale_two, unit_two = norm_rows(stream)
-    normed_blocks = ring_blocks((unit_two * gain_two).astype(bf16))
-    hidden_blocks, gate_low, up_low, back_parts, out_parts = [], [], [], [], []
-    for normed, masked in zip(normed_blocks, masked_blocks):
-        glu_gate = matmul(normed, gate_w)
-        glu_up = matmul(normed, up_w)
-        hidden = (silu_of(glu_gate) * glu_up).astype(bf16)
-        grad_hidden = matmul(masked, down_w)
-        grad_gate = (grad_hidden * glu_up * silu_slope(glu_gate)).astype(bf16)
-        grad_up = (grad_hidden * silu_of(glu_gate)).astype(bf16)
-        back_parts.append((matmul_rt(grad_gate, gate_w) + matmul_rt(grad_up, up_w)).astype(bf16))
-        out_parts.append(matmul_rt(hidden, down_w).astype(bf16))
-        hidden_blocks.append(hidden)
-        gate_low.append(grad_gate)
-        up_low.append(grad_up)
-    grad_norm_two = ring_scatter(back_parts)
-    output = live_own * (stream + ring_scatter(out_parts))
-
-    all_normed = jnp.concatenate(normed_blocks)
-    all_masked = jnp.concatenate(masked_blocks)
-    by_owner = (data_parts, width // data_parts, hidden_here)
-    grad_gate_w = matmul_lt(all_normed, jnp.concatenate(gate_low)).astype(bf16).reshape(by_owner)
-    grad_up_w = matmul_lt(all_normed, jnp.concatenate(up_low)).astype(bf16).reshape(by_owner)
-    grad_down_t = (
-        matmul_lt(all_masked, jnp.concatenate(hidden_blocks)).astype(bf16).reshape(by_owner)
-    )
-    grad_gate_mine = scatter_bits(grad_gate_w, first[::-1])
-    grad_up_mine = scatter_bits(grad_up_w, second[::-1])
-    grad_down_mine = scatter_rows(grad_down_t, all_masks).T
+    normed_two = (unit_two * gain_two).astype(bf16)
+    out_rows, grad_norm_two, *weight_sums = swiglu(
+        normed_two, masked_own, masked_first, masked_others, gate_w, up_w, down_w, copies, 4
+    )
+    if copies > 1:
+        weight_sums = [
+            scatter_bits(total.reshape(copies, width // data_parts, hidden_here), copy_masks, f32)
+            for total in weight_sums
+        ]
+    grad_gate_mine, grad_up_mine, grad_down_mine = weight_sums
+    grad_down_mine = grad_down_mine.T
+
+    out_rows = out_rows.reshape(tensor_parts * rows_here, width)
+    out_sum = lax.psum_scatter(out_rows, "tensor", scatter_dimension=0, tiled=True)
 
     gain_two_part = jnp.sum(grad_norm_two * unit_two, axis=0)
     grad_stream = masked_grad + norm_back(grad_norm_two, unit_two, scale_two, gain_two)
-    stream_low = gather_rows(grad_stream.astype(bf16), group_masks)
-    stream_low = stream_low.reshape(group * rows_here, width)
+    (stream_low,) = plane_gather(grad_stream.astype(bf16), copies, 5)
+    stream_low = stream_low.reshape(rows_all, width)
 
     grad_out_w = matmul_lt(mixed_low, stream_low).astype(bf16)
     grad_mixed = matmul_rt(stream_low, out_w)
@@ -331,7 +1044,7 @@
     part_after = part_after.reshape(shaped)
     first_forget = forget.reshape(shaped)[:, 0]
     begins = jnp.stack([first_forget * part_carried[:, 0], first_forget * part_after[:, 0]])
-    all_begins = lax.all_gather(begins, "tensor", axis=0, tiled=False)
+    all_begins = in_order(shifted_blocks(begins))
     coming = jnp.zeros((group, channels), f32)
     entering = coming
     for k in range(tensor_parts - 1, 0, -1):
@@ -345,35 +1058,48 @@
     grad_bound = jnp.sum(grad_forget * (1.0 - forget_sig), axis=0)
     grad_forget_pre = (grad_forget * (1.0 - bound) * forget_sig * (1.0 - forget_sig)).astype(bf16)
     grad_pre = jnp.concatenate([grad_input_pre, grad_forget_pre, grad_gate_pre], axis=1)
-    grad_normed = matmul_rt(grad_pre, mixer_w).astype(bf16).reshape(group, rows_here, width)
-    grad_norm_one = scatter_rows(grad_normed, group_masks)
+    grad_parts = grad_pre.reshape(group, rows_here, 3 * channels)
+    grad_mixer = matmul_lt(normed_one, grad_pre).astype(bf16)
+    mixer_sums = jnp.concatenate(
+        [
+            grad_mixer.reshape(group, copies, tensor_parts, own_rows, 3 * channels).transpose(
+                2, 1, 0, 3, 4
+            ),
+            grad_out_w.reshape(copies, tensor_parts, own_rows, group, channels).transpose(
+                1, 0, 3, 2, 4
+            ),
+        ],
+        axis=-1,
+    ).reshape(tensor_parts, copies * group * own_rows, 4 * channels)
+    grad_norm_one, mixer_sums = plane_scatter(
+        grad_parts, mixer_w, copies, True, 3, sums=mixer_sums, before=[out_sum]
+    )
+    output = live_own * (stream + after(out_sum, grad_norm_one).astype(f32))
     gain_one_part = jnp.sum(grad_norm_one * unit_one, axis=0)
     grad_inputs = grad_stream + norm_back(grad_norm_one, unit_one, scale_one, gain_one)
 
-    grad_mixer = matmul_lt(normed_one, grad_pre).astype(bf16)
-    grad_mixer = grad_mixer.reshape(data_parts, tensor_parts, own_rows, 3 * channels)
-    grad_mixer = grad_mixer.transpose(1, 0, 2, 3)
-    grad_mixer = lax.psum_scatter(grad_mixer, "tensor", scatter_dimension=0, tiled=False)
-    grad_out = grad_out_w.reshape(copies, tensor_parts, own_rows, width).transpose(1, 0, 2, 3)
-    grad_out = lax.psum_scatter(grad_out, "tensor", scatter_dimension=0, tiled=False)
+    mixer_sums = mixer_sums.reshape(copies, group, own_rows, 4 * channels)
     if copies > 1:
-        grad_mixer = grad_mixer.reshape(group, copies, own_rows, 3 * channels)
-        grad_mixer = scatter_bits(grad_mixer.transpose(1, 0, 2, 3), copy_masks).astype(bf16)
-        grad_out = scatter_bits(grad_out, copy_masks)
-    grad_mixer = grad_mixer.reshape(group, own_rows, 3 * channels)
+        mixer_sums = scatter_bits(mixer_sums, copy_masks, f32)
+    mixer_sums = mixer_sums.reshape(group, own_rows, 4 * channels)
+    grad_out = mixer_sums[..., 3 * channels :].transpose(1, 0, 2).reshape(own_rows, width)
     grad_mixer = lax.all_to_all(
-        grad_mixer, "dp", 0, 0, axis_index_groups=group_lists if copies > 1 else None, tiled=True
+        mixer_sums[..., : 3 * channels].astype(bf16),
+        "dp",
+        0,
+        0,
+        axis_index_groups=group_lists if copies > 1 else None,
+        tiled=True,
     )
     grad_mixer = grad_mixer.reshape(group, own_rows, 3, channels).transpose(2, 1, 0, 3)
     grad_mixer = grad_mixer.reshape(3, own_rows, width).astype(f32)
-    grad_out = grad_out.reshape(own_rows, width).astype(f32)
 
     bound_part = lax.dynamic_update_slice_in_dim(
         jnp.zeros((width,), f32), grad_bound, group_index * channels, 0
     )
     sums = jnp.stack([gain_one_part, gain_two_part, bound_part])
-    sums = sums.reshape(3, data_parts * tensor_parts, own_rows).transpose(1, 0, 2)
-    sums = lax.psum_scatter(sums, ("dp", "tensor"), scatter_dimension=0, tiled=False)
+    sums = sums.reshape(3, data_parts, tensor_parts, own_rows).transpose(1, 2, 0, 3)
+    sums = scatter_straight(scatter_bits(sums, sorted(all_masks), f32))
     return (
         output,
         grad_inputs,

time: 927 us -> 658 us (0.71)
  Pallas kernels: 12.6 us -> 462 us
  waiting for transfers between devices: 334 us -> 20.2 us
  blocking collectives: 155 us -> 0 us
  matrix products: 148 us -> 28.9 us
  other arithmetic: 121 us -> 41.5 us
  local copies, waits for them, and re-layouts: 84 us -> 44.4 us
  starting transfers between devices: 46.7 us -> 35 us
    pallas_call x0 -> x6, Pallas kernels: none -> 449 us  [the longest x1 176 us: swiglu(): pl.pallas_call(functools.partial(swiglu_kernel, copies), out_shape=[jax.S...]
    ppermute x48 -> x6, waiting for transfers between devices: 204 us -> 15.6 us  [swap(): lax.ppermute(value, 'dp', [(i, i ^ mask) for i in range(lax.axis_size('dp...]
    ppermute x12 -> x1, waiting for transfers between devices: 121 us -> 0.01 us  [ring(): lax.ppermute(value, 'tensor', [(i, (i + 1) % parts) for i in range(parts)])]
    all_gather x3 -> x0, blocking collectives: 96.8 us -> none  [the longest x1 67.5 us: on_device(): lax.all_gather(small, ('dp', 'tensor'), axis=0, tiled=False).astype(f32)]
    select_n x40 -> x4, other arithmetic: 47.6 us -> 0.06 us  [gather_bits(): value = jnp.where(own_bit(mask) == 0, low, high)]
    dot_general x14 -> x1, matrix products: 50 us -> 6.86 us  [matmul(): return jnp.dot(left, right, preferred_element_type=f32)]
    dot_general x5 -> x2, matrix products: 53.2 us -> 12.2 us  [matmul_lt(): lax.dot_general(left, right, (((0,), (0,)), ((), ())), preferred_element_...]
    unnamed x1 -> x0, blocking collectives: 40 us -> none
  transfers between devices with their start and end apart: 65 -> 25, of which waited for: 27 -> 6; matrix products, arithmetic and copies ran while one was open for 35% -> 14% of each run, Pallas kernels for 1% -> 32%
where the time goes in v2:
time: 658 us; the launch traced here: 648 us
  Pallas kernels  462 us (70%)
  local copies, waits for them, and re-layouts  44.4 us (7%)
  other arithmetic  41.5 us (6%)
  starting transfers between devices  35 us (5%)
  matrix products  28.9 us (4%)
  waiting for transfers between devices  20.2 us (3%)
  between operations  16.1 us (2%)
    pallas_call x1, Pallas kernels, swiglu(): pl.pallas_call(functools.partial(swiglu_kernel, copies), out_shape=[jax.S...  176 us
    pallas_call x2, Pallas kernels, plane_gather(): pl.pallas_call(functools.partial(gather_late_kernel, copies, len(before),...  145 us
    pallas_call x2, Pallas kernels, plane_scatter(): pl.pallas_call(functools.partial(scatter_late_kernel, copies, transposed,...  128 us
    unnamed x136, local copies, waits for them, and re-layouts  28.5 us
    ppermute x6, waiting for transfers between devices, swap(): lax.ppermute(value, 'dp', [(i, i ^ mask) for i in range(lax.axis_size('dp...  15.6 us
  transfers between devices with their start and end apart: 25, of which 6 were waited for; matrix products, arithmetic and copies ran while one was open for 14% of the time, Pallas kernels for 32%

profile of v2, /device:TPU:0, one launch (start us, length us, event | category | flops | bytes accessed | tf_op | source)
XLA Modules:
  0.0 647.9 jit_solution(13724976108611153208)
XLA Ops:
  7.3 2.4 copy.82
  11.3 5.1 collective-permute-start
  16.4 1.0 collective-permute-start.2
  17.4 1.1 multiply_convert_fusion.6.own_ref
  18.5 2.5 collective-permute-start.6
  22.1 4.2 all-to-all-start
  28.5 2.0 collective-permute-start.3
  30.5 7.0 %collective-permute-done.3 = bf16[4,4,64]{2,1,0:T(4,128)(2,1)S(1)} collective-permute-done((bf16[4,4,64]{2,1,0:T(4,128)(2,1)S(1)}, bf16[4,4,64]{2,1,0:T(4,128)(2,1)S(1)}, u32[]{:S(2)}, u32[]{:S(2)}) %collective-permute-start.3) | collective-permute-done | bytes 2080 | tf_op jit(solution)/shard_map/ppermute | solution.py:63
  37.5 3.6 collective-permute-start.4
  41.2 1.6 collective-permute-done.4
  42.9 1.1 collective-permute-done.5
  44.6 1.2 multiply_convert_fusion.5.value_ref
  45.8 2.2 pad_maximum_fusion.3
  49.0 105.3 %shard_map.220 = (bf16[8,256,2048]{2,1,0:T(8,128)(2,1)}, bf16[4,512,1024]{2,1,0:T(8,128)(2,1)}) custom-call(bf16[256,2048]{1,0:T(8,128)(2,1)} %multiply_convert_fusion.5.value_ref, bf16[512,1024]{1,0:T(8,128)(2,1)} %bitcast.238, bf16[256,2048]{1,0:T(8,128)(2,1)} %copy-done.9), custom_call_target="tpu_custom_call" | custom-call | bytes 167772160 | tf_op jit(solution)/shard_map/pallas_call | solution.py:312
  154.3 2.4 slice.158
  157.0 2.8 copy-done.49
  159.8 6.9 %fusion.18 = f32[2048,768]{1,0:T(8,128)S(1)} fusion(bf16[2048,2048]{1,0:T(8,128)(2,1)S(1)} %bitcast.297, bf16[2048,768]{1,0:T(8,128)(2,1)S(1)} %bitcast.247), kind=kOutput, calls=%fused_computation.147 | convolution fusion | flops 6442450944 | bytes 17825792 | tf_op jit(solution)/shard_map/dot_general | solution.py:16
  166.7 1.2 multiply_multiply_fusion
  167.9 1.4 copy-done.19
  169.3 5.9 shard_map.221
  175.2 1.3 copy-done
  177.2 1.5 collective-permute-start.7
  178.8 1.5 collective-permute-start.8
  180.3 1.3 slice.166
  182.6 1.0 collective-permute-done.8
  183.7 2.2 collective-permute-done.9
  186.1 2.3 multiply_convert_fusion.4
  188.4 49.1 %shard_map.222 = (f32[256,2048]{1,0:T(8,128)S(1)}, bf16[2,256,2048]{2,1,0:T(8,128)(2,1)}) custom-call(bf16[8,256,256]{2,1,0:T(8,128)(2,1)S(1)} %bitcast.227, bf16[256,2048]{1,0:T(8,128)(2,1)S(1)} %bitcast.228, bf16[256,2048]{1,0:T(8,128)(2,1)S(1)} %copy-done.10), custom_call_target="tpu_custom_call" | custom-call | flops 2147483648 | bytes 209715200 | tf_op jit(solution)/shard_map/pallas_call | solution.py:530
  237.8 1.3 copy-done.16
  239.1 1.2 multiply_convert_fusion.3.normed_ref
  240.3 176.3 %shard_map.223 = (bf16[4,256,2048]{2,1,0:T(8,128)(2,1)}, f32[256,2048]{1,0:T(8,128)}, f32[256,1408]{1,0:T(8,128)}, f32[256,1408]{1,0:T(8,128)}, f32[256,1408]{1,0:T(8,128)}) custom-call(bf16[256,2048]{1,0:T(8,128)(2,1)} %multiply_convert_fusion.3.normed_ref, bf16[256,2048]{1,0:T(8,128)(2,1)} %multiply_convert_fusion.6.own_ref, bf16[256,2048]{1,0:T(8,128)(2,1)} %copy-done.9, ...), custom_call_target="tpu_custom_call" | custom-call | flops 53150220288 | bytes 576716800 | tf_op jit(solution)/shard_map/pallas_call | solution.py:820
  416.8 2.5 slice_add_fusion
  419.3 1.6 pad_maximum_fusion.2
  422.5 1.2 multiply_reduce_fusion.1
  424.1 2.4 fusion.15
  426.5 39.7 %shard_map.224 = bf16[8,256,2048]{2,1,0:T(8,128)(2,1)} custom-call(bf16[256,2048]{1,0:T(8,128)(2,1)} %get-tuple-element.96.value_ref), custom_call_target="tpu_custom_call" | custom-call | bytes 167772160 | tf_op jit(solution)/shard_map/pallas_call | solution.py:312
  466.2 9.8 %fusion.8 = (f32[2048,256]{1,0:T(8,128)S(1)}, bf16[2048,256]{1,0:T(8,128)(2,1)}) fusion(f32[2048,768]{1,0:T(8,128)} %copy-done.19, f32[2048,256]{1,0:T(8,128)} %copy-done, f32[2048,256]{1,0:T(8,128)} %copy-done.2, f32[8,256]{1,0:T(8,128)S(1)} %bitcast.270, bf16[2048,2048]{1,0:T(8,128)(2,1)} %bitcast.234, bf16[256,2048]{1,0:T(8,128)(2,1)} %bitcast.229), kind=kOutput, calls=%fused_computation.50 | convolution fusion | flops 2154823680 | bytes 18882560 | tf_op jit(solution)/shard_map/dot_general | solution.py:20
  476.1 6.6 %shard_map.225 = (f32[2048,256]{1,0:T(8,128)S(1)}, f32[2048,256]{1,0:T(8,128)S(1)}) custom-call(f32[2048,256]{1,0:T(8,128)S(1)} %get-tuple-element.101.forget_ref, f32[2048,256]{1,0:T(8,128)S(1)} %get-tuple-element.105.drive_ref), custom_call_target="tpu_custom_call" | custom-call | flops 2097152 | bytes 8388608 | tf_op jit(solution)/shard_map/pallas_call | solution.py:890
  483.5 2.0 collective-permute-start.12
  485.5 2.3 convolution_convert_fusion.1
  488.2 1.2 copy.130
  489.4 1.4 stack.189
  490.7 1.5 copy.94
  496.8 5.2 multiply_reduce_fusion
  502.0 2.6 multiply_convert_fusion.1
  504.6 9.8 %convolution_convert_fusion = bf16[2048,768]{1,0:T(8,128)(2,1)S(1)} fusion(bf16[2048,2048]{1,0:T(8,128)(2,1)} %bitcast.296, bf16[2048,256]{1,0:T(8,128)(2,1)S(1)} %copy-done.23, bf16[2048,256]{1,0:T(8,128)(2,1)S(1)} %multiply_convert_fusion.1, bf16[2048,256]{1,0:T(8,128)(2,1)S(1)} %get-tuple-element.104), kind=kOutput, calls=%fused_computation.1 | convolution fusion | flops 6453460992 | bytes 14680064 | tf_op jit(solution)/shard_map/dot_general | solution.py:24
  516.0 4.0 pad_maximum_fusion
  520.0 1.8 pad_maximum_fusion.1
  521.8 1.2 copy-done.6
  523.0 78.8 %shard_map.226 = (f32[256,2048]{1,0:T(8,128)S(1)}, f32[512,1024]{1,0:T(8,128)S(1)}) custom-call(bf16[8,256,768]{2,1,0:T(8,128)(2,1)} %bitcast.249, bf16[2048,768]{1,0:T(8,128)(2,1)} %bitcast.248, bf16[4,512,1024]{2,1,0:T(8,128)(2,1)} %bitcast.243, bf16[256,2048]{1,0:T(8,128)(2,1)S(1)} %copy-done.6), custom_call_target="tpu_custom_call" | custom-call | flops 6442450944 | bytes 209715200 | tf_op jit(solution)/shard_map/pallas_call | solution.py:530
  603.4 2.4 slice.224
  605.8 3.5 all-to-all-start.1
  609.4 2.0 collective-permute-start.14
  611.4 4.0 multiply_add_fusion
  615.4 5.8 collective-permute-done.14
  621.2 1.6 collective-permute-start.15
  622.8 2.8 add_multiply_fusion
  625.6 1.5 collective-permute-start.16
  627.8 2.0 collective-permute-start.18
  629.8 1.1 slice_bitcast_fusion
  632.3 1.1 reshape.574
  633.4 1.5 fusion.16
  638.7 1.1 copy.165
  639.8 1.1 copy.166
  (233 shorter events, 24.7 us)
Async XLA Ops:
  7.2 4.1 copy-start.48
  7.2 4.1 copy-start.47
  7.2 4.0 copy-start.46
  7.2 10.2 %copy-start.20 = (f32[256,2048]{1,0:T(8,128)S(1)}, f32[256,2048]{1,0:T(8,128)}, u32[]{:S(2)}) copy-start(f32[256,2048]{1,0:T(8,128)} %param.25) | copy-start | bytes 6291460
  7.2 233.1 %all-gather.8.cloned.1.call-start = ((), (), s32[]{:S(2)}) async-start(), calls=%async_computation.5 | async-start | bytes 6488064 | tf_op jit(solution)/shard_map/all_gather | solution.py:986
  9.7 11.3 %copy-start.33 = (bf16[64,2048]{1,0:T(8,128)(2,1)S(1)}, bf16[64,2048]{1,0:T(8,128)(2,1)}, u32[]{:S(2)}) copy-start(bf16[64,2048]{1,0:T(8,128)(2,1)} %param.18) | copy-start | bytes 786436
  9.7 11.3 %copy-start.34 = (bf16[64,2048]{1,0:T(8,128)(2,1)S(1)}, bf16[64,2048]{1,0:T(8,128)(2,1)}, u32[]{:S(2)}) copy-start(bf16[64,2048]{1,0:T(8,128)(2,1)} %param.20) | copy-start | bytes 786436
  9.7 11.3 %copy-start.35 = (bf16[64,2048]{1,0:T(8,128)(2,1)S(1)}, bf16[64,2048]{1,0:T(8,128)(2,1)}, u32[]{:S(2)}) copy-start(bf16[64,2048]{1,0:T(8,128)(2,1)} %param.19) | copy-start | bytes 786436
  9.7 230.6 %all-gather.4.cloned.1.call-start = ((), (), s32[]{:S(2)}) async-start(), calls=%async_computation.3 | async-start | bytes 6488064 | tf_op jit(solution)/shard_map/all_gather | solution.py:986
  11.3 17.1 %collective-permute-start = (bf16[4,64]{1,0:T(4,128)(2,1)S(1)}, bf16[4,64]{1,0:T(4,128)(2,1)S(1)}, u32[]{:S(2)}, u32[]{:S(2)}) collective-permute-start(bf16[4,64]{1,0:T(4,128)(2,1)S(1)} %pad_maximum_fusion.7), channel_id=1, source_target_pairs={{0,3},{1,0},{2,1},{3,2},{4,7},{5,4},{6,5},{7,6},{8,11},{9,8},{10,9... | collective-permute-start | bytes 1544 | tf_op jit(solution)/shard_map/ppermute | solution.py:148
  16.4 12.0 %collective-permute-start.1 = (bf16[4,64]{1,0:T(4,128)(2,1)S(1)}, bf16[4,64]{1,0:T(4,128)(2,1)S(1)}, u32[]{:S(2)}, u32[]{:S(2)}) collective-permute-start(bf16[4,64]{1,0:T(4,128)(2,1)S(1)} %pad_maximum_fusion.7), channel_id=1, source_target_pairs={{0,2},{1,3},{2,0},{3,1},{4,6},{5,7},{6,4},{7,5},{8,10},{9,11},{10,... | collective-permute-start | bytes 1544 | tf_op jit(solution)/shard_map/ppermute | solution.py:148
  16.4 12.0 %collective-permute-start.2 = (bf16[4,64]{1,0:T(4,128)(2,1)S(1)}, bf16[4,64]{1,0:T(4,128)(2,1)S(1)}, u32[]{:S(2)}, u32[]{:S(2)}) collective-permute-start(bf16[4,64]{1,0:T(4,128)(2,1)S(1)} %pad_maximum_fusion.7), channel_id=1, source_target_pairs={{0,1},{1,2},{2,3},{3,0},{4,5},{5,6},{6,7},{7,4},{8,9},{9,10},{10,1... | collective-permute-start | bytes 1544 | tf_op jit(solution)/shard_map/ppermute | solution.py:148
  17.4 406.3 %copy-start.40 = (f32[256]{0:T(256)}, f32[256]{0:T(256)S(1)}, u32[]{:S(2)}) copy-start(f32[256]{0:T(256)S(1)} %compare_convert_fusion) | copy-start | bytes 3076
  18.5 29.5 %collective-permute-start.6 = (bf16[256,2048]{1,0:T(8,128)(2,1)}, bf16[256,2048]{1,0:T(8,128)(2,1)S(1)}, u32[]{:S(2)}, u32[]{:S(2)}) collective-permute-start(bf16[256,2048]{1,0:T(8,128)(2,1)} %multiply_convert_fusion.6.own_ref), channel_id=1, source_target_pairs={{0,1},{1,2},{2,3},{3,0},{4,5},{5,6},{6,7},{7,4},{8,9},{9,10},{10,1... | collective-permute-start | bytes 3145736 | tf_op jit(solution)/shard_map/ppermute | solution.py:122
  21.1 6.0 copy-start.13
  22.1 23.7 %all-to-all-start = ((bf16[8,64,768]{2,1,0:T(8,128)(2,1)}), bf16[8,64,768]{2,1,0:T(8,128)(2,1)}, u32[]{:S(2)}, u32[]{:S(2)}) async-start(bf16[8,64,768]{2,1,0:T(8,128)(2,1)} %pad_maximum_fusion.4), calls=%async_computation | async-start | bytes 1572864 | tf_op jit(solution)/shard_map/all_to_all | solution.py:958
  26.3 214.0 %all-gather.6.cloned.1.call-start = ((), (), s32[]{:S(2)}) async-start(), calls=%async_computation.4 | async-start | bytes 6488064 | tf_op jit(solution)/shard_map/all_gather | solution.py:986
  27.0 494.7 %reduce-scatter.2.cloned.1.call-start = ((), (), s32[]{:S(2)}) async-start(), calls=%async_computation.6 | async-start | bytes 5242880 | tf_op jit(solution)/shard_map/reduce_scatter | solution.py:1031
  27.4 18.4 %copy-start.42 = (f32[256]{0:T(256)}, f32[256]{0:T(256)S(1)}, u32[]{:S(2)}) copy-start(f32[256]{0:T(256)S(1)} %add_rsqrt_fusion.1) | copy-start | bytes 3076
  28.5 9.0 %collective-permute-start.3 = (bf16[4,4,64]{2,1,0:T(4,128)(2,1)S(1)}, bf16[4,4,64]{2,1,0:T(4,128)(2,1)S(1)}, u32[]{:S(2)}, u32[]{:S(2)}) collective-permute-start(bf16[4,4,64]{2,1,0:T(4,128)(2,1)S(1)} %constant_dynamic-slice_fusion.6), channel_id=1, source_target_pairs={{0,16},{4,20},{8,24},{12,28},{16,0},{20,4},{24,8},{28,12},{1,17},{... | collective-permute-start | bytes 6152 | tf_op jit(solution)/shard_map/ppermute | solution.py:63
  37.5 5.3 collective-permute-start.4
  42.8 1.2 collective-permute-start.5
  44.4 3.6 copy-start.36
  44.4 122.2 %copy-start.38 = (f32[1,2,8,128]{3,1,2,0:T(2,128)}, f32[1,2,8,128]{3,1,2,0:T(2,128)S(1)}, u32[]{:S(2)}) copy-start(f32[1,2,8,128]{3,1,2,0:T(2,128)S(1)} %copy.109) | copy-start | bytes 24580
  44.6 122.1 %copy-start.44 = (f32[256]{0:T(256)}, f32[256]{0:T(256)S(1)}, u32[]{:S(2)}) copy-start(f32[256]{0:T(256)S(1)} %get-tuple-element.102) | copy-start | bytes 3076
  154.3 5.5 copy-start.49
  157.0 9.6 %copy-start.29 = (bf16[4,1,8,64,768]{4,3,0,2,1:T(8,128)(2,1)}, bf16[4,1,8,64,768]{4,3,0,2,1:T(8,128)(2,1)S(1)}, u32[]{:S(2)}) copy-start(bf16[4,1,8,64,768]{4,3,0,2,1:T(8,128)(2,1)S(1)} %copy.102) | copy-start | bytes 9437188
  166.7 2.6 copy-start.19
  177.2 5.4 collective-permute-start.7
  178.8 4.8 collective-permute-start.8
  180.3 5.5 collective-permute-start.9
  181.7 4.4 copy-start.1
  181.7 4.4 copy-start.3
  182.6 5.7 copy-start.5
  188.4 49.1 %copy-start.14 = (f32[256,2048]{1,0:T(8,128)S(1)}, f32[256,2048]{1,0:T(8,128)}, u32[]{:S(2)}) copy-start(f32[256,2048]{1,0:T(8,128)} %param.13) | copy-start | bytes 6291460
  419.3 2.6 copy-start.17
  419.3 3.2 copy-start.22
  466.2 19.3 %copy-start.12 = (bf16[8,256,2048]{2,1,0:T(8,128)(2,1)S(1)}, bf16[8,256,2048]{2,1,0:T(8,128)(2,1)}, u32[]{:S(2)}) copy-start(bf16[8,256,2048]{2,1,0:T(8,128)(2,1)} %shard_map.224) | copy-start | bytes 25165828
  482.7 5.1 copy-start.7
  482.7 5.1 copy-start.8
  483.4 8.8 %collective-permute-start.10 = (f32[2,8,256]{2,0,1:T(2,128)}, f32[2,8,256]{2,0,1:T(2,128)}, u32[]{:S(2)}, u32[]{:S(2)}) collective-permute-start(f32[2,8,256]{2,0,1:T(2,128)} %pad_maximum_fusion.6), channel_id=1, source_target_pairs={{0,3},{1,0},{2,1},{3,2},{4,7},{5,4},{6,5},{7,6},{8,11},{9,8},{10,9... | collective-permute-start | bytes 49160 | tf_op jit(solution)/shard_map/ppermute | solution.py:148
  483.4 9.6 %collective-permute-start.11 = (f32[2,8,256]{2,0,1:T(2,128)}, f32[2,8,256]{2,0,1:T(2,128)}, u32[]{:S(2)}, u32[]{:S(2)}) collective-permute-start(f32[2,8,256]{2,0,1:T(2,128)} %pad_maximum_fusion.6), channel_id=1, source_target_pairs={{0,2},{1,3},{2,0},{3,1},{4,6},{5,7},{6,4},{7,5},{8,10},{9,11},{10,... | collective-permute-start | bytes 49160 | tf_op jit(solution)/shard_map/ppermute | solution.py:148
  483.5 10.3 %collective-permute-start.12 = (f32[2,8,256]{2,0,1:T(2,128)}, f32[2,8,256]{2,0,1:T(2,128)}, u32[]{:S(2)}, u32[]{:S(2)}) collective-permute-start(f32[2,8,256]{2,0,1:T(2,128)} %pad_maximum_fusion.6), channel_id=1, source_target_pairs={{0,1},{1,2},{2,3},{3,0},{4,5},{5,6},{6,7},{7,4},{8,9},{9,10},{10,1... | collective-permute-start | bytes 49160 | tf_op jit(solution)/shard_map/ppermute | solution.py:148
  487.8 2.9 copy-start.32
  496.7 5.2 copy-start.45
  502.0 2.6 copy-start.25
  502.0 2.6 copy-start.23
  504.6 9.9 %copy-start.27 = (bf16[2048,256]{1,0:T(8,128)(2,1)}, bf16[2048,256]{1,0:T(8,128)(2,1)S(1)}, u32[]{:S(2)}) copy-start(bf16[2048,256]{1,0:T(8,128)(2,1)S(1)} %multiply_convert_fusion.1) | copy-start | bytes 3145732
  515.9 4.0 copy-start.24
  515.9 4.0 copy-start.26
  516.0 4.0 copy-start.28
  523.0 78.9 %copy-start.15 = (f32[256,2048]{1,0:T(8,128)S(1)}, f32[256,2048]{1,0:T(8,128)}, u32[]{:S(2)}) copy-start(f32[256,2048]{1,0:T(8,128)} %param.13) | copy-start | bytes 6291460
  523.0 78.9 %copy-start.37 = (f32[2048]{0:T(1024)S(1)}, f32[2048]{0:T(1024)}, u32[]{:S(2)}) copy-start(f32[2048]{0:T(1024)} %copy-done.36) | copy-start | bytes 24580
  523.0 78.9 %copy-start.43 = (f32[256]{0:T(256)S(1)}, f32[256]{0:T(256)}, u32[]{:S(2)}) copy-start(f32[256]{0:T(256)} %copy-done.42) | copy-start | bytes 3076
  601.8 9.5 %copy-start.4 = (f32[256,2048]{1,0:T(8,128)}, f32[256,2048]{1,0:T(8,128)S(1)}, u32[]{:S(2)}) copy-start(f32[256,2048]{1,0:T(8,128)S(1)} %get-tuple-element.37.refs_1_) | copy-start | bytes 6291460
  603.3 6.0 collective-permute-start.13
  605.8 26.5 %all-to-all-start.1 = ((bf16[8,64,768]{2,1,0:T(8,128)(2,1)}), bf16[8,64,768]{2,1,0:T(8,128)(2,1)S(1)}, u32[]{:S(2)}, u32[]{:S(2)}) async-start(bf16[8,64,768]{2,1,0:T(8,128)(2,1)} %slice.224), calls=%async_computation.2 | async-start | bytes 1572864 | tf_op jit(solution)/shard_map/all_to_all | solution.py:1086
  609.4 11.8 %collective-permute-start.14 = (f32[2,4,3,64]{3,1,2,0:T(4,128)S(1)}, f32[2,4,3,64]{3,1,2,0:T(4,128)S(1)}, u32[]{:S(2)}, u32[]{:S(2)}) collective-permute-start(f32[2,4,3,64]{3,1,2,0:T(4,128)S(1)} %dynamic-slice_bitcast_fusion), channel_id=1, source_target_pairs={{0,8},{4,12},{8,0},{12,4},{16,24},{20,28},{24,16},{28,20},{1,9},{5... | collective-permute-start | bytes 18440 | tf_op jit(solution)/shard_map/ppermute | solution.py:63
  615.4 7.3 %copy-start.18 = (f32[256,2048]{1,0:T(8,128)S(1)}, f32[256,2048]{1,0:T(8,128)}, u32[]{:S(2)}) copy-start(f32[256,2048]{1,0:T(8,128)} %copy-done.16) | copy-start | bytes 6291460
  615.4 7.3 %copy-start.41 = (f32[256]{0:T(256)S(1)}, f32[256]{0:T(256)}, u32[]{:S(2)}) copy-start(f32[256]{0:T(256)} %copy-done.40) | copy-start | bytes 3076
  621.2 4.4 collective-permute-start.15
  625.6 6.1 collective-permute-start.16
  627.1 4.6 collective-permute-start.17
  627.8 3.9 collective-permute-start.18
  (11 other events, 18.0 us)
Sparse Core Ops, SparseCore 0:
  9.9 61.9 all-gather.7
  73.8 52.7 all-gather.3
  128.6 43.3 all-gather.5
  416.8 74.4 reduce-scatter.1

commit v3 on v2

--- a/solution.py
+++ b/solution.py
@@ -206,34 +206,19 @@
     )
 
 
-def plane_gather_kernel(
-    copies, value_ref, all_ref, own_sem, send_sem, recv_sem, weight_ref=None, weights_ref=None,
-    ring_send=None, ring_recv=None,
-):
+def plane_gather_steps(copies, value_ref, all_ref, own_sem, send_sem, recv_sem):
     near, one, two = copies, 2 * copies, 4 * copies
     half = value_ref.shape[0] // 2
     top, low = pl.ds(0, half), pl.ds(half, half)
     mine = slot_of(copies, ())
     at_one, at_two = slot_of(copies, (one,)), slot_of(copies, (two,))
     at_both = slot_of(copies, (one, two))
-    greet((near, one, two), weight_ref is not None)
-    local = pltpu.make_async_copy(value_ref, all_ref.at[mine], own_sem.at[0])
-    local.start()
-    copies_out = []
-    ring_steps = []
-    if weight_ref is not None:
-        own = beside(0)
-        keep = pltpu.make_async_copy(weight_ref, weights_ref.at[own], own_sem.at[1])
-        keep.start()
-        for k in range(lax.axis_size("tensor") - 1):
-            source = weight_ref if k == 0 else weights_ref.at[beside(-k)]
-            ring_steps.append(
-                to_right(source, weights_ref.at[beside(-k)], ring_send.at[k], ring_recv.at[k])
-            )
-        ring_steps[0].start()
+    local = pltpu.make_async_copy(value_ref, all_ref.at[mine], own_sem)
+    sent = []
+    last = []
 
     def send(source, slot, rows, mask):
-        index = len(copies_out)
+        index = len(sent)
         copy = pltpu.make_async_remote_copy(
             src_ref=source,
             dst_ref=all_ref.at[slot, rows],
@@ -243,96 +228,100 @@
             device_id_type=pl.DeviceIdType.MESH,
         )
         copy.start()
-        copies_out.append(copy)
+        sent.append(copy)
+        if mask == near:
+            last.append(copy)
         return copy
 
     def forward(slot, rows, mask):
         return send(all_ref.at[slot, rows], slot, rows, mask)
 
-    two_top = send(value_ref.at[top], mine, top, two)
-    one_low = send(value_ref.at[low], mine, low, one)
-    two_low = send(value_ref.at[low], mine, low, two)
-    one_top = send(value_ref.at[top], mine, top, one)
-    last = [send(value_ref.at[top], mine, top, near), send(value_ref.at[low], mine, low, near)]
-    two_top.wait_recv()
-    over_one = forward(at_two, top, one)
-    last.append(forward(at_two, top, near))
-    one_low.wait_recv()
-    over_two = forward(at_one, low, two)
-    last.append(forward(at_one, low, near))
-    two_low.wait_recv()
-    last.append(forward(at_two, low, near))
-    one_top.wait_recv()
-    last.append(forward(at_one, top, near))
-    over_one.wait_recv()
-    last.append(forward(at_both, top, near))
-    over_two.wait_recv()
-    last.append(forward(at_both, low, near))
-    for k, step in enumerate(ring_steps):
-        step.wait_recv()
-        if k + 1 < len(ring_steps):
-            ring_steps[k + 1].start()
-    for copy in last:
-        copy.wait_recv()
-    for copy in copies_out + ring_steps:
-        copy.wait_send()
-    local.wait()
-    if weight_ref is not None:
-        keep.wait()
-
-
-def gather_late_kernel(copies, late, weighty, value_ref, *refs):
-    if weighty:
-        weight_ref, all_ref, weights_ref = refs[0], refs[1 + late], refs[2 + late]
-        own_sem, send_sem, recv_sem, ring_send, ring_recv = refs[3 + late :]
-        plane_gather_kernel(
-            copies, value_ref, all_ref, own_sem, send_sem, recv_sem, weight_ref, weights_ref,
-            ring_send, ring_recv,
-        )
-    else:
-        plane_gather_kernel(copies, value_ref, *refs[late:])
-
-
-def plane_gather(value, copies, collective, weight=None, before=()):
+    first = []
+    second = []
+
+    def begin():
+        local.start()
+        first.append(send(value_ref.at[top], mine, top, two))
+        first.append(send(value_ref.at[low], mine, low, one))
+        first.append(send(value_ref.at[low], mine, low, two))
+        first.append(send(value_ref.at[top], mine, top, one))
+        send(value_ref.at[top], mine, top, near)
+        send(value_ref.at[low], mine, low, near)
+
+    def pass_first():
+        first[0].wait_recv()
+        second.append(forward(at_two, top, one))
+        forward(at_two, top, near)
+        first[1].wait_recv()
+        second.append(forward(at_one, low, two))
+        forward(at_one, low, near)
+
+    def pass_second():
+        first[2].wait_recv()
+        forward(at_two, low, near)
+        first[3].wait_recv()
+        forward(at_one, top, near)
+
+    def pass_last():
+        second[0].wait_recv()
+        forward(at_both, top, near)
+        second[1].wait_recv()
+        forward(at_both, low, near)
+
+    def arrive(some=slice(None)):
+        for copy in last[some]:
+            copy.wait_recv()
+        if some == slice(None):
+            local.wait()
+
+    def finish():
+        for copy in sent:
+            copy.wait_send()
+
+    return begin, pass_first, pass_second, pass_last, arrive, finish
+
+
+def plane_gather_kernel(copies, value_ref, all_ref, own_sem, send_sem, recv_sem):
+    greet((copies, 2 * copies, 4 * copies))
+    for step in plane_gather_steps(
+        copies, value_ref, all_ref, own_sem.at[0], send_sem, recv_sem
+    ):
+        step()
+
+
+def plane_gather(value, copies, collective):
     rows, width = value.shape
-    parts = lax.axis_size("tensor")
     somewhere = pl.BlockSpec(memory_space=pl.ANY)
-    shapes = [jax.ShapeDtypeStruct((8, rows, width), value.dtype)]
-    operands = [value]
-    scratch = [
-        pltpu.SemaphoreType.DMA((2,)),
-        pltpu.SemaphoreType.DMA((14,)),
-        pltpu.SemaphoreType.DMA((14,)),
-    ]
-    if weight is not None:
-        shapes.append(jax.ShapeDtypeStruct((parts,) + weight.shape, weight.dtype))
-        operands.append(weight)
-        scratch += [pltpu.SemaphoreType.DMA((parts - 1,))] * 2
-    operands += before
     return pl.pallas_call(
-        functools.partial(gather_late_kernel, copies, len(before), weight is not None),
-        out_shape=shapes,
-        in_specs=[somewhere] * len(operands),
-        out_specs=[somewhere] * len(shapes),
-        scratch_shapes=scratch,
+        functools.partial(plane_gather_kernel, copies),
+        out_shape=jax.ShapeDtypeStruct((8, rows, width), value.dtype),
+        in_specs=[somewhere],
+        out_specs=somewhere,
+        scratch_shapes=[
+            pltpu.SemaphoreType.DMA((1,)),
+            pltpu.SemaphoreType.DMA((14,)),
+            pltpu.SemaphoreType.DMA((14,)),
+        ],
         compiler_params=pltpu.CompilerParams(collective_id=collective, has_side_effects=True),
         cost_estimate=pl.CostEstimate(
             flops=0, bytes_accessed=320 * rows * width, transcendentals=0
         ),
-    )(*operands)
+    )(value)
 
 
 def plane_scatter_kernel(
     copies, transposed, left_ref, right_ref, sum_ref, near_ref, one_ref, two_ref, part_ref,
     send_sem, recv_sem, block_ref=None, blocks_ref=None, ring_send=None, ring_recv=None,
-    total_ref=None, shares=None, ring_buf=None, load_sem=None,
+    total_ref=None, shares=None, ring_buf=None, load_sem=None, greeted=False, product=None,
+    between=lambda point: None,
 ):
     near, one, two = copies, 2 * copies, 4 * copies
     rows, width = sum_ref.shape
     half = rows // 2
     top, low = pl.ds(0, half), pl.ds(half, half)
     tile = min(512, width)
-    greet((near, one, two), ring_send is not None)
+    if not greeted:
+        greet((near, one, two), ring_send is not None)
     ring_steps = []
     parts = lax.axis_size("tensor")
     if shares is not None:
@@ -378,12 +367,14 @@
         def _(k):
             body(pl.ds(pl.multiple_of(k * tile, tile), tile))
 
-    def product(slot, columns):
+    def block_product(slot, columns):
         left = left_ref[slot]
         if transposed:
             return matmul_rt(left, right_ref[columns, :])
         return matmul(left, right_ref[:, columns])
 
+    product = product or block_product
+
     arriving = {}
     for k in (3, 1, 2, 0):
         slot = slot_of(copies, flips[k] + (near,))
@@ -393,6 +384,8 @@
 
         each_tile(theirs)
         arriving[k] = send(part_ref.at[k], near_ref.at[k], near)
+
+    between("sent")
 
     def added(k):
         slot = slot_of(copies, flips[k])
@@ -415,6 +408,7 @@
     added(2)
     two_second = send(near_ref.at[2, low], two_ref.at[1], two)
     added(0)
+    between("added")
 
     one_first.wait_recv()
 
@@ -424,6 +418,7 @@
 
     each_tile(pass_top)
     two_last = send(near_ref.at[2, top], two_ref.at[2], two)
+    between("top")
     two_first.wait_recv()
 
     def pass_low(columns):
@@ -432,6 +427,7 @@
 
     each_tile(pass_low)
     one_last = send(near_ref.at[1, low], one_ref.at[2], one)
+    between("low")
 
     def finish(rows_at, first, at_first, second, at_second):
         def body(columns):
@@ -470,6 +466,7 @@
     two_second.wait_recv()
     one_last.wait_recv()
     finish(low, two_ref, 1, one_ref, 2)
+    between("whole")
     if shares is not None:
         for k in range(1, parts - 1):
             sum_step(k)
@@ -848,56 +845,755 @@
     )(normed, own, first, others, gate_w, up_w, down_w)
 
 
-def forward_kernel(steps, seqs, forget_ref, drive_ref, state_ref, decay_ref):
-    width = forget_ref.shape[1]
+def greet_all(copies, masks):
+    barrier = pltpu.get_barrier_semaphore()
+    others = [{"dp": group_member(copies, k)} for k in range(1, 8)]
+    others += [{"tensor": beside(k)} for k in range(1, lax.axis_size("tensor"))]
+    others += [{"dp": partner(mask)} for mask in masks]
+    for other in others:
+        pl.semaphore_signal(
+            barrier, inc=1, device_id=other, device_id_type=pl.DeviceIdType.MESH
+        )
+    pl.semaphore_wait(barrier, len(others))
+
+
+def group_member(copies, step):
+    me = lax.axis_index("dp")
+    return lax.rem(lax.div(me, copies) + step, 8) * copies + lax.rem(me, copies)
+
+
+def mixer_forward_kernel(
+    copies,
+    own_ref, input_hbm, forget_hbm, gate_hbm, out_hbm, masked_hbm, bound_ref, live_ref,
+    normed_out, weights_out, project_out, pre_out, squash_out, state_out, entering_out, mixed_out,
+    masked_out, sum_ref,
+    normed, weights, project, pre, squashed, forget, state, decay, ends, entering, mixed,
+    near_buf, one_buf, two_buf, part_buf,
+    own_sem, gather_send, gather_recv, spread_send, spread_recv, spread_own, ring_send, ring_recv,
+    carry_send, carry_recv, scatter_send, scatter_recv, masked_send, masked_recv, out_sem,
+):
+    parts = lax.axis_size("tensor")
+    here = lax.axis_index("tensor")
+    seqs, rows, width = normed.shape
+    strips, _, lanes = forget.shape
+    channels = strips * lanes
+    mine = slot_of(copies, ())
+    greet_all(copies, ())
+
+    def own_rows_of(index):
+        return pl.ds(pl.multiple_of(index * copies, copies), copies)
+
+    def columns_of(index):
+        return pl.ds(pl.multiple_of(index * channels, channels), channels)
+
+    spread = []
+    for kind, source in enumerate((input_hbm, forget_hbm, gate_hbm)):
+        target = weights.at[kind, own_rows_of(mine), here]
+        kept = pltpu.make_async_copy(
+            source.at[:, :, columns_of(mine)], target, spread_own.at[kind]
+        )
+        sent = []
+        for k in range(1, 8):
+            there = group_member(copies, k)
+            sent.append(
+                pltpu.make_async_remote_copy(
+                    src_ref=source.at[:, :, columns_of(lax.div(there, copies))],
+                    dst_ref=target,
+                    send_sem=spread_send.at[kind, k - 1],
+                    recv_sem=spread_recv.at[kind, k - 1],
+                    device_id={"dp": there},
+                    device_id_type=pl.DeviceIdType.MESH,
+                )
+            )
+        spread.append((kept, sent))
+
+    def ring_copy(kind, k):
+        at = beside(-k)
+        target = project.at[:, at] if kind == 3 else weights.at[kind, :, at]
+        source = out_hbm if kind == 3 and k == 0 else target
+        return to_right(source, target, ring_send.at[kind, k], ring_recv.at[kind, k])
+
+    def spread_arrive(kind):
+        kept, sent = spread[kind]
+        kept.wait()
+        for copy in sent:
+            copy.wait_recv()
+
+    out_kept = pltpu.make_async_copy(out_hbm, project.at[:, here], spread_own.at[3])
+    out_kept.start()
+    for kept, sent in spread:
+        kept.start()
+        for copy in sent:
+            copy.start()
+    ring_copy(3, 0).start()
+    begin, pass_first, pass_second, pass_last, arrive, finish = plane_gather_steps(
+        copies, own_ref, normed, own_sem, gather_send, gather_recv
+    )
+    begin()
+    spread_arrive(0)
+    ring_copy(0, 0).start()
+    spread_arrive(1)
+    ring_copy(3, 0).wait_recv()
+    ring_copy(1, 0).start()
+    spread_arrive(2)
+    pass_first()
+    for k in range(parts - 2):
+        ring_copy(0, k).wait_recv()
+        ring_copy(0, k + 1).start()
+        if k == 0:
+            pass_second()
+        ring_copy(1, k).wait_recv()
+        ring_copy(1, k + 1).start()
+    ring_copy(0, parts - 2).wait_recv()
+    ring_copy(2, 0).start()
+    pass_last()
+    ring_copy(1, parts - 2).wait_recv()
+    ring_copy(3, 1).start()
+    arrive()
+
+    many = 2
+
+    def project_rows(kind, at):
+        left = normed[pl.ds(at * many, many)].reshape(many * rows, width)
+        return matmul(left, weights[kind].reshape(width, channels))
+
+    def rows_at(at):
+        return pl.ds(pl.multiple_of(at * many * rows, many * rows), many * rows)
+
+    def strip_of(value, n):
+        return value[:, n * lanes : (n + 1) * lanes]
+
+    @pl.loop(0, seqs // many)
+    def _(at):
+        some = rows_at(at)
+        value = project_rows(0, at)
+        pre[0, some, :] = value
+        inflow = live_ref[some, :] * silu_of(value)
+        for n in range(strips):
+            state[n, some, :] = strip_of(inflow, n)
+
+    ring_copy(2, 0).wait_recv()
+    ring_copy(2, 1).start()
+
+    @pl.loop(0, seqs // many)
+    def _(at):
+        some = rows_at(at)
+        squash = jax.nn.sigmoid(project_rows(1, at))
+        bound = bound_ref[...]
+        value = bound + (1.0 - bound) * squash
+        for n in range(strips):
+            squashed[n, some, :] = strip_of(squash, n)
+            forget[n, some, :] = strip_of(value, n)
+            state[n, some, :] = (1.0 - strip_of(value, n)) * state[n, some, :]
+
+    ring_copy(3, 1).wait_recv()
+    ring_copy(3, 2).start()
 
     def step(at, carry):
-        state, decay = carry
-        rows = pl.ds(at, seqs, stride=steps)
-        forget = forget_ref[rows, :]
-        state = forget * state + drive_ref[rows, :]
-        decay = decay * forget
-        state_ref[rows, :] = state
-        decay_ref[rows, :] = decay
-        return state, decay
-
-    lax.fori_loop(
-        0, steps, step, (jnp.zeros((seqs, width), f32), jnp.ones((seqs, width), f32)), unroll=8
+        some = pl.ds(at, seqs, stride=rows)
+        following = []
+        for n, (total, product) in enumerate(carry):
+            keep = forget[n, some, :]
+            total = keep * total + state[n, some, :]
+            product = product * keep
+            state[n, some, :] = total
+            decay[n, some, :] = product
+            following.append((total, product))
+        return tuple(following)
+
+    start = (jnp.zeros((seqs, lanes), f32), jnp.ones((seqs, lanes), f32))
+    carry = lax.fori_loop(0, rows, step, (start,) * strips, unroll=8)
+    for n, (total, product) in enumerate(carry):
+        ends[here, 0, :, n * lanes : (n + 1) * lanes] = total
+        ends[here, 1, :, n * lanes : (n + 1) * lanes] = product
+    carries = []
+    for k in range(1, parts):
+        copy = pltpu.make_async_remote_copy(
+            src_ref=ends.at[here],
+            dst_ref=ends.at[here],
+            send_sem=carry_send.at[k - 1],
+            recv_sem=carry_recv.at[k - 1],
+            device_id={"tensor": beside(k)},
+            device_id_type=pl.DeviceIdType.MESH,
+        )
+        copy.start()
+        carries.append(copy)
+    ring_copy(2, 1).wait_recv()
+    ring_copy(2, 2).start()
+    for copy in carries:
+        copy.wait_recv()
+    coming = jnp.zeros((seqs, channels), f32)
+    entered = coming
+    for k in range(parts - 1):
+        coming = ends[k, 1] * coming + ends[k, 0]
+        entered = jnp.where(here == k + 1, coming, entered)
+    for n in range(seqs):
+        entering[n] = entered[n : n + 1]
+    ring_copy(3, 2).wait_recv()
+    ring_copy(2, 2).wait_recv()
+
+    @pl.loop(0, seqs // many)
+    def _(at):
+        some = rows_at(at)
+        value = project_rows(2, at)
+        pre[1, some, :] = value
+        act = silu_of(value)
+        for n in range(many):
+            slot = at * many + n
+            one = pl.ds(pl.multiple_of(slot * rows, rows), rows)
+            for strip in range(strips):
+                columns = slice(strip * lanes, (strip + 1) * lanes)
+                whole = state[strip, one, :] + (
+                    decay[strip, one, :] * entering[slot, :, columns]
+                )
+                state[strip, one, :] = whole
+                mixed[slot, :, columns] = (
+                    whole * act[n * rows : (n + 1) * rows, columns]
+                ).astype(bf16)
+
+    out_kept.wait()
+    stores = [
+        pltpu.make_async_copy(source, target, out_sem.at[n])
+        for n, (source, target) in enumerate(
+            (
+                (normed, normed_out),
+                (weights, weights_out),
+                (project, project_out),
+                (pre, pre_out),
+                (squashed, squash_out),
+                (state, state_out),
+                (entering, entering_out),
+                (mixed, mixed_out),
+            )
+        )
+    ]
+    for store in stores:
+        store.start()
+
+    def out_product(slot, columns):
+        right = project[:, :, :, columns]
+        return matmul(mixed[slot], right.reshape(channels, right.shape[-1]))
+
+    plane_scatter_kernel(
+        copies, False, None, None, sum_ref, near_buf, one_buf, two_buf, part_buf, scatter_send,
+        scatter_recv, masked_hbm, masked_out, masked_send, masked_recv, greeted=True,
+        product=out_product,
     )
-
-
-def backward_kernel(steps, seqs, forget_ref, drive_ref, carried_ref, decay_ref):
-    width = forget_ref.shape[1]
+    finish()
+    for kept, sent in spread:
+        for copy in sent:
+            copy.wait_send()
+    for kind in range(4):
+        for k in range(parts - 1):
+            ring_copy(kind, k).wait_send()
+    for copy in carries:
+        copy.wait_send()
+    for store in stores:
+        store.wait()
+
+
+def mixer_forward(
+    normed, w_input, w_forget, w_gate, w_out, masked, bound, live, copies, collective
+):
+    parts = lax.axis_size("tensor")
+    rows, width = normed.shape
+    channels = width // 8
+    own_rows = w_input.shape[1]
+    somewhere = pl.BlockSpec(memory_space=pl.ANY)
+    vmem = pl.BlockSpec(memory_space=pltpu.VMEM)
+    wide = (8, rows, width)
+    weights = (3, 8 * copies, parts, own_rows, channels)
+    project = (copies, parts, own_rows, width)
+    flat = (8 * rows, channels)
+    lanes = min(128, channels)
+    strips = (channels // lanes, 8 * rows, lanes)
+    shaped = (8, rows, channels)
+    half = rows // 2
+    dma = pltpu.SemaphoreType.DMA
+    return pl.pallas_call(
+        functools.partial(mixer_forward_kernel, copies),
+        out_shape=[
+            jax.ShapeDtypeStruct(wide, bf16),
+            jax.ShapeDtypeStruct(weights, bf16),
+            jax.ShapeDtypeStruct(project, bf16),
+            jax.ShapeDtypeStruct((2,) + flat, f32),
+            jax.ShapeDtypeStruct(strips, f32),
+            jax.ShapeDtypeStruct(strips, f32),
+            jax.ShapeDtypeStruct((8, 1, channels), f32),
+            jax.ShapeDtypeStruct(shaped, bf16),
+            jax.ShapeDtypeStruct((parts - 2, rows, width), bf16),
+            jax.ShapeDtypeStruct((rows, width), f32),
+        ],
+        in_specs=[somewhere] * 6 + [vmem] * 2,
+        out_specs=[somewhere] * 9 + [vmem],
+        scratch_shapes=[
+            pltpu.VMEM(wide, bf16),
+            pltpu.VMEM(weights, bf16),
+            pltpu.VMEM(project, bf16),
+            pltpu.VMEM((2,) + flat, f32),
+            pltpu.VMEM(strips, f32),
+            pltpu.VMEM(strips, f32),
+            pltpu.VMEM(strips, f32),
+            pltpu.VMEM(strips, f32),
+            pltpu.VMEM((parts, 2, 8, channels), f32),
+            pltpu.VMEM((8, 1, channels), f32),
+            pltpu.VMEM(shaped, bf16),
+            pltpu.VMEM((4, rows, width), bf16),
+            pltpu.VMEM((3, half, width), bf16),
+            pltpu.VMEM((3, half, width), bf16),
+            pltpu.VMEM((4, rows, width), bf16),
+            dma,
+            dma((14,)),
+            dma((14,)),
+            dma((3, 7)),
+            dma((3, 7)),
+            dma((4,)),
+            dma((4, parts - 1)),
+            dma((4, parts - 1)),
+            dma((parts - 1,)),
+            dma((parts - 1,)),
+            dma((10,)),
+            dma((10,)),
+            dma((parts - 2,)),
+            dma((parts - 2,)),
+            dma((8,)),
+        ],
+        compiler_params=pltpu.CompilerParams(
+            collective_id=collective, has_side_effects=True, vmem_limit_bytes=56 * 1024 * 1024
+        ),
+        cost_estimate=pl.CostEstimate(
+            flops=8 * rows * width * width,
+            bytes_accessed=900 * rows * width,
+            transcendentals=0,
+        ),
+    )(normed, w_input, w_forget, w_gate, w_out, masked, bound, live)
+
+
+def mixer_backward_kernel(
+    copies, masks,
+    own_ref, normed_hbm, weights_hbm, project_hbm, pre_hbm, squash_hbm, state_hbm, mixed_hbm,
+    unit_hbm, stream_hbm, entering_ref, bound_ref, live_ref, gain_ref, scale_ref, gain_two_ref,
+    result_ref, weight_sums, project_sum, small_sums,
+    rows_buf, weights, project, pre, squashed, state, mixed, unit, stream, drive, decay, ends,
+    entered, grad_pre, grad_w, grad_project, ring_w, ring_project, bound_sum, whole_w, spread_w,
+    small_recv, small_ring, near_buf, one_buf, two_buf, part_buf,
+    load_sem, gather_send, gather_recv, carry_send, carry_recv, ring_send, ring_recv,
+    scatter_send, scatter_recv, spread_send, spread_recv, spread_own, small_send, small_got,
+):
+    parts = lax.axis_size("tensor")
+    here = lax.axis_index("tensor")
+    seqs, rows, width = rows_buf.shape
+    strips, _, lanes = drive.shape
+    channels = strips * lanes
+    own_rows = weights.shape[3]
+    near, one, two = copies, 2 * copies, 4 * copies
+    mine = slot_of(copies, ())
+    greet_all(copies, masks)
+    begin, pass_first, pass_second, pass_last, arrive, finish = plane_gather_steps(
+        copies, own_ref, rows_buf, load_sem.at[0], gather_send, gather_recv
+    )
+    begin()
+    loads = [
+        pltpu.make_async_copy(source, target, load_sem.at[n + 1])
+        for n, (source, target) in enumerate(
+            (
+                (project_hbm, project),
+                (pre_hbm, pre),
+                (state_hbm, state),
+                (mixed_hbm, mixed),
+                (squash_hbm, squashed),
+                (weights_hbm, weights),
+                (unit_hbm, unit),
+                (stream_hbm, stream),
+            )
+        )
+    ]
+    for load in loads:
+        load.start()
+    for load in loads[:3]:
+        load.wait()
+
+    def slot_rows(slot):
+        return pl.ds(pl.multiple_of(slot * rows, rows), rows)
+
+    def take(slot):
+        some = slot_rows(slot)
+        grad_mixed = matmul_rt(rows_buf[slot], project[...].reshape(channels, width))
+        gate = pre[1, some, :]
+        squash = jax.nn.sigmoid(gate)
+        act = gate * squash
+        slope = squash * (1.0 + gate * (1.0 - squash))
+        for n in range(strips):
+            columns = slice(n * lanes, (n + 1) * lanes)
+            part = grad_mixed[:, columns]
+            drive[n, some, :] = part * act[:, columns]
+            at = 2 * channels + n * lanes
+            grad_pre[slot, :, at : at + lanes] = (
+                part * state[n, some, :] * slope[:, columns]
+            ).astype(bf16)
+
+    pass_first()
+    pass_second()
+    arrive(slice(0, 6))
+    pltpu.make_async_copy(own_ref, rows_buf.at[mine], load_sem.at[0]).wait()
+    for flips in ((), (near,), (one,), (two,), (near, one), (near, two)):
+        take(slot_of(copies, flips))
+    pass_last()
+    take(slot_of(copies, (one, two)))
+    arrive(slice(6, 8))
+    take(slot_of(copies, (near, one, two)))
+
+    tile = min(512, width)
+    loads[3].wait()
+
+    @pl.loop(0, width // tile)
+    def _(k):
+        columns = pl.ds(pl.multiple_of(k * tile, tile), tile)
+        value = matmul_lt(
+            mixed[...].reshape(seqs * rows, channels),
+            rows_buf[:, :, columns].reshape(seqs * rows, tile),
+        )
+        grad_project[:, :, :, columns] = value.astype(bf16).reshape(
+            copies, parts, own_rows, tile
+        )
+
+    def ring_copy(kind, k):
+        at = beside(-(k + 1))
+        if kind == 3:
+            source, target = grad_project.at[:, at], ring_project.at[k]
+        else:
+            source, target = grad_w.at[kind, :, at], ring_w.at[kind, k]
+        return to_right(source, target, ring_send.at[kind, k], ring_recv.at[kind, k])
+
+    def advance(kind, k):
+        ring_copy(kind, k).wait_recv()
+        at = beside(-(k + 2))
+        if kind == 3:
+            total = grad_project[:, at].astype(f32) + ring_project[k].astype(f32)
+        else:
+            total = grad_w[kind, :, at].astype(f32) + ring_w[kind, k].astype(f32)
+        if k + 1 < parts - 1:
+            if kind == 3:
+                grad_project[:, at] = total.astype(bf16)
+            else:
+                grad_w[kind, :, at] = total.astype(bf16)
+            ring_copy(kind, k + 1).start()
+        elif kind == 3:
+            project_sum[...] = total
+        else:
+            whole_w[kind] = total.astype(bf16)
+            for copy in spread_copies(kind):
+                copy.start()
+
+    def spread_copies(kind, own=True):
+        found = []
+        for k in range(1, 8):
+            there = group_member(copies, k)
+            source = pl.ds(pl.multiple_of(lax.div(there, copies) * copies, copies), copies)
+            found.append(
+                pltpu.make_async_remote_copy(
+                    src_ref=whole_w.at[kind, source],
+                    dst_ref=spread_w.at[kind, mine],
+                    send_sem=spread_send.at[kind, k - 1],
+                    recv_sem=spread_recv.at[kind, k - 1],
+                    device_id={"dp": there},
+                    device_id_type=pl.DeviceIdType.MESH,
+                )
+            )
+        if own:
+            source = pl.ds(pl.multiple_of(mine * copies, copies), copies)
+            found.append(
+                pltpu.make_async_copy(
+                    whole_w.at[kind, source], spread_w.at[kind, mine], spread_own.at[kind]
+                )
+            )
+        return found
+
+    ring_copy(3, 0).start()
+    finish()
+    normed_load = pltpu.make_async_copy(normed_hbm, rows_buf, load_sem.at[0])
+    normed_load.start()
+    loads[4].wait()
 
     def step(k, carry):
-        coming, decay = carry
-        rows = pl.ds(steps - 1 - k, seqs, stride=steps)
-        forget = forget_ref[rows, :]
-        carried = drive_ref[rows, :] + coming
-        carried_ref[rows, :] = carried
-        decay_ref[rows, :] = decay
-        return forget * carried, decay * forget
-
-    lax.fori_loop(
-        0, steps, step, (jnp.zeros((seqs, width), f32), jnp.ones((seqs, width), f32)), unroll=8
+        some = pl.ds(rows - 1 - k, seqs, stride=rows)
+        following = []
+        for n, (coming, product) in enumerate(carry):
+            bound = bound_ref[:, n * lanes : (n + 1) * lanes]
+            keep = bound + (1.0 - bound) * squashed[n, some, :]
+            carried = drive[n, some, :] + coming
+            drive[n, some, :] = carried
+            decay[n, some, :] = product
+            following.append((keep * carried, product * keep))
+        return tuple(following)
+
+    start = (jnp.zeros((seqs, lanes), f32), jnp.ones((seqs, lanes), f32))
+    carry = lax.fori_loop(0, rows, step, (start,) * strips, unroll=8)
+    for n, (coming, product) in enumerate(carry):
+        ends[here, 0, :, n * lanes : (n + 1) * lanes] = coming
+        ends[here, 1, :, n * lanes : (n + 1) * lanes] = product
+    carries = []
+    for k in range(1, parts):
+        copy = pltpu.make_async_remote_copy(
+            src_ref=ends.at[here],
+            dst_ref=ends.at[here],
+            send_sem=carry_send.at[k - 1],
+            recv_sem=carry_recv.at[k - 1],
+            device_id={"tensor": beside(k)},
+            device_id_type=pl.DeviceIdType.MESH,
+        )
+        copy.start()
+        carries.append(copy)
+    normed_load.wait()
+
+    def weight_grad(kind):
+        @pl.loop(0, width // tile)
+        def _(k):
+            columns = pl.ds(pl.multiple_of(k * tile, tile), tile)
+            value = matmul_lt(
+                grad_pre[:, :, kind * channels : (kind + 1) * channels].reshape(
+                    seqs * rows, channels
+                ),
+                rows_buf[:, :, columns].reshape(seqs * rows, tile),
+            )
+            count = tile // (parts * own_rows)
+            grad_w[kind, pl.ds(k * count, count)] = value.T.astype(bf16).reshape(
+                count, parts, own_rows, channels
+            )
+
+        ring_copy(kind, 0).start()
+
+    advance(3, 0)
+    weight_grad(2)
+    for copy in carries:
+        copy.wait_recv()
+    coming = jnp.zeros((seqs, channels), f32)
+    arrived = coming
+    for k in range(parts - 1, 0, -1):
+        coming = ends[k, 1] * coming + ends[k, 0]
+        arrived = jnp.where(here == k - 1, coming, arrived)
+    for n in range(seqs):
+        entered[n] = arrived[n : n + 1]
+    bound_sum[...] = jnp.zeros_like(bound_sum)
+    first_row = lax.broadcasted_iota(jnp.int32, (rows, lanes), 0) == 0
+
+    @pl.loop(0, seqs)
+    def _(slot):
+        some = slot_rows(slot)
+        alive = live_ref[some, :]
+        for n in range(strips):
+            columns = slice(n * lanes, (n + 1) * lanes)
+            bound = bound_ref[:, columns]
+            squash = squashed[n, some, :]
+            keep = bound + (1.0 - bound) * squash
+            carried = drive[n, some, :] + decay[n, some, :] * entered[slot, :, columns]
+            prior = jnp.where(
+                first_row, entering_ref[slot, :, columns], pltpu.roll(state[n, some, :], 1, 0)
+            )
+            value = pre[0, some, columns]
+            gate = jax.nn.sigmoid(value)
+            slope = gate * (1.0 + value * (1.0 - gate))
+            grad_forget = carried * prior - carried * alive * value * gate
+            at = n * lanes
+            grad_pre[slot, :, at : at + lanes] = (
+                carried * alive * (1.0 - keep) * slope
+            ).astype(bf16)
+            at = channels + n * lanes
+            grad_pre[slot, :, at : at + lanes] = (
+                grad_forget * (1.0 - bound) * squash * (1.0 - squash)
+            ).astype(bf16)
+            bound_sum[:, columns] += jnp.sum(
+                grad_forget * (1.0 - squash), axis=0, keepdims=True
+            )
+
+    advance(3, 1)
+    weight_grad(0)
+    advance(2, 0)
+    weight_grad(1)
+    loads[5].wait()
+
+    def normed_product(slot, columns):
+        at = lax.div(columns.start, parts * own_rows)
+        count = tile // (parts * own_rows)
+        total = None
+        for kind in range(3):
+            part = matmul_rt(
+                grad_pre[slot, :, kind * channels : (kind + 1) * channels],
+                weights[kind, pl.ds(at, count)].reshape(tile, channels),
+            )
+            total = part if total is None else total + part
+        return total
+
+    def between(point):
+        if point == "sent":
+            advance(3, 2)
+            advance(2, 1)
+        elif point == "added":
+            advance(0, 0)
+            advance(2, 2)
+        elif point == "top":
+            advance(1, 0)
+        elif point == "low":
+            advance(0, 1)
+            advance(1, 1)
+
+    plane_scatter_kernel(
+        copies, True, None, None, result_ref, near_buf, one_buf, two_buf, part_buf, scatter_send,
+        scatter_recv, greeted=True, product=normed_product, between=between,
     )
 
-
-def local_scan(body, seqs, forget, drive):
-    rows, width = forget.shape
-    lanes = 128 if width % 128 == 0 else width
-    spec = pl.BlockSpec((rows, lanes), lambda c: (0, c))
+    for load in loads[6:]:
+        load.wait()
+    small_sums[...] = jnp.zeros_like(small_sums)
+    small_sums[1:2, :] = gain_two_ref[...]
+    small_sums[2:3, pl.ds(pl.multiple_of(mine * channels, channels), channels)] = bound_sum[...]
+    some_rows = min(64, rows)
+
+    @pl.loop(0, rows // some_rows)
+    def _(k):
+        some = pl.ds(pl.multiple_of(k * some_rows, some_rows), some_rows)
+        grad_norm = result_ref[some, :]
+        units = unit[some, :]
+        small_sums[0:1, :] += jnp.sum(grad_norm * units, axis=0, keepdims=True)
+        scaled = grad_norm * gain_ref[...]
+        mean = jnp.mean(scaled * units, axis=-1, keepdims=True)
+        result_ref[some, :] = stream[some, :] + scale_ref[some, :] * (scaled - units * mean)
+
+    def small_copy(n):
+        return pltpu.make_async_remote_copy(
+            src_ref=small_sums,
+            dst_ref=small_recv.at[n],
+            send_sem=small_send.at[n],
+            recv_sem=small_got.at[n],
+            device_id={"dp": partner(masks[n])},
+            device_id_type=pl.DeviceIdType.MESH,
+        )
+
+    def small_step(n):
+        small_copy(n).wait()
+        small_sums[...] += small_recv[n]
+
+    small_copy(0).start()
+    advance(0, 2)
+    advance(1, 2)
+    for n in range(len(masks)):
+        small_step(n)
+        if n + 1 < len(masks):
+            small_copy(n + 1).start()
+    ring_small = []
+    for k in range(1, parts):
+        copy = pltpu.make_async_remote_copy(
+            src_ref=small_sums,
+            dst_ref=small_ring.at[k - 1],
+            send_sem=small_send.at[len(masks) + k - 1],
+            recv_sem=small_got.at[len(masks) + k - 1],
+            device_id={"tensor": beside(k)},
+            device_id_type=pl.DeviceIdType.MESH,
+        )
+        copy.start()
+        ring_small.append(copy)
+    for kind in (2, 0, 1):
+        spread = spread_copies(kind)
+        for copy in spread[:-1]:
+            copy.wait_recv()
+        spread[-1].wait()
+        for slot in range(8):
+            weight_sums[kind, :, :, slot * channels : (slot + 1) * channels] = spread_w[
+                kind, slot
+            ].astype(f32)
+    for copy in ring_small:
+        copy.wait()
+    for k in range(parts - 1):
+        small_sums[...] += small_ring[k]
+    for kind in range(4):
+        for k in range(parts - 1):
+            ring_copy(kind, k).wait_send()
+    for kind in range(3):
+        for copy in spread_copies(kind, False):
+            copy.wait_send()
+    for copy in carries:
+        copy.wait_send()
+
+
+def mixer_backward(
+    own, normed, weights, project, pre, squashed, state, mixed, unit, stream, entering, bound,
+    live, gain, scale, gain_two, copies, masks, collective,
+):
+    parts = lax.axis_size("tensor")
+    _, rows, width = normed.shape
+    channels = width // 8
+    own_rows = project.shape[2]
+    somewhere = pl.BlockSpec(memory_space=pl.ANY)
+    vmem = pl.BlockSpec(memory_space=pltpu.VMEM)
+    half = rows // 2
+    dma = pltpu.SemaphoreType.DMA
+    blocks = (8 * copies, own_rows, channels)
+    small = pltpu.VMEM((len(masks), 8, width), f32)
     return pl.pallas_call(
-        functools.partial(body, rows // seqs, seqs),
-        grid=(width // lanes,),
-        in_specs=[spec, spec],
-        out_specs=[spec, spec],
-        out_shape=[jax.ShapeDtypeStruct((rows, width), f32)] * 2,
-        compiler_params=pltpu.CompilerParams(vmem_limit_bytes=32 * 1024 * 1024),
+        functools.partial(mixer_backward_kernel, copies, masks),
+        out_shape=[
+            jax.ShapeDtypeStruct((rows, width), f32),
+            jax.ShapeDtypeStruct((3, copies, own_rows, width), f32),
+            jax.ShapeDtypeStruct((copies, own_rows, width), f32),
+            jax.ShapeDtypeStruct((8, width), f32),
+        ],
+        in_specs=[somewhere] * 10 + [vmem] * 6,
+        out_specs=[vmem] * 4,
+        scratch_shapes=[
+            pltpu.VMEM(normed.shape, bf16),
+            pltpu.VMEM(weights.shape, bf16),
+            pltpu.VMEM(project.shape, bf16),
+            pltpu.VMEM(pre.shape, f32),
+            pltpu.VMEM(squashed.shape, f32),
+            pltpu.VMEM(state.shape, f32),
+            pltpu.VMEM(mixed.shape, bf16),
+            pltpu.VMEM((rows, width), f32),
+            pltpu.VMEM((rows, width), f32),
+            pltpu.VMEM(state.shape, f32),
+            pltpu.VMEM(state.shape, f32),
+            pltpu.VMEM((parts, 2, 8, channels), f32),
+            pltpu.VMEM((8, 1, channels), f32),
+            pltpu.VMEM((8, rows, 3 * channels), bf16),
+            pltpu.VMEM(weights.shape, bf16),
+            pltpu.VMEM(project.shape, bf16),
+            pltpu.VMEM((3, parts - 1) + blocks, bf16),
+            pltpu.VMEM((parts - 1, copies, own_rows, width), bf16),
+            pltpu.VMEM((1, channels), f32),
+            pltpu.VMEM((3,) + blocks, bf16),
+            pltpu.VMEM((3, 8, copies, own_rows, channels), bf16),
+            small,
+            pltpu.VMEM((parts - 1, 8, width), f32),
+            pltpu.VMEM((4, rows, width), bf16),
+            pltpu.VMEM((3, half, width), bf16),
+            pltpu.VMEM((3, half, width), bf16),
+            pltpu.VMEM((4, rows, width), bf16),
+            dma((9,)),
+            dma((14,)),
+            dma((14,)),
+            dma((parts - 1,)),
+            dma((parts - 1,)),
+            dma((4, parts - 1)),
+            dma((4, parts - 1)),
+            dma((10,)),
+            dma((10,)),
+            dma((3, 7)),
+            dma((3, 7)),
+            dma((3,)),
+            dma((len(masks) + parts - 1,)),
+            dma((len(masks) + parts - 1,)),
+        ],
+        compiler_params=pltpu.CompilerParams(
+            collective_id=collective, has_side_effects=True, vmem_limit_bytes=62 * 1024 * 1024
+        ),
         cost_estimate=pl.CostEstimate(
-            flops=4 * rows * width, bytes_accessed=16 * rows * width, transcendentals=0
+            flops=16 * rows * width * width,
+            bytes_accessed=900 * rows * width,
+            transcendentals=0,
         ),
-    )(forget, drive)
+    )(
+        own, normed, weights, project, pre, squashed, state, mixed, unit, stream, entering, bound,
+        live, gain, scale, gain_two,
+    )
 
 
 def on_device(
@@ -951,68 +1647,35 @@
     live = (position[None, :] < group_lengths[:, None]).astype(f32)
     live = live.reshape(group * rows_here, 1)
 
-    def spread(weight):
-        return weight.reshape(own_rows, group, channels).transpose(1, 0, 2)
-
-    pieces = jnp.concatenate([spread(w_input), spread(w_forget), spread(w_gate_mix)], axis=2)
-    pieces = lax.all_to_all(
-        pieces, "dp", 0, 0, axis_index_groups=group_lists if copies > 1 else None, tiled=True
-    )
-    pieces = jnp.concatenate([pieces, spread(w_out)], axis=2)
+    mixer_weights = [w_input, w_forget, w_gate_mix, w_out]
     if copies > 1:
-        pieces = gather_bits(pieces, copy_masks[::-1])
-    pieces = pieces.reshape(copies, group, own_rows, 4 * channels)
+        mixer_weights = [gather_bits(weight, copy_masks[::-1]) for weight in mixer_weights]
+    mixer_weights = [weight.reshape(copies, own_rows, width) for weight in mixer_weights]
+
     masked_grad = live_own * cotangent
     masked_own = masked_grad.astype(bf16)
     masked_first = ring(masked_own)
 
     scale_one, unit_one = norm_rows(inputs)
-    normed_one, pieces = plane_gather(
-        (unit_one * gain_one).astype(bf16),
-        copies,
-        1,
-        pieces.reshape(copies * group * own_rows, 4 * channels),
-        [masked_first],
+    rows_all = group * rows_here
+    *mixer_kept, mixed, masked_others, mixed_sum = (
+        mixer_forward(
+            (unit_one * gain_one).astype(bf16),
+            *mixer_weights,
+            masked_first,
+            bound[None, :],
+            live,
+            copies,
+            1,
+        )
     )
-    rows_all = group * rows_here
-    normed_one = normed_one.reshape(rows_all, width)
-    pieces = pieces.reshape(tensor_parts, copies, group, own_rows, 4 * channels)
-    mixer_w = pieces[..., : 3 * channels].transpose(2, 1, 0, 3, 4).reshape(width, 3 * channels)
-    out_w = pieces[..., 3 * channels :].transpose(1, 0, 3, 2, 4).reshape(channels, width)
+    stream = inputs + mixed_sum
 
     first, second = orders(all_masks)
     hidden_here = w_gate.shape[1]
     gate_w, up_w, down_w = (
         lax.all_gather(weight, "dp", axis=0, tiled=True) for weight in (w_gate, w_up, w_down.T)
     )
-
-    pre = matmul(normed_one, mixer_w)
-    input_pre = pre[:, :channels]
-    forget_sig = jax.nn.sigmoid(pre[:, channels : 2 * channels])
-    gate_pre = pre[:, 2 * channels :]
-    forget = bound + (1.0 - bound) * forget_sig
-    input_act = silu_of(input_pre)
-    gate_act = silu_of(gate_pre)
-    inflow = live * (1.0 - forget) * input_act
-    part_state, part_decay = local_scan(forward_kernel, group, forget, inflow)
-    shaped = (group, rows_here, channels)
-    part_state = part_state.reshape(shaped)
-    part_decay = part_decay.reshape(shaped)
-    ends = jnp.stack([part_state[:, -1], part_decay[:, -1]])
-    all_ends = in_order(shifted_blocks(ends))
-    coming = jnp.zeros((group, channels), f32)
-    entering = coming
-    for k in range(tensor_parts - 1):
-        coming = all_ends[k, 1] * coming + all_ends[k, 0]
-        entering = jnp.where(tensor_index == k + 1, coming, entering)
-    state = part_state + part_decay * entering[:, None, :]
-    prior_state = jnp.concatenate([entering[:, None, :], state[:, :-1]], axis=1)
-    state = state.reshape(group * rows_here, channels)
-    prior_state = prior_state.reshape(group * rows_here, channels)
-    mixed_low = (state * gate_act).astype(bf16)
-    mixed = mixed_low.reshape(shaped)
-    mixed_sum, masked_others = plane_scatter(mixed, out_w, copies, False, 2, masked_first)
-    stream = inputs + mixed_sum
 
     scale_two, unit_two = norm_rows(stream)
     normed_two = (unit_two * gain_two).astype(bf16)
@@ -1032,84 +1695,43 @@
 
     gain_two_part = jnp.sum(grad_norm_two * unit_two, axis=0)
     grad_stream = masked_grad + norm_back(grad_norm_two, unit_two, scale_two, gain_two)
-    (stream_low,) = plane_gather(grad_stream.astype(bf16), copies, 5)
-    stream_low = stream_low.reshape(rows_all, width)
-
-    grad_out_w = matmul_lt(mixed_low, stream_low).astype(bf16)
-    grad_mixed = matmul_rt(stream_low, out_w)
-    grad_gate_pre = (grad_mixed * state * silu_slope(gate_pre)).astype(bf16)
-    grad_state = grad_mixed * gate_act
-    part_carried, part_after = local_scan(backward_kernel, group, forget, grad_state)
-    part_carried = part_carried.reshape(shaped)
-    part_after = part_after.reshape(shaped)
-    first_forget = forget.reshape(shaped)[:, 0]
-    begins = jnp.stack([first_forget * part_carried[:, 0], first_forget * part_after[:, 0]])
-    all_begins = in_order(shifted_blocks(begins))
-    coming = jnp.zeros((group, channels), f32)
-    entering = coming
-    for k in range(tensor_parts - 1, 0, -1):
-        coming = all_begins[k, 1] * coming + all_begins[k, 0]
-        entering = jnp.where(tensor_index == k - 1, coming, entering)
-    carried = (part_carried + part_after * entering[:, None, :]).reshape(
-        group * rows_here, channels
+
+    normed_one, mixer_w, out_w, pre, squashed, state, entering = mixer_kept
+    grad_inputs, mixer_sums, out_w_sum, small_sums = mixer_backward(
+        grad_stream.astype(bf16),
+        normed_one,
+        mixer_w,
+        out_w,
+        pre,
+        squashed,
+        state,
+        mixed,
+        unit_one,
+        grad_stream,
+        entering,
+        bound[None, :],
+        live,
+        gain_one[None, :],
+        scale_one,
+        gain_two_part[None, :],
+        copies,
+        all_masks,
+        3,
     )
-    grad_forget = carried * prior_state - carried * live * input_act
-    grad_input_pre = (carried * live * (1.0 - forget) * silu_slope(input_pre)).astype(bf16)
-    grad_bound = jnp.sum(grad_forget * (1.0 - forget_sig), axis=0)
-    grad_forget_pre = (grad_forget * (1.0 - bound) * forget_sig * (1.0 - forget_sig)).astype(bf16)
-    grad_pre = jnp.concatenate([grad_input_pre, grad_forget_pre, grad_gate_pre], axis=1)
-    grad_parts = grad_pre.reshape(group, rows_here, 3 * channels)
-    grad_mixer = matmul_lt(normed_one, grad_pre).astype(bf16)
-    mixer_sums = jnp.concatenate(
-        [
-            grad_mixer.reshape(group, copies, tensor_parts, own_rows, 3 * channels).transpose(
-                2, 1, 0, 3, 4
-            ),
-            grad_out_w.reshape(copies, tensor_parts, own_rows, group, channels).transpose(
-                1, 0, 3, 2, 4
-            ),
-        ],
-        axis=-1,
-    ).reshape(tensor_parts, copies * group * own_rows, 4 * channels)
-    grad_norm_one, mixer_sums = plane_scatter(
-        grad_parts, mixer_w, copies, True, 3, sums=mixer_sums, before=[out_sum]
-    )
-    output = live_own * (stream + after(out_sum, grad_norm_one).astype(f32))
-    gain_one_part = jnp.sum(grad_norm_one * unit_one, axis=0)
-    grad_inputs = grad_stream + norm_back(grad_norm_one, unit_one, scale_one, gain_one)
-
-    mixer_sums = mixer_sums.reshape(copies, group, own_rows, 4 * channels)
+    output = live_own * (stream + after(out_sum, small_sums).astype(f32))
+    grad_weights = [mixer_sums[0], mixer_sums[1], mixer_sums[2], out_w_sum]
     if copies > 1:
-        mixer_sums = scatter_bits(mixer_sums, copy_masks, f32)
-    mixer_sums = mixer_sums.reshape(group, own_rows, 4 * channels)
-    grad_out = mixer_sums[..., 3 * channels :].transpose(1, 0, 2).reshape(own_rows, width)
-    grad_mixer = lax.all_to_all(
-        mixer_sums[..., : 3 * channels].astype(bf16),
-        "dp",
-        0,
-        0,
-        axis_index_groups=group_lists if copies > 1 else None,
-        tiled=True,
-    )
-    grad_mixer = grad_mixer.reshape(group, own_rows, 3, channels).transpose(2, 1, 0, 3)
-    grad_mixer = grad_mixer.reshape(3, own_rows, width).astype(f32)
-
-    bound_part = lax.dynamic_update_slice_in_dim(
-        jnp.zeros((width,), f32), grad_bound, group_index * channels, 0
-    )
-    sums = jnp.stack([gain_one_part, gain_two_part, bound_part])
-    sums = sums.reshape(3, data_parts, tensor_parts, own_rows).transpose(1, 2, 0, 3)
-    sums = scatter_straight(scatter_bits(sums, sorted(all_masks), f32))
+        grad_weights = [scatter_bits(total, copy_masks, f32) for total in grad_weights]
+    grad_weights = [total.reshape(own_rows, width) for total in grad_weights]
+    place = (data_index * tensor_parts + tensor_index) * own_rows
+    small_own = lax.dynamic_slice(small_sums, (0, place), (3, own_rows))
     return (
         output,
         grad_inputs,
-        sums[0],
-        sums[1],
-        sums[2],
-        grad_mixer[0],
-        grad_mixer[1],
-        grad_mixer[2],
-        grad_out,
+        small_own[0],
+        small_own[1],
+        small_own[2],
+        *grad_weights,
         grad_gate_mine,
         grad_up_mine,
         grad_down_mine,

time: 658 us -> 572 us (0.87); the launches traced: 648 us -> 572 us
  Pallas kernels: 462 us -> 496 us
  matrix products: 28.9 us -> 0 us
  local copies, waits for them, and re-layouts: 44.4 us -> 16.1 us
  other arithmetic: 41.5 us -> 16.1 us
  starting transfers between devices: 35 us -> 12.1 us
    pallas_call x6 -> x2, Pallas kernels: 285 us -> 321 us  [the longest x1 165 us: mixer_backward(): pl.pallas_call(functools.partial(mixer_backward_kernel, copies, masks), o...]
    dot_general x4 -> x0, matrix products: 28.9 us -> none  [the longest x2 12.2 us: matmul_lt(): lax.dot_general(left, right, (((0,), (0,)), ((), ())), preferred_element_...]
    unnamed x136 -> x44, local copies, waits for them, and re-layouts: 28.5 us -> 9.73 us
    concatenate x5 -> x0, other arithmetic: 10.5 us -> none  [the longest x1 3.99 us: on_device(): jnp.concatenate([grad_mixer.reshape(group, copies, tensor_parts, own_rows...]
    ppermute x6 -> x3, waiting for transfers between devices: 15.6 us -> 5.53 us  [swap(): lax.ppermute(value, 'dp', [(i, i ^ mask) for i in range(lax.axis_size('dp...]
    ppermute x1, waiting for transfers between devices: 0.01 us -> 9.6 us  [ring(): lax.ppermute(value, 'tensor', [(i, (i + 1) % parts) for i in range(parts)])]
    slice x7 -> x0, local copies, waits for them, and re-layouts: 8.46 us -> none  [the longest x1 2.37 us: on_device(): mixer_sums[..., :3 * channels].astype(bf16)]
    all_to_all x2 -> x0, starting transfers between devices: 7.75 us -> none  [the longest x1 4.2 us: on_device(): lax.all_to_all(pieces, 'dp', 0, 0, axis_index_groups=group_lists if copie...]
  transfers between devices with their start and end apart: 25 -> 11, of which waited for: 6 -> 4; matrix products, arithmetic and copies ran while one was open for 14% -> 4% of each run, Pallas kernels for 32% -> 56%
where the time goes in v3:
time: 572 us
  Pallas kernels  496 us (87%)
  waiting for transfers between devices  16.6 us (3%)
  local copies, waits for them, and re-layouts  16.1 us (3%)
  other arithmetic  16.1 us (3%)
  between operations  14.7 us (3%)
  starting transfers between devices  12.1 us (2%)
    pallas_call x1, Pallas kernels, swiglu(): pl.pallas_call(functools.partial(swiglu_kernel, copies), out_shape=[jax.S...  175 us
    pallas_call x1, Pallas kernels, mixer_backward(): pl.pallas_call(functools.partial(mixer_backward_kernel, copies, masks), o...  165 us
    pallas_call x1, Pallas kernels, mixer_forward(): pl.pallas_call(functools.partial(mixer_forward_kernel, copies), out_shape...  156 us
  transfers between devices with their start and end apart: 11, of which 4 were waited for; matrix products, arithmetic and copies ran while one was open for 4% of the time, Pallas kernels for 56%

profile of v3, /device:TPU:0, one launch (start us, length us, event | category | flops | bytes accessed | tf_op | source)
XLA Modules:
  0.0 571.6 jit_solution(10069598352440448576)
XLA Ops:
  7.2 0.0 copy-start.14
  7.2 0.0 copy-start.13
  7.2 0.0 copy-start.12
  7.2 0.0 all-gather.8.cloned.1.call-start
  7.3 2.2 copy.31
  9.5 0.0 all-gather.8.cloned.1.call-update
  9.5 0.0 all-gather.4.cloned.1.call-start
  9.6 0.7 all-gather.4.cloned.1.call-update
  10.3 0.0 copy-start.2
  10.3 0.0 all-gather.6.cloned.1.call-start
  10.3 0.7 all-gather.6.cloned.1.call-update
  11.0 0.0 reduce-scatter.2.cloned.1.call-start
  11.8 0.1 maximum_bitcast_fusion
  11.8 0.0 copy-done.14
  11.9 5.1 collective-permute-start
  17.0 0.0 collective-permute-start.1
  17.0 1.0 collective-permute-start.2
  18.0 1.9 multiply_convert_fusion.2.own_ref
  19.9 0.0 copy-start.10
  19.9 2.6 collective-permute-start.6
  22.5 0.2 multiply_reduce_fusion.3
  22.7 0.0 collective-permute-done
  22.7 0.0 collective-permute-done.1
  22.8 0.0 collective-permute-done.2
  22.9 1.6 collective-permute-start.3
  24.5 2.1 collective-permute-done.3
  26.6 1.6 collective-permute-start.4
  28.2 2.3 collective-permute-done.4
  30.5 0.1 collective-permute-start.5
  30.6 1.1 collective-permute-done.5
  31.8 0.1 mul.103
  31.9 0.1 copy.29
  32.0 0.1 convert_bitcast_fusion
  32.1 1.3 copy.36
  33.4 0.1 reshape_squeeze.15
  33.5 0.1 mul.112
  33.6 0.6 dynamic_slice.12
  34.2 1.9 multiply_convert_fusion.1
  36.2 9.6 %collective-permute-done.6.masked_hbm.first_ref = bf16[256,2048]{1,0:T(8,128)(2,1)} collective-permute-done((bf16[256,2048]{1,0:T(8,128)(2,1)S(1)}, bf16[256,2048]{1,0:T(8,128)(2,1)}, u32[]{:S(2)}, u32[]{:S(2)}) %collective-permute-start.6) | collective-permute-done | bytes 1048608 | tf_op jit(solution)/shard_map/ppermute | solution.py:122
  45.8 155.8 %shard_map.220 = (bf16[8,256,2048]{2,1,0:T(8,128)(2,1)}, bf16[3,8,4,64,256]{4,3,2,1,0:T(8,128)(2,1)}, bf16[1,4,64,2048]{3,2,1,0:T(8,128)(2,1)}, f32[2,2048,256]{...) custom-call(bf16[256,2048]{1,0:T(8,128)(2,1)} %get-tuple-element.80., ...), custom_call_target="tpu_custom_call" | custom-call | flops 8589934592 | bytes 471859200 | tf_op jit(solution)/shard_map/pallas_call | solution.py:1113
  201.6 1.9 multiply_reduce_fusion.2
  203.5 1.5 multiply_convert_fusion.normed_ref
  205.0 174.9 %shard_map.221 = (bf16[4,256,2048]{2,1,0:T(8,128)(2,1)}, f32[256,2048]{1,0:T(8,128)}, f32[256,1408]{1,0:T(8,128)}, f32[256,1408]{1,0:T(8,128)}, f32[256,1408]{1,0:T(8,128)}) custom-call(bf16[256,2048]{1,0:T(8,128)(2,1)} %multiply_convert_fusion.normed_ref, bf16[256,2048]{1,0:T(8,128)(2,1)} %copy-done.10, ...), custom_call_target="tpu_custom_call" | custom-call | flops 53150220288 | bytes 576716800 | tf_op jit(solution)/shard_map/pallas_call | solution.py:817
  379.8 0.0 reduce-scatter.2.cloned.1.call-update
  379.9 0.8 copy.33.scale_ref
  380.7 0.7 broadcast_in_dim_reshape_squeeze.2.gain_ref
  381.4 2.9 multiply_reduce_fusion
  384.3 0.0 copy-done
  384.3 0.0 copy-done.5
  384.3 2.4 fusion.1
  386.7 165.4 %shard_map.222 = (f32[256,2048]{1,0:T(8,128)}, f32[3,1,64,2048]{3,2,1,0:T(8,128)}, f32[1,64,2048]{2,1,0:T(8,128)}, f32[8,2048]{1,0:T(8,128)}) custom-call(bf16[256,2048]{1,0:T(8,128)(2,1)} %get-tuple-element.76.own_ref, bf16[8,256,2048]{2,1,0:T(8,128)(2,1)} %get-tuple-element.35.normed_hbm, bf16[3,8,4,64,256]{4,3,2,1,0:T(8,128)(2,1)} %get-tuple-element.36.weights_hbm, ...), custom_call_target="tpu_custom_call" | custom-call | flops 17179869184 | bytes 471859200 | tf_op jit(solution)/shard_map/pallas_call | solution.py:1532
  552.1 1.5 copy.34
  553.6 0.7 constant_dynamic-slice_fusion
  554.4 0.5 slice_bitcast_fusion.3
  554.9 2.7 slice_bitcast_fusion
  557.6 0.0 copy-done.1
  557.6 3.0 add_multiply_fusion
  560.6 1.3 copy.50
  561.9 0.1 copy-done.11
  561.9 0.8 copy.51
  562.7 0.1 copy-done.8
  562.9 1.1 copy.52
  564.0 0.0 copy-done.7
  564.0 1.1 copy.53
  (52 shorter events, 0.3 us)
Async XLA Ops:
  7.2 4.7 copy-start.14
  7.2 4.6 copy-start.13
  7.2 4.6 copy-start.12
  7.2 197.7 %all-gather.8.cloned.1.call-start = ((), (), s32[]{:S(2)}) async-start(), calls=%async_computation.3 | async-start | bytes 6488064 | tf_op jit(solution)/shard_map/all_gather | solution.py:1677
  9.5 195.4 %all-gather.4.cloned.1.call-start = ((), (), s32[]{:S(2)}) async-start(), calls=%async_computation.1 | async-start | bytes 6488064 | tf_op jit(solution)/shard_map/all_gather | solution.py:1677
  10.3 12.2 %copy-start.2 = (f32[256,2048]{1,0:T(8,128)S(1)}, f32[256,2048]{1,0:T(8,128)}, u32[]{:S(2)}) copy-start(f32[256,2048]{1,0:T(8,128)} %param.13) | copy-start | bytes 6291460
  10.3 194.7 %all-gather.6.cloned.1.call-start = ((), (), s32[]{:S(2)}) async-start(), calls=%async_computation.2 | async-start | bytes 6488064 | tf_op jit(solution)/shard_map/all_gather | solution.py:1677
  11.0 546.6 %reduce-scatter.2.cloned.1.call-start = ((), (), s32[]{:S(2)}) async-start(), calls=%async_computation.4 | async-start | bytes 5242880 | tf_op jit(solution)/shard_map/reduce_scatter | solution.py:1694
  11.9 10.9 %collective-permute-start = (bf16[4,64]{1,0:T(4,128)(2,1)S(1)}, bf16[4,64]{1,0:T(4,128)(2,1)S(1)}, u32[]{:S(2)}, u32[]{:S(2)}) collective-permute-start(bf16[4,64]{1,0:T(4,128)(2,1)S(1)} %pad_maximum_fusion), channel_id=1, source_target_pairs={{0,3},{1,0},{2,1},{3,2},{4,7},{5,4},{6,5},{7,6},{8,11},{9,8},{10,9... | collective-permute-start | bytes 1544 | tf_op jit(solution)/shard_map/ppermute | solution.py:148
  17.0 5.8 %collective-permute-start.1 = (bf16[4,64]{1,0:T(4,128)(2,1)S(1)}, bf16[4,64]{1,0:T(4,128)(2,1)S(1)}, u32[]{:S(2)}, u32[]{:S(2)}) collective-permute-start(bf16[4,64]{1,0:T(4,128)(2,1)S(1)} %pad_maximum_fusion), channel_id=1, source_target_pairs={{0,2},{1,3},{2,0},{3,1},{4,6},{5,7},{6,4},{7,5},{8,10},{9,11},{10,... | collective-permute-start | bytes 1544 | tf_op jit(solution)/shard_map/ppermute | solution.py:148
  17.0 5.8 %collective-permute-start.2 = (bf16[4,64]{1,0:T(4,128)(2,1)S(1)}, bf16[4,64]{1,0:T(4,128)(2,1)S(1)}, u32[]{:S(2)}, u32[]{:S(2)}) collective-permute-start(bf16[4,64]{1,0:T(4,128)(2,1)S(1)} %pad_maximum_fusion), channel_id=1, source_target_pairs={{0,1},{1,2},{2,3},{3,0},{4,5},{5,6},{6,7},{7,4},{8,9},{9,10},{10,1... | collective-permute-start | bytes 1544 | tf_op jit(solution)/shard_map/ppermute | solution.py:148
  19.9 16.3 %copy-start.10 = (bf16[256,2048]{1,0:T(8,128)(2,1)}, bf16[256,2048]{1,0:T(8,128)(2,1)S(1)}, u32[]{:S(2)}) copy-start(bf16[256,2048]{1,0:T(8,128)(2,1)S(1)} %multiply_convert_fusion.2.own_ref) | copy-start | bytes 3145732
  19.9 25.9 %collective-permute-start.6 = (bf16[256,2048]{1,0:T(8,128)(2,1)S(1)}, bf16[256,2048]{1,0:T(8,128)(2,1)}, u32[]{:S(2)}, u32[]{:S(2)}) collective-permute-start(bf16[256,2048]{1,0:T(8,128)(2,1)S(1)} %multiply_convert_fusion.2.own_ref), channel_id=1, source_target_pairs={{0,1},{1,2},{2,3},{3,0},{4,5},{5,6},{6,7},{7,4},{8,9},{9,10},{10,1... | collective-permute-start | bytes 3145736 | tf_op jit(solution)/shard_map/ppermute | solution.py:122
  22.9 3.7 collective-permute-start.3
  26.6 3.9 collective-permute-start.4
  30.5 1.2 collective-permute-start.5
  45.8 155.8 %copy-start.3 = (f32[256,2048]{1,0:T(8,128)S(1)}, f32[256,2048]{1,0:T(8,128)}, u32[]{:S(2)}) copy-start(f32[256,2048]{1,0:T(8,128)} %param.13) | copy-start | bytes 6291460
  203.5 180.8 %copy-start = (f32[256,2048]{1,0:T(8,128)}, f32[256,2048]{1,0:T(8,128)S(1)}, u32[]{:S(2)}) copy-start(f32[256,2048]{1,0:T(8,128)S(1)} %get-tuple-element.79) | copy-start | bytes 6291460
  381.4 2.9 copy-start.4
  381.4 2.9 copy-start.5
  386.7 165.4 %copy-start.9 = (f32[256,1408]{1,0:T(8,128)S(1)}, f32[256,1408]{1,0:T(8,128)}, u32[]{:S(2)}) copy-start(f32[256,1408]{1,0:T(8,128)} %get-tuple-element.49) | copy-start | bytes 4325380
  554.9 2.7 copy-start.1
  557.6 3.0 copy-start.6
  560.6 1.4 copy-start.11
  560.6 2.3 copy-start.8
  561.9 2.0 copy-start.7
Sparse Core Ops, SparseCore 0:
  9.9 51.8 all-gather.7
  63.7 57.6 all-gather.3
  123.3 56.9 all-gather.5
  380.0 92.4 reduce-scatter.1

commit v4 on v3

--- a/solution.py
+++ b/solution.py
@@ -206,6 +206,17 @@
     )
 
 
+def along(step, source, target, send_sem, recv_sem):
+    return pltpu.make_async_remote_copy(
+        src_ref=source,
+        dst_ref=target,
+        send_sem=send_sem,
+        recv_sem=recv_sem,
+        device_id={"tensor": beside(step)},
+        device_id_type=pl.DeviceIdType.MESH,
+    )
+
+
 def plane_gather_steps(copies, value_ref, all_ref, own_sem, send_sem, recv_sem):
     near, one, two = copies, 2 * copies, 4 * copies
     half = value_ref.shape[0] // 2
@@ -281,70 +292,15 @@
     return begin, pass_first, pass_second, pass_last, arrive, finish
 
 
-def plane_gather_kernel(copies, value_ref, all_ref, own_sem, send_sem, recv_sem):
-    greet((copies, 2 * copies, 4 * copies))
-    for step in plane_gather_steps(
-        copies, value_ref, all_ref, own_sem.at[0], send_sem, recv_sem
-    ):
-        step()
-
-
-def plane_gather(value, copies, collective):
-    rows, width = value.shape
-    somewhere = pl.BlockSpec(memory_space=pl.ANY)
-    return pl.pallas_call(
-        functools.partial(plane_gather_kernel, copies),
-        out_shape=jax.ShapeDtypeStruct((8, rows, width), value.dtype),
-        in_specs=[somewhere],
-        out_specs=somewhere,
-        scratch_shapes=[
-            pltpu.SemaphoreType.DMA((1,)),
-            pltpu.SemaphoreType.DMA((14,)),
-            pltpu.SemaphoreType.DMA((14,)),
-        ],
-        compiler_params=pltpu.CompilerParams(collective_id=collective, has_side_effects=True),
-        cost_estimate=pl.CostEstimate(
-            flops=0, bytes_accessed=320 * rows * width, transcendentals=0
-        ),
-    )(value)
-
-
-def plane_scatter_kernel(
-    copies, transposed, left_ref, right_ref, sum_ref, near_ref, one_ref, two_ref, part_ref,
-    send_sem, recv_sem, block_ref=None, blocks_ref=None, ring_send=None, ring_recv=None,
-    total_ref=None, shares=None, ring_buf=None, load_sem=None, greeted=False, product=None,
-    between=lambda point: None,
+def plane_scatter_steps(
+    copies, sum_ref, near_ref, one_ref, two_ref, part_ref,
+    send_sem, recv_sem, product, between,
 ):
     near, one, two = copies, 2 * copies, 4 * copies
     rows, width = sum_ref.shape
     half = rows // 2
     top, low = pl.ds(0, half), pl.ds(half, half)
     tile = min(512, width)
-    if not greeted:
-        greet((near, one, two), ring_send is not None)
-    ring_steps = []
-    parts = lax.axis_size("tensor")
-    if shares is not None:
-        loads = [
-            pltpu.make_async_copy(block_ref.at[beside(-k)], shares.at[k], load_sem.at[k])
-            for k in range(parts)
-        ]
-        for load in loads:
-            load.start()
-        for load in loads:
-            load.wait()
-        sum_steps = [
-            to_right(shares.at[k + 1], ring_buf.at[k], ring_send.at[k], ring_recv.at[k])
-            for k in range(parts - 1)
-        ]
-        sum_steps[0].start()
-    elif block_ref is not None:
-        for k in range(blocks_ref.shape[0]):
-            source = block_ref if k == 0 else blocks_ref.at[k - 1]
-            ring_steps.append(
-                to_right(source, blocks_ref.at[k], ring_send.at[k], ring_recv.at[k])
-            )
-        ring_steps[0].start()
     flips = [(), (one,), (two,), (one, two)]
     copies_out = []
 
@@ -367,14 +323,6 @@
         def _(k):
             body(pl.ds(pl.multiple_of(k * tile, tile), tile))
 
-    def block_product(slot, columns):
-        left = left_ref[slot]
-        if transposed:
-            return matmul_rt(left, right_ref[columns, :])
-        return matmul(left, right_ref[:, columns])
-
-    product = product or block_product
-
     arriving = {}
     for k in (3, 1, 2, 0):
         slot = slot_of(copies, flips[k] + (near,))
@@ -437,110 +385,14 @@
 
         each_tile(body)
 
-    def sum_step(k):
-        sum_steps[k].wait_recv()
-        many = shares.shape[1] // 4
-
-        @pl.loop(0, 4)
-        def _(n):
-            some = pl.ds(pl.multiple_of(n * many, many), many)
-            at = (k + 2) % parts
-            total = shares[at, some, :].astype(f32) + ring_buf[k, some, :].astype(f32)
-            if at:
-                shares[at, some, :] = total.astype(bf16)
-            else:
-                total_ref[some, :] = total
-
-        if k + 1 < parts - 1:
-            sum_steps[k + 1].start()
-
-    if shares is not None:
-        sum_step(0)
-    for k, step in enumerate(ring_steps):
-        step.wait_recv()
-        if k + 1 < len(ring_steps):
-            ring_steps[k + 1].start()
     one_second.wait_recv()
     two_last.wait_recv()
     finish(top, one_ref, 1, two_ref, 2)
     two_second.wait_recv()
     one_last.wait_recv()
     finish(low, two_ref, 1, one_ref, 2)
-    between("whole")
-    if shares is not None:
-        for k in range(1, parts - 1):
-            sum_step(k)
-        ring_steps = sum_steps
-    for copy in copies_out + ring_steps:
+    for copy in copies_out:
         copy.wait_send()
-
-
-def scatter_late_kernel(copies, transposed, late, left_ref, right_ref, block_ref, *refs):
-    sum_ref, blocks_ref = refs[late : late + 2]
-    refs = refs[late + 2 :]
-    if len(refs) == 8:
-        plane_scatter_kernel(
-            copies, transposed, left_ref, right_ref, sum_ref, *refs[:6], block_ref, blocks_ref,
-            *refs[6:],
-        )
-    else:
-        plane_scatter_kernel(
-            copies, transposed, left_ref, right_ref, sum_ref, *refs[:6], block_ref, None,
-            *refs[6:8], blocks_ref, *refs[8:],
-        )
-
-
-def plane_scatter(left, right, copies, transposed, collective, block=None, sums=None, before=()):
-    group, rows, depth = left.shape
-    width = right.shape[0] if transposed else right.shape[1]
-    half = rows // 2
-    vmem = pl.BlockSpec(memory_space=pltpu.VMEM)
-    somewhere = pl.BlockSpec(memory_space=pl.ANY)
-    scratch = [
-        pltpu.VMEM((4, rows, width), bf16),
-        pltpu.VMEM((3, half, width), bf16),
-        pltpu.VMEM((3, half, width), bf16),
-        pltpu.VMEM((4, rows, width), bf16),
-        pltpu.SemaphoreType.DMA((10,)),
-        pltpu.SemaphoreType.DMA((10,)),
-    ]
-    shapes = [jax.ShapeDtypeStruct((rows, width), f32)]
-    out_specs = [vmem]
-    parts = lax.axis_size("tensor")
-    if block is not None:
-        operands = [left, right, block]
-        steps = parts - 2
-        shapes.append(jax.ShapeDtypeStruct((steps,) + block.shape, block.dtype))
-        out_specs.append(somewhere)
-        scratch += [pltpu.SemaphoreType.DMA((steps,))] * 2
-    else:
-        operands = [left, right, sums]
-        shapes.append(jax.ShapeDtypeStruct(sums.shape[1:], f32))
-        out_specs.append(vmem)
-        scratch += [pltpu.SemaphoreType.DMA((parts - 1,))] * 2
-        scratch += [
-            pltpu.VMEM(sums.shape, bf16),
-            pltpu.VMEM((parts - 1,) + sums.shape[1:], bf16),
-            pltpu.SemaphoreType.DMA((parts,)),
-        ]
-    operands += before
-    return pl.pallas_call(
-        functools.partial(
-            scatter_late_kernel, copies, transposed, len(before)
-        ),
-        out_shape=shapes,
-        in_specs=[vmem, vmem] + [somewhere] * (len(operands) - 2),
-        out_specs=out_specs,
-        scratch_shapes=scratch,
-        compiler_params=pltpu.CompilerParams(
-            collective_id=collective, has_side_effects=True, vmem_limit_bytes=48 * 1024 * 1024
-        ),
-        cost_estimate=pl.CostEstimate(
-            flops=2 * group * rows * depth * width,
-            bytes_accessed=400 * rows * width,
-            transcendentals=0,
-        ),
-    )(*operands)
 
 
 def column_tiles(width, most=512):
@@ -549,64 +401,77 @@
 
 def swiglu_kernel(
     copies,
-    normed_ref, own_ref, first_ref, others_ref, gate_hbm, up_hbm, down_hbm,
-    rows_out, norm_sum, gate_sum, up_sum, down_sum,
+    normed_ref, own_ref, first_ref, others_ref, gate_hbm, up_hbm, down_ref,
+    rows_out, moved_out, norm_sum, gate_sum, up_sum, down_sum,
     normed, masked, gate_w, up_w, down_w, hidden, gate_low, up_low, back, rows, ring_buf,
-    one_buf, two_buf, in_sem, out_sem, send_sem, recv_sem, sum_send, sum_recv, near_send,
-    near_recv, one_send, one_recv, two_send, two_recv, ready_sem,
+    one_buf, two_buf, lead, lead_near, in_sem, out_sem, gather_send, gather_recv, send_sem,
+    recv_sem, sum_send, sum_recv, near_send, near_recv, one_send, one_recv, two_send, two_recv,
+    ready_sem, moved_send, moved_recv,
 ):
     parts = lax.axis_size("tensor")
     near, one, two = copies, 2 * copies, 4 * copies
     greet((near, one, two), True)
     own = pltpu.make_async_copy(normed_ref, normed.at[0], in_sem.at[0])
     own.start()
+    gather = plane_gather_steps(
+        copies, down_ref, down_w, in_sem.at[4], gather_send, gather_recv
+    )
+    gather[0]()
     loads = [
         pltpu.make_async_copy(gate_hbm, gate_w, in_sem.at[1]),
         pltpu.make_async_copy(up_hbm, up_w, in_sem.at[2]),
         pltpu.make_async_copy(own_ref, masked.at[0], in_sem.at[3]),
-        pltpu.make_async_copy(down_hbm, down_w, in_sem.at[4]),
         pltpu.make_async_copy(first_ref, masked.at[1], in_sem.at[5]),
         pltpu.make_async_copy(others_ref, masked.at[pl.ds(2, parts - 2)], in_sem.at[6]),
     ]
     own.wait()
     for load in loads:
         load.start()
-    width = normed.shape[2]
-    tile = min(512, width)
-
-    def hop(k):
-        return to_right(normed.at[k], normed.at[k + 1], send_sem.at[k], recv_sem.at[k])
-
-    def sum_hop(k):
-        return to_right(back.at[k + 1], ring_buf.at[k], sum_send.at[k], sum_recv.at[k])
-
-    hop(0).start()
+    _, block_rows, width = normed.shape
+    hidden_width = hidden.shape[2]
+    share = width // 8
+    half = share // 2
+    many = 2
+    tile = many * share
+    both = [pl.ds(n * (block_rows // 2), block_rows // 2) for n in range(2)]
+
+    def hop(k, n):
+        return to_right(
+            normed.at[k, both[n]], normed.at[k + 1, both[n]], send_sem.at[k, n], recv_sem.at[k, n]
+        )
+
+    def sum_hop(k, n):
+        return to_right(
+            back.at[k + 1, both[n]], ring_buf.at[k, both[n]], sum_send.at[k, n], sum_recv.at[k, n]
+        )
+
+    for n in range(2):
+        hop(0, n).start()
     for load in loads:
         load.wait()
+    gather[1]()
+    gather[2]()
+    for n in range(2):
+        hop(0, n).wait_recv()
+        hop(1, n).start()
+    gather[3]()
+    gather[4]()
 
     def store(k):
         home = lax.rem(lax.axis_index("tensor") + parts - k, parts)
         slot = lax.rem(k, 2)
         return pltpu.make_async_copy(rows.at[slot], rows_out.at[home], out_sem.at[slot])
 
-    def block(k, nothing):
-        @pl.when(k > 0)
-        def _():
-            hop(k - 1).wait_recv()
-
-        @pl.when(jnp.logical_and(k > 0, k < parts - 1))
-        def _():
-            hop(k).start()
-
-        @pl.when(k == parts - 1)
-        def _():
-            sum_hop(0).start()
-
-        for at, size in column_tiles(hidden.shape[2]):
+    def front(k):
+        for at, size in column_tiles(hidden_width):
             columns = pl.ds(at, size)
-            glu_gate = matmul(normed[k], gate_w[:, columns])
-            glu_up = matmul(normed[k], up_w[:, columns])
-            grad_hidden = matmul(masked[k], down_w[:, columns])
+
+            def weight(ref):
+                return ref[:, :, columns].reshape(width, size)
+
+            glu_gate = matmul(normed[k], weight(gate_w))
+            glu_up = matmul(normed[k], weight(up_w))
+            grad_hidden = matmul(masked[k], weight(down_w))
             squash = jax.nn.sigmoid(glu_gate)
             act = glu_gate * squash
             slope = squash * (1.0 + glu_gate * (1.0 - squash))
@@ -614,60 +479,68 @@
             gate_low[k, :, columns] = (grad_hidden * glu_up * slope).astype(bf16)
             up_low[k, :, columns] = (grad_hidden * act).astype(bf16)
 
-        @pl.when(k > 1)
-        def _():
-            store(k - 2).wait()
-
+    def rear(k):
         slot = lax.rem(k, 2)
 
-        @pl.loop(0, width // tile)
+        @pl.loop(0, 8 // many)
         def _(n):
             some = pl.ds(pl.multiple_of(n * tile, tile), tile)
+
+            def weight(ref):
+                return ref[pl.ds(n * many, many)].reshape(tile, hidden_width)
+
             back[k, :, some] = (
-                matmul_rt(gate_low[k], gate_w[some, :]) + matmul_rt(up_low[k], up_w[some, :])
+                matmul_rt(gate_low[k], weight(gate_w)) + matmul_rt(up_low[k], weight(up_w))
             ).astype(bf16)
-            rows[slot, :, some] = matmul_rt(hidden[k], down_w[some, :]).astype(bf16)
+            rows[slot, :, some] = matmul_rt(hidden[k], weight(down_w)).astype(bf16)
 
         store(k).start()
+
+    def block(k, nothing):
+        for n in range(2):
+
+            @pl.when(jnp.logical_and(k > 0, k < parts - 2))
+            def _():
+                hop(k, n).wait_recv()
+                hop(k + 1, n).start()
+
+            @pl.when(k == parts - 1)
+            def _():
+                hop(parts - 2, n).wait_recv()
+                sum_hop(0, n).start()
+
+        front(k)
+
+        @pl.when(k > 1)
+        def _():
+            store(k - 2).wait()
+
+        @pl.when(k < parts - 1)
+        def _():
+            rear(k)
+
         return nothing
 
     lax.fori_loop(0, parts, block, 0)
 
-    pl.semaphore_signal(
-        ready_sem,
-        inc=1,
-        device_id={"dp": partner(near)},
-        device_id_type=pl.DeviceIdType.MESH,
-    )
-    share = width // 8
-    half = share // 2
-    hidden_width = hidden.shape[2]
-    tall = parts * normed.shape[1]
+    tall = parts * block_rows
     kinds = (
         (normed, gate_low, gate_w, gate_sum),
         (normed, up_low, up_w, up_sum),
         (masked, hidden, down_w, down_sum),
     )
 
-    def product(kind, slot):
+    def product(kind, slot, store):
         left, right, _, _ = kinds[kind]
         some = pl.ds(pl.multiple_of(slot * share, share), share)
-        return matmul_lt(
-            left[:, :, some].reshape(tall, share), right[...].reshape(tall, hidden_width)
-        )
-
-    def part_at(k):
-        return pl.ds(pl.multiple_of(k * share, share), share)
-
-    def near_at(k):
-        return pl.ds(pl.multiple_of((4 + k) * share, share), share)
-
-    def halves(k):
-        at = (4 + k) * share
-        return (
-            pl.ds(pl.multiple_of(at, half), half),
-            pl.ds(pl.multiple_of(at + half, half), half),
-        )
+        for at, size in column_tiles(hidden_width):
+            columns = pl.ds(at, size)
+            store(
+                columns,
+                matmul_lt(
+                    left[:, :, some].reshape(tall, share), right[:, :, columns].reshape(tall, size)
+                ),
+            )
 
     def across(source, target, send, recv, mask):
         return pltpu.make_async_remote_copy(
@@ -679,25 +552,31 @@
             device_id_type=pl.DeviceIdType.MESH,
         )
 
+    top, low = pl.ds(0, half), pl.ds(half, half)
+
     def near_copy(kind, k):
         room = kinds[kind][2]
         return across(
-            room.at[part_at(k)], room.at[near_at(k)], near_send.at[kind, k],
-            near_recv.at[kind, k], near,
+            room.at[k], room.at[4 + k], near_send.at[kind, k], near_recv.at[kind, k], near
+        )
+
+    def lead_copy(kind):
+        return across(
+            lead.at[kind], lead_near.at[kind], near_send.at[kind, 3], near_recv.at[kind, 3], near
         )
 
     def one_copy(kind, n):
         room = kinds[kind][2]
-        rows_at = (halves(3)[0], halves(1)[0], halves(1)[1])[n]
+        source = (lead_near.at[kind, top], room.at[5, top], room.at[5, low])[n]
         return across(
-            room.at[rows_at], one_buf.at[kind, n], one_send.at[kind, n], one_recv.at[kind, n], one
+            source, one_buf.at[kind, n], one_send.at[kind, n], one_recv.at[kind, n], one
         )
 
     def two_copy(kind, n):
         room = kinds[kind][2]
-        rows_at = (halves(3)[1], halves(2)[1], halves(2)[0])[n]
+        source = (lead_near.at[kind, low], room.at[6, low], room.at[6, top])[n]
         return across(
-            room.at[rows_at], two_buf.at[kind, n], two_send.at[kind, n], two_recv.at[kind, n], two
+            source, two_buf.at[kind, n], two_send.at[kind, n], two_recv.at[kind, n], two
         )
 
     def flipped(k, near_too):
@@ -709,82 +588,110 @@
         there = me + turn(one, lax.rem(k, 2)) + turn(two, lax.div(k, 2)) + turn(near, near_too)
         return lax.div(there, copies)
 
-    def in_turn(i):
-        return 3 - 2 * i + 3 * lax.div(i, 2)
-
     def sum_step(k):
-        sum_hop(k).wait_recv()
-        if k + 1 < parts - 1:
-
-            @pl.loop(0, width // tile)
-            def _(n):
-                some = pl.ds(pl.multiple_of(n * tile, tile), tile)
-                total = back[k + 2, :, some].astype(f32) + ring_buf[k, :, some].astype(f32)
-                back[k + 2, :, some] = total.astype(bf16)
-
-            sum_hop(k + 1).start()
-        else:
-
-            @pl.loop(0, width // tile)
-            def _(n):
-                some = pl.ds(pl.multiple_of(n * tile, tile), tile)
-                norm_sum[:, some] = back[0, :, some].astype(f32) + ring_buf[k, :, some].astype(f32)
-
+        for n in range(2):
+            sum_hop(k, n).wait_recv()
+
+            @pl.loop(0, 8 // many)
+            def _(at):
+                some = pl.ds(pl.multiple_of(at * tile, tile), tile)
+                moved = ring_buf[k, both[n], some].astype(f32)
+                if k + 1 < parts - 1:
+                    total = back[k + 2, both[n], some].astype(f32) + moved
+                    back[k + 2, both[n], some] = total.astype(bf16)
+                else:
+                    norm_sum[both[n], some] = back[0, both[n], some].astype(f32) + moved
+
+            if k + 1 < parts - 1:
+                sum_hop(k + 1, n).start()
+
+    def keep(ref, at):
+        def store(columns, value):
+            ref[at, :, columns] = value.astype(bf16)
+
+        return store
+
+    def add(ref, at):
+        def store(columns, value):
+            ref[at, :, columns] = (value + ref[at, :, columns].astype(f32)).astype(bf16)
+
+        return store
+
+    def add_wide(total_ref, ref, at):
+        def store(columns, value):
+            total_ref[:, columns] = value + ref[at, :, columns].astype(f32)
+
+        return store
+
+    for kind in range(3):
+        product(kind, flipped(3, 1), keep(lead, kind))
+        lead_copy(kind).start()
+    for kind in range(3):
+        lead_copy(kind).wait_recv()
+        product(kind, flipped(3, 0), add(lead_near, kind))
+        one_copy(kind, 0).start()
+        two_copy(kind, 0).start()
+    rear(parts - 1)
+
+    gather[5]()
+    pl.semaphore_signal(
+        ready_sem,
+        inc=1,
+        device_id={"dp": partner(near)},
+        device_id_type=pl.DeviceIdType.MESH,
+    )
     pl.semaphore_wait(ready_sem, 1)
 
-    def theirs(i, nothing):
-        k = in_turn(i)
-        slot = flipped(k, 1)
+    def theirs(k):
         for kind in range(3):
-            kinds[kind][2][part_at(k), :] = product(kind, slot).astype(bf16)
+            product(kind, flipped(k, 1), keep(kinds[kind][2], k))
             near_copy(kind, k).start()
-        return nothing
-
-    lax.fori_loop(0, 4, theirs, 0)
-    sum_step(0)
-
-    def mine(i, nothing):
-        k = in_turn(i)
-        slot = flipped(k, 0)
+
+    def mine(k):
         for kind in range(3):
             near_copy(kind, k).wait_recv()
-            room = kinds[kind][2]
-            total = product(kind, slot) + room[near_at(k), :].astype(f32)
-            room[near_at(k), :] = total.astype(bf16)
-
-            @pl.when(k == 3)
-            def _():
-                one_copy(kind, 0).start()
-                two_copy(kind, 0).start()
-
-            @pl.when(k == 1)
-            def _():
+            product(kind, flipped(k, 0), add(kinds[kind][2], 4 + k))
+            if k == 1:
                 one_copy(kind, 1).start()
-
-            @pl.when(k == 2)
-            def _():
+            else:
                 two_copy(kind, 1).start()
 
-        return nothing
-
-    lax.fori_loop(0, 3, mine, 0)
+    sum_step(0)
+    theirs(1)
+    theirs(2)
+    mine(1)
+    mine(2)
+    theirs(0)
+    for kind in range(3):
+        one_copy(kind, 0).wait_recv()
+        room = kinds[kind][2]
+        room[6, top] = (room[6, top].astype(f32) + one_buf[kind, 0].astype(f32)).astype(bf16)
+        two_copy(kind, 2).start()
+        two_copy(kind, 0).wait_recv()
+        room[5, low] = (room[5, low].astype(f32) + two_buf[kind, 0].astype(f32)).astype(bf16)
+        one_copy(kind, 2).start()
     for k in range(1, parts - 2):
         sum_step(k)
     for kind in range(3):
         near_copy(kind, 0).wait_recv()
         room, total_ref = kinds[kind][2:]
-        total_ref[...] = product(kind, flipped(0, 0)) + room[near_at(0), :].astype(f32)
-    for kind in range(3):
-        room = kinds[kind][2]
-        one_copy(kind, 0).wait_recv()
-        at = halves(2)[0]
-        room[at, :] = (room[at, :].astype(f32) + one_buf[kind, 0].astype(f32)).astype(bf16)
-        two_copy(kind, 2).start()
-        two_copy(kind, 0).wait_recv()
-        at = halves(1)[1]
-        room[at, :] = (room[at, :].astype(f32) + two_buf[kind, 0].astype(f32)).astype(bf16)
-        one_copy(kind, 2).start()
+        product(kind, flipped(0, 0), add_wide(total_ref, room, 4))
     sum_step(parts - 2)
+    for k in (parts - 2, parts - 1):
+        store(k).wait()
+    here = lax.axis_index("tensor")
+    at_start, at_end = here == 0, here == parts - 1
+    moved_up = along(1, rows_out.at[parts - 1], moved_out, moved_send, moved_recv)
+    moved_down = along(-1, rows_out.at[0], moved_out, moved_send, moved_recv)
+
+    @pl.when(at_start)
+    def _():
+        moved_up.start()
+
+    @pl.when(at_end)
+    def _():
+        moved_down.start()
+
     for kind in range(3):
         total_ref = kinds[kind][3]
         one_copy(kind, 1).wait_recv()
@@ -794,34 +701,50 @@
         one_copy(kind, 2).wait_recv()
         total_ref[half:, :] += two_buf[kind, 1].astype(f32) + one_buf[kind, 2].astype(f32)
     for kind in range(3):
-        for k in range(4):
+        lead_copy(kind).wait_send()
+        for k in range(3):
             near_copy(kind, k).wait_send()
         for n in range(3):
             one_copy(kind, n).wait_send()
             two_copy(kind, n).wait_send()
     for k in range(parts - 1):
-        hop(k).wait_send()
-        sum_hop(k).wait_send()
-    for k in (parts - 2, parts - 1):
-        store(k).wait()
+        for n in range(2):
+            hop(k, n).wait_send()
+            sum_hop(k, n).wait_send()
+
+    @pl.when(at_start)
+    def _():
+        moved_up.wait_send()
+
+    @pl.when(at_end)
+    def _():
+        moved_down.wait_send()
+
+    @pl.when(jnp.logical_not(jnp.logical_or(at_start, at_end)))
+    def _():
+        moved_up.wait_recv()
 
 
 def swiglu(normed, own, first, others, gate_w, up_w, down_w, copies, collective):
     parts = lax.axis_size("tensor")
     rows, width = normed.shape
-    hidden = gate_w.shape[1]
+    hidden = gate_w.shape[2]
     share = width // 8
     somewhere = pl.BlockSpec(memory_space=pl.ANY)
     vmem = pl.BlockSpec(memory_space=pltpu.VMEM)
     wide, narrow = (parts, rows, width), (parts, rows, hidden)
     return pl.pallas_call(
         functools.partial(swiglu_kernel, copies),
-        out_shape=[jax.ShapeDtypeStruct(wide, bf16), jax.ShapeDtypeStruct((rows, width), f32)]
+        out_shape=[
+            jax.ShapeDtypeStruct(wide, bf16),
+            jax.ShapeDtypeStruct((rows, width), bf16),
+            jax.ShapeDtypeStruct((rows, width), f32),
+        ]
         + [jax.ShapeDtypeStruct((share, hidden), f32)] * 3,
         in_specs=[somewhere] * 7,
-        out_specs=[somewhere] + [vmem] * 4,
+        out_specs=[somewhere] * 2 + [vmem] * 4,
         scratch_shapes=[pltpu.VMEM(wide, bf16)] * 2
-        + [pltpu.VMEM((width, hidden), bf16)] * 3
+        + [pltpu.VMEM((8, share, hidden), bf16)] * 3
         + [pltpu.VMEM(narrow, bf16)] * 3
         + [
             pltpu.VMEM(wide, bf16),
@@ -829,13 +752,16 @@
             pltpu.VMEM((parts - 1, rows, width), bf16),
         ]
         + [pltpu.VMEM((3, 3, share // 2, hidden), bf16)] * 2
+        + [pltpu.VMEM((3, share, hidden), bf16)] * 2
         + [pltpu.SemaphoreType.DMA((7,)), pltpu.SemaphoreType.DMA((2,))]
-        + [pltpu.SemaphoreType.DMA((parts - 1,))] * 4
+        + [pltpu.SemaphoreType.DMA((14,))] * 2
+        + [pltpu.SemaphoreType.DMA((parts - 1, 2))] * 4
         + [pltpu.SemaphoreType.DMA((3, 4))] * 2
         + [pltpu.SemaphoreType.DMA((3, 3))] * 4
-        + [pltpu.SemaphoreType.REGULAR],
+        + [pltpu.SemaphoreType.REGULAR]
+        + [pltpu.SemaphoreType.DMA] * 2,
         compiler_params=pltpu.CompilerParams(
-            collective_id=collective, has_side_effects=True, vmem_limit_bytes=60 * 1024 * 1024
+            collective_id=collective, has_side_effects=True, vmem_limit_bytes=62 * 1024 * 1024
         ),
         cost_estimate=pl.CostEstimate(
             flops=18 * parts * rows * width * hidden,
@@ -1020,6 +946,11 @@
         carries.append(copy)
     ring_copy(2, 1).wait_recv()
     ring_copy(2, 2).start()
+
+    def masked_copy(k):
+        source = masked_hbm if k == 0 else masked_out.at[k - 1]
+        return to_right(source, masked_out.at[k], masked_send.at[k], masked_recv.at[k])
+
     for copy in carries:
         copy.wait_recv()
     coming = jnp.zeros((seqs, channels), f32)
@@ -1074,11 +1005,21 @@
         right = project[:, :, :, columns]
         return matmul(mixed[slot], right.reshape(channels, right.shape[-1]))
 
-    plane_scatter_kernel(
-        copies, False, None, None, sum_ref, near_buf, one_buf, two_buf, part_buf, scatter_send,
-        scatter_recv, masked_hbm, masked_out, masked_send, masked_recv, greeted=True,
-        product=out_product,
+    masked_copy(0).start()
+
+    def between(point):
+        if point == "low":
+            for k in range(parts - 3):
+                masked_copy(k).wait_recv()
+                masked_copy(k + 1).start()
+
+    plane_scatter_steps(
+        copies, sum_ref, near_buf, one_buf, two_buf, part_buf, scatter_send, scatter_recv,
+        out_product, between,
     )
+    masked_copy(parts - 3).wait_recv()
+    for k in range(parts - 2):
+        masked_copy(k).wait_send()
     finish()
     for kept, sent in spread:
         for copy in sent:
@@ -1173,12 +1114,14 @@
     copies, masks,
     own_ref, normed_hbm, weights_hbm, project_hbm, pre_hbm, squash_hbm, state_hbm, mixed_hbm,
     unit_hbm, stream_hbm, entering_ref, bound_ref, live_ref, gain_ref, scale_ref, gain_two_ref,
-    result_ref, weight_sums, project_sum, small_sums,
+    rows_hbm, moved_hbm,
+    result_ref, weight_sums, project_sum, small_sums, moved_out,
     rows_buf, weights, project, pre, squashed, state, mixed, unit, stream, drive, decay, ends,
-    entered, grad_pre, grad_w, grad_project, ring_w, ring_project, bound_sum, whole_w, spread_w,
+    entered, grad_pre, grad_w, grad_project, line_w, line_project, bound_sum, whole_w, spread_w,
     small_recv, small_ring, near_buf, one_buf, two_buf, part_buf,
-    load_sem, gather_send, gather_recv, carry_send, carry_recv, ring_send, ring_recv,
+    load_sem, gather_send, gather_recv, carry_send, carry_recv, up_send, down_send, line_recv,
     scatter_send, scatter_recv, spread_send, spread_recv, spread_own, small_send, small_got,
+    moved_sem, moved_send, moved_recv,
 ):
     parts = lax.axis_size("tensor")
     here = lax.axis_index("tensor")
@@ -1193,6 +1136,90 @@
         copies, own_ref, rows_buf, load_sem.at[0], gather_send, gather_recv
     )
     begin()
+
+    at_start, at_end = here == 0, here == parts - 1
+    inside = jnp.logical_not(jnp.logical_or(at_start, at_end))
+    low_half = here == 1
+
+    def fetch(block, came, first, second):
+        loads = (
+            pltpu.make_async_copy(rows_hbm.at[block], part_buf.at[first], moved_sem.at[0]),
+            pltpu.make_async_copy(came, part_buf.at[second], moved_sem.at[1]),
+        )
+        for load in loads:
+            load.start()
+        for load in loads:
+            load.wait()
+        part_buf[first] = (
+            part_buf[first].astype(f32) + part_buf[second].astype(f32)
+        ).astype(bf16)
+
+    def moved_copy(n, step, source):
+        return along(step, source, moved_out.at[n], moved_send.at[n], moved_recv.at[n])
+
+    def moved_second():
+        @pl.when(at_start)
+        def _():
+            moved_copy(0, 1, rows_hbm.at[2]).start()
+
+        @pl.when(at_end)
+        def _():
+            moved_copy(1, -1, rows_hbm.at[1]).start()
+
+        @pl.when(inside)
+        def _():
+            fetch(3 - 3 * (here - 1), moved_hbm, 0, 1)
+
+        @pl.when(low_half)
+        def _():
+            moved_copy(0, 1, part_buf.at[0]).start()
+
+        @pl.when(here == 2)
+        def _():
+            moved_copy(1, -1, part_buf.at[0]).start()
+
+    def moved_last():
+        @pl.when(at_start)
+        def _():
+            moved_copy(0, 1, rows_hbm.at[2]).wait_send()
+            moved_copy(2, 1, rows_hbm.at[1]).start()
+
+        @pl.when(at_end)
+        def _():
+            moved_copy(1, -1, rows_hbm.at[1]).wait_send()
+            moved_copy(3, -1, rows_hbm.at[2]).start()
+
+        @pl.when(inside)
+        def _():
+            moved_copy(0, 1, part_buf.at[0]).wait_recv()
+            fetch(here + 1, moved_out.at[0], 1, 2)
+            moved_copy(2, 1, part_buf.at[1]).start()
+
+        @pl.when(low_half)
+        def _():
+            moved_copy(0, 1, part_buf.at[0]).wait_send()
+
+        @pl.when(here == 2)
+        def _():
+            moved_copy(1, -1, part_buf.at[0]).wait_send()
+
+        @pl.when(inside)
+        def _():
+            moved_copy(1, -1, part_buf.at[0]).wait_recv()
+            fetch(here - 1, moved_out.at[1], 2, 3)
+            moved_copy(3, -1, part_buf.at[2]).start()
+
+    def moved_end():
+        @pl.when(here < parts - 1)
+        def _():
+            moved_copy(2, 1, part_buf.at[1]).wait_send()
+            moved_copy(3, -1, part_buf.at[2]).wait_recv()
+
+        @pl.when(here > 0)
+        def _():
+            moved_copy(3, -1, part_buf.at[2]).wait_send()
+            moved_copy(2, 1, part_buf.at[1]).wait_recv()
+
     loads = [
         pltpu.make_async_copy(source, target, load_sem.at[n + 1])
         for n, (source, target) in enumerate(
@@ -1210,6 +1237,7 @@
     ]
     for load in loads:
         load.start()
+    moved_second()
     for load in loads[:3]:
         load.wait()
 
@@ -1238,6 +1266,7 @@
     pltpu.make_async_copy(own_ref, rows_buf.at[mine], load_sem.at[0]).wait()
     for flips in ((), (near,), (one,), (two,), (near, one), (near, two)):
         take(slot_of(copies, flips))
+    moved_last()
     pass_last()
     take(slot_of(copies, (one, two)))
     arrive(slice(6, 8))
@@ -1257,33 +1286,101 @@
             copies, parts, own_rows, tile
         )
 
-    def ring_copy(kind, k):
-        at = beside(-(k + 1))
+    def part_of(kind, block):
+        return grad_project.at[:, block] if kind == 3 else grad_w.at[kind, :, block]
+
+    def room_of(kind, index):
+        return line_project.at[index] if kind == 3 else line_w.at[kind, index]
+
+    def line_up(kind, k):
+        block = parts - 1 - k + here
+        return along(
+            1, part_of(kind, block), room_of(kind, block), up_send.at[kind, k],
+            line_recv.at[kind, block],
+        )
+
+    def line_down(kind, k):
+        block = k - parts + 1 + here
+        index = parts if k == parts - 2 else block
+        return along(
+            -1, part_of(kind, block), room_of(kind, index), down_send.at[kind, k],
+            line_recv.at[kind, index],
+        )
+
+    def came(kind, index):
+        return along(1, part_of(kind, 0), room_of(kind, index), up_send.at[kind, 0],
+                     line_recv.at[kind, index])
+
+    def add_came(kind, block):
+        came(kind, block).wait_recv()
         if kind == 3:
-            source, target = grad_project.at[:, at], ring_project.at[k]
+            total = grad_project[:, block].astype(f32) + line_project[block].astype(f32)
+            grad_project[:, block] = total.astype(bf16)
         else:
-            source, target = grad_w.at[kind, :, at], ring_w.at[kind, k]
-        return to_right(source, target, ring_send.at[kind, k], ring_recv.at[kind, k])
+            total = grad_w[kind, :, block].astype(f32) + line_w[kind, block].astype(f32)
+            grad_w[kind, :, block] = total.astype(bf16)
+
+    def goes_up(k):
+        return jnp.logical_and(here <= k, here < parts - 1)
+
+    def goes_down(k):
+        return jnp.logical_and(parts - 1 - here <= k, here > 0)
+
+    def line_step(kind, k):
+        @pl.when(jnp.logical_and(goes_up(k), here > 0))
+        def _():
+            add_came(kind, parts - 1 - k + here)
+
+        @pl.when(goes_up(k))
+        def _():
+            line_up(kind, k).start()
+
+        @pl.when(jnp.logical_and(goes_down(k), here < parts - 1))
+        def _():
+            add_came(kind, k - parts + 1 + here)
+
+        @pl.when(goes_down(k))
+        def _():
+            line_down(kind, k).start()
 
     def advance(kind, k):
-        ring_copy(kind, k).wait_recv()
-        at = beside(-(k + 2))
+        if k + 1 < parts - 1:
+            line_step(kind, k + 1)
+            return
+
+        @pl.when(here > 0)
+        def _():
+            came(kind, here).wait_recv()
+
+        @pl.when(here < parts - 1)
+        def _():
+            came(kind, parts).wait_recv()
+
         if kind == 3:
-            total = grad_project[:, at].astype(f32) + ring_project[k].astype(f32)
+            project_sum[...] = (
+                grad_project[:, here].astype(f32)
+                + line_project[here].astype(f32)
+                + line_project[parts].astype(f32)
+            )
         else:
-            total = grad_w[kind, :, at].astype(f32) + ring_w[kind, k].astype(f32)
-        if k + 1 < parts - 1:
-            if kind == 3:
-                grad_project[:, at] = total.astype(bf16)
-            else:
-                grad_w[kind, :, at] = total.astype(bf16)
-            ring_copy(kind, k + 1).start()
-        elif kind == 3:
-            project_sum[...] = total
-        else:
+            total = (
+                grad_w[kind, :, here].astype(f32)
+                + line_w[kind, here].astype(f32)
+                + line_w[kind, parts].astype(f32)
+            )
             whole_w[kind] = total.astype(bf16)
             for copy in spread_copies(kind):
                 copy.start()
+
+    @pl.when(at_start)
+    def _():
+        line_w[:, 0] = jnp.zeros_like(line_w[:, 0])
+        line_project[0] = jnp.zeros_like(line_project[0])
+
+    @pl.when(at_end)
+    def _():
+        line_w[:, parts] = jnp.zeros_like(line_w[:, parts])
+        line_project[parts] = jnp.zeros_like(line_project[parts])
 
     def spread_copies(kind, own=True):
         found = []
@@ -1309,7 +1406,7 @@
             )
         return found
 
-    ring_copy(3, 0).start()
+    line_step(3, 0)
     finish()
     normed_load = pltpu.make_async_copy(normed_hbm, rows_buf, load_sem.at[0])
     normed_load.start()
@@ -1361,7 +1458,7 @@
                 count, parts, own_rows, channels
             )
 
-        ring_copy(kind, 0).start()
+        line_step(kind, 0)
 
     advance(3, 0)
     weight_grad(2)
@@ -1411,6 +1508,7 @@
     advance(2, 0)
     weight_grad(1)
     loads[5].wait()
+    moved_end()
 
     def normed_product(slot, columns):
         at = lax.div(columns.start, parts * own_rows)
@@ -1427,19 +1525,19 @@
     def between(point):
         if point == "sent":
             advance(3, 2)
+        elif point == "added":
             advance(2, 1)
-        elif point == "added":
             advance(0, 0)
-            advance(2, 2)
         elif point == "top":
             advance(1, 0)
+            advance(2, 2)
         elif point == "low":
             advance(0, 1)
             advance(1, 1)
 
-    plane_scatter_kernel(
-        copies, True, None, None, result_ref, near_buf, one_buf, two_buf, part_buf, scatter_send,
-        scatter_recv, greeted=True, product=normed_product, between=between,
+    plane_scatter_steps(
+        copies, result_ref, near_buf, one_buf, two_buf, part_buf, scatter_send, scatter_recv,
+        normed_product, between,
     )
 
     for load in loads[6:]:
@@ -1507,7 +1605,15 @@
         small_sums[...] += small_ring[k]
     for kind in range(4):
         for k in range(parts - 1):
-            ring_copy(kind, k).wait_send()
+
+            @pl.when(goes_up(k))
+            def _():
+                line_up(kind, k).wait_send()
+
+            @pl.when(goes_down(k))
+            def _():
+                line_down(kind, k).wait_send()
+
     for kind in range(3):
         for copy in spread_copies(kind, False):
             copy.wait_send()
@@ -1517,7 +1623,7 @@
 
 def mixer_backward(
     own, normed, weights, project, pre, squashed, state, mixed, unit, stream, entering, bound,
-    live, gain, scale, gain_two, copies, masks, collective,
+    live, gain, scale, gain_two, out_rows, out_moved, copies, masks, collective,
 ):
     parts = lax.axis_size("tensor")
     _, rows, width = normed.shape
@@ -1536,9 +1642,10 @@
             jax.ShapeDtypeStruct((3, copies, own_rows, width), f32),
             jax.ShapeDtypeStruct((copies, own_rows, width), f32),
             jax.ShapeDtypeStruct((8, width), f32),
+            jax.ShapeDtypeStruct((4, rows, width), bf16),
         ],
-        in_specs=[somewhere] * 10 + [vmem] * 6,
-        out_specs=[vmem] * 4,
+        in_specs=[somewhere] * 10 + [vmem] * 6 + [somewhere] * 2,
+        out_specs=[vmem] * 4 + [somewhere],
         scratch_shapes=[
             pltpu.VMEM(normed.shape, bf16),
             pltpu.VMEM(weights.shape, bf16),
@@ -1556,8 +1663,8 @@
             pltpu.VMEM((8, rows, 3 * channels), bf16),
             pltpu.VMEM(weights.shape, bf16),
             pltpu.VMEM(project.shape, bf16),
-            pltpu.VMEM((3, parts - 1) + blocks, bf16),
-            pltpu.VMEM((parts - 1, copies, own_rows, width), bf16),
+            pltpu.VMEM((3, parts + 1) + blocks, bf16),
+            pltpu.VMEM((parts + 1, copies, own_rows, width), bf16),
             pltpu.VMEM((1, channels), f32),
             pltpu.VMEM((3,) + blocks, bf16),
             pltpu.VMEM((3, 8, copies, own_rows, channels), bf16),
@@ -1574,6 +1681,7 @@
             dma((parts - 1,)),
             dma((4, parts - 1)),
             dma((4, parts - 1)),
+            dma((4, parts + 1)),
             dma((10,)),
             dma((10,)),
             dma((3, 7)),
@@ -1581,6 +1689,9 @@
             dma((3,)),
             dma((len(masks) + parts - 1,)),
             dma((len(masks) + parts - 1,)),
+            dma((2,)),
+            dma((4,)),
+            dma((4,)),
         ],
         compiler_params=pltpu.CompilerParams(
             collective_id=collective, has_side_effects=True, vmem_limit_bytes=62 * 1024 * 1024
@@ -1592,7 +1703,7 @@
         ),
     )(
         own, normed, weights, project, pre, squashed, state, mixed, unit, stream, entering, bound,
-        live, gain, scale, gain_two,
+        live, gain, scale, gain_two, out_rows, out_moved,
     )
 
 
@@ -1671,16 +1782,19 @@
     )
     stream = inputs + mixed_sum
 
-    first, second = orders(all_masks)
     hidden_here = w_gate.shape[1]
-    gate_w, up_w, down_w = (
-        lax.all_gather(weight, "dp", axis=0, tiled=True) for weight in (w_gate, w_up, w_down.T)
+    gate_w, up_w = (
+        lax.all_gather(weight, "dp", axis=0, tiled=True).reshape(group, channels, hidden_here)
+        for weight in (w_gate, w_up)
     )
+    down_part = w_down.T
+    if copies > 1:
+        down_part = gather_bits(down_part, copy_masks[::-1]).reshape(channels, hidden_here)
 
     scale_two, unit_two = norm_rows(stream)
     normed_two = (unit_two * gain_two).astype(bf16)
-    out_rows, grad_norm_two, *weight_sums = swiglu(
-        normed_two, masked_own, masked_first, masked_others, gate_w, up_w, down_w, copies, 4
+    out_rows, out_moved, grad_norm_two, *weight_sums = swiglu(
+        normed_two, masked_own, masked_first, masked_others, gate_w, up_w, down_part, copies, 4
     )
     if copies > 1:
         weight_sums = [
@@ -1690,14 +1804,11 @@
     grad_gate_mine, grad_up_mine, grad_down_mine = weight_sums
     grad_down_mine = grad_down_mine.T
 
-    out_rows = out_rows.reshape(tensor_parts * rows_here, width)
-    out_sum = lax.psum_scatter(out_rows, "tensor", scatter_dimension=0, tiled=True)
-
     gain_two_part = jnp.sum(grad_norm_two * unit_two, axis=0)
     grad_stream = masked_grad + norm_back(grad_norm_two, unit_two, scale_two, gain_two)
 
     normed_one, mixer_w, out_w, pre, squashed, state, entering = mixer_kept
-    grad_inputs, mixer_sums, out_w_sum, small_sums = mixer_backward(
+    grad_inputs, mixer_sums, out_w_sum, small_sums, out_others = mixer_backward(
         grad_stream.astype(bf16),
         normed_one,
         mixer_w,
@@ -1714,11 +1825,16 @@
         gain_one[None, :],
         scale_one,
         gain_two_part[None, :],
+        out_rows,
+        out_moved,
         copies,
         all_masks,
         3,
     )
-    output = live_own * (stream + after(out_sum, small_sums).astype(f32))
+    out_sum = lax.dynamic_index_in_dim(out_rows, tensor_index, 0, keepdims=False).astype(f32)
+    out_sum += jnp.where(tensor_index > 0, out_others[2].astype(f32), 0.0)
+    out_sum += jnp.where(tensor_index < tensor_parts - 1, out_others[3].astype(f32), 0.0)
+    output = live_own * (stream + out_sum)
     grad_weights = [mixer_sums[0], mixer_sums[1], mixer_sums[2], out_w_sum]
     if copies > 1:
         grad_weights = [scatter_bits(total, copy_masks, f32) for total in grad_weights]

time: 572 us -> 553 us (0.967)
  Pallas kernels: 496 us -> 472 us
    pallas_call x1, Pallas kernels: 165 us -> 144 us  [mixer_backward(): pl.pallas_call(functools.partial(mixer_backward_kernel, copies, masks), o...]
    pallas_call x1, Pallas kernels: 156 us -> 148 us  [mixer_forward(): pl.pallas_call(functools.partial(mixer_forward_kernel, copies), out_shape...]
  transfers between devices with their start and end apart: 11 -> 9, of which waited for: 4 -> 4; matrix products, arithmetic and copies ran while one was open for 4% -> 3% of each run, Pallas kernels for 56% -> 27%
where the time goes in v4:
time: 553 us; the launch traced here: 549 us
  Pallas kernels  472 us (85%)
  other arithmetic  19.7 us (4%)
  local copies, waits for them, and re-layouts  17.7 us (3%)
  between operations  15.2 us (3%)
  waiting for transfers between devices  13.1 us (2%)
  starting transfers between devices  11.7 us (2%)
    pallas_call x1, Pallas kernels, swiglu(): pl.pallas_call(functools.partial(swiglu_kernel, copies), out_shape=[jax.S...  180 us
    pallas_call x1, Pallas kernels, mixer_forward(): pl.pallas_call(functools.partial(mixer_forward_kernel, copies), out_shape...  148 us
    pallas_call x1, Pallas kernels, mixer_backward(): pl.pallas_call(functools.partial(mixer_backward_kernel, copies, masks), o...  144 us
    unnamed x42, local copies, waits for them, and re-layouts  11.2 us
  transfers between devices with their start and end apart: 9, of which 4 were waited for; matrix products, arithmetic and copies ran while one was open for 3% of the time, Pallas kernels for 27%

profile of v4, /device:TPU:0, one launch (start us, length us, event | category | flops | bytes accessed | tf_op | source)
XLA Modules:
  0.0 549.5 jit_solution(3895402131472766611)
XLA Ops:
  7.2 0.0 all-gather.3.cloned.1.call-start
  7.2 0.7 all-gather.3.cloned.1.call-update
  7.9 0.0 copy-start.3
  7.9 0.0 all-gather.5.cloned.1.call-start
  8.0 0.7 all-gather.5.cloned.1.call-update
  9.3 0.1 maximum_bitcast_fusion
  9.4 0.7 pad_maximum_fusion
  10.1 5.1 collective-permute-start
  15.2 0.0 collective-permute-start.1
  15.2 1.0 collective-permute-start.2
  16.3 1.8 multiply_convert_fusion.2.own_ref
  18.0 0.0 copy-start.9
  18.0 0.0 copy-start.11
  18.0 0.0 copy-start.12
  18.1 0.0 copy-start.13
  18.1 2.5 collective-permute-start.6
  20.6 0.0 copy-done.3
  20.6 0.2 multiply_reduce_fusion.3
  20.8 2.4 copy.30
  23.2 0.8 copy.32.scale_ref
  24.0 0.0 collective-permute-done
  24.0 0.0 collective-permute-done.1
  24.0 0.0 collective-permute-done.2
  24.1 0.0 copy-done.11
  24.2 1.5 collective-permute-start.3
  25.7 2.2 collective-permute-done.3
  27.9 1.5 collective-permute-start.4
  29.4 2.2 collective-permute-done.4
  31.7 0.1 collective-permute-start.5
  31.8 1.1 collective-permute-done.5
  33.0 0.1 mul.103
  33.1 0.7 broadcast_in_dim_reshape_squeeze.2.gain_ref
  33.8 0.1 copy.28
  33.9 0.1 convert_bitcast_fusion
  33.9 1.3 copy.35
  35.3 0.1 reshape_squeeze.15
  35.4 0.1 mul.112
  35.4 0.6 dynamic_slice.16
  36.1 1.9 multiply_convert_fusion.1
  38.0 6.1 %collective-permute-done.6.masked_hbm.first_ref = bf16[256,2048]{1,0:T(8,128)(2,1)} collective-permute-done((bf16[256,2048]{1,0:T(8,128)(2,1)S(1)}, bf16[256,2048]{1,0:T(8,128)(2,1)}, u32[]{:S(2)}, u32[]{:S(2)}) %collective-permute-start.6) | collective-permute-done | bytes 1048608 | tf_op jit(solution)/shard_map/ppermute | solution.py:122
  44.1 148.2 %shard_map.220 = (bf16[8,256,2048]{2,1,0:T(8,128)(2,1)}, bf16[3,8,4,64,256]{4,3,2,1,0:T(8,128)(2,1)}, bf16[1,4,64,2048]{3,2,1,0:T(8,128)(2,1)}, f32[2,2048,256]{...) custom-call(bf16[256,2048]{1,0:T(8,128)(2,1)} %get-tuple-element.84., ...), custom_call_target="tpu_custom_call" | custom-call | flops 8589934592 | bytes 471859200 | tf_op jit(solution)/shard_map/pallas_call | solution.py:1054
  192.3 1.9 multiply_reduce_fusion.2
  194.2 1.3 copy-done
  195.5 1.2 multiply_convert_fusion.normed_ref
  196.7 179.6 %shard_map.221 = (bf16[4,256,2048]{2,1,0:T(8,128)(2,1)}, bf16[256,2048]{1,0:T(8,128)(2,1)}, f32[256,2048]{1,0:T(8,128)}, f32[256,1408]{1,0:T(8,128)}, f32[256,1408]{1,0:T(8,128)}, /*index=5*/f32[256,1408]{1,0:T(8,128)}) custom-call(bf16[256,2048]{1,0:T(8,128)(2,1)} %multiply_convert_fusion.normed_ref, bf16[256,2048]{1,0:T(8,128)(2,1)} %copy-done.9, ...), custom_call_target="tpu_custom_call" | custom-call | flops 53150220288 | bytes 576716800 | tf_op jit(solution)/shard_map/pallas_call | solution.py:736
  376.4 0.0 copy-start.1
  376.4 0.0 copy-start.4
  376.4 3.5 multiply_reduce_fusion
  379.9 0.0 copy-done.4
  379.9 4.0 fusion.2
  383.9 144.4 %shard_map.222 = (f32[256,2048]{1,0:T(8,128)}, f32[3,1,64,2048]{3,2,1,0:T(8,128)}, f32[1,64,2048]{2,1,0:T(8,128)}, f32[8,2048]{1,0:T(8,128)}, bf16[4,256,2048]{2,1,0:T(8,128)(2,1)}) custom-call(bf16[256,2048]{1,0:T(8,128)(2,1)} %get-tuple-element.80.own_ref, bf16[8,256,2048]{2,1,0:T(8,128)(2,1)} %get-tuple-element.37.normed_hbm, ...), custom_call_target="tpu_custom_call" | custom-call | flops 17179869184 | bytes 471859200 | tf_op jit(solution)/shard_map/pallas_call | solution.py:1638
  528.3 0.0 copy-start.8
  528.3 2.6 slice_bitcast_fusion
  531.0 0.9 constant_dynamic-slice_fusion
  531.9 0.5 slice_bitcast_fusion.3
  532.4 1.5 copy.33
  533.9 4.0 fusion
  538.0 1.3 copy.48
  539.3 0.1 copy-done.10
  539.3 0.8 copy.49
  540.1 0.1 copy-done.7
  540.3 1.1 copy.50
  541.4 0.0 copy-done.6
  541.4 1.1 copy.51
  (43 shorter events, 0.3 us)
Async XLA Ops:
  7.2 189.6 %all-gather.3.cloned.1.call-start = ((), (), s32[]{:S(2)}) async-start(), calls=%async_computation | async-start | bytes 6488064 | tf_op jit(solution)/shard_map/all_gather | solution.py:1787
  7.9 12.7 %copy-start.3 = (f32[256,2048]{1,0:T(8,128)S(1)}, f32[256,2048]{1,0:T(8,128)}, u32[]{:S(2)}) copy-start(f32[256,2048]{1,0:T(8,128)} %param.13) | copy-start | bytes 6291460
  7.9 188.8 %all-gather.5.cloned.1.call-start = ((), (), s32[]{:S(2)}) async-start(), calls=%async_computation.1 | async-start | bytes 6488064 | tf_op jit(solution)/shard_map/all_gather | solution.py:1787
  10.1 13.9 %collective-permute-start = (bf16[4,64]{1,0:T(4,128)(2,1)S(1)}, bf16[4,64]{1,0:T(4,128)(2,1)S(1)}, u32[]{:S(2)}, u32[]{:S(2)}) collective-permute-start(bf16[4,64]{1,0:T(4,128)(2,1)S(1)} %pad_maximum_fusion), channel_id=1, source_target_pairs={{0,3},{1,0},{2,1},{3,2},{4,7},{5,4},{6,5},{7,6},{8,11},{9,8},{10,9... | collective-permute-start | bytes 1544 | tf_op jit(solution)/shard_map/ppermute | solution.py:148
  15.2 8.8 %collective-permute-start.1 = (bf16[4,64]{1,0:T(4,128)(2,1)S(1)}, bf16[4,64]{1,0:T(4,128)(2,1)S(1)}, u32[]{:S(2)}, u32[]{:S(2)}) collective-permute-start(bf16[4,64]{1,0:T(4,128)(2,1)S(1)} %pad_maximum_fusion), channel_id=1, source_target_pairs={{0,2},{1,3},{2,0},{3,1},{4,6},{5,7},{6,4},{7,5},{8,10},{9,11},{10,... | collective-permute-start | bytes 1544 | tf_op jit(solution)/shard_map/ppermute | solution.py:148
  15.2 8.8 %collective-permute-start.2 = (bf16[4,64]{1,0:T(4,128)(2,1)S(1)}, bf16[4,64]{1,0:T(4,128)(2,1)S(1)}, u32[]{:S(2)}, u32[]{:S(2)}) collective-permute-start(bf16[4,64]{1,0:T(4,128)(2,1)S(1)} %pad_maximum_fusion), channel_id=1, source_target_pairs={{0,1},{1,2},{2,3},{3,0},{4,5},{5,6},{6,7},{7,4},{8,9},{9,10},{10,1... | collective-permute-start | bytes 1544 | tf_op jit(solution)/shard_map/ppermute | solution.py:148
  18.0 15.0 %copy-start.9 = (bf16[256,2048]{1,0:T(8,128)(2,1)}, bf16[256,2048]{1,0:T(8,128)(2,1)S(1)}, u32[]{:S(2)}) copy-start(bf16[256,2048]{1,0:T(8,128)(2,1)S(1)} %multiply_convert_fusion.2.own_ref) | copy-start | bytes 3145732
  18.0 6.0 %copy-start.11 = (bf16[64]{0:T(256)(128)(2,1)S(1)}, bf16[64]{0:T(256)(128)(2,1)}, u32[]{:S(2)}) copy-start(bf16[64]{0:T(256)(128)(2,1)} %param.17) | copy-start | bytes 388
  18.0 6.0 %copy-start.12 = (bf16[64]{0:T(256)(128)(2,1)S(1)}, bf16[64]{0:T(256)(128)(2,1)}, u32[]{:S(2)}) copy-start(bf16[64]{0:T(256)(128)(2,1)} %param.16) | copy-start | bytes 388
  18.1 6.0 %copy-start.13 = (bf16[64]{0:T(256)(128)(2,1)S(1)}, bf16[64]{0:T(256)(128)(2,1)}, u32[]{:S(2)}) copy-start(bf16[64]{0:T(256)(128)(2,1)} %param.15) | copy-start | bytes 388
  18.1 26.0 %collective-permute-start.6 = (bf16[256,2048]{1,0:T(8,128)(2,1)S(1)}, bf16[256,2048]{1,0:T(8,128)(2,1)}, u32[]{:S(2)}, u32[]{:S(2)}) collective-permute-start(bf16[256,2048]{1,0:T(8,128)(2,1)S(1)} %multiply_convert_fusion.2.own_ref), channel_id=1, source_target_pairs={{0,1},{1,2},{2,3},{3,0},{4,5},{5,6},{6,7},{7,4},{8,9},{9,10},{10,1... | collective-permute-start | bytes 3145736 | tf_op jit(solution)/shard_map/ppermute | solution.py:122
  24.2 3.7 collective-permute-start.3
  27.9 3.7 collective-permute-start.4
  31.7 1.2 collective-permute-start.5
  194.2 1.3 copy-start
  376.4 3.6 copy-start.1
  376.4 3.6 copy-start.4
  528.3 4.1 copy-start.8
  531.0 3.0 copy-start.2
  533.9 4.0 copy-start.5
  538.0 1.4 copy-start.10
  538.0 2.3 copy-start.7
  539.3 2.0 copy-start.6
Sparse Core Ops, SparseCore 0:
  9.9 55.0 all-gather.2
  66.9 54.4 all-gather.4

commit v5 on v4

--- a/solution.py
+++ b/solution.py
@@ -401,7 +401,7 @@
 
 def swiglu_kernel(
     copies,
-    normed_ref, own_ref, first_ref, others_ref, gate_hbm, up_hbm, down_ref,
+    normed_ref, own_ref, below_ref, above_ref, others_ref, gate_hbm, up_hbm, down_ref,
     rows_out, moved_out, norm_sum, gate_sum, up_sum, down_sum,
     normed, masked, gate_w, up_w, down_w, hidden, gate_low, up_low, back, rows, ring_buf,
     one_buf, two_buf, lead, lead_near, in_sem, out_sem, gather_send, gather_recv, send_sem,
@@ -421,12 +421,32 @@
         pltpu.make_async_copy(gate_hbm, gate_w, in_sem.at[1]),
         pltpu.make_async_copy(up_hbm, up_w, in_sem.at[2]),
         pltpu.make_async_copy(own_ref, masked.at[0], in_sem.at[3]),
-        pltpu.make_async_copy(first_ref, masked.at[1], in_sem.at[5]),
-        pltpu.make_async_copy(others_ref, masked.at[pl.ds(2, parts - 2)], in_sem.at[6]),
     ]
     own.wait()
     for load in loads:
         load.start()
+    here = lax.axis_index("tensor")
+    at_start, at_end = here == 0, here == parts - 1
+
+    def load_masked(k, source):
+        return pltpu.make_async_copy(source, masked.at[k], in_sem.at[4 + k])
+
+    for k in range(1, parts):
+        far = load_masked(k, others_ref.at[beside(-k)])
+        if 1 < k < parts - 1:
+            far.start()
+        else:
+            next_to, ref = (at_start, below_ref) if k == 1 else (at_end, above_ref)
+
+            @pl.when(next_to)
+            def _():
+                far.start()
+
+            @pl.when(jnp.logical_not(next_to))
+            def _():
+                load_masked(k, ref).start()
+
+        loads.append(far)
     _, block_rows, width = normed.shape
     hidden_width = hidden.shape[2]
     share = width // 8
@@ -679,8 +699,6 @@
     sum_step(parts - 2)
     for k in (parts - 2, parts - 1):
         store(k).wait()
-    here = lax.axis_index("tensor")
-    at_start, at_end = here == 0, here == parts - 1
     moved_up = along(1, rows_out.at[parts - 1], moved_out, moved_send, moved_recv)
     moved_down = along(-1, rows_out.at[0], moved_out, moved_send, moved_recv)
 
@@ -725,7 +743,7 @@
         moved_up.wait_recv()
 
 
-def swiglu(normed, own, first, others, gate_w, up_w, down_w, copies, collective):
+def swiglu(normed, own, below, above, others, gate_w, up_w, down_w, copies, collective):
     parts = lax.axis_size("tensor")
     rows, width = normed.shape
     hidden = gate_w.shape[2]
@@ -741,7 +759,7 @@
             jax.ShapeDtypeStruct((rows, width), f32),
         ]
         + [jax.ShapeDtypeStruct((share, hidden), f32)] * 3,
-        in_specs=[somewhere] * 7,
+        in_specs=[somewhere] * 8,
         out_specs=[somewhere] * 2 + [vmem] * 4,
         scratch_shapes=[pltpu.VMEM(wide, bf16)] * 2
         + [pltpu.VMEM((8, share, hidden), bf16)] * 3
@@ -753,7 +771,7 @@
         ]
         + [pltpu.VMEM((3, 3, share // 2, hidden), bf16)] * 2
         + [pltpu.VMEM((3, share, hidden), bf16)] * 2
-        + [pltpu.SemaphoreType.DMA((7,)), pltpu.SemaphoreType.DMA((2,))]
+        + [pltpu.SemaphoreType.DMA((8,)), pltpu.SemaphoreType.DMA((2,))]
         + [pltpu.SemaphoreType.DMA((14,))] * 2
         + [pltpu.SemaphoreType.DMA((parts - 1, 2))] * 4
         + [pltpu.SemaphoreType.DMA((3, 4))] * 2
@@ -768,7 +786,7 @@
             bytes_accessed=1100 * rows * width,
             transcendentals=parts * rows * hidden,
         ),
-    )(normed, own, first, others, gate_w, up_w, down_w)
+    )(normed, own, below, above, others, gate_w, up_w, down_w)
 
 
 def greet_all(copies, masks):
@@ -790,13 +808,13 @@
 
 def mixer_forward_kernel(
     copies,
-    own_ref, input_hbm, forget_hbm, gate_hbm, out_hbm, masked_hbm, bound_ref, live_ref,
+    own_ref, input_hbm, forget_hbm, gate_hbm, out_hbm, below_hbm, above_hbm, bound_ref, live_ref,
     normed_out, weights_out, project_out, pre_out, squash_out, state_out, entering_out, mixed_out,
     masked_out, sum_ref,
     normed, weights, project, pre, squashed, forget, state, decay, ends, entering, mixed,
     near_buf, one_buf, two_buf, part_buf,
-    own_sem, gather_send, gather_recv, spread_send, spread_recv, spread_own, ring_send, ring_recv,
-    carry_send, carry_recv, scatter_send, scatter_recv, masked_send, masked_recv, out_sem,
+    own_sem, gather_send, gather_recv, spread_send, spread_recv, spread_own, up_send, down_send, line_recv,
+    carry_send, carry_recv, scatter_send, scatter_recv, masked_up, masked_down, masked_recv, out_sem,
 ):
     parts = lax.axis_size("tensor")
     here = lax.axis_index("tensor")
@@ -833,11 +851,37 @@
             )
         spread.append((kept, sent))
 
-    def ring_copy(kind, k):
-        at = beside(-k)
-        target = project.at[:, at] if kind == 3 else weights.at[kind, :, at]
+    def block_of(kind, block):
+        return project.at[:, block] if kind == 3 else weights.at[kind, :, block]
+
+    def line_copy(kind, k, step):
+        block = here - step * k
+        target = block_of(kind, block)
         source = out_hbm if kind == 3 and k == 0 else target
-        return to_right(source, target, ring_send.at[kind, k], ring_recv.at[kind, k])
+        sems = up_send if step == 1 else down_send
+        return along(step, source, target, sems.at[kind, k], line_recv.at[kind, block])
+
+    def goes(k, step):
+        if step == 1:
+            return jnp.logical_and(here >= k, here < parts - 1)
+        return jnp.logical_and(here + k < parts, here > 0)
+
+    def comes(k, step):
+        return here >= k if step == 1 else here + k < parts
+
+    def line_step(kind, k):
+        for step in (1, -1):
+            if k > 0:
+
+                @pl.when(comes(k, step))
+                def _():
+                    line_copy(kind, k, step).wait_recv()
+
+            if k < parts - 1:
+
+                @pl.when(goes(k, step))
+                def _():
+                    line_copy(kind, k, step).start()
 
     def spread_arrive(kind):
         kept, sent = spread[kind]
@@ -851,30 +895,27 @@
         kept.start()
         for copy in sent:
             copy.start()
-    ring_copy(3, 0).start()
+    line_step(3, 0)
     begin, pass_first, pass_second, pass_last, arrive, finish = plane_gather_steps(
         copies, own_ref, normed, own_sem, gather_send, gather_recv
     )
     begin()
     spread_arrive(0)
-    ring_copy(0, 0).start()
+    line_step(0, 0)
     spread_arrive(1)
-    ring_copy(3, 0).wait_recv()
-    ring_copy(1, 0).start()
+    line_step(1, 0)
     spread_arrive(2)
     pass_first()
-    for k in range(parts - 2):
-        ring_copy(0, k).wait_recv()
-        ring_copy(0, k + 1).start()
-        if k == 0:
-            pass_second()
-        ring_copy(1, k).wait_recv()
-        ring_copy(1, k + 1).start()
-    ring_copy(0, parts - 2).wait_recv()
-    ring_copy(2, 0).start()
+    line_step(0, 1)
+    pass_second()
+    line_step(1, 1)
+    line_step(0, 2)
+    line_step(1, 2)
+    line_step(0, 3)
+    line_step(2, 0)
     pass_last()
-    ring_copy(1, parts - 2).wait_recv()
-    ring_copy(3, 1).start()
+    line_step(1, 3)
+    line_step(3, 1)
     arrive()
 
     many = 2
@@ -898,8 +939,7 @@
         for n in range(strips):
             state[n, some, :] = strip_of(inflow, n)
 
-    ring_copy(2, 0).wait_recv()
-    ring_copy(2, 1).start()
+    line_step(2, 1)
 
     @pl.loop(0, seqs // many)
     def _(at):
@@ -912,8 +952,7 @@
             forget[n, some, :] = strip_of(value, n)
             state[n, some, :] = (1.0 - strip_of(value, n)) * state[n, some, :]
 
-    ring_copy(3, 1).wait_recv()
-    ring_copy(3, 2).start()
+    line_step(3, 2)
 
     def step(at, carry):
         some = pl.ds(at, seqs, stride=rows)
@@ -944,12 +983,30 @@
         )
         copy.start()
         carries.append(copy)
-    ring_copy(2, 1).wait_recv()
-    ring_copy(2, 2).start()
-
-    def masked_copy(k):
-        source = masked_hbm if k == 0 else masked_out.at[k - 1]
-        return to_right(source, masked_out.at[k], masked_send.at[k], masked_recv.at[k])
+    line_step(2, 2)
+
+    def masked_copy(k, step):
+        block = here - step * k
+        if k > 1:
+            source = masked_out.at[block]
+        else:
+            source = below_hbm if step == 1 else above_hbm
+        sems = masked_up if step == 1 else masked_down
+        return along(step, source, masked_out.at[block], sems.at[k], masked_recv.at[block])
+
+    def masked_step(k):
+        for step in (1, -1):
+            if k > 1:
+
+                @pl.when(comes(k, step))
+                def _():
+                    masked_copy(k, step).wait_recv()
+
+            if k < parts - 1:
+
+                @pl.when(goes(k, step))
+                def _():
+                    masked_copy(k, step).start()
 
     for copy in carries:
         copy.wait_recv()
@@ -960,8 +1017,8 @@
         entered = jnp.where(here == k + 1, coming, entered)
     for n in range(seqs):
         entering[n] = entered[n : n + 1]
-    ring_copy(3, 2).wait_recv()
-    ring_copy(2, 2).wait_recv()
+    line_step(3, 3)
+    line_step(2, 3)
 
     @pl.loop(0, seqs // many)
     def _(at):
@@ -1005,28 +1062,36 @@
         right = project[:, :, :, columns]
         return matmul(mixed[slot], right.reshape(channels, right.shape[-1]))
 
-    masked_copy(0).start()
+    masked_step(1)
 
     def between(point):
         if point == "low":
-            for k in range(parts - 3):
-                masked_copy(k).wait_recv()
-                masked_copy(k + 1).start()
+            masked_step(2)
 
     plane_scatter_steps(
         copies, sum_ref, near_buf, one_buf, two_buf, part_buf, scatter_send, scatter_recv,
         out_product, between,
     )
-    masked_copy(parts - 3).wait_recv()
-    for k in range(parts - 2):
-        masked_copy(k).wait_send()
+    masked_step(3)
+    for k in (1, 2):
+        for step in (1, -1):
+
+            @pl.when(goes(k, step))
+            def _():
+                masked_copy(k, step).wait_send()
+
     finish()
     for kept, sent in spread:
         for copy in sent:
             copy.wait_send()
     for kind in range(4):
         for k in range(parts - 1):
-            ring_copy(kind, k).wait_send()
+            for step in (1, -1):
+
+                @pl.when(goes(k, step))
+                def _():
+                    line_copy(kind, k, step).wait_send()
+
     for copy in carries:
         copy.wait_send()
     for store in stores:
@@ -1034,7 +1099,7 @@
 
 
 def mixer_forward(
-    normed, w_input, w_forget, w_gate, w_out, masked, bound, live, copies, collective
+    normed, w_input, w_forget, w_gate, w_out, below, above, bound, live, copies, collective
 ):
     parts = lax.axis_size("tensor")
     rows, width = normed.shape
@@ -1062,10 +1127,10 @@
             jax.ShapeDtypeStruct(strips, f32),
             jax.ShapeDtypeStruct((8, 1, channels), f32),
             jax.ShapeDtypeStruct(shaped, bf16),
-            jax.ShapeDtypeStruct((parts - 2, rows, width), bf16),
+            jax.ShapeDtypeStruct((parts, rows, width), bf16),
             jax.ShapeDtypeStruct((rows, width), f32),
         ],
-        in_specs=[somewhere] * 6 + [vmem] * 2,
+        in_specs=[somewhere] * 7 + [vmem] * 2,
         out_specs=[somewhere] * 9 + [vmem],
         scratch_shapes=[
             pltpu.VMEM(wide, bf16),
@@ -1091,12 +1156,14 @@
             dma((4,)),
             dma((4, parts - 1)),
             dma((4, parts - 1)),
+            dma((4, parts)),
             dma((parts - 1,)),
             dma((parts - 1,)),
             dma((10,)),
             dma((10,)),
-            dma((parts - 2,)),
-            dma((parts - 2,)),
+            dma((parts - 1,)),
+            dma((parts - 1,)),
+            dma((parts,)),
             dma((8,)),
         ],
         compiler_params=pltpu.CompilerParams(
@@ -1107,7 +1174,7 @@
             bytes_accessed=900 * rows * width,
             transcendentals=0,
         ),
-    )(normed, w_input, w_forget, w_gate, w_out, masked, bound, live)
+    )(normed, w_input, w_forget, w_gate, w_out, below, above, bound, live)
 
 
 def mixer_backward_kernel(
@@ -1115,7 +1182,7 @@
     own_ref, normed_hbm, weights_hbm, project_hbm, pre_hbm, squash_hbm, state_hbm, mixed_hbm,
     unit_hbm, stream_hbm, entering_ref, bound_ref, live_ref, gain_ref, scale_ref, gain_two_ref,
     rows_hbm, moved_hbm,
-    result_ref, weight_sums, project_sum, small_sums, moved_out,
+    result_ref, input_sum, forget_sum, gate_sum, project_sum, small_sums, moved_out,
     rows_buf, weights, project, pre, squashed, state, mixed, unit, stream, drive, decay, ends,
     entered, grad_pre, grad_w, grad_project, line_w, line_project, bound_sum, whole_w, spread_w,
     small_recv, small_ring, near_buf, one_buf, two_buf, part_buf,
@@ -1129,6 +1196,7 @@
     strips, _, lanes = drive.shape
     channels = strips * lanes
     own_rows = weights.shape[3]
+    weight_sums = (input_sum, forget_sum, gate_sum)
     near, one, two = copies, 2 * copies, 4 * copies
     mine = slot_of(copies, ())
     greet_all(copies, masks)
@@ -1596,7 +1664,7 @@
             copy.wait_recv()
         spread[-1].wait()
         for slot in range(8):
-            weight_sums[kind, :, :, slot * channels : (slot + 1) * channels] = spread_w[
+            weight_sums[kind][:, :, slot * channels : (slot + 1) * channels] = spread_w[
                 kind, slot
             ].astype(f32)
     for copy in ring_small:
@@ -1639,13 +1707,14 @@
         functools.partial(mixer_backward_kernel, copies, masks),
         out_shape=[
             jax.ShapeDtypeStruct((rows, width), f32),
-            jax.ShapeDtypeStruct((3, copies, own_rows, width), f32),
-            jax.ShapeDtypeStruct((copies, own_rows, width), f32),
+        ]
+        + [jax.ShapeDtypeStruct((copies, own_rows, width), f32)] * 4
+        + [
             jax.ShapeDtypeStruct((8, width), f32),
             jax.ShapeDtypeStruct((4, rows, width), bf16),
         ],
         in_specs=[somewhere] * 10 + [vmem] * 6 + [somewhere] * 2,
-        out_specs=[vmem] * 4 + [somewhere],
+        out_specs=[vmem] * 6 + [somewhere],
         scratch_shapes=[
             pltpu.VMEM(normed.shape, bf16),
             pltpu.VMEM(weights.shape, bf16),
@@ -1765,7 +1834,14 @@
 
     masked_grad = live_own * cotangent
     masked_own = masked_grad.astype(bf16)
-    masked_first = ring(masked_own)
+    masked_below, masked_above = (
+        lax.ppermute(
+            masked_own,
+            "tensor",
+            [(i, i + step) for i in range(tensor_parts) if 0 <= i + step < tensor_parts],
+        )
+        for step in (1, -1)
+    )
 
     scale_one, unit_one = norm_rows(inputs)
     rows_all = group * rows_here
@@ -1773,7 +1849,8 @@
         mixer_forward(
             (unit_one * gain_one).astype(bf16),
             *mixer_weights,
-            masked_first,
+            masked_below,
+            masked_above,
             bound[None, :],
             live,
             copies,
@@ -1794,7 +1871,16 @@
     scale_two, unit_two = norm_rows(stream)
     normed_two = (unit_two * gain_two).astype(bf16)
     out_rows, out_moved, grad_norm_two, *weight_sums = swiglu(
-        normed_two, masked_own, masked_first, masked_others, gate_w, up_w, down_part, copies, 4
+        normed_two,
+        masked_own,
+        masked_below,
+        masked_above,
+        masked_others,
+        gate_w,
+        up_w,
+        down_part,
+        copies,
+        4,
     )
     if copies > 1:
         weight_sums = [
@@ -1808,7 +1894,7 @@
     grad_stream = masked_grad + norm_back(grad_norm_two, unit_two, scale_two, gain_two)
 
     normed_one, mixer_w, out_w, pre, squashed, state, entering = mixer_kept
-    grad_inputs, mixer_sums, out_w_sum, small_sums, out_others = mixer_backward(
+    grad_inputs, *grad_weights, small_sums, out_others = mixer_backward(
         grad_stream.astype(bf16),
         normed_one,
         mixer_w,
@@ -1835,7 +1921,6 @@
     out_sum += jnp.where(tensor_index > 0, out_others[2].astype(f32), 0.0)
     out_sum += jnp.where(tensor_index < tensor_parts - 1, out_others[3].astype(f32), 0.0)
     output = live_own * (stream + out_sum)
-    grad_weights = [mixer_sums[0], mixer_sums[1], mixer_sums[2], out_w_sum]
     if copies > 1:
         grad_weights = [scatter_bits(total, copy_masks, f32) for total in grad_weights]
     grad_weights = [total.reshape(own_rows, width) for total in grad_weights]

time: 553 us -> 547 us (0.989)
  Pallas kernels: 472 us -> 462 us
    pallas_call x1, Pallas kernels: 148 us -> 140 us  [mixer_forward(): pl.pallas_call(functools.partial(mixer_forward_kernel, copies), out_shape...]
    unnamed x42 -> x51, local copies, waits for them, and re-layouts: 11.2 us -> 13.3 us
  transfers between devices with their start and end apart: 9 -> 10, of which waited for: 4 -> 5; matrix products, arithmetic and copies ran while one was open for 3% -> 3% of each run, Pallas kernels for 27% -> 26%
where the time goes in v5:
time: 547 us; the launch traced here: 544 us
  Pallas kernels  462 us (84%)
  other arithmetic  19.7 us (4%)
  local copies, waits for them, and re-layouts  17.2 us (3%)
  starting transfers between devices  16.2 us (3%)
  between operations  15.2 us (3%)
  waiting for transfers between devices  13.9 us (3%)
    pallas_call x1, Pallas kernels, swiglu(): pl.pallas_call(functools.partial(swiglu_kernel, copies), out_shape=[jax.S...  177 us
    pallas_call x1, Pallas kernels, mixer_backward(): pl.pallas_call(functools.partial(mixer_backward_kernel, copies, masks), o...  145 us
    pallas_call x1, Pallas kernels, mixer_forward(): pl.pallas_call(functools.partial(mixer_forward_kernel, copies), out_shape...  140 us
    unnamed x51, local copies, waits for them, and re-layouts  13.3 us
  transfers between devices with their start and end apart: 10, of which 5 were waited for; matrix products, arithmetic and copies ran while one was open for 3% of the time, Pallas kernels for 26%

profile of v5, /device:TPU:0, one launch (start us, length us, event | category | flops | bytes accessed | tf_op | source)
XLA Modules:
  0.0 543.8 jit_solution(3941809709514123120)
XLA Ops:
  7.2 0.0 all-gather.3.cloned.1.call-start
  7.2 0.7 all-gather.3.cloned.1.call-update
  7.9 0.0 all-gather.5.cloned.1.call-start
  8.0 0.7 all-gather.5.cloned.1.call-update
  9.3 0.1 maximum_bitcast_fusion
  9.4 0.7 pad_maximum_fusion
  10.1 5.1 collective-permute-start
  15.2 0.0 collective-permute-start.1
  15.2 1.0 collective-permute-start.2
  16.3 1.8 multiply_convert_fusion.2.own_ref
  18.0 0.0 copy-start.9
  18.0 0.0 copy-start.14
  18.0 0.0 copy-start.15
  18.1 0.0 copy-start.16
  18.1 5.5 %collective-permute-start.6 = (bf16[256,2048]{1,0:T(8,128)(2,1)S(1)}, bf16[256,2048]{1,0:T(8,128)(2,1)}, u32[]{:S(2)}, u32[]{:S(2)}) collective-permute-start(bf16[256,2048]{1,0:T(8,128)(2,1)S(1)} %multiply_convert_fusion.2.own_ref), channel_id=1, source_target_pairs={{0,1},{1,2},{2,3},{4,5},{5,6},{6,7},{8,9},{9,10},{10,11},{12,13},{... | collective-permute-start | bytes 3145736 | tf_op jit(solution)/shard_map/ppermute | solution.py:1838
  23.6 1.3 collective-permute-start.7
  24.9 0.2 multiply_reduce_fusion.3
  25.2 2.2 copy.30
  27.4 0.8 copy.32.scale_ref
  28.2 0.0 collective-permute-done
  28.2 0.0 collective-permute-done.1
  28.2 0.0 collective-permute-done.2
  28.4 1.6 collective-permute-start.3
  30.0 2.1 collective-permute-done.3
  32.1 1.6 collective-permute-start.4
  33.7 2.1 collective-permute-done.4
  35.8 0.1 collective-permute-start.5
  35.9 1.2 collective-permute-done.5
  37.1 0.1 mul.103
  37.2 0.7 broadcast_in_dim_reshape_squeeze.2.gain_ref
  37.9 0.1 copy.28
  38.0 0.1 convert_bitcast_fusion
  38.1 1.3 copy.35
  39.4 0.1 reshape_squeeze.6
  39.5 0.1 mul.112
  39.6 0.6 dynamic_slice.16
  40.2 1.9 multiply_convert_fusion.1
  42.2 2.0 collective-permute-done.6.below_hbm.below_ref
  44.2 5.2 collective-permute-done.7.above_hbm.above_ref
  49.4 140.0 %shard_map.220 = (bf16[8,256,2048]{2,1,0:T(8,128)(2,1)}, bf16[3,8,4,64,256]{4,3,2,1,0:T(8,128)(2,1)}, bf16[1,4,64,2048]{3,2,1,0:T(8,128)(2,1)}, f32[2,2048,256]{...) custom-call(bf16[256,2048]{1,0:T(8,128)(2,1)} %get-tuple-element.88., ...), custom_call_target="tpu_custom_call" | custom-call | flops 8589934592 | bytes 471859200 | tf_op jit(solution)/shard_map/pallas_call | solution.py:1119
  189.3 1.9 multiply_reduce_fusion.2
  191.3 1.3 copy-done
  192.6 1.2 multiply_convert_fusion.normed_ref
  193.8 177.1 %shard_map.221 = (bf16[4,256,2048]{2,1,0:T(8,128)(2,1)}, bf16[256,2048]{1,0:T(8,128)(2,1)}, f32[256,2048]{1,0:T(8,128)}, f32[256,1408]{1,0:T(8,128)}, f32[256,1408]{1,0:T(8,128)}, /*index=5*/f32[256,1408]{1,0:T(8,128)}) custom-call(bf16[256,2048]{1,0:T(8,128)(2,1)} %multiply_convert_fusion.normed_ref, bf16[256,2048]{1,0:T(8,128)(2,1)} %copy-done.9, ...), custom_call_target="tpu_custom_call" | custom-call | flops 53150220288 | bytes 576716800 | tf_op jit(solution)/shard_map/pallas_call | solution.py:754
  370.9 0.0 copy-start.1
  370.9 0.0 copy-start.4
  370.9 3.5 multiply_reduce_fusion
  374.5 0.0 copy-done.1
  374.5 4.0 fusion.2
  378.5 144.5 %shard_map.222 = (f32[256,2048]{1,0:T(8,128)}, f32[1,64,2048]{2,1,0:T(8,128)}, f32[1,64,2048]{2,1,0:T(8,128)}, f32[1,64,2048]{2,1,0:T(8,128)}, f32[1,64,2048]{2,...) custom-call(bf16[256,2048]{1,0:T(8,128)(2,1)} %get-tuple-element.84.own_ref, ...), custom_call_target="tpu_custom_call" | custom-call | flops 17179869184 | bytes 471859200 | tf_op jit(solution)/shard_map/pallas_call | solution.py:1706
  523.0 0.0 copy-start.2
  523.0 0.9 constant_dynamic-slice_fusion
  523.9 0.5 slice_bitcast_fusion
  524.5 1.5 copy.33
  526.0 4.0 fusion
  530.0 0.0 copy-done.5
  530.1 1.3 copy.51
  531.4 0.0 copy-done.13
  531.4 0.8 copy.52
  532.2 0.8 copy.53
  533.0 0.8 copy.54
  533.8 0.8 copy.55
  534.6 1.1 copy.56
  535.7 1.1 copy.57
  (53 shorter events, 0.3 us)
Async XLA Ops:
  7.2 186.6 %all-gather.3.cloned.1.call-start = ((), (), s32[]{:S(2)}) async-start(), calls=%async_computation | async-start | bytes 6488064 | tf_op jit(solution)/shard_map/all_gather | solution.py:1864
  7.9 17.0 %copy-start.3 = (f32[256,2048]{1,0:T(8,128)S(1)}, f32[256,2048]{1,0:T(8,128)}, u32[]{:S(2)}) copy-start(f32[256,2048]{1,0:T(8,128)} %param.13) | copy-start | bytes 6291460
  7.9 185.9 %all-gather.5.cloned.1.call-start = ((), (), s32[]{:S(2)}) async-start(), calls=%async_computation.1 | async-start | bytes 6488064 | tf_op jit(solution)/shard_map/all_gather | solution.py:1864
  10.1 18.1 %collective-permute-start = (bf16[4,64]{1,0:T(4,128)(2,1)S(1)}, bf16[4,64]{1,0:T(4,128)(2,1)S(1)}, u32[]{:S(2)}, u32[]{:S(2)}) collective-permute-start(bf16[4,64]{1,0:T(4,128)(2,1)S(1)} %pad_maximum_fusion), channel_id=1, source_target_pairs={{0,3},{1,0},{2,1},{3,2},{4,7},{5,4},{6,5},{7,6},{8,11},{9,8},{10,9... | collective-permute-start | bytes 1544 | tf_op jit(solution)/shard_map/ppermute | solution.py:148
  15.2 13.0 %collective-permute-start.1 = (bf16[4,64]{1,0:T(4,128)(2,1)S(1)}, bf16[4,64]{1,0:T(4,128)(2,1)S(1)}, u32[]{:S(2)}, u32[]{:S(2)}) collective-permute-start(bf16[4,64]{1,0:T(4,128)(2,1)S(1)} %pad_maximum_fusion), channel_id=1, source_target_pairs={{0,2},{1,3},{2,0},{3,1},{4,6},{5,7},{6,4},{7,5},{8,10},{9,11},{10,... | collective-permute-start | bytes 1544 | tf_op jit(solution)/shard_map/ppermute | solution.py:148
  15.2 13.0 %collective-permute-start.2 = (bf16[4,64]{1,0:T(4,128)(2,1)S(1)}, bf16[4,64]{1,0:T(4,128)(2,1)S(1)}, u32[]{:S(2)}, u32[]{:S(2)}) collective-permute-start(bf16[4,64]{1,0:T(4,128)(2,1)S(1)} %pad_maximum_fusion), channel_id=1, source_target_pairs={{0,1},{1,2},{2,3},{3,0},{4,5},{5,6},{6,7},{7,4},{8,9},{9,10},{10,1... | collective-permute-start | bytes 1544 | tf_op jit(solution)/shard_map/ppermute | solution.py:148
  18.0 19.1 %copy-start.9 = (bf16[256,2048]{1,0:T(8,128)(2,1)}, bf16[256,2048]{1,0:T(8,128)(2,1)S(1)}, u32[]{:S(2)}) copy-start(bf16[256,2048]{1,0:T(8,128)(2,1)S(1)} %multiply_convert_fusion.2.own_ref) | copy-start | bytes 3145732
  18.0 10.2 %copy-start.14 = (bf16[64]{0:T(256)(128)(2,1)S(1)}, bf16[64]{0:T(256)(128)(2,1)}, u32[]{:S(2)}) copy-start(bf16[64]{0:T(256)(128)(2,1)} %param.17) | copy-start | bytes 388
  18.0 10.2 %copy-start.15 = (bf16[64]{0:T(256)(128)(2,1)S(1)}, bf16[64]{0:T(256)(128)(2,1)}, u32[]{:S(2)}) copy-start(bf16[64]{0:T(256)(128)(2,1)} %param.16) | copy-start | bytes 388
  18.1 10.2 %copy-start.16 = (bf16[64]{0:T(256)(128)(2,1)S(1)}, bf16[64]{0:T(256)(128)(2,1)}, u32[]{:S(2)}) copy-start(bf16[64]{0:T(256)(128)(2,1)} %param.15) | copy-start | bytes 388
  18.1 26.1 %collective-permute-start.6 = (bf16[256,2048]{1,0:T(8,128)(2,1)S(1)}, bf16[256,2048]{1,0:T(8,128)(2,1)}, u32[]{:S(2)}, u32[]{:S(2)}) collective-permute-start(bf16[256,2048]{1,0:T(8,128)(2,1)S(1)} %multiply_convert_fusion.2.own_ref), channel_id=1, source_target_pairs={{0,1},{1,2},{2,3},{4,5},{5,6},{6,7},{8,9},{9,10},{10,11},{12,13},{... | collective-permute-start | bytes 3145736 | tf_op jit(solution)/shard_map/ppermute | solution.py:1838
  23.6 25.8 %collective-permute-start.7 = (bf16[256,2048]{1,0:T(8,128)(2,1)S(1)}, bf16[256,2048]{1,0:T(8,128)(2,1)}, u32[]{:S(2)}, u32[]{:S(2)}) collective-permute-start(bf16[256,2048]{1,0:T(8,128)(2,1)S(1)} %multiply_convert_fusion.2.own_ref), channel_id=1, source_target_pairs={{1,0},{2,1},{3,2},{5,4},{6,5},{7,6},{9,8},{10,9},{11,10},{13,12},{... | collective-permute-start | bytes 3145736 | tf_op jit(solution)/shard_map/ppermute | solution.py:1838
  28.4 3.7 collective-permute-start.3
  32.1 3.7 collective-permute-start.4
  35.8 1.3 collective-permute-start.5
  191.2 1.3 copy-start
  370.9 3.6 copy-start.1
  370.9 3.6 copy-start.4
  378.5 146.0 %copy-start.8 = (f32[256,1408]{1,0:T(8,128)S(1)}, f32[256,1408]{1,0:T(8,128)}, u32[]{:S(2)}) copy-start(f32[256,1408]{1,0:T(8,128)} %get-tuple-element.57) | copy-start | bytes 4325380
  523.0 3.0 copy-start.2
  526.0 4.0 copy-start.5
  530.0 1.4 copy-start.13
  530.0 2.2 copy-start.12
  530.0 3.0 copy-start.11
  531.4 2.4 copy-start.10
  531.4 3.2 copy-start.7
  533.8 1.9 copy-start.6
Sparse Core Ops, SparseCore 0:
  9.9 46.1 all-gather.2
  58.0 63.9 all-gather.4

commit v6 on v5

--- a/solution.py
+++ b/solution.py
@@ -224,7 +224,9 @@
     mine = slot_of(copies, ())
     at_one, at_two = slot_of(copies, (one,)), slot_of(copies, (two,))
     at_both = slot_of(copies, (one, two))
-    local = pltpu.make_async_copy(value_ref, all_ref.at[mine], own_sem)
+    local = None
+    if own_sem is not None:
+        local = pltpu.make_async_copy(value_ref, all_ref.at[mine], own_sem)
     sent = []
     last = []
 
@@ -251,7 +253,8 @@
     second = []
 
     def begin():
-        local.start()
+        if local is not None:
+            local.start()
         first.append(send(value_ref.at[top], mine, top, two))
         first.append(send(value_ref.at[low], mine, low, one))
         first.append(send(value_ref.at[low], mine, low, two))
@@ -282,7 +285,7 @@
     def arrive(some=slice(None)):
         for copy in last[some]:
             copy.wait_recv()
-        if some == slice(None):
+        if some == slice(None) and local is not None:
             local.wait()
 
     def finish():
@@ -808,13 +811,14 @@
 
 def mixer_forward_kernel(
     copies,
-    own_ref, input_hbm, forget_hbm, gate_hbm, out_hbm, below_hbm, above_hbm, bound_ref, live_ref,
+    own_ref, input_hbm, forget_hbm, gate_hbm, out_hbm, below_hbm, above_hbm, inputs_hbm, bound_ref,
+    live_ref, gain_ref,
     normed_out, weights_out, project_out, pre_out, squash_out, state_out, entering_out, mixed_out,
-    masked_out, sum_ref,
+    masked_out, stream_ref, following_ref,
     normed, weights, project, pre, squashed, forget, state, decay, ends, entering, mixed,
-    near_buf, one_buf, two_buf, part_buf,
+    near_buf, one_buf, two_buf, part_buf, inputs,
     own_sem, gather_send, gather_recv, spread_send, spread_recv, spread_own, up_send, down_send, line_recv,
-    carry_send, carry_recv, scatter_send, scatter_recv, masked_up, masked_down, masked_recv, out_sem,
+    carry_send, carry_recv, scatter_send, scatter_recv, masked_up, masked_down, masked_recv, out_sem, inputs_sem,
 ):
     parts = lax.axis_size("tensor")
     here = lax.axis_index("tensor")
@@ -889,6 +893,8 @@
         for copy in sent:
             copy.wait_recv()
 
+    inputs_load = pltpu.make_async_copy(inputs_hbm, inputs, inputs_sem)
+    inputs_load.start()
     out_kept = pltpu.make_async_copy(out_hbm, project.at[:, here], spread_own.at[3])
     out_kept.start()
     for kept, sent in spread:
@@ -1069,9 +1075,20 @@
             masked_step(2)
 
     plane_scatter_steps(
-        copies, sum_ref, near_buf, one_buf, two_buf, part_buf, scatter_send, scatter_recv,
+        copies, stream_ref, near_buf, one_buf, two_buf, part_buf, scatter_send, scatter_recv,
         out_product, between,
     )
+
+    inputs_load.wait()
+    some_rows = min(64, rows)
+
+    @pl.loop(0, rows // some_rows)
+    def _(k):
+        some = pl.ds(pl.multiple_of(k * some_rows, some_rows), some_rows)
+        stream = inputs[some, :] + stream_ref[some, :]
+        stream_ref[some, :] = stream
+        following_ref[some, :] = (norm_rows(stream)[1] * gain_ref[...]).astype(bf16)
+
     masked_step(3)
     for k in (1, 2):
         for step in (1, -1):
@@ -1099,7 +1116,8 @@
 
 
 def mixer_forward(
-    normed, w_input, w_forget, w_gate, w_out, below, above, bound, live, copies, collective
+    normed, w_input, w_forget, w_gate, w_out, below, above, inputs, bound, live, gain, copies,
+    collective,
 ):
     parts = lax.axis_size("tensor")
     rows, width = normed.shape
@@ -1129,9 +1147,10 @@
             jax.ShapeDtypeStruct(shaped, bf16),
             jax.ShapeDtypeStruct((parts, rows, width), bf16),
             jax.ShapeDtypeStruct((rows, width), f32),
+            jax.ShapeDtypeStruct((rows, width), bf16),
         ],
-        in_specs=[somewhere] * 7 + [vmem] * 2,
-        out_specs=[somewhere] * 9 + [vmem],
+        in_specs=[somewhere] * 8 + [vmem] * 3,
+        out_specs=[somewhere] * 9 + [vmem] * 2,
         scratch_shapes=[
             pltpu.VMEM(wide, bf16),
             pltpu.VMEM(weights, bf16),
@@ -1148,6 +1167,7 @@
             pltpu.VMEM((3, half, width), bf16),
             pltpu.VMEM((3, half, width), bf16),
             pltpu.VMEM((4, rows, width), bf16),
+            pltpu.VMEM((rows, width), f32),
             dma,
             dma((14,)),
             dma((14,)),
@@ -1165,6 +1185,7 @@
             dma((parts - 1,)),
             dma((parts,)),
             dma((8,)),
+            dma,
         ],
         compiler_params=pltpu.CompilerParams(
             collective_id=collective, has_side_effects=True, vmem_limit_bytes=56 * 1024 * 1024
@@ -1174,21 +1195,21 @@
             bytes_accessed=900 * rows * width,
             transcendentals=0,
         ),
-    )(normed, w_input, w_forget, w_gate, w_out, below, above, bound, live)
+    )(normed, w_input, w_forget, w_gate, w_out, below, above, inputs, bound, live, gain)
 
 
 def mixer_backward_kernel(
     copies, masks,
-    own_ref, normed_hbm, weights_hbm, project_hbm, pre_hbm, squash_hbm, state_hbm, mixed_hbm,
-    unit_hbm, stream_hbm, entering_ref, bound_ref, live_ref, gain_ref, scale_ref, gain_two_ref,
+    norm_hbm, normed_hbm, weights_hbm, project_hbm, pre_hbm, squash_hbm, state_hbm, mixed_hbm,
+    unit_hbm, stream_hbm, cotangent_hbm, entering_ref, bound_ref, live_ref, gain_ref, scale_ref, gain_two_ref,
     rows_hbm, moved_hbm,
     result_ref, input_sum, forget_sum, gate_sum, project_sum, small_sums, moved_out,
     rows_buf, weights, project, pre, squashed, state, mixed, unit, stream, drive, decay, ends,
     entered, grad_pre, grad_w, grad_project, line_w, line_project, bound_sum, whole_w, spread_w,
-    small_recv, small_ring, near_buf, one_buf, two_buf, part_buf,
+    small_recv, small_ring, gain_sum, gain_two_sum, near_buf, one_buf, two_buf, part_buf,
     load_sem, gather_send, gather_recv, carry_send, carry_recv, up_send, down_send, line_recv,
     scatter_send, scatter_recv, spread_send, spread_recv, spread_own, small_send, small_got,
-    moved_sem, moved_send, moved_recv,
+    moved_sem, moved_send, moved_recv, first_sem,
 ):
     parts = lax.axis_size("tensor")
     here = lax.axis_index("tensor")
@@ -1200,10 +1221,17 @@
     near, one, two = copies, 2 * copies, 4 * copies
     mine = slot_of(copies, ())
     greet_all(copies, masks)
+    firsts = [
+        pltpu.make_async_copy(source, target, first_sem.at[n])
+        for n, (source, target) in enumerate(
+            ((norm_hbm, result_ref), (stream_hbm, unit), (cotangent_hbm, stream))
+        )
+    ]
+    for load in firsts:
+        load.start()
     begin, pass_first, pass_second, pass_last, arrive, finish = plane_gather_steps(
-        copies, own_ref, rows_buf, load_sem.at[0], gather_send, gather_recv
+        copies, rows_buf.at[mine], rows_buf, None, gather_send, gather_recv
     )
-    begin()
 
     at_start, at_end = here == 0, here == parts - 1
     inside = jnp.logical_not(jnp.logical_or(at_start, at_end))
@@ -1299,12 +1327,32 @@
                 (squash_hbm, squashed),
                 (weights_hbm, weights),
                 (unit_hbm, unit),
-                (stream_hbm, stream),
             )
         )
     ]
-    for load in loads:
+    for load in loads[:-1]:
         load.start()
+
+    for load in firsts:
+        load.wait()
+    gain_two_sum[...] = jnp.zeros_like(gain_two_sum)
+    some_rows = min(64, rows)
+
+    @pl.loop(0, rows // some_rows)
+    def _(k):
+        some = pl.ds(pl.multiple_of(k * some_rows, some_rows), some_rows)
+        at = pl.ds(pl.multiple_of(mine * rows + k * some_rows, some_rows), some_rows)
+        scale, units = norm_rows(unit[some, :])
+        grad_norm = result_ref[some, :]
+        gain_two_sum[...] += jnp.sum(grad_norm * units, axis=0, keepdims=True)
+        total = live_ref[at, :] * stream[some, :] + norm_back(
+            grad_norm, units, scale, gain_two_ref[...]
+        )
+        stream[some, :] = total
+        rows_buf[mine, some, :] = total.astype(bf16)
+
+    begin()
+    loads[-1].start()
     moved_second()
     for load in loads[:3]:
         load.wait()
@@ -1331,7 +1379,6 @@
     pass_first()
     pass_second()
     arrive(slice(0, 6))
-    pltpu.make_async_copy(own_ref, rows_buf.at[mine], load_sem.at[0]).wait()
     for flips in ((), (near,), (one,), (two,), (near, one), (near, two)):
         take(slot_of(copies, flips))
     moved_last()
@@ -1572,9 +1619,6 @@
             )
 
     advance(3, 1)
-    weight_grad(0)
-    advance(2, 0)
-    weight_grad(1)
     loads[5].wait()
     moved_end()
 
@@ -1592,6 +1636,9 @@
 
     def between(point):
         if point == "sent":
+            weight_grad(0)
+            advance(2, 0)
+            weight_grad(1)
             advance(3, 2)
         elif point == "added":
             advance(2, 1)
@@ -1608,51 +1655,65 @@
         normed_product, between,
     )
 
-    for load in loads[6:]:
-        load.wait()
-    small_sums[...] = jnp.zeros_like(small_sums)
-    small_sums[1:2, :] = gain_two_ref[...]
-    small_sums[2:3, pl.ds(pl.multiple_of(mine * channels, channels), channels)] = bound_sum[...]
-    some_rows = min(64, rows)
+    loads[6].wait()
+    gain_sum[...] = jnp.zeros_like(gain_sum)
 
     @pl.loop(0, rows // some_rows)
     def _(k):
         some = pl.ds(pl.multiple_of(k * some_rows, some_rows), some_rows)
         grad_norm = result_ref[some, :]
         units = unit[some, :]
-        small_sums[0:1, :] += jnp.sum(grad_norm * units, axis=0, keepdims=True)
+        gain_sum[...] += jnp.sum(grad_norm * units, axis=0, keepdims=True)
         scaled = grad_norm * gain_ref[...]
         mean = jnp.mean(scaled * units, axis=-1, keepdims=True)
         result_ref[some, :] = stream[some, :] + scale_ref[some, :] * (scaled - units * mean)
 
+    for n in range(8):
+        columns = slice(n * channels, (n + 1) * channels)
+        small_sums[n : n + 1, :] = gain_sum[:, columns]
+        small_sums[8 + n : 9 + n, :] = gain_two_sum[:, columns]
+        small_sums[16 + n : 17 + n, :] = jnp.where(mine == n, bound_sum[...], 0.0)
+
+    plane_small = []
+    for k in range(1, 8):
+        copy = pltpu.make_async_remote_copy(
+            src_ref=small_sums,
+            dst_ref=small_recv.at[k - 1],
+            send_sem=small_send.at[k - 1],
+            recv_sem=small_got.at[k - 1],
+            device_id={"dp": group_member(copies, k)},
+            device_id_type=pl.DeviceIdType.MESH,
+        )
+        copy.start()
+        plane_small.append(copy)
+
     def small_copy(n):
         return pltpu.make_async_remote_copy(
             src_ref=small_sums,
-            dst_ref=small_recv.at[n],
-            send_sem=small_send.at[n],
-            recv_sem=small_got.at[n],
+            dst_ref=small_recv.at[7 + n],
+            send_sem=small_send.at[7 + n],
+            recv_sem=small_got.at[7 + n],
             device_id={"dp": partner(masks[n])},
             device_id_type=pl.DeviceIdType.MESH,
         )
 
-    def small_step(n):
-        small_copy(n).wait()
-        small_sums[...] += small_recv[n]
-
-    small_copy(0).start()
     advance(0, 2)
     advance(1, 2)
+    for copy in plane_small:
+        copy.wait()
+    for k in range(7):
+        small_sums[...] += small_recv[k]
     for n in range(len(masks)):
-        small_step(n)
-        if n + 1 < len(masks):
-            small_copy(n + 1).start()
+        small_copy(n).start()
+        small_copy(n).wait()
+        small_sums[...] += small_recv[7 + n]
     ring_small = []
     for k in range(1, parts):
         copy = pltpu.make_async_remote_copy(
             src_ref=small_sums,
             dst_ref=small_ring.at[k - 1],
-            send_sem=small_send.at[len(masks) + k - 1],
-            recv_sem=small_got.at[len(masks) + k - 1],
+            send_sem=small_send.at[7 + len(masks) + k - 1],
+            recv_sem=small_got.at[7 + len(masks) + k - 1],
             device_id={"tensor": beside(k)},
             device_id_type=pl.DeviceIdType.MESH,
         )
@@ -1690,8 +1751,8 @@
 
 
 def mixer_backward(
-    own, normed, weights, project, pre, squashed, state, mixed, unit, stream, entering, bound,
-    live, gain, scale, gain_two, out_rows, out_moved, copies, masks, collective,
+    grad_norm, normed, weights, project, pre, squashed, state, mixed, unit, stream, cotangent,
+    entering, bound, live, gain, scale, gain_two, out_rows, out_moved, copies, masks, collective,
 ):
     parts = lax.axis_size("tensor")
     _, rows, width = normed.shape
@@ -1702,7 +1763,7 @@
     half = rows // 2
     dma = pltpu.SemaphoreType.DMA
     blocks = (8 * copies, own_rows, channels)
-    small = pltpu.VMEM((len(masks), 8, width), f32)
+    small = (24, channels)
     return pl.pallas_call(
         functools.partial(mixer_backward_kernel, copies, masks),
         out_shape=[
@@ -1710,10 +1771,10 @@
         ]
         + [jax.ShapeDtypeStruct((copies, own_rows, width), f32)] * 4
         + [
-            jax.ShapeDtypeStruct((8, width), f32),
+            jax.ShapeDtypeStruct(small, f32),
             jax.ShapeDtypeStruct((4, rows, width), bf16),
         ],
-        in_specs=[somewhere] * 10 + [vmem] * 6 + [somewhere] * 2,
+        in_specs=[somewhere] * 11 + [vmem] * 6 + [somewhere] * 2,
         out_specs=[vmem] * 6 + [somewhere],
         scratch_shapes=[
             pltpu.VMEM(normed.shape, bf16),
@@ -1737,8 +1798,10 @@
             pltpu.VMEM((1, channels), f32),
             pltpu.VMEM((3,) + blocks, bf16),
             pltpu.VMEM((3, 8, copies, own_rows, channels), bf16),
-            small,
-            pltpu.VMEM((parts - 1, 8, width), f32),
+            pltpu.VMEM((7 + len(masks),) + small, f32),
+            pltpu.VMEM((parts - 1,) + small, f32),
+            pltpu.VMEM((1, width), f32),
+            pltpu.VMEM((1, width), f32),
             pltpu.VMEM((4, rows, width), bf16),
             pltpu.VMEM((3, half, width), bf16),
             pltpu.VMEM((3, half, width), bf16),
@@ -1756,11 +1819,12 @@
             dma((3, 7)),
             dma((3, 7)),
             dma((3,)),
-            dma((len(masks) + parts - 1,)),
-            dma((len(masks) + parts - 1,)),
+            dma((7 + len(masks) + parts - 1,)),
+            dma((7 + len(masks) + parts - 1,)),
             dma((2,)),
             dma((4,)),
             dma((4,)),
+            dma((3,)),
         ],
         compiler_params=pltpu.CompilerParams(
             collective_id=collective, has_side_effects=True, vmem_limit_bytes=62 * 1024 * 1024
@@ -1771,8 +1835,8 @@
             transcendentals=0,
         ),
     )(
-        own, normed, weights, project, pre, squashed, state, mixed, unit, stream, entering, bound,
-        live, gain, scale, gain_two, out_rows, out_moved,
+        grad_norm, normed, weights, project, pre, squashed, state, mixed, unit, stream, cotangent,
+        entering, bound, live, gain, scale, gain_two, out_rows, out_moved,
     )
 
 
@@ -1832,8 +1896,7 @@
         mixer_weights = [gather_bits(weight, copy_masks[::-1]) for weight in mixer_weights]
     mixer_weights = [weight.reshape(copies, own_rows, width) for weight in mixer_weights]
 
-    masked_grad = live_own * cotangent
-    masked_own = masked_grad.astype(bf16)
+    masked_own = (live_own * cotangent).astype(bf16)
     masked_below, masked_above = (
         lax.ppermute(
             masked_own,
@@ -1845,19 +1908,20 @@
 
     scale_one, unit_one = norm_rows(inputs)
     rows_all = group * rows_here
-    *mixer_kept, mixed, masked_others, mixed_sum = (
+    *mixer_kept, mixed, masked_others, stream, normed_two = (
         mixer_forward(
             (unit_one * gain_one).astype(bf16),
             *mixer_weights,
             masked_below,
             masked_above,
+            inputs,
             bound[None, :],
             live,
+            gain_two[None, :],
             copies,
             1,
         )
     )
-    stream = inputs + mixed_sum
 
     hidden_here = w_gate.shape[1]
     gate_w, up_w = (
@@ -1868,8 +1932,6 @@
     if copies > 1:
         down_part = gather_bits(down_part, copy_masks[::-1]).reshape(channels, hidden_here)
 
-    scale_two, unit_two = norm_rows(stream)
-    normed_two = (unit_two * gain_two).astype(bf16)
     out_rows, out_moved, grad_norm_two, *weight_sums = swiglu(
         normed_two,
         masked_own,
@@ -1890,12 +1952,9 @@
     grad_gate_mine, grad_up_mine, grad_down_mine = weight_sums
     grad_down_mine = grad_down_mine.T
 
-    gain_two_part = jnp.sum(grad_norm_two * unit_two, axis=0)
-    grad_stream = masked_grad + norm_back(grad_norm_two, unit_two, scale_two, gain_two)
-
     normed_one, mixer_w, out_w, pre, squashed, state, entering = mixer_kept
     grad_inputs, *grad_weights, small_sums, out_others = mixer_backward(
-        grad_stream.astype(bf16),
+        grad_norm_two,
         normed_one,
         mixer_w,
         out_w,
@@ -1904,17 +1963,18 @@
         state,
         mixed,
         unit_one,
-        grad_stream,
+        stream,
+        cotangent,
         entering,
         bound[None, :],
         live,
         gain_one[None, :],
         scale_one,
-        gain_two_part[None, :],
+        gain_two[None, :],
         out_rows,
         out_moved,
         copies,
-        all_masks,
+        copy_masks,
         3,
     )
     out_sum = lax.dynamic_index_in_dim(out_rows, tensor_index, 0, keepdims=False).astype(f32)
@@ -1925,7 +1985,7 @@
         grad_weights = [scatter_bits(total, copy_masks, f32) for total in grad_weights]
     grad_weights = [total.reshape(own_rows, width) for total in grad_weights]
     place = (data_index * tensor_parts + tensor_index) * own_rows
-    small_own = lax.dynamic_slice(small_sums, (0, place), (3, own_rows))
+    small_own = lax.dynamic_slice(small_sums.reshape(3, width), (0, place), (3, own_rows))
     return (
         output,
         grad_inputs,

time: 547 us -> 534 us (0.976)
  other arithmetic: 19.7 us -> 8.99 us
    unnamed x51 -> x45, local copies, waits for them, and re-layouts: 13.3 us -> 12 us
  transfers between devices with their start and end apart: 10 -> 10, of which waited for: 5 -> 5; matrix products, arithmetic and copies ran while one was open for 3% -> 2% of each run, Pallas kernels for 26% -> 27%
where the time goes in v6:
time: 534 us; the launch traced here: 531 us
  Pallas kernels  459 us (86%)
  local copies, waits for them, and re-layouts  17.8 us (3%)
  starting transfers between devices  16.2 us (3%)
  between operations  15.2 us (3%)
  waiting for transfers between devices  13.4 us (3%)
  other arithmetic  8.99 us (2%)
    pallas_call x1, Pallas kernels, swiglu(): pl.pallas_call(functools.partial(swiglu_kernel, copies), out_shape=[jax.S...  177 us
    pallas_call x1, Pallas kernels, mixer_forward(): pl.pallas_call(functools.partial(mixer_forward_kernel, copies), out_shape...  141 us
    pallas_call x1, Pallas kernels, mixer_backward(): pl.pallas_call(functools.partial(mixer_backward_kernel, copies, masks), o...  141 us
    unnamed x45, local copies, waits for them, and re-layouts  12 us
  transfers between devices with their start and end apart: 10, of which 5 were waited for; matrix products, arithmetic and copies ran while one was open for 2% of the time, Pallas kernels for 27%

profile of v6, /device:TPU:0, one launch (start us, length us, event | category | flops | bytes accessed | tf_op | source)
XLA Modules:
  0.0 530.7 jit_solution(5176617766445808803)
XLA Ops:
  7.2 0.0 all-gather.3.cloned.1.call-start
  7.2 0.7 all-gather.3.cloned.1.call-update
  7.9 0.0 copy-start
  7.9 0.0 all-gather.5.cloned.1.call-start
  8.0 0.7 all-gather.5.cloned.1.call-update
  9.4 0.1 maximum_bitcast_fusion
  9.4 0.7 pad_maximum_fusion
  10.1 5.1 collective-permute-start
  15.2 0.0 collective-permute-start.1
  15.2 1.0 collective-permute-start.2
  16.3 1.8 multiply_convert_fusion.own_ref
  18.0 0.0 copy-start.6
  18.0 0.0 copy-start.11
  18.0 0.0 copy-start.12
  18.1 0.0 copy-start.13
  18.1 5.5 %collective-permute-start.6 = (bf16[256,2048]{1,0:T(8,128)(2,1)S(1)}, bf16[256,2048]{1,0:T(8,128)(2,1)}, u32[]{:S(2)}, u32[]{:S(2)}) collective-permute-start(bf16[256,2048]{1,0:T(8,128)(2,1)S(1)} %multiply_convert_fusion.own_ref), channel_id=1, source_target_pairs={{0,1},{1,2},{2,3},{4,5},{5,6},{6,7},{8,9},{9,10},{10,11},{12,13},{... | collective-permute-start | bytes 3145736 | tf_op jit(solution)/shard_map/ppermute | solution.py:1901
  23.6 1.3 collective-permute-start.7
  24.9 0.0 copy-done
  24.9 0.2 multiply_reduce_fusion
  25.1 2.2 copy.30
  27.4 0.8 copy.32.scale_ref
  28.2 0.0 collective-permute-done
  28.2 0.0 collective-permute-done.1
  28.2 0.0 collective-permute-done.2
  28.2 0.0 copy-done.11
  28.2 0.0 copy-done.12
  28.3 0.0 copy-done.13
  28.4 1.6 collective-permute-start.3
  30.0 2.1 collective-permute-done.3
  32.0 1.6 collective-permute-start.4
  33.6 2.1 collective-permute-done.4
  35.8 0.1 collective-permute-start.5
  35.9 1.2 collective-permute-done.5
  37.1 0.0 copy-done.6
  37.1 0.1 mul.56
  37.2 0.7 broadcast_in_dim_reshape_squeeze.9.gain_ref
  37.9 0.1 copy.28
  38.0 0.1 convert_bitcast_fusion
  38.1 1.3 copy.35
  39.4 0.1 reshape_squeeze.6
  39.5 0.7 broadcast_in_dim_reshape_squeeze.8.gain_ref.gain_two_ref
  40.2 0.6 dynamic_slice.16
  40.8 1.9 multiply_convert_fusion.1
  42.8 1.4 collective-permute-done.6.below_hbm.below_ref
  44.2 5.2 collective-permute-done.7.above_hbm.above_ref
  49.3 141.1 %shard_map.220 = (bf16[8,256,2048]{2,1,0:T(8,128)(2,1)}, bf16[3,8,4,64,256]{4,3,2,1,0:T(8,128)(2,1)}, bf16[1,4,64,2048]{3,2,1,0:T(8,128)(2,1)}, f32[2,2048,256]{...) custom-call(bf16[256,2048]{1,0:T(8,128)(2,1)} %get-tuple-element.84., ...), custom_call_target="tpu_custom_call" | custom-call | flops 8589934592 | bytes 471859200 | tf_op jit(solution)/shard_map/pallas_call | solution.py:1137
  190.4 0.0 all-gather.3.cloned.1.call-done
  190.4 0.0 all-gather.5.cloned.1.call-done
  190.5 177.3 %shard_map.221 = (bf16[4,256,2048]{2,1,0:T(8,128)(2,1)}, bf16[256,2048]{1,0:T(8,128)(2,1)}, f32[256,2048]{1,0:T(8,128)}, f32[256,1408]{1,0:T(8,128)}, f32[256,1408]{1,0:T(8,128)}, /*index=5*/f32[256,1408]{1,0:T(8,128)}) custom-call(bf16[256,2048]{1,0:T(8,128)(2,1)} %get-tuple-element.37.normed_ref, bf16[256,2048]{1,0:T(8,128)(2,1)} %copy-done.6, ...), custom_call_target="tpu_custom_call" | custom-call | flops 53150220288 | bytes 576716800 | tf_op jit(solution)/shard_map/pallas_call | solution.py:757
  367.8 140.7 %shard_map.222 = (f32[256,2048]{1,0:T(8,128)}, f32[1,64,2048]{2,1,0:T(8,128)}, f32[1,64,2048]{2,1,0:T(8,128)}, f32[1,64,2048]{2,1,0:T(8,128)}, f32[1,64,2048]{2,...) custom-call(f32[256,2048]{1,0:T(8,128)} %get-tuple-element.40.norm_hbm, ...), custom_call_target="tpu_custom_call" | custom-call | flops 17179869184 | bytes 471859200 | tf_op jit(solution)/shard_map/pallas_call | solution.py:1767
  508.5 1.5 reshape.331
  510.0 0.8 constant_dynamic-slice_fusion
  510.8 0.5 slice_bitcast_fusion
  511.3 1.5 copy.33
  512.9 4.0 fusion
  516.9 1.3 copy.51
  518.2 0.0 copy-done.10
  518.3 0.8 copy.52
  519.1 0.0 copy-done.9
  519.1 0.8 copy.53
  519.9 0.8 copy.54
  520.7 0.8 copy.55
  521.5 1.1 copy.56
  522.6 1.1 copy.57
  (42 shorter events, 0.3 us)
Async XLA Ops:
  7.2 183.2 %all-gather.3.cloned.1.call-start = ((), (), s32[]{:S(2)}) async-start(), calls=%async_computation | async-start | bytes 6488064 | tf_op jit(solution)/shard_map/all_gather | solution.py:1928
  7.9 17.0 %copy-start = (f32[256,2048]{1,0:T(8,128)S(1)}, f32[256,2048]{1,0:T(8,128)}, u32[]{:S(2)}) copy-start(f32[256,2048]{1,0:T(8,128)} %inputs_hbm.1) | copy-start | bytes 6291460
  7.9 182.5 %all-gather.5.cloned.1.call-start = ((), (), s32[]{:S(2)}) async-start(), calls=%async_computation.1 | async-start | bytes 6488064 | tf_op jit(solution)/shard_map/all_gather | solution.py:1928
  10.1 18.1 %collective-permute-start = (bf16[4,64]{1,0:T(4,128)(2,1)S(1)}, bf16[4,64]{1,0:T(4,128)(2,1)S(1)}, u32[]{:S(2)}, u32[]{:S(2)}) collective-permute-start(bf16[4,64]{1,0:T(4,128)(2,1)S(1)} %pad_maximum_fusion), channel_id=1, source_target_pairs={{0,3},{1,0},{2,1},{3,2},{4,7},{5,4},{6,5},{7,6},{8,11},{9,8},{10,9... | collective-permute-start | bytes 1544 | tf_op jit(solution)/shard_map/ppermute | solution.py:148
  15.2 13.0 %collective-permute-start.1 = (bf16[4,64]{1,0:T(4,128)(2,1)S(1)}, bf16[4,64]{1,0:T(4,128)(2,1)S(1)}, u32[]{:S(2)}, u32[]{:S(2)}) collective-permute-start(bf16[4,64]{1,0:T(4,128)(2,1)S(1)} %pad_maximum_fusion), channel_id=1, source_target_pairs={{0,2},{1,3},{2,0},{3,1},{4,6},{5,7},{6,4},{7,5},{8,10},{9,11},{10,... | collective-permute-start | bytes 1544 | tf_op jit(solution)/shard_map/ppermute | solution.py:148
  15.2 13.0 %collective-permute-start.2 = (bf16[4,64]{1,0:T(4,128)(2,1)S(1)}, bf16[4,64]{1,0:T(4,128)(2,1)S(1)}, u32[]{:S(2)}, u32[]{:S(2)}) collective-permute-start(bf16[4,64]{1,0:T(4,128)(2,1)S(1)} %pad_maximum_fusion), channel_id=1, source_target_pairs={{0,1},{1,2},{2,3},{3,0},{4,5},{5,6},{6,7},{7,4},{8,9},{9,10},{10,1... | collective-permute-start | bytes 1544 | tf_op jit(solution)/shard_map/ppermute | solution.py:148
  18.0 19.1 %copy-start.6 = (bf16[256,2048]{1,0:T(8,128)(2,1)}, bf16[256,2048]{1,0:T(8,128)(2,1)S(1)}, u32[]{:S(2)}) copy-start(bf16[256,2048]{1,0:T(8,128)(2,1)S(1)} %multiply_convert_fusion.own_ref) | copy-start | bytes 3145732
  18.0 10.2 %copy-start.11 = (bf16[64]{0:T(256)(128)(2,1)S(1)}, bf16[64]{0:T(256)(128)(2,1)}, u32[]{:S(2)}) copy-start(bf16[64]{0:T(256)(128)(2,1)} %param.17) | copy-start | bytes 388
  18.0 10.2 %copy-start.12 = (bf16[64]{0:T(256)(128)(2,1)S(1)}, bf16[64]{0:T(256)(128)(2,1)}, u32[]{:S(2)}) copy-start(bf16[64]{0:T(256)(128)(2,1)} %param.16) | copy-start | bytes 388
  18.1 10.2 %copy-start.13 = (bf16[64]{0:T(256)(128)(2,1)S(1)}, bf16[64]{0:T(256)(128)(2,1)}, u32[]{:S(2)}) copy-start(bf16[64]{0:T(256)(128)(2,1)} %param.15) | copy-start | bytes 388
  18.1 26.1 %collective-permute-start.6 = (bf16[256,2048]{1,0:T(8,128)(2,1)S(1)}, bf16[256,2048]{1,0:T(8,128)(2,1)}, u32[]{:S(2)}, u32[]{:S(2)}) collective-permute-start(bf16[256,2048]{1,0:T(8,128)(2,1)S(1)} %multiply_convert_fusion.own_ref), channel_id=1, source_target_pairs={{0,1},{1,2},{2,3},{4,5},{5,6},{6,7},{8,9},{9,10},{10,11},{12,13},{... | collective-permute-start | bytes 3145736 | tf_op jit(solution)/shard_map/ppermute | solution.py:1901
  23.6 25.8 %collective-permute-start.7 = (bf16[256,2048]{1,0:T(8,128)(2,1)S(1)}, bf16[256,2048]{1,0:T(8,128)(2,1)}, u32[]{:S(2)}, u32[]{:S(2)}) collective-permute-start(bf16[256,2048]{1,0:T(8,128)(2,1)S(1)} %multiply_convert_fusion.own_ref), channel_id=1, source_target_pairs={{1,0},{2,1},{3,2},{5,4},{6,5},{7,6},{9,8},{10,9},{11,10},{13,12},{... | collective-permute-start | bytes 3145736 | tf_op jit(solution)/shard_map/ppermute | solution.py:1901
  28.4 3.7 collective-permute-start.3
  32.0 3.7 collective-permute-start.4
  35.8 1.3 collective-permute-start.5
  367.8 143.5 %copy-start.5 = (f32[256,1408]{1,0:T(8,128)S(1)}, f32[256,1408]{1,0:T(8,128)}, u32[]{:S(2)}) copy-start(f32[256,1408]{1,0:T(8,128)} %get-tuple-element.59) | copy-start | bytes 4325380
  508.5 4.3 copy-start.2
  512.9 4.0 copy-start.1
  516.9 1.4 copy-start.10
  516.9 2.2 copy-start.9
  516.9 3.0 copy-start.8
  518.3 2.4 copy-start.7
  518.3 3.2 copy-start.4
  520.7 1.9 copy-start.3
Sparse Core Ops, SparseCore 0:
  9.9 46.1 all-gather.2
  57.9 63.9 all-gather.4

commit v7 on v6

--- a/solution.py
+++ b/solution.py
@@ -404,7 +404,7 @@
 
 def swiglu_kernel(
     copies,
-    normed_ref, own_ref, below_ref, above_ref, others_ref, gate_hbm, up_hbm, down_ref,
+    normed_ref, own_ref, below_ref, others_ref, gate_hbm, up_hbm, down_ref,
     rows_out, moved_out, norm_sum, gate_sum, up_sum, down_sum,
     normed, masked, gate_w, up_w, down_w, hidden, gate_low, up_low, back, rows, ring_buf,
     one_buf, two_buf, lead, lead_near, in_sem, out_sem, gather_send, gather_recv, send_sem,
@@ -431,25 +431,11 @@
     here = lax.axis_index("tensor")
     at_start, at_end = here == 0, here == parts - 1
 
-    def load_masked(k, source):
-        return pltpu.make_async_copy(source, masked.at[k], in_sem.at[4 + k])
-
     for k in range(1, parts):
-        far = load_masked(k, others_ref.at[beside(-k)])
-        if 1 < k < parts - 1:
-            far.start()
-        else:
-            next_to, ref = (at_start, below_ref) if k == 1 else (at_end, above_ref)
-
-            @pl.when(next_to)
-            def _():
-                far.start()
-
-            @pl.when(jnp.logical_not(next_to))
-            def _():
-                load_masked(k, ref).start()
-
-        loads.append(far)
+        source = below_ref if k == 1 else others_ref.at[beside(-k)]
+        loads.append(pltpu.make_async_copy(source, masked.at[k], in_sem.at[4 + k]))
+        loads[-1].start()
+
     _, block_rows, width = normed.shape
     hidden_width = hidden.shape[2]
     share = width // 8
@@ -746,7 +732,7 @@
         moved_up.wait_recv()
 
 
-def swiglu(normed, own, below, above, others, gate_w, up_w, down_w, copies, collective):
+def swiglu(normed, own, below, others, gate_w, up_w, down_w, copies, collective):
     parts = lax.axis_size("tensor")
     rows, width = normed.shape
     hidden = gate_w.shape[2]
@@ -762,7 +748,7 @@
             jax.ShapeDtypeStruct((rows, width), f32),
         ]
         + [jax.ShapeDtypeStruct((share, hidden), f32)] * 3,
-        in_specs=[somewhere] * 8,
+        in_specs=[somewhere] * 7,
         out_specs=[somewhere] * 2 + [vmem] * 4,
         scratch_shapes=[pltpu.VMEM(wide, bf16)] * 2
         + [pltpu.VMEM((8, share, hidden), bf16)] * 3
@@ -789,7 +775,7 @@
             bytes_accessed=1100 * rows * width,
             transcendentals=parts * rows * hidden,
         ),
-    )(normed, own, below, above, others, gate_w, up_w, down_w)
+    )(normed, own, below, others, gate_w, up_w, down_w)
 
 
 def greet_all(copies, masks):
@@ -811,7 +797,7 @@
 
 def mixer_forward_kernel(
     copies,
-    own_ref, input_hbm, forget_hbm, gate_hbm, out_hbm, below_hbm, above_hbm, inputs_hbm, bound_ref,
+    own_ref, input_hbm, forget_hbm, gate_hbm, out_hbm, masked_hbm, below_hbm, inputs_hbm, bound_ref,
     live_ref, gain_ref,
     normed_out, weights_out, project_out, pre_out, squash_out, state_out, entering_out, mixed_out,
     masked_out, stream_ref, following_ref,
@@ -991,28 +977,59 @@
         carries.append(copy)
     line_step(2, 2)
 
-    def masked_copy(k, step):
-        block = here - step * k
-        if k > 1:
-            source = masked_out.at[block]
+    inner = jnp.logical_and(here > 0, here < parts - 1)
+
+    def masked_down_copy(k):
+        block = here + k
+        source = masked_hbm if k == 0 else masked_out.at[block]
+        return along(-1, source, masked_out.at[block], masked_down.at[k], masked_recv.at[block])
+
+    def masked_up_copy(k):
+        block = here - 1 - k
+        source = below_hbm if k == 0 else masked_out.at[block]
+        return along(1, source, masked_out.at[block], masked_up.at[k], masked_recv.at[block])
+
+    def masked_came(block):
+        along(1, below_hbm, masked_out.at[block], masked_up.at[0], masked_recv.at[block]).wait_recv()
+
+    def masked_step(k):
+        if k == 1:
+
+            @pl.when(here > 0)
+            def _():
+                masked_down_copy(0).start()
+
+            @pl.when(inner)
+            def _():
+                masked_up_copy(0).start()
+
+        elif k == 2:
+
+            @pl.when(here < parts - 1)
+            def _():
+                masked_came(here + 1)
+
+            @pl.when(inner)
+            def _():
+                masked_down_copy(1).start()
+
+            @pl.when(here > 1)
+            def _():
+                masked_came(here - 2)
+
+            @pl.when(here == 2)
+            def _():
+                masked_up_copy(1).start()
+
         else:
-            source = below_hbm if step == 1 else above_hbm
-        sems = masked_up if step == 1 else masked_down
-        return along(step, source, masked_out.at[block], sems.at[k], masked_recv.at[block])
-
-    def masked_step(k):
-        for step in (1, -1):
-            if k > 1:
-
-                @pl.when(comes(k, step))
-                def _():
-                    masked_copy(k, step).wait_recv()
-
-            if k < parts - 1:
-
-                @pl.when(goes(k, step))
-                def _():
-                    masked_copy(k, step).start()
+
+            @pl.when(here < 2)
+            def _():
+                masked_came(here + 2)
+
+            @pl.when(here == parts - 1)
+            def _():
+                masked_came(0)
 
     for copy in carries:
         copy.wait_recv()
@@ -1090,12 +1107,19 @@
         following_ref[some, :] = (norm_rows(stream)[1] * gain_ref[...]).astype(bf16)
 
     masked_step(3)
-    for k in (1, 2):
-        for step in (1, -1):
-
-            @pl.when(goes(k, step))
-            def _():
-                masked_copy(k, step).wait_send()
+
+    @pl.when(here > 0)
+    def _():
+        masked_down_copy(0).wait_send()
+
+    @pl.when(inner)
+    def _():
+        masked_up_copy(0).wait_send()
+        masked_down_copy(1).wait_send()
+
+    @pl.when(here == 2)
+    def _():
+        masked_up_copy(1).wait_send()
 
     finish()
     for kept, sent in spread:
@@ -1116,7 +1140,7 @@
 
 
 def mixer_forward(
-    normed, w_input, w_forget, w_gate, w_out, below, above, inputs, bound, live, gain, copies,
+    normed, w_input, w_forget, w_gate, w_out, masked, below, inputs, bound, live, gain, copies,
     collective,
 ):
     parts = lax.axis_size("tensor")
@@ -1195,7 +1219,7 @@
             bytes_accessed=900 * rows * width,
             transcendentals=0,
         ),
-    )(normed, w_input, w_forget, w_gate, w_out, below, above, inputs, bound, live, gain)
+    )(normed, w_input, w_forget, w_gate, w_out, masked, below, inputs, bound, live, gain)
 
 
 def mixer_backward_kernel(
@@ -1897,14 +1921,7 @@
     mixer_weights = [weight.reshape(copies, own_rows, width) for weight in mixer_weights]
 
     masked_own = (live_own * cotangent).astype(bf16)
-    masked_below, masked_above = (
-        lax.ppermute(
-            masked_own,
-            "tensor",
-            [(i, i + step) for i in range(tensor_parts) if 0 <= i + step < tensor_parts],
-        )
-        for step in (1, -1)
-    )
+    masked_below = ring(masked_own)
 
     scale_one, unit_one = norm_rows(inputs)
     rows_all = group * rows_here
@@ -1912,8 +1929,8 @@
         mixer_forward(
             (unit_one * gain_one).astype(bf16),
             *mixer_weights,
+            masked_own,
             masked_below,
-            masked_above,
             inputs,
             bound[None, :],
             live,
@@ -1936,7 +1953,6 @@
         normed_two,
         masked_own,
         masked_below,
-        masked_above,
         masked_others,
         gate_w,
         up_w,
@@ -1985,7 +2001,11 @@
         grad_weights = [scatter_bits(total, copy_masks, f32) for total in grad_weights]
     grad_weights = [total.reshape(own_rows, width) for total in grad_weights]
     place = (data_index * tensor_parts + tensor_index) * own_rows
-    small_own = lax.dynamic_slice(small_sums.reshape(3, width), (0, place), (3, own_rows))
+    small_own = lax.dynamic_slice(
+        small_sums.reshape(3, 8, channels),
+        (0, lax.div(place, channels), lax.rem(place, channels)),
+        (3, 1, own_rows),
+    )[:, 0]
     return (
         output,
         grad_inputs,

time: 534 us -> 531 us (level)
  transfers between devices with their start and end apart: 10 -> 9, of which waited for: 5 -> 4; matrix products, arithmetic and copies ran while one was open for 2% -> 2% of each run, Pallas kernels for 27% -> 27%
where the time goes in v7:
time: 531 us; the launch traced here: 529 us
  Pallas kernels  464 us (87%)
  local copies, waits for them, and re-layouts  16.9 us (3%)
  between operations  15.2 us (3%)
  waiting for transfers between devices  12.5 us (2%)
  starting transfers between devices  11.7 us (2%)
  other arithmetic  9.13 us (2%)
    pallas_call x1, Pallas kernels, swiglu(): pl.pallas_call(functools.partial(swiglu_kernel, copies), out_shape=[jax.S...  178 us
    pallas_call x1, Pallas kernels, mixer_forward(): pl.pallas_call(functools.partial(mixer_forward_kernel, copies), out_shape...  144 us
    pallas_call x1, Pallas kernels, mixer_backward(): pl.pallas_call(functools.partial(mixer_backward_kernel, copies, masks), o...  141 us
    unnamed x45, local copies, waits for them, and re-layouts  12.5 us
  transfers between devices with their start and end apart: 9, of which 4 were waited for; matrix products, arithmetic and copies ran while one was open for 2% of the time, Pallas kernels for 27%

profile of v7, /device:TPU:0, one launch (start us, length us, event | category | flops | bytes accessed | tf_op | source)
XLA Modules:
  0.0 528.9 jit_solution(2127896087136284821)
XLA Ops:
  7.2 0.0 all-gather.3.cloned.1.call-start
  7.2 0.7 all-gather.3.cloned.1.call-update
  7.9 0.0 all-gather.5.cloned.1.call-start
  8.0 0.7 all-gather.5.cloned.1.call-update
  9.3 0.1 maximum_bitcast_fusion
  9.4 0.7 pad_maximum_fusion
  10.1 5.1 collective-permute-start
  15.2 0.0 collective-permute-start.1
  15.2 1.0 collective-permute-start.2
  16.2 1.9 multiply_convert_fusion.masked_hbm.own_ref
  18.2 0.0 copy-start.6
  18.2 0.0 copy-start.11
  18.2 0.0 copy-start.12
  18.2 0.0 copy-start.13
  18.2 2.5 collective-permute-start.6
  20.7 2.4 copy.30
  23.1 0.0 copy-done
  23.1 0.2 multiply_reduce_fusion
  23.4 0.8 copy.32.scale_ref
  24.2 0.0 collective-permute-done
  24.2 0.0 collective-permute-done.1
  24.2 0.0 collective-permute-done.2
  24.2 0.0 copy-done.11
  24.2 0.0 copy-done.12
  24.2 0.0 copy-done.13
  24.3 1.5 collective-permute-start.3
  25.8 2.3 collective-permute-done.3
  28.1 1.4 collective-permute-start.4
  29.6 2.2 collective-permute-done.4
  31.8 0.1 collective-permute-start.5
  31.9 1.1 collective-permute-done.5
  33.1 0.0 copy-done.6
  33.2 0.1 mul.56
  33.2 0.7 broadcast_in_dim_reshape_squeeze.9.gain_ref
  33.9 0.1 copy.28
  34.0 0.1 convert_bitcast_fusion
  34.1 1.3 copy.35
  35.4 0.1 reshape_squeeze.6
  35.5 0.7 broadcast_in_dim_reshape_squeeze.8.gain_ref.gain_two_ref
  36.2 0.6 dynamic_slice.16
  36.8 1.9 multiply_convert_fusion.1
  38.8 5.5 %collective-permute-done.6.below_hbm.below_ref = bf16[256,2048]{1,0:T(8,128)(2,1)} collective-permute-done((bf16[256,2048]{1,0:T(8,128)(2,1)S(1)}, bf16[256,2048]{1,0:T(8,128)(2,1)}, u32[]{:S(2)}, u32[]{:S(2)}) %collective-permute-start.6) | collective-permute-done | bytes 1048608 | tf_op jit(solution)/shard_map/ppermute | solution.py:122
  44.2 144.4 %shard_map.220 = (bf16[8,256,2048]{2,1,0:T(8,128)(2,1)}, bf16[3,8,4,64,256]{4,3,2,1,0:T(8,128)(2,1)}, bf16[1,4,64,2048]{3,2,1,0:T(8,128)(2,1)}, f32[2,2048,256]{...) custom-call(bf16[256,2048]{1,0:T(8,128)(2,1)} %get-tuple-element.84., ...), custom_call_target="tpu_custom_call" | custom-call | flops 8589934592 | bytes 471859200 | tf_op jit(solution)/shard_map/pallas_call | solution.py:1161
  188.7 0.0 all-gather.3.cloned.1.call-done
  188.7 0.0 all-gather.5.cloned.1.call-done
  188.7 178.2 %shard_map.221 = (bf16[4,256,2048]{2,1,0:T(8,128)(2,1)}, bf16[256,2048]{1,0:T(8,128)(2,1)}, f32[256,2048]{1,0:T(8,128)}, f32[256,1408]{1,0:T(8,128)}, f32[256,1408]{1,0:T(8,128)}, /*index=5*/f32[256,1408]{1,0:T(8,128)}) custom-call(bf16[256,2048]{1,0:T(8,128)(2,1)} %get-tuple-element.37.normed_ref, bf16[256,2048]{1,0:T(8,128)(2,1)} %copy-done.6, ...), custom_call_target="tpu_custom_call" | custom-call | flops 53150220288 | bytes 576716800 | tf_op jit(solution)/shard_map/pallas_call | solution.py:743
  366.9 0.0 copy-start.5
  367.0 140.9 %shard_map.222 = (f32[256,2048]{1,0:T(8,128)}, f32[1,64,2048]{2,1,0:T(8,128)}, f32[1,64,2048]{2,1,0:T(8,128)}, f32[1,64,2048]{2,1,0:T(8,128)}, f32[1,64,2048]{2,...) custom-call(f32[256,2048]{1,0:T(8,128)} %get-tuple-element.40.norm_hbm, ...), custom_call_target="tpu_custom_call" | custom-call | flops 17179869184 | bytes 471859200 | tf_op jit(solution)/shard_map/pallas_call | solution.py:1791
  507.8 0.0 copy-start.2
  507.8 0.0 copy-done.5
  507.8 1.5 copy.33
  509.4 0.4 copy-done.2
  509.8 4.0 fusion
  513.8 1.3 dynamic-slice_bitcast_fusion
  515.1 1.3 copy.51
  516.5 0.0 copy-done.10
  516.5 0.8 copy.52
  517.3 0.8 copy.53
  518.1 0.8 copy.54
  518.9 0.0 copy-done.7
  518.9 0.8 copy.55
  519.6 0.0 copy-done.4
  519.7 1.1 copy.56
  520.8 1.1 copy.57
  (38 shorter events, 0.3 us)
Async XLA Ops:
  7.2 181.5 %all-gather.3.cloned.1.call-start = ((), (), s32[]{:S(2)}) async-start(), calls=%async_computation | async-start | bytes 6488064 | tf_op jit(solution)/shard_map/all_gather | solution.py:1945
  7.9 180.8 %all-gather.5.cloned.1.call-start = ((), (), s32[]{:S(2)}) async-start(), calls=%async_computation.1 | async-start | bytes 6488064 | tf_op jit(solution)/shard_map/all_gather | solution.py:1945
  10.1 14.0 %collective-permute-start = (bf16[4,64]{1,0:T(4,128)(2,1)S(1)}, bf16[4,64]{1,0:T(4,128)(2,1)S(1)}, u32[]{:S(2)}, u32[]{:S(2)}) collective-permute-start(bf16[4,64]{1,0:T(4,128)(2,1)S(1)} %pad_maximum_fusion), channel_id=1, source_target_pairs={{0,3},{1,0},{2,1},{3,2},{4,7},{5,4},{6,5},{7,6},{8,11},{9,8},{10,9... | collective-permute-start | bytes 1544 | tf_op jit(solution)/shard_map/ppermute | solution.py:148
  15.2 9.0 %collective-permute-start.1 = (bf16[4,64]{1,0:T(4,128)(2,1)S(1)}, bf16[4,64]{1,0:T(4,128)(2,1)S(1)}, u32[]{:S(2)}, u32[]{:S(2)}) collective-permute-start(bf16[4,64]{1,0:T(4,128)(2,1)S(1)} %pad_maximum_fusion), channel_id=1, source_target_pairs={{0,2},{1,3},{2,0},{3,1},{4,6},{5,7},{6,4},{7,5},{8,10},{9,11},{10,... | collective-permute-start | bytes 1544 | tf_op jit(solution)/shard_map/ppermute | solution.py:148
  15.2 9.0 %collective-permute-start.2 = (bf16[4,64]{1,0:T(4,128)(2,1)S(1)}, bf16[4,64]{1,0:T(4,128)(2,1)S(1)}, u32[]{:S(2)}, u32[]{:S(2)}) collective-permute-start(bf16[4,64]{1,0:T(4,128)(2,1)S(1)} %pad_maximum_fusion), channel_id=1, source_target_pairs={{0,1},{1,2},{2,3},{3,0},{4,5},{5,6},{6,7},{7,4},{8,9},{9,10},{10,1... | collective-permute-start | bytes 1544 | tf_op jit(solution)/shard_map/ppermute | solution.py:148
  16.2 6.9 %copy-start = (f32[256,2048]{1,0:T(8,128)S(1)}, f32[256,2048]{1,0:T(8,128)}, u32[]{:S(2)}) copy-start(f32[256,2048]{1,0:T(8,128)} %inputs_hbm.1) | copy-start | bytes 6291460
  18.2 15.0 %copy-start.6 = (bf16[256,2048]{1,0:T(8,128)(2,1)}, bf16[256,2048]{1,0:T(8,128)(2,1)S(1)}, u32[]{:S(2)}) copy-start(bf16[256,2048]{1,0:T(8,128)(2,1)S(1)} %multiply_convert_fusion.masked_hbm.own_ref) | copy-start | bytes 3145732
  18.2 6.0 %copy-start.11 = (bf16[64]{0:T(256)(128)(2,1)S(1)}, bf16[64]{0:T(256)(128)(2,1)}, u32[]{:S(2)}) copy-start(bf16[64]{0:T(256)(128)(2,1)} %param.17) | copy-start | bytes 388
  18.2 6.0 %copy-start.12 = (bf16[64]{0:T(256)(128)(2,1)S(1)}, bf16[64]{0:T(256)(128)(2,1)}, u32[]{:S(2)}) copy-start(bf16[64]{0:T(256)(128)(2,1)} %param.16) | copy-start | bytes 388
  18.2 6.0 %copy-start.13 = (bf16[64]{0:T(256)(128)(2,1)S(1)}, bf16[64]{0:T(256)(128)(2,1)}, u32[]{:S(2)}) copy-start(bf16[64]{0:T(256)(128)(2,1)} %param.15) | copy-start | bytes 388
  18.2 26.0 %collective-permute-start.6 = (bf16[256,2048]{1,0:T(8,128)(2,1)S(1)}, bf16[256,2048]{1,0:T(8,128)(2,1)}, u32[]{:S(2)}, u32[]{:S(2)}) collective-permute-start(bf16[256,2048]{1,0:T(8,128)(2,1)S(1)} %multiply_convert_fusion.masked_hbm.own_ref), channel_id=1, source_target_pairs={{0,1},{1,2},{2,3},{3,0},{4,5},{5,6},{6,7},{7,4},{8,9},{9,10},{10,1... | collective-permute-start | bytes 3145736 | tf_op jit(solution)/shard_map/ppermute | solution.py:122
  24.3 3.7 collective-permute-start.3
  28.1 3.7 collective-permute-start.4
  31.8 1.2 collective-permute-start.5
  366.9 140.9 %copy-start.5 = (f32[256,1408]{1,0:T(8,128)S(1)}, f32[256,1408]{1,0:T(8,128)}, u32[]{:S(2)}) copy-start(f32[256,1408]{1,0:T(8,128)} %get-tuple-element.59) | copy-start | bytes 4325380
  507.8 2.0 copy-start.2
  509.8 5.3 %copy-start.1 = (f32[256,2048]{1,0:T(8,128)S(1)}, f32[256,2048]{1,0:T(8,128)}, u32[]{:S(2)}) copy-start(f32[256,2048]{1,0:T(8,128)} %get-tuple-element.106) | copy-start | bytes 6291460
  515.1 1.4 copy-start.10
  515.1 2.1 copy-start.9
  515.1 2.9 copy-start.8
  516.5 2.4 copy-start.7
  516.5 3.2 copy-start.4
  518.9 1.9 copy-start.3
Sparse Core Ops, SparseCore 0:
  9.9 54.9 all-gather.2
  66.8 54.5 all-gather.4

commit v8 on v7

--- a/solution.py
+++ b/solution.py
@@ -946,20 +946,25 @@
 
     line_step(3, 2)
 
+    ahead = 8
+
     def step(at, carry):
-        some = pl.ds(at, seqs, stride=rows)
+        places = [pl.ds(at * ahead + u, seqs, stride=rows) for u in range(ahead)]
+        read = [
+            [(forget[n, some, :], state[n, some, :]) for some in places] for n in range(strips)
+        ]
         following = []
         for n, (total, product) in enumerate(carry):
-            keep = forget[n, some, :]
-            total = keep * total + state[n, some, :]
-            product = product * keep
-            state[n, some, :] = total
-            decay[n, some, :] = product
+            for some, (keep, drive) in zip(places, read[n]):
+                total = keep * total + drive
+                product = product * keep
+                state[n, some, :] = total
+                decay[n, some, :] = product
             following.append((total, product))
         return tuple(following)
 
     start = (jnp.zeros((seqs, lanes), f32), jnp.ones((seqs, lanes), f32))
-    carry = lax.fori_loop(0, rows, step, (start,) * strips, unroll=8)
+    carry = lax.fori_loop(0, rows // ahead, step, (start,) * strips)
     for n, (total, product) in enumerate(carry):
         ends[here, 0, :, n * lanes : (n + 1) * lanes] = total
         ends[here, 1, :, n * lanes : (n + 1) * lanes] = product
@@ -1551,20 +1556,28 @@
     normed_load.start()
     loads[4].wait()
 
+    ahead = 8
+
     def step(k, carry):
-        some = pl.ds(rows - 1 - k, seqs, stride=rows)
+        places = [pl.ds(rows - 1 - u - k * ahead, seqs, stride=rows) for u in range(ahead)]
+        read = [
+            [(squashed[n, some, :], drive[n, some, :]) for some in places] for n in range(strips)
+        ]
         following = []
         for n, (coming, product) in enumerate(carry):
             bound = bound_ref[:, n * lanes : (n + 1) * lanes]
-            keep = bound + (1.0 - bound) * squashed[n, some, :]
-            carried = drive[n, some, :] + coming
-            drive[n, some, :] = carried
-            decay[n, some, :] = product
-            following.append((keep * carried, product * keep))
+            for some, (squash, given) in zip(places, read[n]):
+                keep = bound + (1.0 - bound) * squash
+                carried = given + coming
+                drive[n, some, :] = carried
+                decay[n, some, :] = product
+                coming = keep * carried
+                product = product * keep
+            following.append((coming, product))
         return tuple(following)
 
     start = (jnp.zeros((seqs, lanes), f32), jnp.ones((seqs, lanes), f32))
-    carry = lax.fori_loop(0, rows, step, (start,) * strips, unroll=8)
+    carry = lax.fori_loop(0, rows // ahead, step, (start,) * strips)
     for n, (coming, product) in enumerate(carry):
         ends[here, 0, :, n * lanes : (n + 1) * lanes] = coming
         ends[here, 1, :, n * lanes : (n + 1) * lanes] = product

time: 531 us -> 531 us (level)
  no operation moved by 1% of the time
where the time goes in v8:
time: 531 us; the launch traced here: 529 us
  Pallas kernels  464 us (87%)
  local copies, waits for them, and re-layouts  16.9 us (3%)
  between operations  15.2 us (3%)
  waiting for transfers between devices  12.5 us (2%)
  starting transfers between devices  11.7 us (2%)
  other arithmetic  9.13 us (2%)
    pallas_call x1, Pallas kernels, swiglu(): pl.pallas_call(functools.partial(swiglu_kernel, copies), out_shape=[jax.S...  178 us
    pallas_call x1, Pallas kernels, mixer_forward(): pl.pallas_call(functools.partial(mixer_forward_kernel, copies), out_shape...  144 us
    pallas_call x1, Pallas kernels, mixer_backward(): pl.pallas_call(functools.partial(mixer_backward_kernel, copies, masks), o...  141 us
    unnamed x45, local copies, waits for them, and re-layouts  12.5 us
  transfers between devices with their start and end apart: 9, of which 4 were waited for; matrix products, arithmetic and copies ran while one was open for 2% of the time, Pallas kernels for 27%

profile of v8, /device:TPU:0, one launch (start us, length us, event | category | flops | bytes accessed | tf_op | source)
XLA Modules:
  0.0 528.9 jit_solution(14454619360344118004)
XLA Ops:
  7.2 0.0 all-gather.3.cloned.1.call-start
  7.2 0.7 all-gather.3.cloned.1.call-update
  7.9 0.0 all-gather.5.cloned.1.call-start
  8.0 0.7 all-gather.5.cloned.1.call-update
  9.3 0.1 maximum_bitcast_fusion
  9.4 0.7 pad_maximum_fusion
  10.1 5.1 collective-permute-start
  15.2 0.0 collective-permute-start.1
  15.2 1.0 collective-permute-start.2
  16.2 1.9 multiply_convert_fusion.masked_hbm.own_ref
  18.2 0.0 copy-start.6
  18.2 0.0 copy-start.11
  18.2 0.0 copy-start.12
  18.2 0.0 copy-start.13
  18.2 2.5 collective-permute-start.6
  20.7 2.4 copy.30
  23.1 0.0 copy-done
  23.1 0.2 multiply_reduce_fusion
  23.4 0.8 copy.32.scale_ref
  24.2 0.0 collective-permute-done
  24.2 0.0 collective-permute-done.1
  24.2 0.0 collective-permute-done.2
  24.2 0.0 copy-done.11
  24.2 0.0 copy-done.12
  24.2 0.0 copy-done.13
  24.3 1.5 collective-permute-start.3
  25.8 2.3 collective-permute-done.3
  28.1 1.4 collective-permute-start.4
  29.6 2.2 collective-permute-done.4
  31.8 0.1 collective-permute-start.5
  31.9 1.1 collective-permute-done.5
  33.1 0.0 copy-done.6
  33.2 0.1 mul.56
  33.2 0.7 broadcast_in_dim_reshape_squeeze.9.gain_ref
  33.9 0.1 copy.28
  34.0 0.1 convert_bitcast_fusion
  34.1 1.3 copy.35
  35.4 0.1 reshape_squeeze.6
  35.5 0.7 broadcast_in_dim_reshape_squeeze.8.gain_ref.gain_two_ref
  36.2 0.6 dynamic_slice.16
  36.8 1.9 multiply_convert_fusion.1
  38.8 5.5 %collective-permute-done.6.below_hbm.below_ref = bf16[256,2048]{1,0:T(8,128)(2,1)} collective-permute-done((bf16[256,2048]{1,0:T(8,128)(2,1)S(1)}, bf16[256,2048]{1,0:T(8,128)(2,1)}, u32[]{:S(2)}, u32[]{:S(2)}) %collective-permute-start.6) | collective-permute-done | bytes 1048608 | tf_op jit(solution)/shard_map/ppermute | solution.py:122
  44.2 144.4 %shard_map.220 = (bf16[8,256,2048]{2,1,0:T(8,128)(2,1)}, bf16[3,8,4,64,256]{4,3,2,1,0:T(8,128)(2,1)}, bf16[1,4,64,2048]{3,2,1,0:T(8,128)(2,1)}, f32[2,2048,256]{...) custom-call(bf16[256,2048]{1,0:T(8,128)(2,1)} %get-tuple-element.84., ...), custom_call_target="tpu_custom_call" | custom-call | flops 8589934592 | bytes 471859200 | tf_op jit(solution)/shard_map/pallas_call | solution.py:1166
  188.7 0.0 all-gather.3.cloned.1.call-done
  188.7 0.0 all-gather.5.cloned.1.call-done
  188.7 178.2 %shard_map.221 = (bf16[4,256,2048]{2,1,0:T(8,128)(2,1)}, bf16[256,2048]{1,0:T(8,128)(2,1)}, f32[256,2048]{1,0:T(8,128)}, f32[256,1408]{1,0:T(8,128)}, f32[256,1408]{1,0:T(8,128)}, /*index=5*/f32[256,1408]{1,0:T(8,128)}) custom-call(bf16[256,2048]{1,0:T(8,128)(2,1)} %get-tuple-element.37.normed_ref, bf16[256,2048]{1,0:T(8,128)(2,1)} %copy-done.6, ...), custom_call_target="tpu_custom_call" | custom-call | flops 53150220288 | bytes 576716800 | tf_op jit(solution)/shard_map/pallas_call | solution.py:743
  366.9 0.0 copy-start.5
  367.0 140.9 %shard_map.222 = (f32[256,2048]{1,0:T(8,128)}, f32[1,64,2048]{2,1,0:T(8,128)}, f32[1,64,2048]{2,1,0:T(8,128)}, f32[1,64,2048]{2,1,0:T(8,128)}, f32[1,64,2048]{2,...) custom-call(f32[256,2048]{1,0:T(8,128)} %get-tuple-element.40.norm_hbm, ...), custom_call_target="tpu_custom_call" | custom-call | flops 17179869184 | bytes 471859200 | tf_op jit(solution)/shard_map/pallas_call | solution.py:1804
  507.8 0.0 copy-start.2
  507.8 0.0 copy-done.5
  507.9 1.5 copy.33
  509.4 0.4 copy-done.2
  509.8 4.0 fusion
  513.8 1.3 dynamic-slice_bitcast_fusion
  515.1 0.0 copy-done.1
  515.1 1.3 copy.51
  516.5 0.0 copy-done.10
  516.5 0.8 copy.52
  517.3 0.8 copy.53
  518.1 0.0 copy-done.8
  518.1 0.8 copy.54
  518.9 0.8 copy.55
  519.7 1.1 copy.56
  520.8 1.1 copy.57
  (38 shorter events, 0.3 us)
Async XLA Ops:
  7.2 181.5 %all-gather.3.cloned.1.call-start = ((), (), s32[]{:S(2)}) async-start(), calls=%async_computation | async-start | bytes 6488064 | tf_op jit(solution)/shard_map/all_gather | solution.py:1958
  7.9 180.8 %all-gather.5.cloned.1.call-start = ((), (), s32[]{:S(2)}) async-start(), calls=%async_computation.1 | async-start | bytes 6488064 | tf_op jit(solution)/shard_map/all_gather | solution.py:1958
  10.1 14.0 %collective-permute-start = (bf16[4,64]{1,0:T(4,128)(2,1)S(1)}, bf16[4,64]{1,0:T(4,128)(2,1)S(1)}, u32[]{:S(2)}, u32[]{:S(2)}) collective-permute-start(bf16[4,64]{1,0:T(4,128)(2,1)S(1)} %pad_maximum_fusion), channel_id=1, source_target_pairs={{0,3},{1,0},{2,1},{3,2},{4,7},{5,4},{6,5},{7,6},{8,11},{9,8},{10,9... | collective-permute-start | bytes 1544 | tf_op jit(solution)/shard_map/ppermute | solution.py:148
  15.2 9.0 %collective-permute-start.1 = (bf16[4,64]{1,0:T(4,128)(2,1)S(1)}, bf16[4,64]{1,0:T(4,128)(2,1)S(1)}, u32[]{:S(2)}, u32[]{:S(2)}) collective-permute-start(bf16[4,64]{1,0:T(4,128)(2,1)S(1)} %pad_maximum_fusion), channel_id=1, source_target_pairs={{0,2},{1,3},{2,0},{3,1},{4,6},{5,7},{6,4},{7,5},{8,10},{9,11},{10,... | collective-permute-start | bytes 1544 | tf_op jit(solution)/shard_map/ppermute | solution.py:148
  15.2 9.0 %collective-permute-start.2 = (bf16[4,64]{1,0:T(4,128)(2,1)S(1)}, bf16[4,64]{1,0:T(4,128)(2,1)S(1)}, u32[]{:S(2)}, u32[]{:S(2)}) collective-permute-start(bf16[4,64]{1,0:T(4,128)(2,1)S(1)} %pad_maximum_fusion), channel_id=1, source_target_pairs={{0,1},{1,2},{2,3},{3,0},{4,5},{5,6},{6,7},{7,4},{8,9},{9,10},{10,1... | collective-permute-start | bytes 1544 | tf_op jit(solution)/shard_map/ppermute | solution.py:148
  16.2 6.9 %copy-start = (f32[256,2048]{1,0:T(8,128)S(1)}, f32[256,2048]{1,0:T(8,128)}, u32[]{:S(2)}) copy-start(f32[256,2048]{1,0:T(8,128)} %inputs_hbm.1) | copy-start | bytes 6291460
  18.2 15.0 %copy-start.6 = (bf16[256,2048]{1,0:T(8,128)(2,1)}, bf16[256,2048]{1,0:T(8,128)(2,1)S(1)}, u32[]{:S(2)}) copy-start(bf16[256,2048]{1,0:T(8,128)(2,1)S(1)} %multiply_convert_fusion.masked_hbm.own_ref) | copy-start | bytes 3145732
  18.2 6.0 %copy-start.11 = (bf16[64]{0:T(256)(128)(2,1)S(1)}, bf16[64]{0:T(256)(128)(2,1)}, u32[]{:S(2)}) copy-start(bf16[64]{0:T(256)(128)(2,1)} %param.17) | copy-start | bytes 388
  18.2 6.0 %copy-start.12 = (bf16[64]{0:T(256)(128)(2,1)S(1)}, bf16[64]{0:T(256)(128)(2,1)}, u32[]{:S(2)}) copy-start(bf16[64]{0:T(256)(128)(2,1)} %param.16) | copy-start | bytes 388
  18.2 6.0 %copy-start.13 = (bf16[64]{0:T(256)(128)(2,1)S(1)}, bf16[64]{0:T(256)(128)(2,1)}, u32[]{:S(2)}) copy-start(bf16[64]{0:T(256)(128)(2,1)} %param.15) | copy-start | bytes 388
  18.2 26.0 %collective-permute-start.6 = (bf16[256,2048]{1,0:T(8,128)(2,1)S(1)}, bf16[256,2048]{1,0:T(8,128)(2,1)}, u32[]{:S(2)}, u32[]{:S(2)}) collective-permute-start(bf16[256,2048]{1,0:T(8,128)(2,1)S(1)} %multiply_convert_fusion.masked_hbm.own_ref), channel_id=1, source_target_pairs={{0,1},{1,2},{2,3},{3,0},{4,5},{5,6},{6,7},{7,4},{8,9},{9,10},{10,1... | collective-permute-start | bytes 3145736 | tf_op jit(solution)/shard_map/ppermute | solution.py:122
  24.3 3.7 collective-permute-start.3
  28.1 3.7 collective-permute-start.4
  31.8 1.2 collective-permute-start.5
  366.9 140.9 %copy-start.5 = (f32[256,1408]{1,0:T(8,128)S(1)}, f32[256,1408]{1,0:T(8,128)}, u32[]{:S(2)}) copy-start(f32[256,1408]{1,0:T(8,128)} %get-tuple-element.59) | copy-start | bytes 4325380
  507.8 2.0 copy-start.2
  509.8 5.3 %copy-start.1 = (f32[256,2048]{1,0:T(8,128)S(1)}, f32[256,2048]{1,0:T(8,128)}, u32[]{:S(2)}) copy-start(f32[256,2048]{1,0:T(8,128)} %get-tuple-element.106) | copy-start | bytes 6291460
  515.1 1.4 copy-start.10
  515.1 2.1 copy-start.9
  515.1 2.9 copy-start.8
  516.5 2.4 copy-start.7
  516.5 3.2 copy-start.4
  518.9 1.9 copy-start.3
Sparse Core Ops, SparseCore 0:
  9.9 54.9 all-gather.2
  66.8 54.5 all-gather.4
